TPU v7x, 256 devices: a whole 4x4x8 slice. The times are simulated.
256 devices in a mesh: pipe: 8 (over z), tile: 32 (over x, y, core).
Axes of the slice: x: 4, y: 4, z: 8, core: 2. Of those that a mesh axis runs over, the one named last changes fastest.
Arguments:
- x_next: bfloat16 [8, 4096, 8192], P('pipe', 'tile'), may hold values from -6 to 6
- x_saved: bfloat16 [8, 4096, 8192], P('pipe', 'tile'), may hold values from -6 to 6
- pending: bfloat16 [8, 4096, 8192], P('pipe', 'tile'), may hold values from -6 to 6
- gu_rows: int32 [8, 32, 1], P('pipe'), may hold values from 0 to 63, as said below
- gu_cols: int32 [8, 32, 1], P('pipe'), may hold values from 0 to 111
- gu_live: int32 [8, 32], P('pipe'), may hold values from 1 to 1, as said below
- down_rows: int32 [8, 32, 1], P('pipe'), may hold values from 0 to 111, as said below
- down_cols: int32 [8, 32, 1], P('pipe'), may hold values from 0 to 63
- down_live: int32 [8, 32], P('pipe'), may hold values from 1 to 1, as said below
- gate_up_tiles: bfloat16 [8, 32, 1, 2, 128, 128], P('pipe', 'tile'), may hold values from -0.5 to 0.5
- down_tiles: bfloat16 [8, 32, 1, 128, 128], P('pipe', 'tile'), may hold values from -0.5 to 0.5
Outputs:
- y_next: bfloat16 [8, 4096, 8192], P('pipe', 'tile')
- dx_saved: bfloat16 [8, 4096, 8192], P('pipe', 'tile')
- grad_gate_up: float32 [8, 32, 1, 2, 128, 128], P('pipe', 'tile')
- grad_down: float32 [8, 32, 1, 128, 128], P('pipe', 'tile')
Inputs may be any that keep to these rules, and one draw needn't show every extreme that they name: Within a section the 32 x 1 slots of the gate and up lists name distinct tiles (gu_rows, gu_cols). Within a section the 32 x 1 slots of the down list name distinct tiles (down_rows, down_cols). `gu_live`: in every section some owner has all 1 slots live. `down_live`: in every section some owner has all 1 slots live.
All inputs are finite; a program needn't handle non-finite values.
Results may differ from a plain program's by a relative error of at most 0.0067.
Values may be sent and summed in bfloat16 or wider, within the bound.
No kernel may reach another device: no remote copies, remote signals or barrier semaphores. Data moves between devices by JAX's collectives and lax.ppermute only.
A program may use at most 128 MiB of HBM per device.

v0:
```python
import functools

import jax
import jax.numpy as jnp
from jax import lax
from jax.experimental import pallas as pl
from jax.experimental.pallas import tpu as pltpu
from jax.sharding import PartitionSpec as P

B = 128
F32 = jnp.float32
BF16 = jnp.bfloat16
ROWS, LEAD, FIRST, HSLOT, DCOLS = range(5)


def loop(count, unroll, body):
    def group(i, carry):
        body([i * unroll + u for u in range(unroll)])
        return carry

    lax.fori_loop(0, count // unroll, group, 0)


def cols(block_index):
    return pl.ds(pl.multiple_of(block_index * B, B), B)


def rounded(value):
    return value.astype(BF16).astype(F32)


def dot(a, b, contract_a, contract_b):
    return lax.dot_general(
        a, b, (((contract_a,), (contract_b,)), ((), ())), preferred_element_type=F32
    )


def vmem(value):
    return pltpu.with_memory_space_constraint(value, pltpu.VMEM)


def call(body, outs, scratch, args, limit, flops=0):
    specs = [pl.BlockSpec(memory_space=pltpu.SMEM)] + [
        pl.BlockSpec(memory_space=pltpu.VMEM) for _ in args[1:]
    ]
    out = pl.pallas_call(
        body,
        out_shape=[o for o, _ in outs],
        in_specs=specs,
        out_specs=[pl.BlockSpec(memory_space=pltpu.VMEM) for _ in outs],
        scratch_shapes=scratch,
        compiler_params=pltpu.CompilerParams(vmem_limit_bytes=limit << 20),
        cost_estimate=pl.CostEstimate(flops=flops, bytes_accessed=1 << 20, transcendentals=0),
    )(args[0], *[vmem(a) for a in args[1:]])
    return out


def out_vmem(shape, dtype):
    return (pltpu.VMEM(shape, dtype), True)


def out_hbm(shape, dtype):
    return (jax.ShapeDtypeStruct(shape, dtype), False)


def pick_kernel(n, tab, pending, out):
    for k in range(n):
        out[k] = pending[0, :, cols(tab[DCOLS, k])]


def forward_kernel(n, tab, x_next, x_saved, w, coef, h_saved, y, acc, h_next, y_acc):
    def project(ks):
        parts = []
        for k in ks:
            at = cols(tab[ROWS, k])
            x = jnp.concatenate([x_next[0, :, at], x_saved[0, :, at]], axis=0)
            parts.append(rounded(dot(x, w[k, :, : 2 * B], 1, 0)))
        for k, part in zip(ks, parts):
            lead = tab[LEAD, k]
            acc[lead] = jnp.where(tab[FIRST, k] == 1, part, acc[lead] + part)

    loop(n, 4, project)

    def activate(ks):
        for k in ks:

            @pl.when(tab[FIRST, k] == 1)
            def _():
                gate, up = acc[k, :B, :B], acc[k, :B, B:]
                h_next[k] = (gate * jax.nn.sigmoid(gate) * up).astype(BF16)
                gate, up = acc[k, B:, :B], acc[k, B:, B:]
                sig = jax.nn.sigmoid(gate)
                act = gate * sig
                h_saved[k] = (act * up).astype(BF16)
                coef[k, :, :B] = up * sig * (1.0 + gate * (1.0 - sig))
                coef[k, :, B:] = act

    loop(n, 1, activate)
    h_next[n] = jnp.zeros((B, B), BF16)
    h_saved[n] = jnp.zeros((B, B), BF16)
    y_acc[...] = jnp.zeros_like(y_acc)

    def down(js):
        parts = [rounded(dot(h_next[tab[HSLOT, j]], w[j, :, 2 * B :], 1, 0)) for j in js]
        for j, part in zip(js, parts):
            y_acc[tab[DCOLS, j]] += part

    loop(n, 4, down)
    for c in range(y_acc.shape[0]):
        y[0, :, c * B : (c + 1) * B] = y_acc[c].astype(BF16)


def backward_kernel(n, tab, x_saved, w, coef, h_saved, cot, parts_out, d_gu, dh):
    dh[...] = jnp.zeros_like(dh)

    def down(js):
        parts = []
        for j in js:
            c = cot[j]
            parts.append(rounded(dot(c, w[j, :, 2 * B :], 1, 1)))
            parts_out[j, :, 2 * B :] = dot(h_saved[tab[HSLOT, j]], c, 0, 0).astype(BF16)
        for j, part in zip(js, parts):
            dh[tab[HSLOT, j]] += part

    loop(n, 4, down)

    def scale(ks):
        for k in ks:

            @pl.when(tab[FIRST, k] == 1)
            def _():
                d_gu[k, :, :B] = (dh[k] * coef[k, :, :B]).astype(BF16)
                d_gu[k, :, B:] = (dh[k] * coef[k, :, B:]).astype(BF16)

    loop(n, 1, scale)

    def grads(ks):
        for k in ks:
            x = x_saved[0, :, cols(tab[ROWS, k])]
            parts_out[k, :, : 2 * B] = dot(x, d_gu[tab[LEAD, k]], 0, 0).astype(BF16)

    loop(n, 4, grads)


def dx_kernel(n, tab, d_gu, w, dx, acc):
    acc[...] = jnp.zeros_like(acc)

    def back(ks):
        parts = [rounded(dot(d_gu[tab[LEAD, k]], w[k, :, : 2 * B], 1, 1)) for k in ks]
        for k, part in zip(ks, parts):
            acc[tab[ROWS, k]] += part

    loop(n, 4, back)
    for c in range(acc.shape[0]):
        dx[0, :, c * B : (c + 1) * B] = acc[c].astype(BF16)


def total_kernel(n, tab, got, grad_gu, grad_down):
    total = got[0].astype(F32)
    for k in range(1, n):
        total += got[k].astype(F32)
    g_live = tab[0, 0].astype(F32)
    d_live = tab[0, 1].astype(F32)
    grad_gu[0, 0, 0, 0] = total[:, :B] * g_live
    grad_gu[0, 0, 0, 1] = total[:, B : 2 * B] * g_live
    grad_down[0, 0, 0] = total[:, 2 * B :] * d_live


def tables(g_rows, g_cols, d_rows, d_cols):
    n = g_rows.shape[0]
    ids = jnp.arange(n, dtype=jnp.int32)
    lead = jnp.min(jnp.where(g_cols[:, None] == g_cols[None, :], ids[None, :], n), axis=1)
    first = (lead == ids).astype(jnp.int32)
    hslot = jnp.min(jnp.where(d_rows[:, None] == g_cols[None, :], ids[None, :], n), axis=1)
    return jnp.stack([g_rows, lead, first, hslot, d_cols])


def per_device(
    x_next,
    x_saved,
    pending,
    gu_rows,
    gu_cols,
    gu_live,
    down_rows,
    down_cols,
    down_live,
    gate_up_tiles,
    down_tiles,
):
    n = lax.axis_size("tile")
    sections = lax.axis_size("pipe")
    mine = lax.axis_index("tile")
    width = x_next.shape[2]
    blocks = width // B
    tok = x_next.shape[1]
    partial = functools.partial

    g_live = (lax.dynamic_index_in_dim(gu_live[0], mine, 0, keepdims=False) > 0).astype(jnp.int32)
    d_live = (lax.dynamic_index_in_dim(down_live[0], mine, 0, keepdims=False) > 0).astype(jnp.int32)
    live = jnp.stack([g_live, d_live])[None, :]
    tab = tables(
        gu_rows[0].reshape(-1), gu_cols[0].reshape(-1), down_rows[0].reshape(-1), down_cols[0].reshape(-1)
    )

    own = jnp.concatenate(
        [
            gate_up_tiles[0, 0, 0, 0] * g_live.astype(BF16),
            gate_up_tiles[0, 0, 0, 1] * g_live.astype(BF16),
            down_tiles[0, 0, 0] * d_live.astype(BF16),
        ],
        axis=1,
    )
    w = lax.all_gather(own, "tile")

    up_pairs = [(s, (s + 1) % sections) for s in range(sections)]
    down_pairs = [(s, (s - 1) % sections) for s in range(sections)]
    asked = lax.ppermute(tab, "pipe", up_pairs)
    [picked] = call(
        partial(pick_kernel, n), [out_vmem((n, tok, B), BF16)], [], [asked, pending], 8
    )
    cot = lax.ppermute(picked, "pipe", down_pairs)

    coef, h_saved, y = call(
        partial(forward_kernel, n),
        [
            out_vmem((n, tok, 2 * B), F32),
            out_vmem((n + 1, tok, B), BF16),
            out_hbm((1, tok, width), BF16),
        ],
        [
            pltpu.VMEM((n, 2 * tok, 2 * B), F32),
            pltpu.VMEM((n + 1, tok, B), BF16),
            pltpu.VMEM((blocks, tok, B), F32),
        ],
        [tab, x_next, x_saved, w],
        24,
    )
    parts, d_gu = call(
        partial(backward_kernel, n),
        [out_vmem((n, B, 3 * B), BF16), out_vmem((n, tok, 2 * B), BF16)],
        [pltpu.VMEM((n + 1, tok, B), F32)],
        [tab, x_saved, w, coef, h_saved, cot],
        24,
    )
    got = lax.all_to_all(parts, "tile", 0, 0, tiled=True)
    [dx] = call(
        partial(dx_kernel, n),
        [out_hbm((1, tok, width), BF16)],
        [pltpu.VMEM((blocks, tok, B), F32)],
        [tab, d_gu, w],
        24,
    )
    grad_gu, grad_down = call(
        partial(total_kernel, n),
        [out_hbm((1, 1, 1, 2, B, B), F32), out_hbm((1, 1, 1, B, B), F32)],
        [],
        [live, got],
        24,
    )
    return (y, dx, grad_gu, grad_down)


def solution(mesh):
    placed = (
        P("pipe", "tile", None),
        P("pipe", "tile", None),
        P("pipe", "tile", None),
        P("pipe", None, None),
        P("pipe", None, None),
        P("pipe", None),
        P("pipe", None, None),
        P("pipe", None, None),
        P("pipe", None),
        P("pipe", "tile", None, None, None, None),
        P("pipe", "tile", None, None, None),
    )
    return jax.shard_map(
        per_device,
        mesh=mesh,
        in_specs=placed,
        out_specs=(
            P("pipe", "tile", None),
            P("pipe", "tile", None),
            P("pipe", "tile", None, None, None, None),
            P("pipe", "tile", None, None, None),
        ),
        check_vma=False,
    )
```

profile of v0, /device:TPU:6, one launch (start us, length us, event | category | flops | bytes accessed | tf_op | source)
XLA Modules:
  0.0 142.3 jit_solution(13487002041074962920)
XLA Ops:
  7.2 0.0 all-gather.3.cloned.1.call-start
  7.2 1.3 fusion
  9.8 0.8 multiply_bitcast_fusion
  10.6 0.8 multiply_bitcast_fusion.2
  11.3 0.7 pad_maximum_fusion
  12.0 0.0 all-gather.3.cloned.1.call-update
  12.0 0.9 select_reduce_fusion
  12.9 0.7 stack.21.tab
  13.6 2.0 %collective-permute-start = (s32[5,32]{1,0:T(8,128)S(1)}, s32[5,32]{1,0:T(8,128)S(1)}, u32[]{:S(2)}, u32[]{:S(2)}) collective-permute-start(s32[5,32]{1,0:T(8,128)S(1)} %stack.21.tab), channel_id=1, source_target_pairs={{0,32},{32,64},{64,96},{96,128},{128,160},{160,192},{192,224},{224... | collective-permute-start | bytes 1928 | tf_op jit(solution)/shard_map/ppermute | solution.py:218
  15.6 5.5 %collective-permute-done.tab = s32[5,32]{1,0:T(8,128)S(1)} collective-permute-done((s32[5,32]{1,0:T(8,128)S(1)}, s32[5,32]{1,0:T(8,128)S(1)}, u32[]{:S(2)}, u32[]{:S(2)}) %collective-permute-start) | collective-permute-done | bytes 672 | tf_op jit(solution)/shard_map/ppermute | solution.py:218
  21.1 0.0 copy-start.7
  21.1 1.6 %copy-done.7 = bf16[1,128,8192]{2,1,0:T(8,128)(2,1)S(1)} copy-done((bf16[1,128,8192]{2,1,0:T(8,128)(2,1)S(1)}, bf16[1,128,8192]{2,1,0:T(8,128)(2,1)}, u32[]{:S(2)}) %copy-start.7) | copy-done | bytes 2097176
  22.7 1.8 %shard_map.139 = bf16[32,128,128]{2,1,0:T(8,128)(2,1)} custom-call(s32[5,32]{1,0:T(8,128)S(1)} %collective-permute-done.tab, bf16[1,128,8192]{2,1,0:T(8,128)(2,1)S(1)} %copy-done.7), custom_call_target="tpu_custom_call" | custom-call | bytes 1048576 | tf_op jit(solution)/shard_map/pallas_call | solution.py:46
  24.6 2.0 %collective-permute-start.1 = (bf16[32,128,128]{2,1,0:T(8,128)(2,1)}, bf16[32,128,128]{2,1,0:T(8,128)(2,1)}, u32[]{:S(2)}, u32[]{:S(2)}) collective-permute-start(bf16[32,128,128]{2,1,0:T(8,128)(2,1)} %shard_map.139), channel_id=1, source_target_pairs={{0,224},{32,0},{64,32},{96,64},{128,96},{160,128},{192,160},{224,1... | collective-permute-start | bytes 3145736 | tf_op jit(solution)/shard_map/ppermute | solution.py:222
  26.6 38.2 %all-gather.3.cloned.1.call-done = bf16[4096,384]{1,0:T(8,128)(2,1)} async-done(((bf16[128,384]{1,0:T(8,128)(2,1)}), bf16[4096,384]{1,0:T(8,128)(2,1)}) %all-gather.3.cloned.1.call-update) | async-done | bytes 3145744 | tf_op jit(solution)/shard_map/all_gather | solution.py:214
  64.8 0.0 copy-start
  64.8 1.9 %copy-done = bf16[4096,384]{1,0:T(8,128)(2,1)S(1)} copy-done((bf16[4096,384]{1,0:T(8,128)(2,1)S(1)}, bf16[4096,384]{1,0:T(8,128)(2,1)}, u32[]{:S(2)}) %copy-start) | copy-done | bytes 3145752
  66.6 0.0 copy-start.2
  66.6 1.6 %copy-done.2 = bf16[1,128,8192]{2,1,0:T(8,128)(2,1)S(1)} copy-done((bf16[1,128,8192]{2,1,0:T(8,128)(2,1)S(1)}, bf16[1,128,8192]{2,1,0:T(8,128)(2,1)}, u32[]{:S(2)}) %copy-start.2) | copy-done | bytes 2097176
  68.2 0.0 copy-start.4
  68.2 1.6 %copy-done.4 = bf16[1,128,8192]{2,1,0:T(8,128)(2,1)S(1)} copy-done((bf16[1,128,8192]{2,1,0:T(8,128)(2,1)S(1)}, bf16[1,128,8192]{2,1,0:T(8,128)(2,1)}, u32[]{:S(2)}) %copy-start.4) | copy-done | bytes 2097176
  69.8 0.0 copy-start.1
  69.8 8.3 %shard_map.138 = (f32[32,128,256]{2,1,0:T(8,128)S(1)}, bf16[33,128,128]{2,1,0:T(8,128)(2,1)S(1)}, bf16[1,128,8192]{2,1,0:T(8,128)(2,1)}) custom-call(s32[5,32]{1,0:T(8,128)S(1)} %stack.21.tab, bf16[1,128,8192]{2,1,0:T(8,128)(2,1)S(1)} %copy-done.4, bf16[1,128,8192]{2,1,0:T(8,128)(2,1)S(1)} %copy-done.2, bf16[32,128,384]{2,1,0:T(8,128)(2,1)S(1)} %bitcast.20), custom_call_target="tpu_custom_call" | custom-call | bytes 1048576 | tf_op jit(solution)/shard_map/pallas_call | solution.py:46
  78.2 0.0 collective-permute-done.1.cot
  78.2 0.0 copy-done.1
  78.2 6.7 %shard_map.140 = (bf16[32,128,384]{2,1,0:T(8,128)(2,1)S(1)}, bf16[32,128,256]{2,1,0:T(8,128)(2,1)S(1)}) custom-call(s32[5,32]{1,0:T(8,128)S(1)} %stack.21.tab, bf16[1,128,8192]{2,1,0:T(8,128)(2,1)S(1)} %copy-done.2, bf16[32,128,384]{2,1,0:T(8,128)(2,1)S(1)} %bitcast.21, f32[32,128,256]{2,1,0:T(8,128)S(1)} %get-tuple-element.12.coef, ...), custom_call_target="tpu_custom_call" | custom-call | bytes 1048576 | tf_op jit(solution)/shard_map/pallas_call | solution.py:46
  84.9 0.0 copy-start.3
  84.9 1.7 %copy-done.3 = bf16[32,128,384]{2,1,0:T(8,128)(2,1)} copy-done((bf16[32,128,384]{2,1,0:T(8,128)(2,1)}, bf16[32,128,384]{2,1,0:T(8,128)(2,1)S(1)}, u32[]{:S(2)}) %copy-start.3) | copy-done | bytes 3145752
  86.6 0.0 copy-start.5
  86.6 1.3 copy-done.5
  87.9 6.0 %all-to-all-start = ((bf16[32,128,384]{2,1,0:T(8,128)(2,1)}), bf16[32,128,384]{2,1,0:T(8,128)(2,1)}, u32[]{:S(2)}, u32[]{:S(2)}) async-start(bf16[32,128,384]{2,1,0:T(8,128)(2,1)} %copy-done.3), calls=%async_computation | async-start | bytes 6291456 | tf_op jit(solution)/shard_map/all_to_all | solution.py:246
  93.9 0.1 add_bitcast_fusion.tab
  94.0 0.0 copy-start.6
  94.0 1.6 %copy-done.6 = bf16[32,128,256]{2,1,0:T(8,128)(2,1)S(1)} copy-done((bf16[32,128,256]{2,1,0:T(8,128)(2,1)S(1)}, bf16[32,128,256]{2,1,0:T(8,128)(2,1)}, u32[]{:S(2)}) %copy-start.6) | copy-done | bytes 2097176
  95.6 4.5 %shard_map.141 = bf16[1,128,8192]{2,1,0:T(8,128)(2,1)} custom-call(s32[5,32]{1,0:T(8,128)S(1)} %stack.21.tab, bf16[32,128,256]{2,1,0:T(8,128)(2,1)S(1)} %copy-done.6, bf16[32,128,384]{2,1,0:T(8,128)(2,1)S(1)} %bitcast.22), custom_call_target="tpu_custom_call" | custom-call | bytes 1048576 | tf_op jit(solution)/shard_map/pallas_call | solution.py:46
  100.1 32.4 %all-to-all-done.got = bf16[32,128,384]{2,1,0:T(8,128)(2,1)} async-done(((bf16[32,128,384]{2,1,0:T(8,128)(2,1)}), bf16[32,128,384]{2,1,0:T(8,128)(2,1)}, u32[]{:S(2)}, u32[]{:S(2)}) %all-to-all-start) | async-done | bytes 3145760 | tf_op jit(solution)/shard_map/all_to_all | solution.py:246
  132.5 3.0 %shard_map.142 = (f32[1,1,1,2,128,128]{5,4,3,2,1,0:T(8,128)}, f32[1,1,1,128,128]{4,3,2,1,0:T(8,128)}) custom-call(s32[1,2]{1,0:T(1,128)S(1)} %add_bitcast_fusion.tab, bf16[32,128,384]{2,1,0:T(8,128)(2,1)} %all-to-all-done.got), custom_call_target="tpu_custom_call" | custom-call | bytes 1048576 | tf_op jit(solution)/shard_map/pallas_call | solution.py:46
  (1 shorter events, 0.0 us)
Async XLA Ops:
  7.2 57.6 %all-gather.3.cloned.1.call-start = ((), (), s32[]{:S(2)}) async-start(), calls=%async_computation.1 | async-start | bytes 3244032 | tf_op jit(solution)/shard_map/all_gather | solution.py:214
  13.6 7.5 %collective-permute-start = (s32[5,32]{1,0:T(8,128)S(1)}, s32[5,32]{1,0:T(8,128)S(1)}, u32[]{:S(2)}, u32[]{:S(2)}) collective-permute-start(s32[5,32]{1,0:T(8,128)S(1)} %stack.21.tab), channel_id=1, source_target_pairs={{0,32},{32,64},{64,96},{96,128},{128,160},{160,192},{192,224},{224... | collective-permute-start | bytes 1928 | tf_op jit(solution)/shard_map/ppermute | solution.py:218
  21.1 1.6 %copy-start.7 = (bf16[1,128,8192]{2,1,0:T(8,128)(2,1)S(1)}, bf16[1,128,8192]{2,1,0:T(8,128)(2,1)}, u32[]{:S(2)}) copy-start(bf16[1,128,8192]{2,1,0:T(8,128)(2,1)} %pending.1) | copy-start | bytes 6291460
  24.6 53.6 %collective-permute-start.1 = (bf16[32,128,128]{2,1,0:T(8,128)(2,1)}, bf16[32,128,128]{2,1,0:T(8,128)(2,1)}, u32[]{:S(2)}, u32[]{:S(2)}) collective-permute-start(bf16[32,128,128]{2,1,0:T(8,128)(2,1)} %shard_map.139), channel_id=1, source_target_pairs={{0,224},{32,0},{64,32},{96,64},{128,96},{160,128},{192,160},{224,1... | collective-permute-start | bytes 3145736 | tf_op jit(solution)/shard_map/ppermute | solution.py:222
  64.8 1.9 %copy-start = (bf16[4096,384]{1,0:T(8,128)(2,1)S(1)}, bf16[4096,384]{1,0:T(8,128)(2,1)}, u32[]{:S(2)}) copy-start(bf16[4096,384]{1,0:T(8,128)(2,1)} %all-gather.3.cloned.1.call-done) | copy-start | bytes 9437188
  66.6 1.6 %copy-start.2 = (bf16[1,128,8192]{2,1,0:T(8,128)(2,1)S(1)}, bf16[1,128,8192]{2,1,0:T(8,128)(2,1)}, u32[]{:S(2)}) copy-start(bf16[1,128,8192]{2,1,0:T(8,128)(2,1)} %x_saved.3) | copy-start | bytes 6291460
  68.2 1.6 %copy-start.4 = (bf16[1,128,8192]{2,1,0:T(8,128)(2,1)S(1)}, bf16[1,128,8192]{2,1,0:T(8,128)(2,1)}, u32[]{:S(2)}) copy-start(bf16[1,128,8192]{2,1,0:T(8,128)(2,1)} %x_next.1) | copy-start | bytes 6291460
  69.8 8.3 %copy-start.1 = (bf16[4096,384]{1,0:T(8,128)(2,1)S(1)}, bf16[4096,384]{1,0:T(8,128)(2,1)}, u32[]{:S(2)}) copy-start(bf16[4096,384]{1,0:T(8,128)(2,1)} %all-gather.3.cloned.1.call-done) | copy-start | bytes 9437188
  84.9 1.7 %copy-start.3 = (bf16[32,128,384]{2,1,0:T(8,128)(2,1)}, bf16[32,128,384]{2,1,0:T(8,128)(2,1)S(1)}, u32[]{:S(2)}) copy-start(bf16[32,128,384]{2,1,0:T(8,128)(2,1)S(1)} %get-tuple-element.15) | copy-start | bytes 9437188
  86.6 1.3 copy-start.5
  87.9 44.6 %all-to-all-start = ((bf16[32,128,384]{2,1,0:T(8,128)(2,1)}), bf16[32,128,384]{2,1,0:T(8,128)(2,1)}, u32[]{:S(2)}, u32[]{:S(2)}) async-start(bf16[32,128,384]{2,1,0:T(8,128)(2,1)} %copy-done.3), calls=%async_computation | async-start | bytes 6291456 | tf_op jit(solution)/shard_map/all_to_all | solution.py:246
  94.0 1.6 %copy-start.6 = (bf16[32,128,256]{2,1,0:T(8,128)(2,1)S(1)}, bf16[32,128,256]{2,1,0:T(8,128)(2,1)}, u32[]{:S(2)}) copy-start(bf16[32,128,256]{2,1,0:T(8,128)(2,1)} %copy-done.5) | copy-start | bytes 6291460
Sparse Core Ops, SparseCore 0:
  12.1 52.5 all-gather.2
where the time goes:
time: 145 us; the launch traced here: 142 us
  waiting for transfers between devices  76.1 us (52%)
  Pallas kernels  24.4 us (17%)
  between operations  15.4 us (11%)
  local copies, waits for them, and re-layouts  11.9 us (8%)
  starting transfers between devices  10.1 us (7%)
  other arithmetic  4.46 us (3%)
    all_gather x1, waiting for transfers between devices, per_device(): w = lax.all_gather(own, 'tile')  38.2 us
    all_to_all x1, waiting for transfers between devices, per_device(): got = lax.all_to_all(parts, 'tile', 0, 0, tiled=True)  32.4 us
    pallas_call x5, Pallas kernels, call(): pl.pallas_call(body, out_shape=[o for o, _ in outs], in_specs=specs, out_...  24.4 us
    unnamed x16, local copies, waits for them, and re-layouts  11.2 us
    all_to_all x1, starting transfers between devices, per_device(): got = lax.all_to_all(parts, 'tile', 0, 0, tiled=True)  6.04 us
    ppermute x1, waiting for transfers between devices, per_device(): asked = lax.ppermute(tab, 'pipe', up_pairs)  5.52 us
  transfers between devices with their start and end apart: 4, of which 3 were waited for; matrix products, arithmetic and copies ran while one was open for 1% of the time, Pallas kernels for 10%

commit v1 on v0

v1 whole, which is shorter than its diff:
```python
import functools

import jax
import jax.numpy as jnp
from jax import lax
from jax.experimental import pallas as pl
from jax.experimental.pallas import tpu as pltpu
from jax.sharding import PartitionSpec as P

B = 128
SIDE = 4
CHIPS = SIDE * SIDE
F32 = jnp.float32
BF16 = jnp.bfloat16
ROWS, LEAD, FIRST, HSLOT, DCOLS, OWNER = range(6)


def pairs(first, second, core=0):
    out = []
    for x in range(SIDE):
        for y in range(SIDE):
            for c in range(2):
                dx, dy = (second, first) if c else (first, second)
                to = ((x + dx) % SIDE) * SIDE + (y + dy) % SIDE
                out.append(((x * SIDE + y) * 2 + c, to * 2 + (c + core) % 2))
    return out


def send(value, first, second, core=0):
    return lax.ppermute(value, "tile", pairs(first, second, core))


def gather_tiles(own):
    own = own[None]
    one, three, two = send(own, 1, 0), send(own, -1, 0), send(own, 2, 0)
    near = jnp.concatenate([own, one, two, three], axis=0)
    back, ahead = send(near, 0, 1), send(near, 0, -1)
    low, high = send(back[:2], 0, 1), send(ahead[2:], 0, -1)
    mine = [near, back, low, high, ahead]
    return jnp.concatenate(mine + [send(part, 0, 0, 1) for part in mine], axis=0)


def reduce_tiles(mine, others):
    def plus(a, b):
        return (a.astype(F32) + b.astype(F32)).astype(BF16)

    held = (mine + send(others, 0, 0, 1).astype(F32)).astype(BF16)
    held = held.reshape(SIDE, SIDE, B, 3 * B)
    low, high = send(held[2, :2], 0, -1), send(held[2, 2:], 0, 1)
    to_back = jnp.concatenate([plus(held[1, :2], low), held[1, 2:]], axis=0)
    to_ahead = jnp.concatenate([held[3, :2], plus(held[3, 2:], high)], axis=0)
    from_ahead, from_back = send(to_back, 0, -1), send(to_ahead, 0, 1)
    row = held[0].astype(F32) + from_ahead.astype(F32) + from_back.astype(F32)
    out = row[1:].astype(BF16)
    parts = send(out[0], -1, 0), send(out[1], 2, 0), send(out[2], 1, 0)
    return row[0] + sum(part.astype(F32) for part in parts)


def loop(count, unroll, body):
    def group(i, carry):
        body([i * unroll + u for u in range(unroll)])
        return carry

    lax.fori_loop(0, count // unroll, group, 0)


def cols(block_index):
    return pl.ds(pl.multiple_of(block_index * B, B), B)


def rounded(value):
    return value.astype(BF16).astype(F32)


def dot(a, b, contract_a=1, contract_b=0):
    return lax.dot_general(
        a, b, (((contract_a,), (contract_b,)), ((), ())), preferred_element_type=F32
    )


SMEM, VMEM = pltpu.SMEM, pltpu.VMEM


def kept(shape, dtype):
    return pltpu.VMEM(shape, dtype)


def call(body, outs, scratch, scalars, arrays, limit, flops):
    return pl.pallas_call(
        body,
        out_shape=outs,
        in_specs=[pl.BlockSpec(memory_space=SMEM) for _ in scalars]
        + [pl.BlockSpec(memory_space=VMEM) for _ in arrays],
        out_specs=[pl.BlockSpec(memory_space=VMEM) for _ in outs],
        scratch_shapes=scratch,
        compiler_params=pltpu.CompilerParams(vmem_limit_bytes=limit << 20),
        cost_estimate=pl.CostEstimate(flops=flops, bytes_accessed=4 << 20, transcendentals=0),
    )(*scalars, *[pltpu.with_memory_space_constraint(a, VMEM) for a in arrays])


def pack_kernel(g_live, d_live, mine, tiles, down, out):
    o = mine[0]
    g = jnp.where(g_live[0, o] > 0, 1.0, 0.0)
    d = jnp.where(d_live[0, o] > 0, 1.0, 0.0)
    out[:, :B] = (tiles[0, 0, 0, 0].astype(F32) * g).astype(BF16)
    out[:, B : 2 * B] = (tiles[0, 0, 0, 1].astype(F32) * g).astype(BF16)
    out[:, 2 * B :] = (down[0, 0, 0].astype(F32) * d).astype(BF16)


def pick_kernel(n, asked, pending, out):
    for k in range(n):
        out[k] = pending[0, :, cols(asked[0, k])]


def saved_kernel(n, tab, x_saved, out, turned):
    for k in range(n):
        x = x_saved[0, :, cols(tab[ROWS, k])]
        out[k] = x
        turned[k] = x.T


def project(n, tab, x_of, w, acc):
    def some(ks):
        parts = [rounded(dot(x_of(k), w[k, :, : 2 * B])) for k in ks]
        for k, part in zip(ks, parts):
            lead = tab[LEAD, k]
            acc[lead] = jnp.where(tab[FIRST, k] == 1, part, acc[lead] + part)

    loop(n, 4, some)


def forward_saved_kernel(n, tab, x, w, coef, h_turned, acc):
    project(n, tab, lambda k: x[k], w, acc)

    def activate(ks):
        for k in ks:

            @pl.when(tab[FIRST, k] == 1)
            def _():
                gate, up = acc[k, :, :B], acc[k, :, B:]
                sig = jax.nn.sigmoid(gate)
                act = gate * sig
                h_turned[k] = (act * up).astype(BF16).T
                coef[k, :, :B] = up * sig * (1.0 + gate * (1.0 - sig))
                coef[k, :, B:] = act

    loop(n, 1, activate)
    h_turned[n] = jnp.zeros((B, B), BF16)


def forward_next_kernel(n, tab, x_next, w, y, acc, h, y_acc):
    project(n, tab, lambda k: x_next[0, :, cols(tab[ROWS, k])], w, acc)

    def activate(ks):
        for k in ks:

            @pl.when(tab[FIRST, k] == 1)
            def _():
                gate, up = acc[k, :, :B], acc[k, :, B:]
                h[k] = (gate * jax.nn.sigmoid(gate) * up).astype(BF16)

    loop(n, 1, activate)
    h[n] = jnp.zeros((B, B), BF16)
    y_acc[...] = jnp.zeros_like(y_acc)

    def down(js):
        parts = [rounded(dot(h[tab[HSLOT, j]], w[j, :, 2 * B :])) for j in js]
        for j, part in zip(js, parts):
            y_acc[tab[DCOLS, j]] += part

    loop(n, 4, down)
    for c in range(y_acc.shape[0]):
        y[0, :, c * B : (c + 1) * B] = y_acc[c].astype(BF16)


def backward_kernel(n, tab, x_turned, w, coef, h_turned, cot, mine, others, d_gu, dh):
    half = n // 2
    dh[...] = jnp.zeros_like(dh)

    def down(js):
        parts = [dot(cot[tab[OWNER, j]], w[j, :, 2 * B :], 1, 1) for j in js]
        for j, part in zip(js, parts):
            dh[tab[HSLOT, j]] += rounded(part)

    loop(n, 4, down)

    def scale(ks):
        for k in ks:

            @pl.when(tab[FIRST, k] == 1)
            def _():
                d_gu[k, :, :B] = (dh[k] * coef[k, :, :B]).astype(BF16)
                d_gu[k, :, B:] = (dh[k] * coef[k, :, B:]).astype(BF16)

    loop(n, 1, scale)

    def grads(base, out):
        def some(ks):
            for k in ks:
                s = base + k
                gu = dot(x_turned[s], d_gu[tab[LEAD, s]])
                down = dot(h_turned[tab[HSLOT, s]], cot[tab[OWNER, s]])
                out[k, :, : 2 * B] = gu.astype(out.dtype)
                out[k, :, 2 * B :] = down.astype(out.dtype)

        loop(half, 4, some)

    grads(half, others)
    grads(0, mine)


def dx_kernel(n, tab, d_gu, w, dx, acc):
    acc[...] = jnp.zeros_like(acc)

    def back(ks):
        parts = [rounded(dot(d_gu[tab[LEAD, k]], w[k, :, : 2 * B], 1, 1)) for k in ks]
        for k, part in zip(ks, parts):
            acc[tab[ROWS, k]] += part

    loop(n, 4, back)
    for c in range(acc.shape[0]):
        dx[0, :, c * B : (c + 1) * B] = acc[c].astype(BF16)


def tables(mine, g_rows, g_cols, d_rows, d_cols):
    n = g_rows.shape[0]
    ids = jnp.arange(n, dtype=jnp.int32)
    kind = (ids // CHIPS + mine) % 2
    j, i = (ids // SIDE) % SIDE, ids % SIDE
    x = (mine // (2 * SIDE) - jnp.where(kind == 0, i, j)) % SIDE
    y = ((mine // 2) % SIDE - jnp.where(kind == 0, j, i)) % SIDE
    owner = (x * SIDE + y) * 2 + kind
    chosen = owner[:, None] == ids[None, :]

    def by_slot(values):
        return jnp.sum(jnp.where(chosen, values[None, :], 0), axis=1)

    rows, columns = by_slot(g_rows), by_slot(g_cols)
    lead = jnp.min(jnp.where(columns[:, None] == columns[None, :], ids[None, :], n), axis=1)
    first = (lead == ids).astype(jnp.int32)
    hslot = jnp.min(jnp.where(by_slot(d_rows)[:, None] == columns[None, :], ids[None, :], n), axis=1)
    return jnp.stack([rows, lead, first, hslot, by_slot(d_cols), owner])


def per_device(
    x_next,
    x_saved,
    pending,
    gu_rows,
    gu_cols,
    gu_live,
    down_rows,
    down_cols,
    down_live,
    gate_up_tiles,
    down_tiles,
):
    n = lax.axis_size("tile")
    sections = lax.axis_size("pipe")
    mine = lax.axis_index("tile").astype(jnp.int32)
    tok, width = x_next.shape[1:]
    blocks = width // B
    part = functools.partial
    product = 2 * tok * B * B

    up_pairs = [(s, (s + 1) % sections) for s in range(sections)]
    down_pairs = [(s, (s - 1) % sections) for s in range(sections)]
    d_cols = down_cols[0].reshape(1, n)
    asked = lax.ppermute(d_cols, "pipe", up_pairs)

    [own] = call(
        pack_kernel,
        [kept((B, 3 * B), BF16)],
        [],
        [gu_live, down_live, mine[None]],
        [gate_up_tiles, down_tiles],
        2,
        product,
    )
    w = gather_tiles(own)

    [picked] = call(
        part(pick_kernel, n), [kept((n, tok, B), BF16)], [], [asked], [pending], 4, n * product
    )
    cot = lax.ppermute(picked, "pipe", down_pairs)

    tab = tables(
        mine, gu_rows[0].reshape(-1), gu_cols[0].reshape(-1), down_rows[0].reshape(-1), d_cols.reshape(-1)
    )
    x_blocks, x_turned = call(
        part(saved_kernel, n),
        [kept((n, tok, B), BF16), kept((n, B, tok), BF16)],
        [],
        [tab],
        [x_saved],
        4,
        2 * n * product,
    )
    coef, h_turned = call(
        part(forward_saved_kernel, n),
        [kept((n, tok, 2 * B), F32), kept((n + 1, B, tok), BF16)],
        [VMEM((n, tok, 2 * B), F32)],
        [tab],
        [x_blocks, w],
        10,
        3 * n * product,
    )
    partial_mine, partial_others, d_gu = call(
        part(backward_kernel, n),
        [kept((CHIPS, B, 3 * B), F32), kept((CHIPS, B, 3 * B), BF16), kept((n, tok, 2 * B), BF16)],
        [VMEM((n + 1, tok, B), F32)],
        [tab],
        [x_turned, w, coef, h_turned, cot],
        8,
        5 * n * product,
    )
    x_late, partial_mine = lax.optimization_barrier((x_next, partial_mine))
    total = reduce_tiles(partial_mine, partial_others)
    [y] = call(
        part(forward_next_kernel, n),
        [jax.ShapeDtypeStruct((1, tok, width), BF16)],
        [
            VMEM((n, tok, 2 * B), F32),
            VMEM((n + 1, tok, B), BF16),
            VMEM((blocks, tok, B), F32),
        ],
        [tab],
        [x_late, w],
        20,
        5 * n * product,
    )
    [dx] = call(
        part(dx_kernel, n),
        [jax.ShapeDtypeStruct((1, tok, width), BF16)],
        [VMEM((blocks, tok, B), F32)],
        [tab],
        [d_gu, w],
        10,
        4 * n * product,
    )
    g_live = (lax.dynamic_index_in_dim(gu_live[0], mine, 0, keepdims=False) > 0).astype(F32)
    d_live = (lax.dynamic_index_in_dim(down_live[0], mine, 0, keepdims=False) > 0).astype(F32)
    grad_gu = jnp.stack([total[:, :B], total[:, B : 2 * B]]) * g_live
    grad_down = total[:, 2 * B :] * d_live
    return (y, dx, grad_gu[None, None, None], grad_down[None, None, None])


def solution(mesh):
    placed = (
        P("pipe", "tile", None),
        P("pipe", "tile", None),
        P("pipe", "tile", None),
        P("pipe", None, None),
        P("pipe", None, None),
        P("pipe", None),
        P("pipe", None, None),
        P("pipe", None, None),
        P("pipe", None),
        P("pipe", "tile", None, None, None, None),
        P("pipe", "tile", None, None, None),
    )
    return jax.shard_map(
        per_device,
        mesh=mesh,
        in_specs=placed,
        out_specs=(
            P("pipe", "tile", None),
            P("pipe", "tile", None),
            P("pipe", "tile", None, None, None, None),
            P("pipe", "tile", None, None, None),
        ),
        check_vma=False,
    )
```

time: 145 us -> 97.9 us (0.68)
  the two profiles are of different devices: /device:TPU:6 before, /device:TPU:26 now
where the time goes in v1:
time: 97.9 us; the launch traced here: 97.6 us
  starting transfers between devices  33.7 us (34%)
  Pallas kernels  24.8 us (25%)
  waiting for transfers between devices  23.1 us (24%)
  local copies, waits for them, and re-layouts  7.05 us (7%)
  other arithmetic  6.57 us (7%)
  between operations  2.33 us (2%)
    ppermute x20, starting transfers between devices, send(): return lax.ppermute(value, 'tile', pairs(first, second, core))  26.1 us
    pallas_call x7, Pallas kernels, call(): pl.pallas_call(body, out_shape=outs, in_specs=[pl.BlockSpec(memory_space=...  24.8 us
    ppermute x20, waiting for transfers between devices, send(): return lax.ppermute(value, 'tile', pairs(first, second, core))  19.1 us
    unnamed x36, local copies, waits for them, and re-layouts  6.8 us
    ppermute x1, starting transfers between devices, per_device(): cot = lax.ppermute(picked, 'pipe', down_pairs)  5.75 us
    ppermute x1, waiting for transfers between devices, per_device(): cot = lax.ppermute(picked, 'pipe', down_pairs)  4.05 us
  transfers between devices with their start and end apart: 22, of which 8 were waited for; matrix products, arithmetic and copies ran while one was open for 3% of the time, Pallas kernels for 19%

profile of v1, /device:TPU:26, one launch (start us, length us, event | category | flops | bytes accessed | tf_op | source)
XLA Modules:
  0.0 97.6 jit_solution(15480999578897924704)
XLA Ops:
  0.6 0.8 copy-done.5
  1.5 0.8 copy-done.6
  2.2 0.7 copy-done.7
  2.9 0.7 copy-done.9
  3.5 0.6 shard_map.139
  4.1 0.6 collective-permute-start.2
  4.7 2.4 %collective-permute-start.1 = (bf16[1,128,384]{2,1,0:T(8,128)(2,1)S(1)}, bf16[1,128,384]{2,1,0:T(8,128)(2,1)S(1)}, u32[]{:S(2)}, u32[]{:S(2)}) collective-permute-start(bf16[1,128,384]{2,1,0:T(8,128)(2,1)S(1)} %bitcast.51), channel_id=1, source_target_pairs={{0,16},{1,5},{2,18},{3,7},{4,20},{5,1},{6,22},{7,3},{8,24},{9,13},... | collective-permute-start | bytes 294920 | tf_op jit(solution)/shard_map/ppermute | solution.py:30
  7.2 1.8 %collective-permute-start = (bf16[1,128,384]{2,1,0:T(8,128)(2,1)S(1)}, bf16[1,128,384]{2,1,0:T(8,128)(2,1)S(1)}, u32[]{:S(2)}, u32[]{:S(2)}) collective-permute-start(bf16[1,128,384]{2,1,0:T(8,128)(2,1)S(1)} %bitcast.52), channel_id=1, source_target_pairs={{0,8},{1,3},{2,10},{3,5},{4,12},{5,7},{6,14},{7,1},{8,16},{9,11},{... | collective-permute-start | bytes 294920 | tf_op jit(solution)/shard_map/ppermute | solution.py:30
  9.0 1.9 %collective-permute-start.12 = (s32[1,32]{1,0:T(1,128)}, s32[1,32]{1,0:T(1,128)S(1)}, u32[]{:S(2)}, u32[]{:S(2)}) collective-permute-start(s32[1,32]{1,0:T(1,128)} %bitcast.63), channel_id=1, source_target_pairs={{0,32},{32,64},{64,96},{96,128},{128,160},{160,192},{192,224},{224... | collective-permute-start | bytes 392 | tf_op jit(solution)/shard_map/ppermute | solution.py:269
  10.9 0.9 select_reduce_fusion
  11.8 0.2 select_reduce_fusion.1
  12.2 0.8 collective-permute-start.5
  13.0 2.5 %collective-permute-start.3 = (bf16[4,128,384]{2,1,0:T(8,128)(2,1)S(1)}, bf16[4,128,384]{2,1,0:T(8,128)(2,1)S(1)}, u32[]{:S(2)}, u32[]{:S(2)}) collective-permute-start(bf16[4,128,384]{2,1,0:T(8,128)(2,1)S(1)} %pad_maximum_fusion), channel_id=1, source_target_pairs={{0,2},{1,9},{2,4},{3,11},{4,6},{5,13},{6,0},{7,15},{8,10},{9,17},{... | collective-permute-start | bytes 1179656 | tf_op jit(solution)/shard_map/ppermute | solution.py:30
  15.5 1.6 %copy-done.3 = bf16[1,128,8192]{2,1,0:T(8,128)(2,1)S(1)} copy-done((bf16[1,128,8192]{2,1,0:T(8,128)(2,1)S(1)}, bf16[1,128,8192]{2,1,0:T(8,128)(2,1)}, u32[]{:S(2)}) %copy-start.3) | copy-done | bytes 2097176
  17.1 1.1 %shard_map.138 = (bf16[32,128,128]{2,1,0:T(8,128)(2,1)S(1)}, bf16[32,128,128]{2,1,0:T(8,128)(2,1)S(1)}) custom-call(s32[6,32]{1,0:T(8,128)S(1)} %stack.30.tab, bf16[1,128,8192]{2,1,0:T(8,128)(2,1)S(1)} %copy-done.3), custom_call_target="tpu_custom_call" | custom-call | flops 268435456 | bytes 4194304 | tf_op jit(solution)/shard_map/pallas_call | solution.py:89
  18.2 0.5 copy-done.4
  18.7 0.8 shard_map.141
  19.5 5.8 %collective-permute-start.13 = (bf16[32,128,128]{2,1,0:T(8,128)(2,1)S(1)}, bf16[32,128,128]{2,1,0:T(8,128)(2,1)S(1)}, u32[]{:S(2)}, u32[]{:S(2)}) collective-permute-start(bf16[32,128,128]{2,1,0:T(8,128)(2,1)S(1)} %shard_map.141), channel_id=1, source_target_pairs={{0,224},{32,0},{64,32},{96,64},{128,96},{160,128},{192,160},{224,1... | collective-permute-start | bytes 3145736 | tf_op jit(solution)/shard_map/ppermute | solution.py:285
  25.5 3.3 %collective-permute-start.4 = (bf16[2,128,384]{2,1,0:T(8,128)(2,1)S(1)}, bf16[2,128,384]{2,1,0:T(8,128)(2,1)S(1)}, u32[]{:S(2)}, u32[]{:S(2)}) collective-permute-start(bf16[2,128,384]{2,1,0:T(8,128)(2,1)S(1)} %slice.70), channel_id=1, source_target_pairs={{0,2},{1,9},{2,4},{3,11},{4,6},{5,13},{6,0},{7,15},{8,10},{9,17},{... | collective-permute-start | bytes 589832 | tf_op jit(solution)/shard_map/ppermute | solution.py:30
  29.0 3.3 %collective-permute-done.6 = bf16[2,128,384]{2,1,0:T(8,128)(2,1)S(1)} collective-permute-done((bf16[2,128,384]{2,1,0:T(8,128)(2,1)S(1)}, bf16[2,128,384]{2,1,0:T(8,128)(2,1)S(1)}, u32[]{:S(2)}, u32[]{:S(2)}) %collective-permute-start.6) | collective-permute-done | bytes 196640 | tf_op jit(solution)/shard_map/ppermute | solution.py:30
  32.3 1.0 %collective-permute-start.10 = (bf16[2,128,384]{2,1,0:T(8,128)(2,1)S(1)}, bf16[2,128,384]{2,1,0:T(8,128)(2,1)S(1)}, u32[]{:S(2)}, u32[]{:S(2)}) collective-permute-start(bf16[2,128,384]{2,1,0:T(8,128)(2,1)S(1)} %collective-permute-done.6), channel_id=1, source_target_pairs={{0,1},{1,0},{2,3},{3,2},{4,5},{5,4},{6,7},{7,6},{8,9},{9,8},{10,11... | collective-permute-start | bytes 589832 | tf_op jit(solution)/shard_map/ppermute | solution.py:30
  33.5 0.3 collective-permute-start.9
  33.8 0.2 collective-permute-done.8
  34.1 1.1 %collective-permute-done.9 = bf16[2,128,384]{2,1,0:T(8,128)(2,1)S(1)} collective-permute-done((bf16[2,128,384]{2,1,0:T(8,128)(2,1)S(1)}, bf16[2,128,384]{2,1,0:T(8,128)(2,1)S(1)}, u32[]{:S(2)}, u32[]{:S(2)}) %collective-permute-start.9) | collective-permute-done | bytes 196640 | tf_op jit(solution)/shard_map/ppermute | solution.py:30
  35.4 5.4 %shard_map.140 = (f32[32,128,256]{2,1,0:T(8,128)S(1)}, bf16[33,128,128]{2,1,0:T(8,128)(2,1)S(1)}) custom-call(s32[6,32]{1,0:T(8,128)S(1)} %stack.30.tab, bf16[32,128,128]{2,1,0:T(8,128)(2,1)S(1)} %get-tuple-element.14.x, bf16[32,128,384]{2,1,0:T(8,128)(2,1)S(1)} %constant_dynamic-update-slice_fusion.w), custom_call_target="tpu_custom_call" | custom-call | flops 402653184 | bytes 4194304 | tf_op jit(solution)/shard_map/pallas_call | solution.py:89
  40.7 4.1 %collective-permute-done.13.cot = bf16[32,128,128]{2,1,0:T(8,128)(2,1)S(1)} collective-permute-done((bf16[32,128,128]{2,1,0:T(8,128)(2,1)S(1)}, bf16[32,128,128]{2,1,0:T(8,128)(2,1)S(1)}, u32[]{:S(2)}, u32[]{:S(2)}) %collective-permute-start.13) | collective-permute-done | bytes 1048608 | tf_op jit(solution)/shard_map/ppermute | solution.py:285
  44.8 5.4 %shard_map.142 = (f32[16,128,384]{2,1,0:T(8,128)S(1)}, bf16[16,128,384]{2,1,0:T(8,128)(2,1)S(1)}, bf16[32,128,256]{2,1,0:T(8,128)(2,1)S(1)}) custom-call(s32[6,32]{1,0:T(8,128)S(1)} %stack.30.tab, bf16[32,128,128]{2,1,0:T(8,128)(2,1)S(1)} %get-tuple-element.13.x_turned, bf16[32,128,384]{2,1,0:T(8,128)(2,1)S(1)} %constant_dynamic-update-slice_fusion.w, ...), custom_call_target="tpu_custom_call" | custom-call | flops 671088640 | bytes 4194304 | tf_op jit(solution)/shard_map/pallas_call | solution.py:89
  50.2 1.3 %copy-done.1 = bf16[32,128,256]{2,1,0:T(8,128)(2,1)} copy-done((bf16[32,128,256]{2,1,0:T(8,128)(2,1)}, bf16[32,128,256]{2,1,0:T(8,128)(2,1)S(1)}, u32[]{:S(2)}) %copy-start.1) | copy-done | bytes 2097176
  51.6 3.4 %collective-permute-done.14 = bf16[16,128,384]{2,1,0:T(8,128)(2,1)S(1)} collective-permute-done((bf16[16,128,384]{2,1,0:T(8,128)(2,1)S(1)}, bf16[16,128,384]{2,1,0:T(8,128)(2,1)S(1)}, u32[]{:S(2)}, u32[]{:S(2)}) %collective-permute-start.14) | collective-permute-done | bytes 1572896 | tf_op jit(solution)/shard_map/ppermute | solution.py:30
  55.0 0.4 add_convert_fusion
  55.5 0.8 collective-permute-start.15
  56.3 2.5 %collective-permute-start.17 = (bf16[2,128,384]{2,1,0:T(8,128)(2,1)S(1)}, bf16[2,128,384]{2,1,0:T(8,128)(2,1)S(1)}, u32[]{:S(2)}, u32[]{:S(2)}) collective-permute-start(bf16[2,128,384]{2,1,0:T(8,128)(2,1)S(1)} %get-tuple-element.33), channel_id=1, source_target_pairs={{0,2},{1,9},{2,4},{3,11},{4,6},{5,13},{6,0},{7,15},{8,10},{9,17},{... | collective-permute-start | bytes 589832 | tf_op jit(solution)/shard_map/ppermute | solution.py:30
  58.8 3.6 %collective-permute-done.15 = bf16[2,128,384]{2,1,0:T(8,128)(2,1)S(1)} collective-permute-done((bf16[2,128,384]{2,1,0:T(8,128)(2,1)S(1)}, bf16[2,128,384]{2,1,0:T(8,128)(2,1)S(1)}, u32[]{:S(2)}, u32[]{:S(2)}) %collective-permute-start.15) | collective-permute-done | bytes 196640 | tf_op jit(solution)/shard_map/ppermute | solution.py:30
  62.5 0.1 fusion.1
  62.6 0.8 pad_maximum_fusion.2
  63.4 3.2 %collective-permute-start.18 = (bf16[4,128,384]{2,1,0:T(8,128)(2,1)}, bf16[4,128,384]{2,1,0:T(8,128)(2,1)S(1)}, u32[]{:S(2)}, u32[]{:S(2)}) collective-permute-start(bf16[4,128,384]{2,1,0:T(8,128)(2,1)} %pad_maximum_fusion.2), channel_id=1, source_target_pairs={{0,2},{1,9},{2,4},{3,11},{4,6},{5,13},{6,0},{7,15},{8,10},{9,17},{... | collective-permute-start | bytes 1179656 | tf_op jit(solution)/shard_map/ppermute | solution.py:30
  66.6 0.8 pad_maximum_fusion.1
  67.4 0.6 fusion.23
  69.4 2.9 %collective-permute-done.18 = bf16[4,128,384]{2,1,0:T(8,128)(2,1)S(1)} collective-permute-done((bf16[4,128,384]{2,1,0:T(8,128)(2,1)}, bf16[4,128,384]{2,1,0:T(8,128)(2,1)S(1)}, u32[]{:S(2)}, u32[]{:S(2)}) %collective-permute-start.18) | collective-permute-done | bytes 393248 | tf_op jit(solution)/shard_map/ppermute | solution.py:30
  72.2 4.5 %collective-permute-done.16 = bf16[4,128,384]{2,1,0:T(8,128)(2,1)} collective-permute-done((bf16[4,128,384]{2,1,0:T(8,128)(2,1)}, bf16[4,128,384]{2,1,0:T(8,128)(2,1)}, u32[]{:S(2)}, u32[]{:S(2)}) %collective-permute-start.16) | collective-permute-done | bytes 393248 | tf_op jit(solution)/shard_map/ppermute | solution.py:30
  76.7 1.3 %fusion.22 = (bf16[4,128,384]{2,1,0:T(8,128)(2,1)S(1)}, f32[4,128,384]{2,1,0:T(8,128)S(1)}) fusion(bf16[4,128,384]{2,1,0:T(8,128)(2,1)S(1)} %collective-permute-done.18, bf16[4,128,384]{2,1,0:T(8,128)(2,1)} %collective-permute-done.16, bf16[16,128,384]{2,1,0:T(8,128)(2,1)} %copy-done.11), kind=kLoop, calls=%fused_computation.110 | loop fusion | flops 1179648 | bytes 2359296 | tf_op jit(solution)/shard_map/convert.4
  78.0 1.6 %collective-permute-start.19 = (bf16[128,384]{1,0:T(8,128)(2,1)S(1)}, bf16[128,384]{1,0:T(8,128)(2,1)S(1)}, u32[]{:S(2)}, u32[]{:S(2)}) collective-permute-start(bf16[128,384]{1,0:T(8,128)(2,1)S(1)} %get-tuple-element.36), channel_id=1, source_target_pairs={{0,24},{1,7},{2,26},{3,1},{4,28},{5,3},{6,30},{7,5},{8,0},{9,15},{... | collective-permute-start | bytes 294920 | tf_op jit(solution)/shard_map/ppermute | solution.py:30
  79.7 0.5 collective-permute-start.21
  80.1 4.5 %collective-permute-start.20 = (bf16[128,384]{1,0:T(8,128)(2,1)S(1)}, bf16[128,384]{1,0:T(8,128)(2,1)S(1)}, u32[]{:S(2)}, u32[]{:S(2)}) collective-permute-start(bf16[128,384]{1,0:T(8,128)(2,1)S(1)} %get-tuple-element.38), channel_id=1, source_target_pairs={{0,16},{1,5},{2,18},{3,7},{4,20},{5,1},{6,22},{7,3},{8,24},{9,13},... | collective-permute-start | bytes 294920 | tf_op jit(solution)/shard_map/ppermute | solution.py:30
  84.7 4.6 %shard_map.144 = bf16[1,128,8192]{2,1,0:T(8,128)(2,1)} custom-call(s32[6,32]{1,0:T(8,128)S(1)} %stack.30.tab, bf16[32,128,256]{2,1,0:T(8,128)(2,1)S(1)} %copy-done.2, bf16[32,128,384]{2,1,0:T(8,128)(2,1)S(1)} %constant_dynamic-update-slice_fusion.w), custom_call_target="tpu_custom_call" | custom-call | flops 536870912 | bytes 4194304 | tf_op jit(solution)/shard_map/pallas_call | solution.py:89
  89.2 7.0 %shard_map.143 = bf16[1,128,8192]{2,1,0:T(8,128)(2,1)} custom-call(s32[6,32]{1,0:T(8,128)S(1)} %stack.30.tab, bf16[1,128,8192]{2,1,0:T(8,128)(2,1)S(1)} %copy-done, bf16[32,128,384]{2,1,0:T(8,128)(2,1)S(1)} %constant_dynamic-update-slice_fusion.w), custom_call_target="tpu_custom_call" | custom-call | flops 671088640 | bytes 4194304 | tf_op jit(solution)/shard_map/pallas_call | solution.py:89
  96.3 0.6 fusion.3
  96.9 0.7 maximum_multiply_fusion
  (60 shorter events, 1.1 us)
Async XLA Ops:
  0.6 0.8 copy-start.5
  1.5 0.8 copy-start.6
  2.2 0.7 copy-start.7
  2.9 0.7 copy-start.9
  4.1 8.0 %collective-permute-start.2 = (bf16[1,128,384]{2,1,0:T(8,128)(2,1)S(1)}, bf16[1,128,384]{2,1,0:T(8,128)(2,1)S(1)}, u32[]{:S(2)}, u32[]{:S(2)}) collective-permute-start(bf16[1,128,384]{2,1,0:T(8,128)(2,1)S(1)} %bitcast.50), channel_id=1, source_target_pairs={{0,24},{1,7},{2,26},{3,1},{4,28},{5,3},{6,30},{7,5},{8,0},{9,15},{... | collective-permute-start | bytes 294920 | tf_op jit(solution)/shard_map/ppermute | solution.py:30
  4.7 7.4 %collective-permute-start.1 = (bf16[1,128,384]{2,1,0:T(8,128)(2,1)S(1)}, bf16[1,128,384]{2,1,0:T(8,128)(2,1)S(1)}, u32[]{:S(2)}, u32[]{:S(2)}) collective-permute-start(bf16[1,128,384]{2,1,0:T(8,128)(2,1)S(1)} %bitcast.51), channel_id=1, source_target_pairs={{0,16},{1,5},{2,18},{3,7},{4,20},{5,1},{6,22},{7,3},{8,24},{9,13},... | collective-permute-start | bytes 294920 | tf_op jit(solution)/shard_map/ppermute | solution.py:30
  7.2 5.0 %collective-permute-start = (bf16[1,128,384]{2,1,0:T(8,128)(2,1)S(1)}, bf16[1,128,384]{2,1,0:T(8,128)(2,1)S(1)}, u32[]{:S(2)}, u32[]{:S(2)}) collective-permute-start(bf16[1,128,384]{2,1,0:T(8,128)(2,1)S(1)} %bitcast.52), channel_id=1, source_target_pairs={{0,8},{1,3},{2,10},{3,5},{4,12},{5,7},{6,14},{7,1},{8,16},{9,11},{... | collective-permute-start | bytes 294920 | tf_op jit(solution)/shard_map/ppermute | solution.py:30
  9.0 9.2 %collective-permute-start.12 = (s32[1,32]{1,0:T(1,128)}, s32[1,32]{1,0:T(1,128)S(1)}, u32[]{:S(2)}, u32[]{:S(2)}) collective-permute-start(s32[1,32]{1,0:T(1,128)} %bitcast.63), channel_id=1, source_target_pairs={{0,32},{32,64},{64,96},{96,128},{128,160},{160,192},{192,224},{224... | collective-permute-start | bytes 392 | tf_op jit(solution)/shard_map/ppermute | solution.py:269
  12.2 13.1 %collective-permute-start.5 = (bf16[4,128,384]{2,1,0:T(8,128)(2,1)S(1)}, bf16[4,128,384]{2,1,0:T(8,128)(2,1)S(1)}, u32[]{:S(2)}, u32[]{:S(2)}) collective-permute-start(bf16[4,128,384]{2,1,0:T(8,128)(2,1)S(1)} %pad_maximum_fusion), channel_id=1, source_target_pairs={{0,6},{1,25},{2,0},{3,27},{4,2},{5,29},{6,4},{7,31},{8,14},{9,1},{... | collective-permute-start | bytes 1179656 | tf_op jit(solution)/shard_map/ppermute | solution.py:30
  13.0 12.4 %collective-permute-start.3 = (bf16[4,128,384]{2,1,0:T(8,128)(2,1)S(1)}, bf16[4,128,384]{2,1,0:T(8,128)(2,1)S(1)}, u32[]{:S(2)}, u32[]{:S(2)}) collective-permute-start(bf16[4,128,384]{2,1,0:T(8,128)(2,1)S(1)} %pad_maximum_fusion), channel_id=1, source_target_pairs={{0,2},{1,9},{2,4},{3,11},{4,6},{5,13},{6,0},{7,15},{8,10},{9,17},{... | collective-permute-start | bytes 1179656 | tf_op jit(solution)/shard_map/ppermute | solution.py:30
  15.5 1.6 %copy-start.3 = (bf16[1,128,8192]{2,1,0:T(8,128)(2,1)S(1)}, bf16[1,128,8192]{2,1,0:T(8,128)(2,1)}, u32[]{:S(2)}) copy-start(bf16[1,128,8192]{2,1,0:T(8,128)(2,1)} %x_saved.1) | copy-start | bytes 6291460
  17.1 1.6 %copy-start.4 = (bf16[1,128,8192]{2,1,0:T(8,128)(2,1)S(1)}, bf16[1,128,8192]{2,1,0:T(8,128)(2,1)}, u32[]{:S(2)}) copy-start(bf16[1,128,8192]{2,1,0:T(8,128)(2,1)} %pending.1) | copy-start | bytes 6291460
  19.5 25.3 %collective-permute-start.13 = (bf16[32,128,128]{2,1,0:T(8,128)(2,1)S(1)}, bf16[32,128,128]{2,1,0:T(8,128)(2,1)S(1)}, u32[]{:S(2)}, u32[]{:S(2)}) collective-permute-start(bf16[32,128,128]{2,1,0:T(8,128)(2,1)S(1)} %shard_map.141), channel_id=1, source_target_pairs={{0,224},{32,0},{64,32},{96,64},{128,96},{160,128},{192,160},{224,1... | collective-permute-start | bytes 3145736 | tf_op jit(solution)/shard_map/ppermute | solution.py:285
  25.3 8.2 %collective-permute-start.7 = (bf16[4,128,384]{2,1,0:T(8,128)(2,1)S(1)}, bf16[4,128,384]{2,1,0:T(8,128)(2,1)S(1)}, u32[]{:S(2)}, u32[]{:S(2)}) collective-permute-start(bf16[4,128,384]{2,1,0:T(8,128)(2,1)S(1)} %pad_maximum_fusion), channel_id=1, source_target_pairs={{0,1},{1,0},{2,3},{3,2},{4,5},{5,4},{6,7},{7,6},{8,9},{9,8},{10,11... | collective-permute-start | bytes 1179656 | tf_op jit(solution)/shard_map/ppermute | solution.py:30
  25.4 7.0 %collective-permute-start.6 = (bf16[2,128,384]{2,1,0:T(8,128)(2,1)S(1)}, bf16[2,128,384]{2,1,0:T(8,128)(2,1)S(1)}, u32[]{:S(2)}, u32[]{:S(2)}) collective-permute-start(bf16[2,128,384]{2,1,0:T(8,128)(2,1)S(1)} %slice.71), channel_id=1, source_target_pairs={{0,6},{1,25},{2,0},{3,27},{4,2},{5,29},{6,4},{7,31},{8,14},{9,1},{... | collective-permute-start | bytes 589832 | tf_op jit(solution)/shard_map/ppermute | solution.py:30
  25.5 6.8 %collective-permute-start.4 = (bf16[2,128,384]{2,1,0:T(8,128)(2,1)S(1)}, bf16[2,128,384]{2,1,0:T(8,128)(2,1)S(1)}, u32[]{:S(2)}, u32[]{:S(2)}) collective-permute-start(bf16[2,128,384]{2,1,0:T(8,128)(2,1)S(1)} %slice.70), channel_id=1, source_target_pairs={{0,2},{1,9},{2,4},{3,11},{4,6},{5,13},{6,0},{7,15},{8,10},{9,17},{... | collective-permute-start | bytes 589832 | tf_op jit(solution)/shard_map/ppermute | solution.py:30
  28.8 6.5 %collective-permute-start.11 = (bf16[4,128,384]{2,1,0:T(8,128)(2,1)S(1)}, bf16[4,128,384]{2,1,0:T(8,128)(2,1)S(1)}, u32[]{:S(2)}, u32[]{:S(2)}) collective-permute-start(bf16[4,128,384]{2,1,0:T(8,128)(2,1)S(1)} %collective-permute-done.5), channel_id=1, source_target_pairs={{0,1},{1,0},{2,3},{3,2},{4,5},{5,4},{6,7},{7,6},{8,9},{9,8},{10,11... | collective-permute-start | bytes 1179656 | tf_op jit(solution)/shard_map/ppermute | solution.py:30
  32.3 1.7 %collective-permute-start.8 = (bf16[4,128,384]{2,1,0:T(8,128)(2,1)S(1)}, bf16[4,128,384]{2,1,0:T(8,128)(2,1)S(1)}, u32[]{:S(2)}, u32[]{:S(2)}) collective-permute-start(bf16[4,128,384]{2,1,0:T(8,128)(2,1)S(1)} %collective-permute-done.3), channel_id=1, source_target_pairs={{0,1},{1,0},{2,3},{3,2},{4,5},{5,4},{6,7},{7,6},{8,9},{9,8},{10,11... | collective-permute-start | bytes 1179656 | tf_op jit(solution)/shard_map/ppermute | solution.py:30
  32.3 2.9 %collective-permute-start.10 = (bf16[2,128,384]{2,1,0:T(8,128)(2,1)S(1)}, bf16[2,128,384]{2,1,0:T(8,128)(2,1)S(1)}, u32[]{:S(2)}, u32[]{:S(2)}) collective-permute-start(bf16[2,128,384]{2,1,0:T(8,128)(2,1)S(1)} %collective-permute-done.6), channel_id=1, source_target_pairs={{0,1},{1,0},{2,3},{3,2},{4,5},{5,4},{6,7},{7,6},{8,9},{9,8},{10,11... | collective-permute-start | bytes 589832 | tf_op jit(solution)/shard_map/ppermute | solution.py:30
  33.5 1.7 %collective-permute-start.9 = (bf16[2,128,384]{2,1,0:T(8,128)(2,1)S(1)}, bf16[2,128,384]{2,1,0:T(8,128)(2,1)S(1)}, u32[]{:S(2)}, u32[]{:S(2)}) collective-permute-start(bf16[2,128,384]{2,1,0:T(8,128)(2,1)S(1)} %collective-permute-done.4), channel_id=1, source_target_pairs={{0,1},{1,0},{2,3},{3,2},{4,5},{5,4},{6,7},{7,6},{8,9},{9,8},{10,11... | collective-permute-start | bytes 589832 | tf_op jit(solution)/shard_map/ppermute | solution.py:30
  50.2 1.3 %copy-start.1 = (bf16[32,128,256]{2,1,0:T(8,128)(2,1)}, bf16[32,128,256]{2,1,0:T(8,128)(2,1)S(1)}, u32[]{:S(2)}) copy-start(bf16[32,128,256]{2,1,0:T(8,128)(2,1)S(1)} %get-tuple-element.19.d_gu) | copy-start | bytes 6291460
  51.6 3.4 %collective-permute-start.14 = (bf16[16,128,384]{2,1,0:T(8,128)(2,1)S(1)}, bf16[16,128,384]{2,1,0:T(8,128)(2,1)S(1)}, u32[]{:S(2)}, u32[]{:S(2)}) collective-permute-start(bf16[16,128,384]{2,1,0:T(8,128)(2,1)S(1)} %get-tuple-element.21), channel_id=1, source_target_pairs={{0,1},{1,0},{2,3},{3,2},{4,5},{5,4},{6,7},{7,6},{8,9},{9,8},{10,11... | collective-permute-start | bytes 4718600 | tf_op jit(solution)/shard_map/ppermute | solution.py:30
  55.4 7.1 %copy-start.11 = (bf16[16,128,384]{2,1,0:T(8,128)(2,1)}, bf16[16,128,384]{2,1,0:T(8,128)(2,1)S(1)}, u32[]{:S(2)}) copy-start(bf16[16,128,384]{2,1,0:T(8,128)(2,1)S(1)} %add_convert_fusion) | copy-start | bytes 4718596
  55.4 12.0 %copy-start.8 = (s32[1,32]{1,0:T(1,128)S(1)}, s32[1,32]{1,0:T(1,128)}, u32[]{:S(2)}) copy-start(s32[1,32]{1,0:T(1,128)} %g_live.1) | copy-start | bytes 388
  55.4 12.0 %copy-start.10 = (s32[1,32]{1,0:T(1,128)S(1)}, s32[1,32]{1,0:T(1,128)}, u32[]{:S(2)}) copy-start(s32[1,32]{1,0:T(1,128)} %d_live.1) | copy-start | bytes 388
  55.5 7.0 %collective-permute-start.15 = (bf16[2,128,384]{2,1,0:T(8,128)(2,1)S(1)}, bf16[2,128,384]{2,1,0:T(8,128)(2,1)S(1)}, u32[]{:S(2)}, u32[]{:S(2)}) collective-permute-start(bf16[2,128,384]{2,1,0:T(8,128)(2,1)S(1)} %get-tuple-element.32), channel_id=1, source_target_pairs={{0,6},{1,25},{2,0},{3,27},{4,2},{5,29},{6,4},{7,31},{8,14},{9,1},{... | collective-permute-start | bytes 589832 | tf_op jit(solution)/shard_map/ppermute | solution.py:30
  56.3 6.2 %collective-permute-start.17 = (bf16[2,128,384]{2,1,0:T(8,128)(2,1)S(1)}, bf16[2,128,384]{2,1,0:T(8,128)(2,1)S(1)}, u32[]{:S(2)}, u32[]{:S(2)}) collective-permute-start(bf16[2,128,384]{2,1,0:T(8,128)(2,1)S(1)} %get-tuple-element.33), channel_id=1, source_target_pairs={{0,2},{1,9},{2,4},{3,11},{4,6},{5,13},{6,0},{7,15},{8,10},{9,17},{... | collective-permute-start | bytes 589832 | tf_op jit(solution)/shard_map/ppermute | solution.py:30
  63.4 8.8 %collective-permute-start.18 = (bf16[4,128,384]{2,1,0:T(8,128)(2,1)}, bf16[4,128,384]{2,1,0:T(8,128)(2,1)S(1)}, u32[]{:S(2)}, u32[]{:S(2)}) collective-permute-start(bf16[4,128,384]{2,1,0:T(8,128)(2,1)} %pad_maximum_fusion.2), channel_id=1, source_target_pairs={{0,2},{1,9},{2,4},{3,11},{4,6},{5,13},{6,0},{7,15},{8,10},{9,17},{... | collective-permute-start | bytes 1179656 | tf_op jit(solution)/shard_map/ppermute | solution.py:30
  67.4 9.3 %collective-permute-start.16 = (bf16[4,128,384]{2,1,0:T(8,128)(2,1)}, bf16[4,128,384]{2,1,0:T(8,128)(2,1)}, u32[]{:S(2)}, u32[]{:S(2)}) collective-permute-start(bf16[4,128,384]{2,1,0:T(8,128)(2,1)} %pad_maximum_fusion.1), channel_id=1, source_target_pairs={{0,6},{1,25},{2,0},{3,27},{4,2},{5,29},{6,4},{7,31},{8,14},{9,1},{... | collective-permute-start | bytes 1179656 | tf_op jit(solution)/shard_map/ppermute | solution.py:30
  67.4 17.3 %copy-start.2 = (bf16[32,128,256]{2,1,0:T(8,128)(2,1)S(1)}, bf16[32,128,256]{2,1,0:T(8,128)(2,1)}, u32[]{:S(2)}) copy-start(bf16[32,128,256]{2,1,0:T(8,128)(2,1)} %copy-done.1) | copy-start | bytes 6291460
  78.0 18.2 %collective-permute-start.19 = (bf16[128,384]{1,0:T(8,128)(2,1)S(1)}, bf16[128,384]{1,0:T(8,128)(2,1)S(1)}, u32[]{:S(2)}, u32[]{:S(2)}) collective-permute-start(bf16[128,384]{1,0:T(8,128)(2,1)S(1)} %get-tuple-element.36), channel_id=1, source_target_pairs={{0,24},{1,7},{2,26},{3,1},{4,28},{5,3},{6,30},{7,5},{8,0},{9,15},{... | collective-permute-start | bytes 294920 | tf_op jit(solution)/shard_map/ppermute | solution.py:30
  79.7 16.6 %collective-permute-start.21 = (bf16[128,384]{1,0:T(8,128)(2,1)S(1)}, bf16[128,384]{1,0:T(8,128)(2,1)S(1)}, u32[]{:S(2)}, u32[]{:S(2)}) collective-permute-start(bf16[128,384]{1,0:T(8,128)(2,1)S(1)} %get-tuple-element.37), channel_id=1, source_target_pairs={{0,8},{1,3},{2,10},{3,5},{4,12},{5,7},{6,14},{7,1},{8,16},{9,11},{... | collective-permute-start | bytes 294920 | tf_op jit(solution)/shard_map/ppermute | solution.py:30
  80.1 16.1 %collective-permute-start.20 = (bf16[128,384]{1,0:T(8,128)(2,1)S(1)}, bf16[128,384]{1,0:T(8,128)(2,1)S(1)}, u32[]{:S(2)}, u32[]{:S(2)}) collective-permute-start(bf16[128,384]{1,0:T(8,128)(2,1)S(1)} %get-tuple-element.38), channel_id=1, source_target_pairs={{0,16},{1,5},{2,18},{3,7},{4,20},{5,1},{6,22},{7,3},{8,24},{9,13},... | collective-permute-start | bytes 294920 | tf_op jit(solution)/shard_map/ppermute | solution.py:30
  84.7 4.6 %copy-start = (bf16[1,128,8192]{2,1,0:T(8,128)(2,1)S(1)}, bf16[1,128,8192]{2,1,0:T(8,128)(2,1)}, u32[]{:S(2)}) copy-start(bf16[1,128,8192]{2,1,0:T(8,128)(2,1)} %x_next) | copy-start | bytes 6291460

commit v2 on v1

v2 whole, which is shorter than its diff:
```python
import functools

import jax
import jax.numpy as jnp
from jax import lax
from jax.experimental import pallas as pl
from jax.experimental.pallas import tpu as pltpu
from jax.sharding import PartitionSpec as P

B = 128
SIDE = 4
CHIPS = SIDE * SIDE
F32 = jnp.float32
BF16 = jnp.bfloat16
UNROLL = 16
ROWS, LEAD, FIRST, HSLOT, DCOLS, OWNER, GLIVE, DLIVE = range(8)


def pairs(first, second, core=0):
    out = []
    for x in range(SIDE):
        for y in range(SIDE):
            for c in range(2):
                dx, dy = (second, first) if c else (first, second)
                to = ((x + dx) % SIDE) * SIDE + (y + dy) % SIDE
                out.append(((x * SIDE + y) * 2 + c, to * 2 + (c + core) % 2))
    return out


def send(value, first, second, core=0):
    return lax.ppermute(value, "tile", pairs(first, second, core))


def together(*values):
    return lax.optimization_barrier(values)


def gather_tiles(own, cot, late):
    own = own[None]
    one, three, two = send(own, 1, 0), send(own, -1, 0), send(own, 2, 0)
    near = jnp.concatenate([own, one, two, three], axis=0)
    back, ahead = send(near, 0, 1), send(near, 0, -1)
    ahead, late = together(ahead, late)
    low, high = send(back[:2], 0, 1), send(ahead[2:], 0, -1)
    mine = [near, back, low, high, ahead]
    others = [send(part, 0, 0, 1) for part in mine]
    near, cot, *others = together(near, cot, *others)
    return jnp.concatenate([near] + mine[1:] + others, axis=0), cot, late


def plus(a, b):
    return (a.astype(F32) + b.astype(F32)).astype(BF16)


def loop(count, unroll, body):
    def group(i, carry):
        body([i * unroll + u for u in range(unroll)])
        return carry

    lax.fori_loop(0, count // unroll, group, 0)


def cols(block_index):
    return pl.ds(pl.multiple_of(block_index * B, B), B)


def live(tab, row, slot):
    return tab[row, slot].astype(F32)


def rounded(value):
    return value.astype(BF16).astype(F32)


def dot(a, b, contract_a=1, contract_b=0):
    return lax.dot_general(
        a, b, (((contract_a,), (contract_b,)), ((), ())), preferred_element_type=F32
    )


SMEM, VMEM = pltpu.SMEM, pltpu.VMEM


def kept(shape, dtype):
    return pltpu.VMEM(shape, dtype)


def call(body, outs, scratch, scalars, arrays, limit, flops, far=()):
    return pl.pallas_call(
        body,
        out_shape=outs,
        in_specs=[pl.BlockSpec(memory_space=SMEM) for _ in scalars]
        + [pl.BlockSpec(memory_space=pltpu.HBM) for _ in far]
        + [pl.BlockSpec(memory_space=VMEM) for _ in arrays],
        out_specs=[pl.BlockSpec(memory_space=VMEM) for _ in outs],
        scratch_shapes=scratch,
        compiler_params=pltpu.CompilerParams(vmem_limit_bytes=limit << 20),
        cost_estimate=pl.CostEstimate(flops=flops, bytes_accessed=4 << 20, transcendentals=0),
    )(*scalars, *[pltpu.with_memory_space_constraint(a, pltpu.HBM) for a in far], *[pltpu.with_memory_space_constraint(a, VMEM) for a in arrays])


def pick(n, source, table, row, out, sems):
    return [
        pltpu.make_async_copy(source.at[0, :, cols(table[row, k])], out.at[k], sems.at[k])
        for k in range(n)
    ]


def pick_kernel(n, asked, pending, out, sems):
    copies = pick(n, pending, asked, 0, out, sems)
    for copy in copies:
        copy.start()
    for copy in copies:
        copy.wait()


def saved_kernel(n, tab, x_saved, out, turned, sems):
    copies = pick(n, x_saved, tab, ROWS, out, sems)
    for copy in copies:
        copy.start()
    for k, copy in enumerate(copies):
        copy.wait()
        turned[k] = out[k].T


def project(n, tab, x, w, acc):
    def some(ks):
        parts = [rounded(dot(x[k], w[k, :, : 2 * B]) * live(tab, GLIVE, k)) for k in ks]
        for k, part in zip(ks, parts):
            lead = tab[LEAD, k]
            acc[lead] = jnp.where(tab[FIRST, k] == 1, part, acc[lead] + part)

    loop(n, UNROLL, some)


def forward_saved_kernel(n, tab, x, w, coef, h_turned, acc):
    project(n, tab, x, w, acc)

    def activate(ks):
        for k in ks:
            gate, up = acc[k, :, :B], acc[k, :, B:]
            sig = jax.nn.sigmoid(gate)
            act = gate * sig
            h_turned[k] = (act * up).astype(BF16).T
            coef[k, :, :B] = up * sig * (1.0 + gate * (1.0 - sig))
            coef[k, :, B:] = act

    loop(n, 4, activate)
    h_turned[n] = jnp.zeros((B, B), BF16)


def forward_next_kernel(n, tab, x_next, w, h, acc, x, sems):
    copies = pick(n, x_next, tab, ROWS, x, sems)
    for copy in copies:
        copy.start()
    for copy in copies:
        copy.wait()
    project(n, tab, x, w, acc)

    def activate(ks):
        for k in ks:
            gate, up = acc[k, :, :B], acc[k, :, B:]
            h[k] = (gate * jax.nn.sigmoid(gate) * up).astype(BF16)

    loop(n, 4, activate)
    h[n] = jnp.zeros((B, B), BF16)


def down_next_kernel(n, tab, h, w, y, acc):
    acc[...] = jnp.zeros_like(acc)

    def down(js):
        parts = [rounded(dot(h[tab[HSLOT, j]], w[j, :, 2 * B :]) * live(tab, DLIVE, j)) for j in js]
        for j, part in zip(js, parts):
            acc[tab[DCOLS, j]] += part

    loop(n, UNROLL, down)
    for c in range(acc.shape[0]):
        y[0, :, c * B : (c + 1) * B] = acc[c].astype(BF16)


def grads(tab, base, count, x_turned, h_turned, d_gu, cot, out):
    def some(ks):
        for k in ks:
            s = base + k
            gu = dot(x_turned[s], d_gu[tab[LEAD, s]]) * live(tab, GLIVE, s)
            down = dot(h_turned[tab[HSLOT, s]], cot[tab[OWNER, s]]) * live(tab, DLIVE, s)
            out[k, :, : 2 * B] = gu.astype(out.dtype)
            out[k, :, 2 * B :] = down.astype(out.dtype)

    loop(count, UNROLL, some)


def backward_kernel(n, tab, x_turned, w, coef, h_turned, cot, others, d_gu, dh):
    dh[...] = jnp.zeros_like(dh)

    def down(js):
        parts = [dot(cot[tab[OWNER, j]], w[j, :, 2 * B :], 1, 1) * live(tab, DLIVE, j) for j in js]
        for j, part in zip(js, parts):
            dh[tab[HSLOT, j]] += rounded(part)

    loop(n, UNROLL, down)

    def scale(ks):
        for k in ks:
            d_gu[k, :, :B] = (dh[k] * coef[k, :, :B]).astype(BF16)
            d_gu[k, :, B:] = (dh[k] * coef[k, :, B:]).astype(BF16)

    loop(n, 4, scale)
    grads(tab, n // 2, n // 2, x_turned, h_turned, d_gu, cot, others)


def own_grads_kernel(n, tab, x_turned, h_turned, d_gu, cot, mine):
    grads(tab, 0, n // 2, x_turned, h_turned, d_gu, cot, mine)


def dx_kernel(n, tab, d_gu, w, dx, acc):
    acc[...] = jnp.zeros_like(acc)

    def back(ks):
        parts = [
            rounded(dot(d_gu[tab[LEAD, k]], w[k, :, : 2 * B], 1, 1) * live(tab, GLIVE, k)) for k in ks
        ]
        for k, part in zip(ks, parts):
            acc[tab[ROWS, k]] += part

    loop(n, UNROLL, back)
    for c in range(acc.shape[0]):
        dx[0, :, c * B : (c + 1) * B] = acc[c].astype(BF16)


def total_kernel(row, one, two, three, grad_gu, grad_down):
    total = row[...] + (one[...].astype(F32) + two[...].astype(F32) + three[...].astype(F32))
    grad_gu[0, 0, 0, 0] = total[:, :B]
    grad_gu[0, 0, 0, 1] = total[:, B : 2 * B]
    grad_down[0, 0, 0] = total[:, 2 * B :]


def tables(mine, g_rows, g_cols, g_live, d_rows, d_cols, d_live):
    n = g_rows.shape[0]
    ids = jnp.arange(n, dtype=jnp.int32)
    kind = (ids // CHIPS + mine) % 2
    j, i = (ids // SIDE) % SIDE, ids % SIDE
    x = (mine // (2 * SIDE) - jnp.where(kind == 0, i, j)) % SIDE
    y = ((mine // 2) % SIDE - jnp.where(kind == 0, j, i)) % SIDE
    owner = (x * SIDE + y) * 2 + kind
    chosen = owner[:, None] == ids[None, :]

    def by_slot(values):
        return jnp.sum(jnp.where(chosen, values[None, :], 0), axis=1)

    rows, columns = by_slot(g_rows), by_slot(g_cols)
    lead = jnp.min(jnp.where(columns[:, None] == columns[None, :], ids[None, :], n), axis=1)
    first = (lead == ids).astype(jnp.int32)
    hslot = jnp.min(jnp.where(by_slot(d_rows)[:, None] == columns[None, :], ids[None, :], n), axis=1)
    g_on, d_on = ((by_slot(v) > 0).astype(jnp.int32) for v in (g_live, d_live))
    return jnp.stack([rows, lead, first, hslot, by_slot(d_cols), owner, g_on, d_on])


def per_device(
    x_next,
    x_saved,
    pending,
    gu_rows,
    gu_cols,
    gu_live,
    down_rows,
    down_cols,
    down_live,
    gate_up_tiles,
    down_tiles,
):
    n = lax.axis_size("tile")
    sections = lax.axis_size("pipe")
    mine = lax.axis_index("tile").astype(jnp.int32)
    tok, width = x_next.shape[1:]
    blocks = width // B
    part = functools.partial
    product = 2 * tok * B * B

    up_pairs = [(s, (s + 1) % sections) for s in range(sections)]
    down_pairs = [(s, (s - 1) % sections) for s in range(sections)]
    asked = lax.ppermute(down_cols[0].reshape(1, n), "pipe", up_pairs)
    [picked] = call(
        part(pick_kernel, n),
        [kept((n, tok, B), BF16)],
        [pltpu.SemaphoreType.DMA((n,))],
        [asked],
        [],
        2,
        n * product,
        [pending],
    )
    own = jnp.concatenate(
        [gate_up_tiles[0, 0, 0, 0], gate_up_tiles[0, 0, 0, 1], down_tiles[0, 0, 0]], axis=1
    )
    cot = lax.ppermute(picked, "pipe", down_pairs)
    w, cot, x_saved = gather_tiles(own, cot, x_saved)

    tab = tables(
        mine,
        gu_rows[0].reshape(-1),
        gu_cols[0].reshape(-1),
        gu_live[0],
        down_rows[0].reshape(-1),
        down_cols[0].reshape(-1),
        down_live[0],
    )
    x_blocks, x_turned = call(
        part(saved_kernel, n),
        [kept((n, tok, B), BF16), kept((n, B, tok), BF16)],
        [pltpu.SemaphoreType.DMA((n,))],
        [tab],
        [],
        2,
        2 * n * product,
        [x_saved],
    )
    coef, h_turned = call(
        part(forward_saved_kernel, n),
        [kept((n, tok, 2 * B), F32), kept((n + 1, B, tok), BF16)],
        [VMEM((n, tok, 2 * B), F32)],
        [tab],
        [x_blocks, w],
        8,
        3 * n * product,
    )
    others, d_gu = call(
        part(backward_kernel, n),
        [kept((CHIPS, B, 3 * B), BF16), kept((n, tok, 2 * B), BF16)],
        [VMEM((n + 1, tok, B), F32)],
        [tab],
        [x_turned, w, coef, h_turned, cot],
        6,
        4 * n * product,
    )
    arrived = send(others, 0, 0, 1)
    [own_part] = call(
        part(own_grads_kernel, n),
        [kept((CHIPS, B, 3 * B), F32)],
        [],
        [tab],
        [x_turned, h_turned, d_gu, cot],
        4,
        2 * n * product,
    )
    held = plus(own_part, arrived).reshape(SIDE, SIDE, B, 3 * B)
    held, d_gu = together(held, d_gu)
    [dx] = call(
        part(dx_kernel, n),
        [jax.ShapeDtypeStruct((1, tok, width), BF16)],
        [VMEM((blocks, tok, B), F32)],
        [tab],
        [d_gu, w],
        10,
        4 * n * product,
    )
    low, high = send(held[2, :2], 0, -1), send(held[2, 2:], 0, 1)
    low, high, dx = together(low, high, dx)
    to_back = jnp.concatenate([plus(held[1, :2], low), held[1, 2:]], axis=0)
    to_ahead = jnp.concatenate([held[3, :2], plus(held[3, 2:], high)], axis=0)
    to_back, to_ahead, x_next = together(to_back, to_ahead, x_next)
    [h_next] = call(
        part(forward_next_kernel, n),
        [kept((n + 1, tok, B), BF16)],
        [VMEM((n, tok, 2 * B), F32), VMEM((n, tok, B), BF16), pltpu.SemaphoreType.DMA((n,))],
        [tab],
        [w],
        9,
        4 * n * product,
        [x_next],
    )
    from_ahead, from_back = send(to_back, 0, -1), send(to_ahead, 0, 1)
    from_ahead, from_back, h_next = together(from_ahead, from_back, h_next)
    row = held[0].astype(F32) + from_ahead.astype(F32) + from_back.astype(F32)
    row, h_next = together(row, h_next)
    [y] = call(
        part(down_next_kernel, n),
        [jax.ShapeDtypeStruct((1, tok, width), BF16)],
        [VMEM((blocks, tok, B), F32)],
        [tab],
        [h_next, w],
        10,
        4 * n * product,
    )
    out = row[1:].astype(BF16)
    one, two, three = send(out[0], -1, 0), send(out[1], 2, 0), send(out[2], 1, 0)
    one, two, three, y = together(one, two, three, y)
    grad_gu, grad_down = call(
        total_kernel,
        [
            jax.ShapeDtypeStruct((1, 1, 1, 2, B, B), F32),
            jax.ShapeDtypeStruct((1, 1, 1, B, B), F32),
        ],
        [],
        [],
        [row[0], one, two, three],
        2,
        product,
    )
    return (y, dx, grad_gu, grad_down)


def solution(mesh):
    placed = (
        P("pipe", "tile", None),
        P("pipe", "tile", None),
        P("pipe", "tile", None),
        P("pipe", None, None),
        P("pipe", None, None),
        P("pipe", None),
        P("pipe", None, None),
        P("pipe", None, None),
        P("pipe", None),
        P("pipe", "tile", None, None, None, None),
        P("pipe", "tile", None, None, None),
    )
    return jax.shard_map(
        per_device,
        mesh=mesh,
        in_specs=placed,
        out_specs=(
            P("pipe", "tile", None),
            P("pipe", "tile", None),
            P("pipe", "tile", None, None, None, None),
            P("pipe", "tile", None, None, None),
        ),
        check_vma=False,
    )
```

time: 97.9 us -> 86.8 us (0.89)
  the two profiles are of different devices: /device:TPU:26 before, /device:TPU:6 now
where the time goes in v2:
time: 86.8 us; the launch traced here: 86.2 us
  starting transfers between devices  26.6 us (31%)
  waiting for transfers between devices  26.1 us (30%)
  Pallas kernels  24 us (28%)
  local copies, waits for them, and re-layouts  6.31 us (7%)
  other arithmetic  2.13 us (2%)
  between operations  0.99 us (1%)
    pallas_call x9, Pallas kernels, call(): pl.pallas_call(body, out_shape=outs, in_specs=[pl.BlockSpec(memory_space=...  24 us
    ppermute x20, starting transfers between devices, send(): return lax.ppermute(value, 'tile', pairs(first, second, core))  22.6 us
    ppermute x20, waiting for transfers between devices, send(): return lax.ppermute(value, 'tile', pairs(first, second, core))  20.5 us
    ppermute x1, waiting for transfers between devices, per_device(): asked = lax.ppermute(down_cols[0].reshape(1, n), 'pipe', up_pairs)  5.59 us
    unnamed x25, local copies, waits for them, and re-layouts  4.24 us
    ppermute x1, starting transfers between devices, per_device(): cot = lax.ppermute(picked, 'pipe', down_pairs)  2.09 us
    ppermute x1, starting transfers between devices, per_device(): asked = lax.ppermute(down_cols[0].reshape(1, n), 'pipe', up_pairs)  1.92 us
  transfers between devices with their start and end apart: 22, of which 10 were waited for; matrix products, arithmetic and copies ran while one was open for 1% of the time, Pallas kernels for 20%

profile of v2, /device:TPU:6, one launch (start us, length us, event | category | flops | bytes accessed | tf_op | source)
XLA Modules:
  0.0 86.2 jit_solution(5461038751250873697)
XLA Ops:
  0.7 0.8 slice_bitcast_fusion.9
  1.5 0.8 maximum_bitcast_fusion
  2.3 0.9 %collective-permute-start.2 = (bf16[1,128,384]{2,1,0:T(8,128)(2,1)S(1)}, bf16[1,128,384]{2,1,0:T(8,128)(2,1)S(1)}, u32[]{:S(2)}, u32[]{:S(2)}) collective-permute-start(bf16[1,128,384]{2,1,0:T(8,128)(2,1)S(1)} %maximum_bitcast_fusion), channel_id=1, source_target_pairs={{0,24},{1,7},{2,26},{3,1},{4,28},{5,3},{6,30},{7,5},{8,0},{9,15},{... | collective-permute-start | bytes 294920 | tf_op jit(solution)/shard_map/ppermute | solution.py:31
  3.2 2.8 %collective-permute-start.1 = (bf16[1,128,384]{2,1,0:T(8,128)(2,1)S(1)}, bf16[1,128,384]{2,1,0:T(8,128)(2,1)S(1)}, u32[]{:S(2)}, u32[]{:S(2)}) collective-permute-start(bf16[1,128,384]{2,1,0:T(8,128)(2,1)S(1)} %maximum_bitcast_fusion), channel_id=1, source_target_pairs={{0,16},{1,5},{2,18},{3,7},{4,20},{5,1},{6,22},{7,3},{8,24},{9,13},... | collective-permute-start | bytes 294920 | tf_op jit(solution)/shard_map/ppermute | solution.py:31
  6.0 0.4 collective-permute-start
  6.4 1.9 %collective-permute-start.4 = (s32[1,32]{1,0:T(1,128)}, s32[1,32]{1,0:T(1,128)S(1)}, u32[]{:S(2)}, u32[]{:S(2)}) collective-permute-start(s32[1,32]{1,0:T(1,128)} %bitcast.59), channel_id=1, source_target_pairs={{0,32},{32,64},{64,96},{96,128},{128,160},{160,192},{192,224},{224... | collective-permute-start | bytes 392 | tf_op jit(solution)/shard_map/ppermute | solution.py:283
  8.3 5.6 %collective-permute-done.4.asked = s32[1,32]{1,0:T(1,128)S(1)} collective-permute-done((s32[1,32]{1,0:T(1,128)}, s32[1,32]{1,0:T(1,128)S(1)}, u32[]{:S(2)}, u32[]{:S(2)}) %collective-permute-start.4) | collective-permute-done | bytes 160 | tf_op jit(solution)/shard_map/ppermute | solution.py:283
  13.9 2.0 %shard_map.139 = bf16[32,128,128]{2,1,0:T(8,128)(2,1)S(1)} custom-call(s32[1,32]{1,0:T(1,128)S(1)} %collective-permute-done.4.asked, bf16[1,128,8192]{2,1,0:T(8,128)(2,1)} %pending.1), custom_call_target="tpu_custom_call" | custom-call | flops 134217728 | bytes 4194304 | tf_op jit(solution)/shard_map/pallas_call | solution.py:89
  16.0 2.1 %collective-permute-start.5 = (bf16[32,128,128]{2,1,0:T(8,128)(2,1)S(1)}, bf16[32,128,128]{2,1,0:T(8,128)(2,1)S(1)}, u32[]{:S(2)}, u32[]{:S(2)}) collective-permute-start(bf16[32,128,128]{2,1,0:T(8,128)(2,1)S(1)} %shard_map.139), channel_id=1, source_target_pairs={{0,224},{32,0},{64,32},{96,64},{128,96},{160,128},{192,160},{224,1... | collective-permute-start | bytes 3145736 | tf_op jit(solution)/shard_map/ppermute | solution.py:297
  18.1 1.7 %collective-permute-start.7 = (bf16[4,128,384]{2,1,0:T(8,128)(2,1)S(1)}, bf16[4,128,384]{2,1,0:T(8,128)(2,1)S(1)}, u32[]{:S(2)}, u32[]{:S(2)}) collective-permute-start(bf16[4,128,384]{2,1,0:T(8,128)(2,1)S(1)} %pad_maximum_fusion), channel_id=1, source_target_pairs={{0,2},{1,9},{2,4},{3,11},{4,6},{5,13},{6,0},{7,15},{8,10},{9,17},{... | collective-permute-start | bytes 1179656 | tf_op jit(solution)/shard_map/ppermute | solution.py:31
  19.8 1.7 %collective-permute-start.3 = (bf16[4,128,384]{2,1,0:T(8,128)(2,1)S(1)}, bf16[4,128,384]{2,1,0:T(8,128)(2,1)S(1)}, u32[]{:S(2)}, u32[]{:S(2)}) collective-permute-start(bf16[4,128,384]{2,1,0:T(8,128)(2,1)S(1)} %pad_maximum_fusion), channel_id=1, source_target_pairs={{0,6},{1,25},{2,0},{3,27},{4,2},{5,29},{6,4},{7,31},{8,14},{9,1},{... | collective-permute-start | bytes 1179656 | tf_op jit(solution)/shard_map/ppermute | solution.py:31
  21.5 0.3 select_reduce_fusion
  21.8 5.8 %collective-permute-done.3 = bf16[4,128,384]{2,1,0:T(8,128)(2,1)S(1)} collective-permute-done((bf16[4,128,384]{2,1,0:T(8,128)(2,1)S(1)}, bf16[4,128,384]{2,1,0:T(8,128)(2,1)S(1)}, u32[]{:S(2)}, u32[]{:S(2)}) %collective-permute-start.3) | collective-permute-done | bytes 393248 | tf_op jit(solution)/shard_map/ppermute | solution.py:31
  27.6 0.7 collective-permute-start.13
  28.3 1.7 %collective-permute-start.9 = (bf16[2,128,384]{2,1,0:T(8,128)(2,1)S(1)}, bf16[2,128,384]{2,1,0:T(8,128)(2,1)S(1)}, u32[]{:S(2)}, u32[]{:S(2)}) collective-permute-start(bf16[2,128,384]{2,1,0:T(8,128)(2,1)S(1)} %slice.65), channel_id=1, source_target_pairs={{0,2},{1,9},{2,4},{3,11},{4,6},{5,13},{6,0},{7,15},{8,10},{9,17},{... | collective-permute-start | bytes 589832 | tf_op jit(solution)/shard_map/ppermute | solution.py:31
  29.9 1.7 %collective-permute-start.11 = (bf16[2,128,384]{2,1,0:T(8,128)(2,1)S(1)}, bf16[2,128,384]{2,1,0:T(8,128)(2,1)}, u32[]{:S(2)}, u32[]{:S(2)}) collective-permute-start(bf16[2,128,384]{2,1,0:T(8,128)(2,1)S(1)} %slice.53), channel_id=1, source_target_pairs={{0,6},{1,25},{2,0},{3,27},{4,2},{5,29},{6,4},{7,31},{8,14},{9,1},{... | collective-permute-start | bytes 589832 | tf_op jit(solution)/shard_map/ppermute | solution.py:31
  31.6 0.2 select_reduce_fusion.3
  31.8 3.4 %collective-permute-done.9 = bf16[2,128,384]{2,1,0:T(8,128)(2,1)S(1)} collective-permute-done((bf16[2,128,384]{2,1,0:T(8,128)(2,1)S(1)}, bf16[2,128,384]{2,1,0:T(8,128)(2,1)S(1)}, u32[]{:S(2)}, u32[]{:S(2)}) %collective-permute-start.9) | collective-permute-done | bytes 196640 | tf_op jit(solution)/shard_map/ppermute | solution.py:31
  35.2 0.5 collective-permute-done.11
  35.8 3.9 %shard_map.138 = (bf16[32,128,128]{2,1,0:T(8,128)(2,1)S(1)}, bf16[32,128,128]{2,1,0:T(8,128)(2,1)S(1)}) custom-call(s32[8,32]{1,0:T(8,128)S(1)} %stack.23.tab, bf16[1,128,8192]{2,1,0:T(8,128)(2,1)} %x_saved), custom_call_target="tpu_custom_call" | custom-call | flops 268435456 | bytes 4194304 | tf_op jit(solution)/shard_map/pallas_call | solution.py:89
  40.0 1.0 %constant_dynamic-update-slice_fusion.6 = bf16[32,128,384]{2,1,0:T(8,128)(2,1)S(1)} fusion(bf16[32,128,384]{2,1,0:T(8,128)(2,1)S(1)} %constant_dynamic-update-slice_fusion.7, bf16[2,128,384]{2,1,0:T(8,128)(2,1)} %collective-permute-done.11), kind=kLoop, calls=%fused_computation.27 | loop fusion | bytes 393216
  41.1 1.1 %constant_dynamic-update-slice_fusion.3 = bf16[32,128,384]{2,1,0:T(8,128)(2,1)S(1)} fusion(bf16[32,128,384]{2,1,0:T(8,128)(2,1)S(1)} %constant_dynamic-update-slice_fusion.4, bf16[4,128,384]{2,1,0:T(8,128)(2,1)} %collective-permute-done.8), kind=kLoop, calls=%fused_computation.24 | loop fusion | bytes 786432
  42.1 1.0 %constant_dynamic-update-slice_fusion.2 = bf16[32,128,384]{2,1,0:T(8,128)(2,1)S(1)} fusion(bf16[32,128,384]{2,1,0:T(8,128)(2,1)S(1)} %constant_dynamic-update-slice_fusion.3, bf16[2,128,384]{2,1,0:T(8,128)(2,1)} %collective-permute-done.10), kind=kLoop, calls=%fused_computation.23 | loop fusion | bytes 393216
  43.1 1.0 %constant_dynamic-update-slice_fusion.1 = bf16[32,128,384]{2,1,0:T(8,128)(2,1)S(1)} fusion(bf16[32,128,384]{2,1,0:T(8,128)(2,1)S(1)} %constant_dynamic-update-slice_fusion.2, bf16[2,128,384]{2,1,0:T(8,128)(2,1)} %collective-permute-done.12), kind=kLoop, calls=%fused_computation.22 | loop fusion | bytes 393216
  44.1 1.1 %constant_dynamic-update-slice_fusion.w = bf16[32,128,384]{2,1,0:T(8,128)(2,1)S(1)} fusion(bf16[32,128,384]{2,1,0:T(8,128)(2,1)S(1)} %constant_dynamic-update-slice_fusion.1, bf16[4,128,384]{2,1,0:T(8,128)(2,1)} %collective-permute-done.13), kind=kLoop, calls=%fused_computation.21 | loop fusion | bytes 786432 | tf_op jit(solution)/shard_map/concatenate | solution.py:48
  45.1 2.9 %shard_map.140 = (f32[32,128,256]{2,1,0:T(8,128)S(1)}, bf16[33,128,128]{2,1,0:T(8,128)(2,1)S(1)}) custom-call(s32[8,32]{1,0:T(8,128)S(1)} %stack.23.tab, bf16[32,128,128]{2,1,0:T(8,128)(2,1)S(1)} %get-tuple-element.40.x, bf16[32,128,384]{2,1,0:T(8,128)(2,1)S(1)} %constant_dynamic-update-slice_fusion.w), custom_call_target="tpu_custom_call" | custom-call | flops 402653184 | bytes 4194304 | tf_op jit(solution)/shard_map/pallas_call | solution.py:89
  48.1 2.8 %shard_map.141 = (bf16[16,128,384]{2,1,0:T(8,128)(2,1)S(1)}, bf16[32,128,256]{2,1,0:T(8,128)(2,1)S(1)}) custom-call(s32[8,32]{1,0:T(8,128)S(1)} %stack.23.tab, bf16[32,128,128]{2,1,0:T(8,128)(2,1)S(1)} %get-tuple-element.39.x_turned, bf16[32,128,384]{2,1,0:T(8,128)(2,1)S(1)} %constant_dynamic-update-slice_fusion.w, ...), custom_call_target="tpu_custom_call" | custom-call | flops 536870912 | bytes 4194304 | tf_op jit(solution)/shard_map/pallas_call | solution.py:89
  50.9 0.5 collective-permute-start.14
  51.4 1.2 %shard_map.142 = f32[16,128,384]{2,1,0:T(8,128)S(1)} custom-call(s32[8,32]{1,0:T(8,128)S(1)} %stack.23.tab, bf16[32,128,128]{2,1,0:T(8,128)(2,1)S(1)} %get-tuple-element.39.x_turned, bf16[33,128,128]{2,1,0:T(8,128)(2,1)S(1)} %get-tuple-element.48.h_turned, bf16[32,128,256]{2,1,0:T(8,128)(2,1)S(1)} %get-tuple-element.54.d_gu, ...), custom_call_target="tpu_custom_call" | custom-call | flops 268435456 | bytes 4194304 | tf_op jit(solution)/shard_map/pallas_call | solution.py:89
  52.6 1.9 %collective-permute-done.14 = bf16[16,128,384]{2,1,0:T(8,128)(2,1)S(1)} collective-permute-done((bf16[16,128,384]{2,1,0:T(8,128)(2,1)S(1)}, bf16[16,128,384]{2,1,0:T(8,128)(2,1)S(1)}, u32[]{:S(2)}, u32[]{:S(2)}) %collective-permute-start.14) | collective-permute-done | bytes 1572896 | tf_op jit(solution)/shard_map/ppermute | solution.py:31
  54.4 0.4 add_convert_fusion
  54.9 0.1 slice_bitcast_fusion.1
  55.0 1.9 %collective-permute-start.16 = (bf16[2,128,384]{2,1,0:T(8,128)(2,1)S(1)}, bf16[2,128,384]{2,1,0:T(8,128)(2,1)S(1)}, u32[]{:S(2)}, u32[]{:S(2)}) collective-permute-start(bf16[2,128,384]{2,1,0:T(8,128)(2,1)S(1)} %get-tuple-element.82), channel_id=1, source_target_pairs={{0,2},{1,9},{2,4},{3,11},{4,6},{5,13},{6,0},{7,15},{8,10},{9,17},{... | collective-permute-start | bytes 589832 | tf_op jit(solution)/shard_map/ppermute | solution.py:31
  56.8 1.4 %collective-permute-start.15 = (bf16[2,128,384]{2,1,0:T(8,128)(2,1)S(1)}, bf16[2,128,384]{2,1,0:T(8,128)(2,1)S(1)}, u32[]{:S(2)}, u32[]{:S(2)}) collective-permute-start(bf16[2,128,384]{2,1,0:T(8,128)(2,1)S(1)} %get-tuple-element.83), channel_id=1, source_target_pairs={{0,6},{1,25},{2,0},{3,27},{4,2},{5,29},{6,4},{7,31},{8,14},{9,1},{... | collective-permute-start | bytes 589832 | tf_op jit(solution)/shard_map/ppermute | solution.py:31
  58.3 3.5 %shard_map.143 = bf16[1,128,8192]{2,1,0:T(8,128)(2,1)} custom-call(s32[8,32]{1,0:T(8,128)S(1)} %stack.23.tab, bf16[32,128,256]{2,1,0:T(8,128)(2,1)S(1)} %get-tuple-element.54.d_gu, bf16[32,128,384]{2,1,0:T(8,128)(2,1)S(1)} %constant_dynamic-update-slice_fusion.w), custom_call_target="tpu_custom_call" | custom-call | flops 536870912 | bytes 4194304 | tf_op jit(solution)/shard_map/pallas_call | solution.py:89
  61.8 0.1 collective-permute-done.16
  61.9 0.6 collective-permute-done.15
  62.5 0.1 fusion.1
  62.7 2.7 %collective-permute-start.17 = (bf16[4,128,384]{2,1,0:T(8,128)(2,1)S(1)}, bf16[4,128,384]{2,1,0:T(8,128)(2,1)S(1)}, u32[]{:S(2)}, u32[]{:S(2)}) collective-permute-start(bf16[4,128,384]{2,1,0:T(8,128)(2,1)S(1)} %pad_maximum_fusion.1), channel_id=1, source_target_pairs={{0,6},{1,25},{2,0},{3,27},{4,2},{5,29},{6,4},{7,31},{8,14},{9,1},{... | collective-permute-start | bytes 1179656 | tf_op jit(solution)/shard_map/ppermute | solution.py:31
  65.4 3.7 %shard_map.144.h = bf16[33,128,128]{2,1,0:T(8,128)(2,1)S(1)} custom-call(s32[8,32]{1,0:T(8,128)S(1)} %stack.23.tab, bf16[1,128,8192]{2,1,0:T(8,128)(2,1)} %x_next, bf16[32,128,384]{2,1,0:T(8,128)(2,1)S(1)} %constant_dynamic-update-slice_fusion.w), custom_call_target="tpu_custom_call" | custom-call | flops 536870912 | bytes 4194304 | tf_op jit(solution)/shard_map/pallas_call | solution.py:89
  69.1 1.6 %collective-permute-done.17 = bf16[4,128,384]{2,1,0:T(8,128)(2,1)S(1)} collective-permute-done((bf16[4,128,384]{2,1,0:T(8,128)(2,1)S(1)}, bf16[4,128,384]{2,1,0:T(8,128)(2,1)S(1)}, u32[]{:S(2)}, u32[]{:S(2)}) %collective-permute-start.17) | collective-permute-done | bytes 393248 | tf_op jit(solution)/shard_map/ppermute | solution.py:31
  70.7 4.1 %collective-permute-done.18 = bf16[4,128,384]{2,1,0:T(8,128)(2,1)S(1)} collective-permute-done((bf16[4,128,384]{2,1,0:T(8,128)(2,1)S(1)}, bf16[4,128,384]{2,1,0:T(8,128)(2,1)S(1)}, u32[]{:S(2)}, u32[]{:S(2)}) %collective-permute-start.18) | collective-permute-done | bytes 393248 | tf_op jit(solution)/shard_map/ppermute | solution.py:31
  74.8 0.1 fusion
  75.0 0.1 collective-permute-start.21
  75.1 4.5 %collective-permute-start.20 = (bf16[128,384]{1,0:T(8,128)(2,1)S(1)}, bf16[128,384]{1,0:T(8,128)(2,1)S(1)}, u32[]{:S(2)}, u32[]{:S(2)}) collective-permute-start(bf16[128,384]{1,0:T(8,128)(2,1)S(1)} %get-tuple-element.87), channel_id=1, source_target_pairs={{0,16},{1,5},{2,18},{3,7},{4,20},{5,1},{6,22},{7,3},{8,24},{9,13},... | collective-permute-start | bytes 294920 | tf_op jit(solution)/shard_map/ppermute | solution.py:31
  79.7 3.2 %shard_map.145 = bf16[1,128,8192]{2,1,0:T(8,128)(2,1)} custom-call(s32[8,32]{1,0:T(8,128)S(1)} %stack.23.tab, bf16[33,128,128]{2,1,0:T(8,128)(2,1)S(1)} %shard_map.144.h, bf16[32,128,384]{2,1,0:T(8,128)(2,1)S(1)} %constant_dynamic-update-slice_fusion.w), custom_call_target="tpu_custom_call" | custom-call | flops 536870912 | bytes 4194304 | tf_op jit(solution)/shard_map/pallas_call | solution.py:89
  82.9 2.6 %collective-permute-done.19.one = bf16[128,384]{1,0:T(8,128)(2,1)S(1)} collective-permute-done((bf16[128,384]{1,0:T(8,128)(2,1)S(1)}, bf16[128,384]{1,0:T(8,128)(2,1)S(1)}, u32[]{:S(2)}, u32[]{:S(2)}) %collective-permute-start.19) | collective-permute-done | bytes 98336 | tf_op jit(solution)/shard_map/ppermute | solution.py:31
  85.5 0.7 shard_map.146
  (52 shorter events, 0.8 us)
Async XLA Ops:
  0.6 20.8 %copy-start.4 = (s32[1,32,1]{1,2,0:T(1,128)S(1)}, s32[1,32,1]{1,2,0:T(1,128)}, u32[]{:S(2)}) copy-start(s32[1,32,1]{1,2,0:T(1,128)} %param.18) | copy-start | bytes 388
  0.6 20.8 %copy-start.2 = (s32[1,32]{1,0:T(1,128)S(1)}, s32[1,32]{1,0:T(1,128)}, u32[]{:S(2)}) copy-start(s32[1,32]{1,0:T(1,128)} %param.19) | copy-start | bytes 388
  0.7 20.8 %copy-start.5 = (s32[1,32,1]{1,2,0:T(1,128)S(1)}, s32[1,32,1]{1,2,0:T(1,128)}, u32[]{:S(2)}) copy-start(s32[1,32,1]{1,2,0:T(1,128)} %param.17) | copy-start | bytes 388
  0.7 20.8 %copy-start.3 = (s32[1,32]{1,0:T(1,128)S(1)}, s32[1,32]{1,0:T(1,128)}, u32[]{:S(2)}) copy-start(s32[1,32]{1,0:T(1,128)} %param.16) | copy-start | bytes 388
  0.7 20.8 %copy-start.6 = (s32[1,32,1]{1,2,0:T(1,128)S(1)}, s32[1,32,1]{1,2,0:T(1,128)}, u32[]{:S(2)}) copy-start(s32[1,32,1]{1,2,0:T(1,128)} %param.15) | copy-start | bytes 388
  0.7 20.8 %copy-start.7 = (s32[1,32,1]{1,2,0:T(1,128)S(1)}, s32[1,32,1]{1,2,0:T(1,128)}, u32[]{:S(2)}) copy-start(s32[1,32,1]{1,2,0:T(1,128)} %param.14) | copy-start | bytes 388
  2.3 15.8 %collective-permute-start.2 = (bf16[1,128,384]{2,1,0:T(8,128)(2,1)S(1)}, bf16[1,128,384]{2,1,0:T(8,128)(2,1)S(1)}, u32[]{:S(2)}, u32[]{:S(2)}) collective-permute-start(bf16[1,128,384]{2,1,0:T(8,128)(2,1)S(1)} %maximum_bitcast_fusion), channel_id=1, source_target_pairs={{0,24},{1,7},{2,26},{3,1},{4,28},{5,3},{6,30},{7,5},{8,0},{9,15},{... | collective-permute-start | bytes 294920 | tf_op jit(solution)/shard_map/ppermute | solution.py:31
  3.2 14.9 %collective-permute-start.1 = (bf16[1,128,384]{2,1,0:T(8,128)(2,1)S(1)}, bf16[1,128,384]{2,1,0:T(8,128)(2,1)S(1)}, u32[]{:S(2)}, u32[]{:S(2)}) collective-permute-start(bf16[1,128,384]{2,1,0:T(8,128)(2,1)S(1)} %maximum_bitcast_fusion), channel_id=1, source_target_pairs={{0,16},{1,5},{2,18},{3,7},{4,20},{5,1},{6,22},{7,3},{8,24},{9,13},... | collective-permute-start | bytes 294920 | tf_op jit(solution)/shard_map/ppermute | solution.py:31
  6.0 12.0 %collective-permute-start = (bf16[1,128,384]{2,1,0:T(8,128)(2,1)S(1)}, bf16[1,128,384]{2,1,0:T(8,128)(2,1)S(1)}, u32[]{:S(2)}, u32[]{:S(2)}) collective-permute-start(bf16[1,128,384]{2,1,0:T(8,128)(2,1)S(1)} %maximum_bitcast_fusion), channel_id=1, source_target_pairs={{0,8},{1,3},{2,10},{3,5},{4,12},{5,7},{6,14},{7,1},{8,16},{9,11},{... | collective-permute-start | bytes 294920 | tf_op jit(solution)/shard_map/ppermute | solution.py:31
  6.4 7.5 %collective-permute-start.4 = (s32[1,32]{1,0:T(1,128)}, s32[1,32]{1,0:T(1,128)S(1)}, u32[]{:S(2)}, u32[]{:S(2)}) collective-permute-start(s32[1,32]{1,0:T(1,128)} %bitcast.59), channel_id=1, source_target_pairs={{0,32},{32,64},{64,96},{96,128},{128,160},{160,192},{192,224},{224... | collective-permute-start | bytes 392 | tf_op jit(solution)/shard_map/ppermute | solution.py:283
  16.0 23.8 %collective-permute-start.5 = (bf16[32,128,128]{2,1,0:T(8,128)(2,1)S(1)}, bf16[32,128,128]{2,1,0:T(8,128)(2,1)S(1)}, u32[]{:S(2)}, u32[]{:S(2)}) collective-permute-start(bf16[32,128,128]{2,1,0:T(8,128)(2,1)S(1)} %shard_map.139), channel_id=1, source_target_pairs={{0,224},{32,0},{64,32},{96,64},{128,96},{160,128},{192,160},{224,1... | collective-permute-start | bytes 3145736 | tf_op jit(solution)/shard_map/ppermute | solution.py:297
  18.1 10.1 %collective-permute-start.7 = (bf16[4,128,384]{2,1,0:T(8,128)(2,1)S(1)}, bf16[4,128,384]{2,1,0:T(8,128)(2,1)S(1)}, u32[]{:S(2)}, u32[]{:S(2)}) collective-permute-start(bf16[4,128,384]{2,1,0:T(8,128)(2,1)S(1)} %pad_maximum_fusion), channel_id=1, source_target_pairs={{0,2},{1,9},{2,4},{3,11},{4,6},{5,13},{6,0},{7,15},{8,10},{9,17},{... | collective-permute-start | bytes 1179656 | tf_op jit(solution)/shard_map/ppermute | solution.py:31
  19.8 11.8 %collective-permute-start.6 = (bf16[4,128,384]{2,1,0:T(8,128)(2,1)S(1)}, bf16[4,128,384]{2,1,0:T(8,128)(2,1)S(1)}, u32[]{:S(2)}, u32[]{:S(2)}) collective-permute-start(bf16[4,128,384]{2,1,0:T(8,128)(2,1)S(1)} %pad_maximum_fusion), channel_id=1, source_target_pairs={{0,1},{1,0},{2,3},{3,2},{4,5},{5,4},{6,7},{7,6},{8,9},{9,8},{10,11... | collective-permute-start | bytes 1179656 | tf_op jit(solution)/shard_map/ppermute | solution.py:31
  19.8 7.8 %collective-permute-start.3 = (bf16[4,128,384]{2,1,0:T(8,128)(2,1)S(1)}, bf16[4,128,384]{2,1,0:T(8,128)(2,1)S(1)}, u32[]{:S(2)}, u32[]{:S(2)}) collective-permute-start(bf16[4,128,384]{2,1,0:T(8,128)(2,1)S(1)} %pad_maximum_fusion), channel_id=1, source_target_pairs={{0,6},{1,25},{2,0},{3,27},{4,2},{5,29},{6,4},{7,31},{8,14},{9,1},{... | collective-permute-start | bytes 1179656 | tf_op jit(solution)/shard_map/ppermute | solution.py:31
  27.6 12.2 %collective-permute-start.13 = (bf16[4,128,384]{2,1,0:T(8,128)(2,1)S(1)}, bf16[4,128,384]{2,1,0:T(8,128)(2,1)}, u32[]{:S(2)}, u32[]{:S(2)}) collective-permute-start(bf16[4,128,384]{2,1,0:T(8,128)(2,1)S(1)} %collective-permute-done.3), channel_id=1, source_target_pairs={{0,1},{1,0},{2,3},{3,2},{4,5},{5,4},{6,7},{7,6},{8,9},{9,8},{10,11... | collective-permute-start | bytes 1179656 | tf_op jit(solution)/shard_map/ppermute | solution.py:31
  28.3 7.0 %collective-permute-start.9 = (bf16[2,128,384]{2,1,0:T(8,128)(2,1)S(1)}, bf16[2,128,384]{2,1,0:T(8,128)(2,1)S(1)}, u32[]{:S(2)}, u32[]{:S(2)}) collective-permute-start(bf16[2,128,384]{2,1,0:T(8,128)(2,1)S(1)} %slice.65), channel_id=1, source_target_pairs={{0,2},{1,9},{2,4},{3,11},{4,6},{5,13},{6,0},{7,15},{8,10},{9,17},{... | collective-permute-start | bytes 589832 | tf_op jit(solution)/shard_map/ppermute | solution.py:31
  29.9 5.8 %collective-permute-start.11 = (bf16[2,128,384]{2,1,0:T(8,128)(2,1)S(1)}, bf16[2,128,384]{2,1,0:T(8,128)(2,1)}, u32[]{:S(2)}, u32[]{:S(2)}) collective-permute-start(bf16[2,128,384]{2,1,0:T(8,128)(2,1)S(1)} %slice.53), channel_id=1, source_target_pairs={{0,6},{1,25},{2,0},{3,27},{4,2},{5,29},{6,4},{7,31},{8,14},{9,1},{... | collective-permute-start | bytes 589832 | tf_op jit(solution)/shard_map/ppermute | solution.py:31
  31.6 4.2 %copy-start = (bf16[4,128,384]{2,1,0:T(8,128)(2,1)}, bf16[4,128,384]{2,1,0:T(8,128)(2,1)S(1)}, u32[]{:S(2)}) copy-start(bf16[4,128,384]{2,1,0:T(8,128)(2,1)S(1)} %collective-permute-done.6) | copy-start | bytes 1179652
  31.6 8.2 %collective-permute-start.8 = (bf16[4,128,384]{2,1,0:T(8,128)(2,1)S(1)}, bf16[4,128,384]{2,1,0:T(8,128)(2,1)}, u32[]{:S(2)}, u32[]{:S(2)}) collective-permute-start(bf16[4,128,384]{2,1,0:T(8,128)(2,1)S(1)} %collective-permute-done.7), channel_id=1, source_target_pairs={{0,1},{1,0},{2,3},{3,2},{4,5},{5,4},{6,7},{7,6},{8,9},{9,8},{10,11... | collective-permute-start | bytes 1179656 | tf_op jit(solution)/shard_map/ppermute | solution.py:31
  35.2 4.5 %collective-permute-start.10 = (bf16[2,128,384]{2,1,0:T(8,128)(2,1)S(1)}, bf16[2,128,384]{2,1,0:T(8,128)(2,1)}, u32[]{:S(2)}, u32[]{:S(2)}) collective-permute-start(bf16[2,128,384]{2,1,0:T(8,128)(2,1)S(1)} %collective-permute-done.9), channel_id=1, source_target_pairs={{0,1},{1,0},{2,3},{3,2},{4,5},{5,4},{6,7},{7,6},{8,9},{9,8},{10,11... | collective-permute-start | bytes 589832 | tf_op jit(solution)/shard_map/ppermute | solution.py:31
  35.7 4.1 %collective-permute-start.12 = (bf16[2,128,384]{2,1,0:T(8,128)(2,1)}, bf16[2,128,384]{2,1,0:T(8,128)(2,1)}, u32[]{:S(2)}, u32[]{:S(2)}) collective-permute-start(bf16[2,128,384]{2,1,0:T(8,128)(2,1)} %collective-permute-done.11), channel_id=1, source_target_pairs={{0,1},{1,0},{2,3},{3,2},{4,5},{5,4},{6,7},{7,6},{8,9},{9,8},{10,11... | collective-permute-start | bytes 589832 | tf_op jit(solution)/shard_map/ppermute | solution.py:31
  35.8 5.2 %copy-start.1 = (bf16[4,128,384]{2,1,0:T(8,128)(2,1)S(1)}, bf16[4,128,384]{2,1,0:T(8,128)(2,1)}, u32[]{:S(2)}) copy-start(bf16[4,128,384]{2,1,0:T(8,128)(2,1)} %copy-done) | copy-start | bytes 1179652
  50.9 3.6 %collective-permute-start.14 = (bf16[16,128,384]{2,1,0:T(8,128)(2,1)S(1)}, bf16[16,128,384]{2,1,0:T(8,128)(2,1)S(1)}, u32[]{:S(2)}, u32[]{:S(2)}) collective-permute-start(bf16[16,128,384]{2,1,0:T(8,128)(2,1)S(1)} %get-tuple-element.52), channel_id=1, source_target_pairs={{0,1},{1,0},{2,3},{3,2},{4,5},{5,4},{6,7},{7,6},{8,9},{9,8},{10,11... | collective-permute-start | bytes 4718600 | tf_op jit(solution)/shard_map/ppermute | solution.py:31
  55.0 7.0 %collective-permute-start.16 = (bf16[2,128,384]{2,1,0:T(8,128)(2,1)S(1)}, bf16[2,128,384]{2,1,0:T(8,128)(2,1)S(1)}, u32[]{:S(2)}, u32[]{:S(2)}) collective-permute-start(bf16[2,128,384]{2,1,0:T(8,128)(2,1)S(1)} %get-tuple-element.82), channel_id=1, source_target_pairs={{0,2},{1,9},{2,4},{3,11},{4,6},{5,13},{6,0},{7,15},{8,10},{9,17},{... | collective-permute-start | bytes 589832 | tf_op jit(solution)/shard_map/ppermute | solution.py:31
  56.8 5.7 %collective-permute-start.15 = (bf16[2,128,384]{2,1,0:T(8,128)(2,1)S(1)}, bf16[2,128,384]{2,1,0:T(8,128)(2,1)S(1)}, u32[]{:S(2)}, u32[]{:S(2)}) collective-permute-start(bf16[2,128,384]{2,1,0:T(8,128)(2,1)S(1)} %get-tuple-element.83), channel_id=1, source_target_pairs={{0,6},{1,25},{2,0},{3,27},{4,2},{5,29},{6,4},{7,31},{8,14},{9,1},{... | collective-permute-start | bytes 589832 | tf_op jit(solution)/shard_map/ppermute | solution.py:31
  62.7 8.0 %collective-permute-start.17 = (bf16[4,128,384]{2,1,0:T(8,128)(2,1)S(1)}, bf16[4,128,384]{2,1,0:T(8,128)(2,1)S(1)}, u32[]{:S(2)}, u32[]{:S(2)}) collective-permute-start(bf16[4,128,384]{2,1,0:T(8,128)(2,1)S(1)} %pad_maximum_fusion.1), channel_id=1, source_target_pairs={{0,6},{1,25},{2,0},{3,27},{4,2},{5,29},{6,4},{7,31},{8,14},{9,1},{... | collective-permute-start | bytes 1179656 | tf_op jit(solution)/shard_map/ppermute | solution.py:31
  65.4 9.4 %collective-permute-start.18 = (bf16[4,128,384]{2,1,0:T(8,128)(2,1)S(1)}, bf16[4,128,384]{2,1,0:T(8,128)(2,1)S(1)}, u32[]{:S(2)}, u32[]{:S(2)}) collective-permute-start(bf16[4,128,384]{2,1,0:T(8,128)(2,1)S(1)} %pad_maximum_fusion.2), channel_id=1, source_target_pairs={{0,2},{1,9},{2,4},{3,11},{4,6},{5,13},{6,0},{7,15},{8,10},{9,17},{... | collective-permute-start | bytes 1179656 | tf_op jit(solution)/shard_map/ppermute | solution.py:31
  75.0 7.9 %collective-permute-start.21 = (bf16[128,384]{1,0:T(8,128)(2,1)S(1)}, bf16[128,384]{1,0:T(8,128)(2,1)S(1)}, u32[]{:S(2)}, u32[]{:S(2)}) collective-permute-start(bf16[128,384]{1,0:T(8,128)(2,1)S(1)} %get-tuple-element.86), channel_id=1, source_target_pairs={{0,8},{1,3},{2,10},{3,5},{4,12},{5,7},{6,14},{7,1},{8,16},{9,11},{... | collective-permute-start | bytes 294920 | tf_op jit(solution)/shard_map/ppermute | solution.py:31
  75.1 7.8 %collective-permute-start.20 = (bf16[128,384]{1,0:T(8,128)(2,1)S(1)}, bf16[128,384]{1,0:T(8,128)(2,1)S(1)}, u32[]{:S(2)}, u32[]{:S(2)}) collective-permute-start(bf16[128,384]{1,0:T(8,128)(2,1)S(1)} %get-tuple-element.87), channel_id=1, source_target_pairs={{0,16},{1,5},{2,18},{3,7},{4,20},{5,1},{6,22},{7,3},{8,24},{9,13},... | collective-permute-start | bytes 294920 | tf_op jit(solution)/shard_map/ppermute | solution.py:31
  79.7 5.8 %collective-permute-start.19 = (bf16[128,384]{1,0:T(8,128)(2,1)S(1)}, bf16[128,384]{1,0:T(8,128)(2,1)S(1)}, u32[]{:S(2)}, u32[]{:S(2)}) collective-permute-start(bf16[128,384]{1,0:T(8,128)(2,1)S(1)} %get-tuple-element.88), channel_id=1, source_target_pairs={{0,24},{1,7},{2,26},{3,1},{4,28},{5,3},{6,30},{7,5},{8,0},{9,15},{... | collective-permute-start | bytes 294920 | tf_op jit(solution)/shard_map/ppermute | solution.py:31

commit v3 on v2

--- a/solution.py
+++ b/solution.py
@@ -35,17 +35,15 @@
     return lax.optimization_barrier(values)
 
 
-def gather_tiles(own, cot, late):
+def gather_tiles(own, busy):
     own = own[None]
     one, three, two = send(own, 1, 0), send(own, -1, 0), send(own, 2, 0)
     near = jnp.concatenate([own, one, two, three], axis=0)
     back, ahead = send(near, 0, 1), send(near, 0, -1)
-    ahead, late = together(ahead, late)
+    back, ahead, *busy = together(back, ahead, *busy)
     low, high = send(back[:2], 0, 1), send(ahead[2:], 0, -1)
     mine = [near, back, low, high, ahead]
-    others = [send(part, 0, 0, 1) for part in mine]
-    near, cot, *others = together(near, cot, *others)
-    return jnp.concatenate([near] + mine[1:] + others, axis=0), cot, late
+    return mine + [send(part, 0, 0, 1) for part in mine], busy
 
 
 def plus(a, b):
@@ -60,6 +58,11 @@
     lax.fori_loop(0, count // unroll, group, 0)
 
 
+def flat(count, unroll, body):
+    for i in range(0, count, unroll):
+        body(list(range(i, i + unroll)))
+
+
 def cols(block_index):
     return pl.ds(pl.multiple_of(block_index * B, B), B)
 
@@ -85,17 +88,17 @@
     return pltpu.VMEM(shape, dtype)
 
 
-def call(body, outs, scratch, scalars, arrays, limit, flops, far=()):
+def call(body, outs, scratch, scalars, arrays, limit, flops=0, far=(), out_space=VMEM):
     return pl.pallas_call(
         body,
         out_shape=outs,
         in_specs=[pl.BlockSpec(memory_space=SMEM) for _ in scalars]
         + [pl.BlockSpec(memory_space=pltpu.HBM) for _ in far]
         + [pl.BlockSpec(memory_space=VMEM) for _ in arrays],
-        out_specs=[pl.BlockSpec(memory_space=VMEM) for _ in outs],
+        out_specs=[pl.BlockSpec(memory_space=out_space) for _ in outs],
         scratch_shapes=scratch,
         compiler_params=pltpu.CompilerParams(vmem_limit_bytes=limit << 20),
-        cost_estimate=pl.CostEstimate(flops=flops, bytes_accessed=4 << 20, transcendentals=0),
+        cost_estimate=pl.CostEstimate(flops=flops, bytes_accessed=flops // 256, transcendentals=0),
     )(*scalars, *[pltpu.with_memory_space_constraint(a, pltpu.HBM) for a in far], *[pltpu.with_memory_space_constraint(a, VMEM) for a in arrays])
 
 
@@ -106,6 +109,17 @@
     ]
 
 
+def pack_kernel(gate_up, down, out, sems):
+    copies = [
+        pltpu.make_async_copy(gate_up.at[0, 0, 0], out.at[pl.ds(0, 2)], sems.at[0]),
+        pltpu.make_async_copy(down.at[0, 0, 0], out.at[2], sems.at[1]),
+    ]
+    for copy in copies:
+        copy.start()
+    for copy in copies:
+        copy.wait()
+
+
 def pick_kernel(n, asked, pending, out, sems):
     copies = pick(n, pending, asked, 0, out, sems)
     for copy in copies:
@@ -123,18 +137,27 @@
         turned[k] = out[k].T
 
 
-def project(n, tab, x, w, acc):
+def project(n, tab, x, w_of, acc, walk):
     def some(ks):
-        parts = [rounded(dot(x[k], w[k, :, : 2 * B]) * live(tab, GLIVE, k)) for k in ks]
+        parts = [rounded(dot(x[k], w_of(k)) * live(tab, GLIVE, k)) for k in ks]
         for k, part in zip(ks, parts):
             lead = tab[LEAD, k]
             acc[lead] = jnp.where(tab[FIRST, k] == 1, part, acc[lead] + part)
 
-    loop(n, UNROLL, some)
-
-
-def forward_saved_kernel(n, tab, x, w, coef, h_turned, acc):
-    project(n, tab, x, w, acc)
+    walk(n, UNROLL, some)
+
+
+def forward_saved_kernel(n, tab, x, *refs):
+    *pieces, w, coef, h_turned, acc = refs
+    places = [(piece, i) for piece in pieces for i in range(piece.shape[0])]
+
+    def w_of(k):
+        piece, i = places[k]
+        gate, up = piece[i, 0], piece[i, 1]
+        w[k, :, :B], w[k, :, B : 2 * B], w[k, :, 2 * B :] = gate, up, piece[i, 2]
+        return jnp.concatenate([gate, up], axis=1)
+
+    project(n, tab, x, w_of, acc, flat)
 
     def activate(ks):
         for k in ks:
@@ -155,7 +178,7 @@
         copy.start()
     for copy in copies:
         copy.wait()
-    project(n, tab, x, w, acc)
+    project(n, tab, x, lambda k: w[k, :, : 2 * B], acc, loop)
 
     def activate(ks):
         for k in ks:
@@ -166,7 +189,22 @@
     h[n] = jnp.zeros((B, B), BF16)
 
 
-def down_next_kernel(n, tab, h, w, y, acc):
+def put(acc, out, staged, sems):
+    chunks = sems.shape[0]
+    each = acc.shape[0] // chunks
+    copies = []
+    for q in range(chunks):
+        for c in range(q * each, (q + 1) * each):
+            staged[:, c * B : (c + 1) * B] = acc[c].astype(BF16)
+        span = pl.ds(q * each * B, each * B)
+        copy = pltpu.make_async_copy(staged.at[:, span], out.at[0, :, span], sems.at[q])
+        copy.start()
+        copies.append(copy)
+    for copy in copies:
+        copy.wait()
+
+
+def down_next_kernel(n, tab, h, w, y, acc, staged, sems):
     acc[...] = jnp.zeros_like(acc)
 
     def down(js):
@@ -175,23 +213,18 @@
             acc[tab[DCOLS, j]] += part
 
     loop(n, UNROLL, down)
-    for c in range(acc.shape[0]):
-        y[0, :, c * B : (c + 1) * B] = acc[c].astype(BF16)
-
-
-def grads(tab, base, count, x_turned, h_turned, d_gu, cot, out):
-    def some(ks):
-        for k in ks:
-            s = base + k
-            gu = dot(x_turned[s], d_gu[tab[LEAD, s]]) * live(tab, GLIVE, s)
-            down = dot(h_turned[tab[HSLOT, s]], cot[tab[OWNER, s]]) * live(tab, DLIVE, s)
-            out[k, :, : 2 * B] = gu.astype(out.dtype)
-            out[k, :, 2 * B :] = down.astype(out.dtype)
-
-    loop(count, UNROLL, some)
-
-
-def backward_kernel(n, tab, x_turned, w, coef, h_turned, cot, others, d_gu, dh):
+    put(acc, y, staged, sems)
+
+
+def grads(tab, slots, x_turned, h_turned, d_gu, cot, out):
+    for k, s in enumerate(slots):
+        gu = dot(x_turned[s], d_gu[tab[LEAD, s]]) * live(tab, GLIVE, s)
+        down = dot(h_turned[tab[HSLOT, s]], cot[tab[OWNER, s]]) * live(tab, DLIVE, s)
+        out[k, :, : 2 * B] = gu.astype(out.dtype)
+        out[k, :, 2 * B :] = down.astype(out.dtype)
+
+
+def backward_kernel(n, slots, tab, x_turned, w, coef, h_turned, cot, others, own, d_gu, dh):
     dh[...] = jnp.zeros_like(dh)
 
     def down(js):
@@ -207,14 +240,16 @@
             d_gu[k, :, B:] = (dh[k] * coef[k, :, B:]).astype(BF16)
 
     loop(n, 4, scale)
-    grads(tab, n // 2, n // 2, x_turned, h_turned, d_gu, cot, others)
-
-
-def own_grads_kernel(n, tab, x_turned, h_turned, d_gu, cot, mine):
-    grads(tab, 0, n // 2, x_turned, h_turned, d_gu, cot, mine)
-
-
-def dx_kernel(n, tab, d_gu, w, dx, acc):
+    for some, out in zip(slots, (others, own)):
+        grads(tab, some, x_turned, h_turned, d_gu, cot, out)
+
+
+def grads_kernel(slots, tab, x_turned, h_turned, d_gu, cot, *outs):
+    for some, out in zip(slots, outs):
+        grads(tab, some, x_turned, h_turned, d_gu, cot, out)
+
+
+def dx_kernel(n, tab, d_gu, w, dx, acc, staged, sems):
     acc[...] = jnp.zeros_like(acc)
 
     def back(ks):
@@ -225,8 +260,7 @@
             acc[tab[ROWS, k]] += part
 
     loop(n, UNROLL, back)
-    for c in range(acc.shape[0]):
-        dx[0, :, c * B : (c + 1) * B] = acc[c].astype(BF16)
+    put(acc, dx, staged, sems)
 
 
 def total_kernel(row, one, two, three, grad_gu, grad_down):
@@ -288,14 +322,9 @@
         [asked],
         [],
         2,
-        n * product,
-        [pending],
-    )
-    own = jnp.concatenate(
-        [gate_up_tiles[0, 0, 0, 0], gate_up_tiles[0, 0, 0, 1], down_tiles[0, 0, 0]], axis=1
+        far=[pending],
     )
     cot = lax.ppermute(picked, "pipe", down_pairs)
-    w, cot, x_saved = gather_tiles(own, cot, x_saved)
 
     tab = tables(
         mine,
@@ -313,52 +342,75 @@
         [tab],
         [],
         2,
-        2 * n * product,
-        [x_saved],
-    )
-    coef, h_turned = call(
+        far=[x_saved],
+    )
+    [own] = call(
+        pack_kernel,
+        [kept((3, B, B), BF16)],
+        [pltpu.SemaphoreType.DMA((2,))],
+        [],
+        [],
+        2,
+        far=[gate_up_tiles, down_tiles],
+    )
+    pieces, (x_blocks, x_turned) = gather_tiles(own, [x_blocks, x_turned])
+    w, coef, h_turned = call(
         part(forward_saved_kernel, n),
-        [kept((n, tok, 2 * B), F32), kept((n + 1, B, tok), BF16)],
+        [kept((n, B, 3 * B), BF16), kept((n, tok, 2 * B), F32), kept((n + 1, B, tok), BF16)],
         [VMEM((n, tok, 2 * B), F32)],
         [tab],
-        [x_blocks, w],
+        [x_blocks, *pieces],
         8,
-        3 * n * product,
-    )
-    others, d_gu = call(
-        part(backward_kernel, n),
-        [kept((CHIPS, B, 3 * B), BF16), kept((n, tok, 2 * B), BF16)],
+    )
+    ring = [[4 * j + i for i in range(SIDE)] for j in range(SIDE)]
+    late_slots = ring[1] + ring[3] + ring[0]
+    other_first, own_first, d_gu = call(
+        part(backward_kernel, n, [[CHIPS + k for k in ring[2]], ring[2]]),
+        [
+            kept((SIDE, B, 3 * B), BF16),
+            kept((SIDE, B, 3 * B), F32),
+            kept((n, tok, 2 * B), BF16),
+        ],
         [VMEM((n + 1, tok, B), F32)],
         [tab],
         [x_turned, w, coef, h_turned, cot],
         6,
-        4 * n * product,
-    )
-    arrived = send(others, 0, 0, 1)
-    [own_part] = call(
-        part(own_grads_kernel, n),
-        [kept((CHIPS, B, 3 * B), F32)],
+    )
+    first = send(other_first, 0, 0, 1)
+    [other_late] = call(
+        part(grads_kernel, [[CHIPS + k for k in late_slots]]),
+        [kept((CHIPS - SIDE, B, 3 * B), BF16)],
         [],
         [tab],
         [x_turned, h_turned, d_gu, cot],
         4,
-        2 * n * product,
-    )
-    held = plus(own_part, arrived).reshape(SIDE, SIDE, B, 3 * B)
-    held, d_gu = together(held, d_gu)
+    )
+    late = send(other_late, 0, 0, 1)
+    held = plus(own_first, first)
+    low, high = send(held[:2], 0, -1), send(held[2:], 0, 1)
+    [own_late] = call(
+        part(grads_kernel, [late_slots]),
+        [kept((CHIPS - SIDE, B, 3 * B), F32)],
+        [],
+        [tab],
+        [x_turned, h_turned, d_gu, cot],
+        4,
+    )
+    both = (own_late + late.astype(F32)).reshape(SIDE - 1, SIDE, B, 3 * B)
+    both, d_gu = together(both, d_gu)
     [dx] = call(
         part(dx_kernel, n),
         [jax.ShapeDtypeStruct((1, tok, width), BF16)],
-        [VMEM((blocks, tok, B), F32)],
+        [VMEM((blocks, tok, B), F32), VMEM((tok, width), BF16), pltpu.SemaphoreType.DMA((4,))],
         [tab],
         [d_gu, w],
-        10,
+        8,
         4 * n * product,
-    )
-    low, high = send(held[2, :2], 0, -1), send(held[2, 2:], 0, 1)
+        out_space=pltpu.HBM,
+    )
     low, high, dx = together(low, high, dx)
-    to_back = jnp.concatenate([plus(held[1, :2], low), held[1, 2:]], axis=0)
-    to_ahead = jnp.concatenate([held[3, :2], plus(held[3, 2:], high)], axis=0)
+    to_back = jnp.concatenate([plus(both[0, :2], low), both[0, 2:].astype(BF16)], axis=0)
+    to_ahead = jnp.concatenate([both[1, :2].astype(BF16), plus(both[1, 2:], high)], axis=0)
     to_back, to_ahead, x_next = together(to_back, to_ahead, x_next)
     [h_next] = call(
         part(forward_next_kernel, n),
@@ -372,16 +424,17 @@
     )
     from_ahead, from_back = send(to_back, 0, -1), send(to_ahead, 0, 1)
     from_ahead, from_back, h_next = together(from_ahead, from_back, h_next)
-    row = held[0].astype(F32) + from_ahead.astype(F32) + from_back.astype(F32)
+    row = both[2] + from_ahead.astype(F32) + from_back.astype(F32)
     row, h_next = together(row, h_next)
     [y] = call(
         part(down_next_kernel, n),
         [jax.ShapeDtypeStruct((1, tok, width), BF16)],
-        [VMEM((blocks, tok, B), F32)],
+        [VMEM((blocks, tok, B), F32), VMEM((tok, width), BF16), pltpu.SemaphoreType.DMA((4,))],
         [tab],
         [h_next, w],
-        10,
+        8,
         4 * n * product,
+        out_space=pltpu.HBM,
     )
     out = row[1:].astype(BF16)
     one, two, three = send(out[0], -1, 0), send(out[1], 2, 0), send(out[2], 1, 0)

time: 86.8 us -> 76.7 us (0.88)
  the two profiles are of different devices: /device:TPU:6 before, /device:TPU:8 now
where the time goes in v3:
time: 76.7 us; the launch traced here: 76.2 us
  Pallas kernels  25.8 us (34%)
  waiting for transfers between devices  23.8 us (31%)
  starting transfers between devices  23.3 us (30%)
  other arithmetic  2.2 us (3%)
  between operations  0.86 us (1%)
    pallas_call x11, Pallas kernels, call(): pl.pallas_call(body, out_shape=outs, in_specs=[pl.BlockSpec(memory_space=...  25.8 us
    ppermute x21, waiting for transfers between devices, send(): return lax.ppermute(value, 'tile', pairs(first, second, core))  19.5 us
    ppermute x21, starting transfers between devices, send(): return lax.ppermute(value, 'tile', pairs(first, second, core))  19.3 us
    ppermute x1, waiting for transfers between devices, per_device(): asked = lax.ppermute(down_cols[0].reshape(1, n), 'pipe', up_pairs)  4.37 us
    ppermute x1, starting transfers between devices, per_device(): cot = lax.ppermute(picked, 'pipe', down_pairs)  2.1 us
    ppermute x1, starting transfers between devices, per_device(): asked = lax.ppermute(down_cols[0].reshape(1, n), 'pipe', up_pairs)  1.92 us
  transfers between devices with their start and end apart: 23, of which 12 were waited for; matrix products, arithmetic and copies ran while one was open for 2% of the time, Pallas kernels for 27%

profile of v3, /device:TPU:8, one launch (start us, length us, event | category | flops | bytes accessed | tf_op | source)
XLA Modules:
  0.0 76.2 jit_solution(16064330391993992888)
XLA Ops:
  0.6 0.9 %shard_map.138 = bf16[3,128,128]{2,1,0:T(8,128)(2,1)S(1)} custom-call(bf16[1,1,1,2,128,128]{5,4,3,2,1,0:T(8,128)(2,1)} %gate_up.1, bf16[1,1,1,128,128]{4,3,2,1,0:T(8,128)(2,1)} %down.1), custom_call_target="tpu_custom_call" | custom-call | tf_op jit(solution)/shard_map/pallas_call | solution.py:92
  1.5 1.6 %collective-permute-start = (bf16[1,3,128,128]{3,2,1,0:T(8,128)(2,1)S(1)}, bf16[1,3,128,128]{3,2,1,0:T(8,128)(2,1)S(1)}, u32[]{:S(2)}, u32[]{:S(2)}) collective-permute-start(bf16[1,3,128,128]{3,2,1,0:T(8,128)(2,1)S(1)} %bitcast.42), channel_id=1, source_target_pairs={{0,8},{1,3},{2,10},{3,5},{4,12},{5,7},{6,14},{7,1},{8,16},{9,11},{... | collective-permute-start | bytes 294920 | tf_op jit(solution)/shard_map/ppermute | solution.py:31
  3.1 2.7 %collective-permute-start.1 = (bf16[1,3,128,128]{3,2,1,0:T(8,128)(2,1)S(1)}, bf16[1,3,128,128]{3,2,1,0:T(8,128)(2,1)S(1)}, u32[]{:S(2)}, u32[]{:S(2)}) collective-permute-start(bf16[1,3,128,128]{3,2,1,0:T(8,128)(2,1)S(1)} %bitcast.43), channel_id=1, source_target_pairs={{0,16},{1,5},{2,18},{3,7},{4,20},{5,1},{6,22},{7,3},{8,24},{9,13},... | collective-permute-start | bytes 294920 | tf_op jit(solution)/shard_map/ppermute | solution.py:31
  5.8 1.4 %collective-permute-start.2 = (bf16[1,3,128,128]{3,2,1,0:T(8,128)(2,1)S(1)}, bf16[1,3,128,128]{3,2,1,0:T(8,128)(2,1)S(1)}, u32[]{:S(2)}, u32[]{:S(2)}) collective-permute-start(bf16[1,3,128,128]{3,2,1,0:T(8,128)(2,1)S(1)} %bitcast.44), channel_id=1, source_target_pairs={{0,24},{1,7},{2,26},{3,1},{4,28},{5,3},{6,30},{7,5},{8,0},{9,15},{... | collective-permute-start | bytes 294920 | tf_op jit(solution)/shard_map/ppermute | solution.py:31
  7.2 1.9 %collective-permute-start.12 = (s32[1,32]{1,0:T(1,128)}, s32[1,32]{1,0:T(1,128)S(1)}, u32[]{:S(2)}, u32[]{:S(2)}) collective-permute-start(s32[1,32]{1,0:T(1,128)} %bitcast.58), channel_id=1, source_target_pairs={{0,32},{32,64},{64,96},{96,128},{128,160},{160,192},{192,224},{224... | collective-permute-start | bytes 392 | tf_op jit(solution)/shard_map/ppermute | solution.py:317
  9.2 1.0 %select_reduce_fusion = (s32[32]{0:T(128)S(1)}, s32[32]{0:T(128)S(1)}, s32[32]{0:T(128)S(1)}, s32[32]{0:T(128)S(1)}, s32[32]{0:T(128)S(1)}, /*index=5*/s32[32]{0:T(128)S(1)}) fusion(s32[32]{0:T(128)} %bitcast.53, s32[32]{0:T(128)S(1)} %multiply_add_fusion.1, s32[32]{0:T(128)} %bitcast.54, s32[32]{0:T(128)} %bitcast.59, s32[32]{0:T(128)} %bitcast.55, ...), kind=kLoop, calls=%fused_computation.17 | loop fusion | flops 13120 | bytes 1664 | tf_op jit(solution)/shard_map/reduce_sum | solution.py:284
  10.2 0.2 select_reduce_fusion.3
  10.4 4.4 %collective-permute-done.12.asked = s32[1,32]{1,0:T(1,128)S(1)} collective-permute-done((s32[1,32]{1,0:T(1,128)}, s32[1,32]{1,0:T(1,128)S(1)}, u32[]{:S(2)}, u32[]{:S(2)}) %collective-permute-start.12) | collective-permute-done | bytes 160 | tf_op jit(solution)/shard_map/ppermute | solution.py:317
  14.7 2.0 %shard_map.141 = bf16[32,128,128]{2,1,0:T(8,128)(2,1)S(1)} custom-call(s32[1,32]{1,0:T(1,128)S(1)} %collective-permute-done.12.asked, bf16[1,128,8192]{2,1,0:T(8,128)(2,1)} %pending.1), custom_call_target="tpu_custom_call" | custom-call | tf_op jit(solution)/shard_map/pallas_call | solution.py:92
  16.8 2.1 %collective-permute-start.13 = (bf16[32,128,128]{2,1,0:T(8,128)(2,1)S(1)}, bf16[32,128,128]{2,1,0:T(8,128)(2,1)S(1)}, u32[]{:S(2)}, u32[]{:S(2)}) collective-permute-start(bf16[32,128,128]{2,1,0:T(8,128)(2,1)S(1)} %shard_map.141), channel_id=1, source_target_pairs={{0,224},{32,0},{64,32},{96,64},{128,96},{160,128},{192,160},{224,1... | collective-permute-start | bytes 3145736 | tf_op jit(solution)/shard_map/ppermute | solution.py:327
  18.9 0.1 pad_maximum_fusion.refs_0_
  18.9 1.7 %collective-permute-start.3 = (bf16[4,3,128,128]{3,2,1,0:T(8,128)(2,1)S(1)}, bf16[4,3,128,128]{3,2,1,0:T(8,128)(2,1)S(1)}, u32[]{:S(2)}, u32[]{:S(2)}) collective-permute-start(bf16[4,3,128,128]{3,2,1,0:T(8,128)(2,1)S(1)} %pad_maximum_fusion.refs_0_), channel_id=1, source_target_pairs={{0,2},{1,9},{2,4},{3,11},{4,6},{5,13},{6,0},{7,15},{8,10},{9,17},{... | collective-permute-start | bytes 1179656 | tf_op jit(solution)/shard_map/ppermute | solution.py:31
  20.6 0.5 collective-permute-start.4
  21.1 3.9 %shard_map.139 = (bf16[32,128,128]{2,1,0:T(8,128)(2,1)S(1)}, bf16[32,128,128]{2,1,0:T(8,128)(2,1)S(1)}) custom-call(s32[8,32]{1,0:T(8,128)S(1)} %stack.23.tab, bf16[1,128,8192]{2,1,0:T(8,128)(2,1)} %x_saved.1), custom_call_target="tpu_custom_call" | custom-call | tf_op jit(solution)/shard_map/pallas_call | solution.py:92
  25.1 1.7 %collective-permute-done.3.refs_1_ = bf16[4,3,128,128]{3,2,1,0:T(8,128)(2,1)S(1)} collective-permute-done((bf16[4,3,128,128]{3,2,1,0:T(8,128)(2,1)S(1)}, bf16[4,3,128,128]{3,2,1,0:T(8,128)(2,1)S(1)}, u32[]{:S(2)}, u32[]{:S(2)}) %collective-permute-start.3) | collective-permute-done | bytes 393248 | tf_op jit(solution)/shard_map/ppermute | solution.py:31
  26.8 1.6 %collective-permute-done.4.refs_4_ = bf16[4,3,128,128]{3,2,1,0:T(8,128)(2,1)S(1)} collective-permute-done((bf16[4,3,128,128]{3,2,1,0:T(8,128)(2,1)S(1)}, bf16[4,3,128,128]{3,2,1,0:T(8,128)(2,1)S(1)}, u32[]{:S(2)}, u32[]{:S(2)}) %collective-permute-start.4) | collective-permute-done | bytes 393248 | tf_op jit(solution)/shard_map/ppermute | solution.py:31
  28.4 0.5 collective-permute-start.6
  28.9 1.7 %collective-permute-start.5 = (bf16[2,3,128,128]{3,2,1,0:T(8,128)(2,1)S(1)}, bf16[2,3,128,128]{3,2,1,0:T(8,128)(2,1)S(1)}, u32[]{:S(2)}, u32[]{:S(2)}) collective-permute-start(bf16[2,3,128,128]{3,2,1,0:T(8,128)(2,1)S(1)} %slice.46), channel_id=1, source_target_pairs={{0,2},{1,9},{2,4},{3,11},{4,6},{5,13},{6,0},{7,15},{8,10},{9,17},{... | collective-permute-start | bytes 589832 | tf_op jit(solution)/shard_map/ppermute | solution.py:31
  30.6 0.5 collective-permute-start.8
  31.1 3.0 %collective-permute-done.6.refs_3_ = bf16[2,3,128,128]{3,2,1,0:T(8,128)(2,1)S(1)} collective-permute-done((bf16[2,3,128,128]{3,2,1,0:T(8,128)(2,1)S(1)}, bf16[2,3,128,128]{3,2,1,0:T(8,128)(2,1)S(1)}, u32[]{:S(2)}, u32[]{:S(2)}) %collective-permute-start.6) | collective-permute-done | bytes 196640 | tf_op jit(solution)/shard_map/ppermute | solution.py:31
  34.1 1.4 %collective-permute-done.5.refs_2_ = bf16[2,3,128,128]{3,2,1,0:T(8,128)(2,1)S(1)} collective-permute-done((bf16[2,3,128,128]{3,2,1,0:T(8,128)(2,1)S(1)}, bf16[2,3,128,128]{3,2,1,0:T(8,128)(2,1)S(1)}, u32[]{:S(2)}, u32[]{:S(2)}) %collective-permute-start.5) | collective-permute-done | bytes 196640 | tf_op jit(solution)/shard_map/ppermute | solution.py:31
  35.6 1.4 %collective-permute-done.9.refs_7_ = bf16[2,3,128,128]{3,2,1,0:T(8,128)(2,1)S(1)} collective-permute-done((bf16[2,3,128,128]{3,2,1,0:T(8,128)(2,1)S(1)}, bf16[2,3,128,128]{3,2,1,0:T(8,128)(2,1)S(1)}, u32[]{:S(2)}, u32[]{:S(2)}) %collective-permute-start.9) | collective-permute-done | bytes 196640 | tf_op jit(solution)/shard_map/ppermute | solution.py:31
  37.0 3.7 %shard_map.140 = (bf16[32,128,384]{2,1,0:T(8,128)(2,1)S(1)}, f32[32,128,256]{2,1,0:T(8,128)S(1)}, bf16[33,128,128]{2,1,0:T(8,128)(2,1)S(1)}) custom-call(s32[8,32]{1,0:T(8,128)S(1)} %stack.23.tab, bf16[32,128,128]{2,1,0:T(8,128)(2,1)S(1)} %get-tuple-element.38.x, bf16[4,3,128,128]{3,2,1,0:T(8,128)(2,1)S(1)} %pad_maximum_fusion.refs_0_, ...), custom_call_target="tpu_custom_call" | custom-call | tf_op jit(solution)/shard_map/pallas_call | solution.py:92
  40.7 2.6 %shard_map.142 = (bf16[4,128,384]{2,1,0:T(8,128)(2,1)S(1)}, f32[4,128,384]{2,1,0:T(8,128)S(1)}, bf16[32,128,256]{2,1,0:T(8,128)(2,1)S(1)}) custom-call(s32[8,32]{1,0:T(8,128)S(1)} %stack.23.tab, bf16[32,128,128]{2,1,0:T(8,128)(2,1)S(1)} %get-tuple-element.37.x_turned, bf16[32,128,384]{2,1,0:T(8,128)(2,1)S(1)} %get-tuple-element.42.w, ...), custom_call_target="tpu_custom_call" | custom-call | tf_op jit(solution)/shard_map/pallas_call | solution.py:92
  43.3 1.1 %shard_map.144 = bf16[12,128,384]{2,1,0:T(8,128)(2,1)S(1)} custom-call(s32[8,32]{1,0:T(8,128)S(1)} %stack.23.tab, bf16[32,128,128]{2,1,0:T(8,128)(2,1)S(1)} %get-tuple-element.37.x_turned, bf16[33,128,128]{2,1,0:T(8,128)(2,1)S(1)} %get-tuple-element.41.h_turned, bf16[32,128,256]{2,1,0:T(8,128)(2,1)S(1)} %get-tuple-element.48.d_gu, ...), custom_call_target="tpu_custom_call" | custom-call | tf_op jit(solution)/shard_map/pallas_call | solution.py:92
  44.4 0.2 collective-permute-start.14
  44.6 0.4 collective-permute-start.15
  45.0 1.1 %shard_map.143 = f32[12,128,384]{2,1,0:T(8,128)S(1)} custom-call(s32[8,32]{1,0:T(8,128)S(1)} %stack.23.tab, bf16[32,128,128]{2,1,0:T(8,128)(2,1)S(1)} %get-tuple-element.37.x_turned, bf16[33,128,128]{2,1,0:T(8,128)(2,1)S(1)} %get-tuple-element.41.h_turned, bf16[32,128,256]{2,1,0:T(8,128)(2,1)S(1)} %get-tuple-element.48.d_gu, ...), custom_call_target="tpu_custom_call" | custom-call | tf_op jit(solution)/shard_map/pallas_call | solution.py:92
  46.1 1.8 %collective-permute-done.15 = bf16[4,128,384]{2,1,0:T(8,128)(2,1)S(1)} collective-permute-done((bf16[4,128,384]{2,1,0:T(8,128)(2,1)S(1)}, bf16[4,128,384]{2,1,0:T(8,128)(2,1)S(1)}, u32[]{:S(2)}, u32[]{:S(2)}) %collective-permute-start.15) | collective-permute-done | bytes 393248 | tf_op jit(solution)/shard_map/ppermute | solution.py:31
  47.9 0.1 add_convert_fusion
  48.0 3.3 %collective-permute-start.16 = (bf16[2,128,384]{2,1,0:T(8,128)(2,1)S(1)}, bf16[2,128,384]{2,1,0:T(8,128)(2,1)S(1)}, u32[]{:S(2)}, u32[]{:S(2)}) collective-permute-start(bf16[2,128,384]{2,1,0:T(8,128)(2,1)S(1)} %get-tuple-element.82), channel_id=1, source_target_pairs={{0,6},{1,25},{2,0},{3,27},{4,2},{5,29},{6,4},{7,31},{8,14},{9,1},{... | collective-permute-start | bytes 589832 | tf_op jit(solution)/shard_map/ppermute | solution.py:31
  51.3 0.3 convert_add_fusion
  51.6 3.2 %shard_map.145 = bf16[1,128,8192]{2,1,0:T(8,128)(2,1)} custom-call(s32[8,32]{1,0:T(8,128)S(1)} %stack.23.tab, bf16[32,128,256]{2,1,0:T(8,128)(2,1)S(1)} %get-tuple-element.48.d_gu, bf16[32,128,384]{2,1,0:T(8,128)(2,1)S(1)} %get-tuple-element.42.w), custom_call_target="tpu_custom_call" | custom-call | flops 536870912 | bytes 2097152 | tf_op jit(solution)/shard_map/pallas_call | solution.py:92
  54.9 2.1 %collective-permute-done.17 = bf16[2,128,384]{2,1,0:T(8,128)(2,1)S(1)} collective-permute-done((bf16[2,128,384]{2,1,0:T(8,128)(2,1)S(1)}, bf16[2,128,384]{2,1,0:T(8,128)(2,1)S(1)}, u32[]{:S(2)}, u32[]{:S(2)}) %collective-permute-start.17) | collective-permute-done | bytes 196640 | tf_op jit(solution)/shard_map/ppermute | solution.py:31
  57.0 0.2 convert.9
  57.2 0.1 fusion.1
  57.4 1.5 %collective-permute-start.18 = (bf16[4,128,384]{2,1,0:T(8,128)(2,1)S(1)}, bf16[4,128,384]{2,1,0:T(8,128)(2,1)S(1)}, u32[]{:S(2)}, u32[]{:S(2)}) collective-permute-start(bf16[4,128,384]{2,1,0:T(8,128)(2,1)S(1)} %pad_maximum_fusion.1), channel_id=1, source_target_pairs={{0,6},{1,25},{2,0},{3,27},{4,2},{5,29},{6,4},{7,31},{8,14},{9,1},{... | collective-permute-start | bytes 1179656 | tf_op jit(solution)/shard_map/ppermute | solution.py:31
  58.9 0.6 collective-permute-start.19
  59.5 3.6 %shard_map.146.h = bf16[33,128,128]{2,1,0:T(8,128)(2,1)S(1)} custom-call(s32[8,32]{1,0:T(8,128)S(1)} %stack.23.tab, bf16[1,128,8192]{2,1,0:T(8,128)(2,1)} %x_next, bf16[32,128,384]{2,1,0:T(8,128)(2,1)S(1)} %get-tuple-element.42.w), custom_call_target="tpu_custom_call" | custom-call | flops 536870912 | bytes 2097152 | tf_op jit(solution)/shard_map/pallas_call | solution.py:92
  63.2 2.1 %collective-permute-done.18 = bf16[4,128,384]{2,1,0:T(8,128)(2,1)S(1)} collective-permute-done((bf16[4,128,384]{2,1,0:T(8,128)(2,1)S(1)}, bf16[4,128,384]{2,1,0:T(8,128)(2,1)S(1)}, u32[]{:S(2)}, u32[]{:S(2)}) %collective-permute-start.18) | collective-permute-done | bytes 393248 | tf_op jit(solution)/shard_map/ppermute | solution.py:31
  65.3 1.4 %collective-permute-done.19 = bf16[4,128,384]{2,1,0:T(8,128)(2,1)S(1)} collective-permute-done((bf16[4,128,384]{2,1,0:T(8,128)(2,1)S(1)}, bf16[4,128,384]{2,1,0:T(8,128)(2,1)S(1)}, u32[]{:S(2)}, u32[]{:S(2)}) %collective-permute-start.19) | collective-permute-done | bytes 393248 | tf_op jit(solution)/shard_map/ppermute | solution.py:31
  66.7 0.1 fusion
  66.9 0.1 collective-permute-start.20
  67.0 2.7 %collective-permute-start.21 = (bf16[128,384]{1,0:T(8,128)(2,1)S(1)}, bf16[128,384]{1,0:T(8,128)(2,1)S(1)}, u32[]{:S(2)}, u32[]{:S(2)}) collective-permute-start(bf16[128,384]{1,0:T(8,128)(2,1)S(1)} %get-tuple-element.79), channel_id=1, source_target_pairs={{0,16},{1,5},{2,18},{3,7},{4,20},{5,1},{6,22},{7,3},{8,24},{9,13},... | collective-permute-start | bytes 294920 | tf_op jit(solution)/shard_map/ppermute | solution.py:31
  69.7 3.0 %shard_map.147 = bf16[1,128,8192]{2,1,0:T(8,128)(2,1)} custom-call(s32[8,32]{1,0:T(8,128)S(1)} %stack.23.tab, bf16[33,128,128]{2,1,0:T(8,128)(2,1)S(1)} %shard_map.146.h, bf16[32,128,384]{2,1,0:T(8,128)(2,1)S(1)} %get-tuple-element.42.w), custom_call_target="tpu_custom_call" | custom-call | flops 536870912 | bytes 2097152 | tf_op jit(solution)/shard_map/pallas_call | solution.py:92
  72.6 0.6 collective-permute-done.21.two
  73.2 2.3 %collective-permute-done.22.three = bf16[128,384]{1,0:T(8,128)(2,1)S(1)} collective-permute-done((bf16[128,384]{1,0:T(8,128)(2,1)S(1)}, bf16[128,384]{1,0:T(8,128)(2,1)S(1)}, u32[]{:S(2)}, u32[]{:S(2)}) %collective-permute-start.22) | collective-permute-done | bytes 98336 | tf_op jit(solution)/shard_map/ppermute | solution.py:31
  75.5 0.7 shard_map.148
  (31 shorter events, 0.5 us)
Async XLA Ops:
  1.5 17.4 %collective-permute-start = (bf16[1,3,128,128]{3,2,1,0:T(8,128)(2,1)S(1)}, bf16[1,3,128,128]{3,2,1,0:T(8,128)(2,1)S(1)}, u32[]{:S(2)}, u32[]{:S(2)}) collective-permute-start(bf16[1,3,128,128]{3,2,1,0:T(8,128)(2,1)S(1)} %bitcast.42), channel_id=1, source_target_pairs={{0,8},{1,3},{2,10},{3,5},{4,12},{5,7},{6,14},{7,1},{8,16},{9,11},{... | collective-permute-start | bytes 294920 | tf_op jit(solution)/shard_map/ppermute | solution.py:31
  3.1 15.8 %collective-permute-start.1 = (bf16[1,3,128,128]{3,2,1,0:T(8,128)(2,1)S(1)}, bf16[1,3,128,128]{3,2,1,0:T(8,128)(2,1)S(1)}, u32[]{:S(2)}, u32[]{:S(2)}) collective-permute-start(bf16[1,3,128,128]{3,2,1,0:T(8,128)(2,1)S(1)} %bitcast.43), channel_id=1, source_target_pairs={{0,16},{1,5},{2,18},{3,7},{4,20},{5,1},{6,22},{7,3},{8,24},{9,13},... | collective-permute-start | bytes 294920 | tf_op jit(solution)/shard_map/ppermute | solution.py:31
  5.8 13.1 %collective-permute-start.2 = (bf16[1,3,128,128]{3,2,1,0:T(8,128)(2,1)S(1)}, bf16[1,3,128,128]{3,2,1,0:T(8,128)(2,1)S(1)}, u32[]{:S(2)}, u32[]{:S(2)}) collective-permute-start(bf16[1,3,128,128]{3,2,1,0:T(8,128)(2,1)S(1)} %bitcast.44), channel_id=1, source_target_pairs={{0,24},{1,7},{2,26},{3,1},{4,28},{5,3},{6,30},{7,5},{8,0},{9,15},{... | collective-permute-start | bytes 294920 | tf_op jit(solution)/shard_map/ppermute | solution.py:31
  7.2 7.5 %collective-permute-start.12 = (s32[1,32]{1,0:T(1,128)}, s32[1,32]{1,0:T(1,128)S(1)}, u32[]{:S(2)}, u32[]{:S(2)}) collective-permute-start(s32[1,32]{1,0:T(1,128)} %bitcast.58), channel_id=1, source_target_pairs={{0,32},{32,64},{64,96},{96,128},{128,160},{160,192},{192,224},{224... | collective-permute-start | bytes 392 | tf_op jit(solution)/shard_map/ppermute | solution.py:317
  16.8 23.9 %collective-permute-start.13 = (bf16[32,128,128]{2,1,0:T(8,128)(2,1)S(1)}, bf16[32,128,128]{2,1,0:T(8,128)(2,1)S(1)}, u32[]{:S(2)}, u32[]{:S(2)}) collective-permute-start(bf16[32,128,128]{2,1,0:T(8,128)(2,1)S(1)} %shard_map.141), channel_id=1, source_target_pairs={{0,224},{32,0},{64,32},{96,64},{128,96},{160,128},{192,160},{224,1... | collective-permute-start | bytes 3145736 | tf_op jit(solution)/shard_map/ppermute | solution.py:327
  18.9 7.9 %collective-permute-start.3 = (bf16[4,3,128,128]{3,2,1,0:T(8,128)(2,1)S(1)}, bf16[4,3,128,128]{3,2,1,0:T(8,128)(2,1)S(1)}, u32[]{:S(2)}, u32[]{:S(2)}) collective-permute-start(bf16[4,3,128,128]{3,2,1,0:T(8,128)(2,1)S(1)} %pad_maximum_fusion.refs_0_), channel_id=1, source_target_pairs={{0,2},{1,9},{2,4},{3,11},{4,6},{5,13},{6,0},{7,15},{8,10},{9,17},{... | collective-permute-start | bytes 1179656 | tf_op jit(solution)/shard_map/ppermute | solution.py:31
  20.6 7.8 %collective-permute-start.4 = (bf16[4,3,128,128]{3,2,1,0:T(8,128)(2,1)S(1)}, bf16[4,3,128,128]{3,2,1,0:T(8,128)(2,1)S(1)}, u32[]{:S(2)}, u32[]{:S(2)}) collective-permute-start(bf16[4,3,128,128]{3,2,1,0:T(8,128)(2,1)S(1)} %pad_maximum_fusion.refs_0_), channel_id=1, source_target_pairs={{0,6},{1,25},{2,0},{3,27},{4,2},{5,29},{6,4},{7,31},{8,14},{9,1},{... | collective-permute-start | bytes 1179656 | tf_op jit(solution)/shard_map/ppermute | solution.py:31
  21.1 9.5 %collective-permute-start.7 = (bf16[4,3,128,128]{3,2,1,0:T(8,128)(2,1)S(1)}, bf16[4,3,128,128]{3,2,1,0:T(8,128)(2,1)}, u32[]{:S(2)}, u32[]{:S(2)}) collective-permute-start(bf16[4,3,128,128]{3,2,1,0:T(8,128)(2,1)S(1)} %pad_maximum_fusion.refs_0_), channel_id=1, source_target_pairs={{0,1},{1,0},{2,3},{3,2},{4,5},{5,4},{6,7},{7,6},{8,9},{9,8},{10,11... | collective-permute-start | bytes 1179656 | tf_op jit(solution)/shard_map/ppermute | solution.py:31
  28.4 5.7 %collective-permute-start.6 = (bf16[2,3,128,128]{3,2,1,0:T(8,128)(2,1)S(1)}, bf16[2,3,128,128]{3,2,1,0:T(8,128)(2,1)S(1)}, u32[]{:S(2)}, u32[]{:S(2)}) collective-permute-start(bf16[2,3,128,128]{3,2,1,0:T(8,128)(2,1)S(1)} %slice.47), channel_id=1, source_target_pairs={{0,6},{1,25},{2,0},{3,27},{4,2},{5,29},{6,4},{7,31},{8,14},{9,1},{... | collective-permute-start | bytes 589832 | tf_op jit(solution)/shard_map/ppermute | solution.py:31
  28.9 6.6 %collective-permute-start.5 = (bf16[2,3,128,128]{3,2,1,0:T(8,128)(2,1)S(1)}, bf16[2,3,128,128]{3,2,1,0:T(8,128)(2,1)S(1)}, u32[]{:S(2)}, u32[]{:S(2)}) collective-permute-start(bf16[2,3,128,128]{3,2,1,0:T(8,128)(2,1)S(1)} %slice.46), channel_id=1, source_target_pairs={{0,2},{1,9},{2,4},{3,11},{4,6},{5,13},{6,0},{7,15},{8,10},{9,17},{... | collective-permute-start | bytes 589832 | tf_op jit(solution)/shard_map/ppermute | solution.py:31
  30.6 6.4 %collective-permute-start.11 = (bf16[4,3,128,128]{3,2,1,0:T(8,128)(2,1)S(1)}, bf16[4,3,128,128]{3,2,1,0:T(8,128)(2,1)S(1)}, u32[]{:S(2)}, u32[]{:S(2)}) collective-permute-start(bf16[4,3,128,128]{3,2,1,0:T(8,128)(2,1)S(1)} %collective-permute-done.4.refs_4_), channel_id=1, source_target_pairs={{0,1},{1,0},{2,3},{3,2},{4,5},{5,4},{6,7},{7,6},{8,9},{9,8},{10,11... | collective-permute-start | bytes 1179656 | tf_op jit(solution)/shard_map/ppermute | solution.py:31
  30.6 6.4 %collective-permute-start.8 = (bf16[4,3,128,128]{3,2,1,0:T(8,128)(2,1)S(1)}, bf16[4,3,128,128]{3,2,1,0:T(8,128)(2,1)S(1)}, u32[]{:S(2)}, u32[]{:S(2)}) collective-permute-start(bf16[4,3,128,128]{3,2,1,0:T(8,128)(2,1)S(1)} %collective-permute-done.3.refs_1_), channel_id=1, source_target_pairs={{0,1},{1,0},{2,3},{3,2},{4,5},{5,4},{6,7},{7,6},{8,9},{9,8},{10,11... | collective-permute-start | bytes 1179656 | tf_op jit(solution)/shard_map/ppermute | solution.py:31
  34.1 1.4 %collective-permute-start.10 = (bf16[2,3,128,128]{3,2,1,0:T(8,128)(2,1)S(1)}, bf16[2,3,128,128]{3,2,1,0:T(8,128)(2,1)S(1)}, u32[]{:S(2)}, u32[]{:S(2)}) collective-permute-start(bf16[2,3,128,128]{3,2,1,0:T(8,128)(2,1)S(1)} %collective-permute-done.6.refs_3_), channel_id=1, source_target_pairs={{0,1},{1,0},{2,3},{3,2},{4,5},{5,4},{6,7},{7,6},{8,9},{9,8},{10,11... | collective-permute-start | bytes 589832 | tf_op jit(solution)/shard_map/ppermute | solution.py:31
  35.5 1.4 %collective-permute-start.9 = (bf16[2,3,128,128]{3,2,1,0:T(8,128)(2,1)S(1)}, bf16[2,3,128,128]{3,2,1,0:T(8,128)(2,1)S(1)}, u32[]{:S(2)}, u32[]{:S(2)}) collective-permute-start(bf16[2,3,128,128]{3,2,1,0:T(8,128)(2,1)S(1)} %collective-permute-done.5.refs_2_), channel_id=1, source_target_pairs={{0,1},{1,0},{2,3},{3,2},{4,5},{5,4},{6,7},{7,6},{8,9},{9,8},{10,11... | collective-permute-start | bytes 589832 | tf_op jit(solution)/shard_map/ppermute | solution.py:31
  44.4 7.0 %collective-permute-start.14 = (bf16[12,128,384]{2,1,0:T(8,128)(2,1)S(1)}, bf16[12,128,384]{2,1,0:T(8,128)(2,1)S(1)}, u32[]{:S(2)}, u32[]{:S(2)}) collective-permute-start(bf16[12,128,384]{2,1,0:T(8,128)(2,1)S(1)} %shard_map.144), channel_id=1, source_target_pairs={{0,1},{1,0},{2,3},{3,2},{4,5},{5,4},{6,7},{7,6},{8,9},{9,8},{10,11... | collective-permute-start | bytes 3538952 | tf_op jit(solution)/shard_map/ppermute | solution.py:31
  44.6 3.3 %collective-permute-start.15 = (bf16[4,128,384]{2,1,0:T(8,128)(2,1)S(1)}, bf16[4,128,384]{2,1,0:T(8,128)(2,1)S(1)}, u32[]{:S(2)}, u32[]{:S(2)}) collective-permute-start(bf16[4,128,384]{2,1,0:T(8,128)(2,1)S(1)} %get-tuple-element.47), channel_id=1, source_target_pairs={{0,1},{1,0},{2,3},{3,2},{4,5},{5,4},{6,7},{7,6},{8,9},{9,8},{10,11... | collective-permute-start | bytes 1179656 | tf_op jit(solution)/shard_map/ppermute | solution.py:31
  48.0 6.8 %collective-permute-start.16 = (bf16[2,128,384]{2,1,0:T(8,128)(2,1)S(1)}, bf16[2,128,384]{2,1,0:T(8,128)(2,1)S(1)}, u32[]{:S(2)}, u32[]{:S(2)}) collective-permute-start(bf16[2,128,384]{2,1,0:T(8,128)(2,1)S(1)} %get-tuple-element.82), channel_id=1, source_target_pairs={{0,6},{1,25},{2,0},{3,27},{4,2},{5,29},{6,4},{7,31},{8,14},{9,1},{... | collective-permute-start | bytes 589832 | tf_op jit(solution)/shard_map/ppermute | solution.py:31
  51.3 5.7 %collective-permute-start.17 = (bf16[2,128,384]{2,1,0:T(8,128)(2,1)S(1)}, bf16[2,128,384]{2,1,0:T(8,128)(2,1)S(1)}, u32[]{:S(2)}, u32[]{:S(2)}) collective-permute-start(bf16[2,128,384]{2,1,0:T(8,128)(2,1)S(1)} %get-tuple-element.81), channel_id=1, source_target_pairs={{0,2},{1,9},{2,4},{3,11},{4,6},{5,13},{6,0},{7,15},{8,10},{9,17},{... | collective-permute-start | bytes 589832 | tf_op jit(solution)/shard_map/ppermute | solution.py:31
  57.4 7.9 %collective-permute-start.18 = (bf16[4,128,384]{2,1,0:T(8,128)(2,1)S(1)}, bf16[4,128,384]{2,1,0:T(8,128)(2,1)S(1)}, u32[]{:S(2)}, u32[]{:S(2)}) collective-permute-start(bf16[4,128,384]{2,1,0:T(8,128)(2,1)S(1)} %pad_maximum_fusion.1), channel_id=1, source_target_pairs={{0,6},{1,25},{2,0},{3,27},{4,2},{5,29},{6,4},{7,31},{8,14},{9,1},{... | collective-permute-start | bytes 1179656 | tf_op jit(solution)/shard_map/ppermute | solution.py:31
  58.9 7.8 %collective-permute-start.19 = (bf16[4,128,384]{2,1,0:T(8,128)(2,1)S(1)}, bf16[4,128,384]{2,1,0:T(8,128)(2,1)S(1)}, u32[]{:S(2)}, u32[]{:S(2)}) collective-permute-start(bf16[4,128,384]{2,1,0:T(8,128)(2,1)S(1)} %pad_maximum_fusion.2), channel_id=1, source_target_pairs={{0,2},{1,9},{2,4},{3,11},{4,6},{5,13},{6,0},{7,15},{8,10},{9,17},{... | collective-permute-start | bytes 1179656 | tf_op jit(solution)/shard_map/ppermute | solution.py:31
  66.9 5.7 %collective-permute-start.20 = (bf16[128,384]{1,0:T(8,128)(2,1)S(1)}, bf16[128,384]{1,0:T(8,128)(2,1)S(1)}, u32[]{:S(2)}, u32[]{:S(2)}) collective-permute-start(bf16[128,384]{1,0:T(8,128)(2,1)S(1)} %get-tuple-element.80), channel_id=1, source_target_pairs={{0,24},{1,7},{2,26},{3,1},{4,28},{5,3},{6,30},{7,5},{8,0},{9,15},{... | collective-permute-start | bytes 294920 | tf_op jit(solution)/shard_map/ppermute | solution.py:31
  67.0 6.2 %collective-permute-start.21 = (bf16[128,384]{1,0:T(8,128)(2,1)S(1)}, bf16[128,384]{1,0:T(8,128)(2,1)S(1)}, u32[]{:S(2)}, u32[]{:S(2)}) collective-permute-start(bf16[128,384]{1,0:T(8,128)(2,1)S(1)} %get-tuple-element.79), channel_id=1, source_target_pairs={{0,16},{1,5},{2,18},{3,7},{4,20},{5,1},{6,22},{7,3},{8,24},{9,13},... | collective-permute-start | bytes 294920 | tf_op jit(solution)/shard_map/ppermute | solution.py:31
  69.6 5.8 %collective-permute-start.22 = (bf16[128,384]{1,0:T(8,128)(2,1)S(1)}, bf16[128,384]{1,0:T(8,128)(2,1)S(1)}, u32[]{:S(2)}, u32[]{:S(2)}) collective-permute-start(bf16[128,384]{1,0:T(8,128)(2,1)S(1)} %get-tuple-element.78), channel_id=1, source_target_pairs={{0,8},{1,3},{2,10},{3,5},{4,12},{5,7},{6,14},{7,1},{8,16},{9,11},{... | collective-permute-start | bytes 294920 | tf_op jit(solution)/shard_map/ppermute | solution.py:31

commit v4 on v3

--- a/solution.py
+++ b/solution.py
@@ -14,6 +14,14 @@
 BF16 = jnp.bfloat16
 UNROLL = 16
 ROWS, LEAD, FIRST, HSLOT, DCOLS, OWNER, GLIVE, DLIVE = range(8)
+
+OTHER = (0, 0, 0, 1, 0, 1, 1, 1)
+STEPS = (0, 1, 3, 0, 2, 1, 3, 2)
+
+
+def group(other, j):
+    [g] = [g for g in range(len(STEPS)) if (OTHER[g], STEPS[g]) == (other, j)]
+    return [g * SIDE + i for i in range(SIDE)]
 
 
 def pairs(first, second, core=0):
@@ -35,15 +43,8 @@
     return lax.optimization_barrier(values)
 
 
-def gather_tiles(own, busy):
-    own = own[None]
-    one, three, two = send(own, 1, 0), send(own, -1, 0), send(own, 2, 0)
-    near = jnp.concatenate([own, one, two, three], axis=0)
-    back, ahead = send(near, 0, 1), send(near, 0, -1)
-    back, ahead, *busy = together(back, ahead, *busy)
-    low, high = send(back[:2], 0, 1), send(ahead[2:], 0, -1)
-    mine = [near, back, low, high, ahead]
-    return mine + [send(part, 0, 0, 1) for part in mine], busy
+def core(value):
+    return send(value, 0, 0, 1)
 
 
 def plus(a, b):
@@ -58,11 +59,6 @@
     lax.fori_loop(0, count // unroll, group, 0)
 
 
-def flat(count, unroll, body):
-    for i in range(0, count, unroll):
-        body(list(range(i, i + unroll)))
-
-
 def cols(block_index):
     return pl.ds(pl.multiple_of(block_index * B, B), B)
 
@@ -88,7 +84,7 @@
     return pltpu.VMEM(shape, dtype)
 
 
-def call(body, outs, scratch, scalars, arrays, limit, flops=0, far=(), out_space=VMEM):
+def call(body, outs, scratch, scalars, arrays, limit, flops=0, far=(), out_space=VMEM, aliases={}):
     return pl.pallas_call(
         body,
         out_shape=outs,
@@ -97,16 +93,10 @@
         + [pl.BlockSpec(memory_space=VMEM) for _ in arrays],
         out_specs=[pl.BlockSpec(memory_space=out_space) for _ in outs],
         scratch_shapes=scratch,
+        input_output_aliases=aliases,
         compiler_params=pltpu.CompilerParams(vmem_limit_bytes=limit << 20),
         cost_estimate=pl.CostEstimate(flops=flops, bytes_accessed=flops // 256, transcendentals=0),
     )(*scalars, *[pltpu.with_memory_space_constraint(a, pltpu.HBM) for a in far], *[pltpu.with_memory_space_constraint(a, VMEM) for a in arrays])
-
-
-def pick(n, source, table, row, out, sems):
-    return [
-        pltpu.make_async_copy(source.at[0, :, cols(table[row, k])], out.at[k], sems.at[k])
-        for k in range(n)
-    ]
 
 
 def pack_kernel(gate_up, down, out, sems):
@@ -120,44 +110,57 @@
         copy.wait()
 
 
-def pick_kernel(n, asked, pending, out, sems):
-    copies = pick(n, pending, asked, 0, out, sems)
-    for copy in copies:
-        copy.start()
-    for copy in copies:
-        copy.wait()
-
-
-def saved_kernel(n, tab, x_saved, out, turned, sems):
-    copies = pick(n, x_saved, tab, ROWS, out, sems)
-    for copy in copies:
-        copy.start()
-    for k, copy in enumerate(copies):
-        copy.wait()
-        turned[k] = out[k].T
-
-
-def project(n, tab, x, w_of, acc, walk):
-    def some(ks):
-        parts = [rounded(dot(x[k], w_of(k)) * live(tab, GLIVE, k)) for k in ks]
-        for k, part in zip(ks, parts):
-            lead = tab[LEAD, k]
-            acc[lead] = jnp.where(tab[FIRST, k] == 1, part, acc[lead] + part)
-
-    walk(n, UNROLL, some)
-
-
-def forward_saved_kernel(n, tab, x, *refs):
-    *pieces, w, coef, h_turned, acc = refs
+def fetch_kernel(source, out, sem):
+    copy = pltpu.make_async_copy(source.at[0], out, sem)
+    copy.start()
+    copy.wait()
+
+
+def pick_kernel(n, asked, pending, out):
+    for k in range(n):
+        out[k] = pending[:, cols(asked[0, k])]
+
+
+def saved_kernel(n, tab, x_saved, out, turned, x, sem):
+    fetch_kernel(x_saved, x, sem)
+    for k in range(n):
+        block = x[:, cols(tab[ROWS, k])]
+        out[k] = block
+        turned[k] = block.T
+
+
+def project(tab, slots, x_of, w_of, acc):
+    parts = [rounded(dot(x_of(k), w_of(k)) * live(tab, GLIVE, k)) for k in slots]
+    for k, part in zip(slots, parts):
+        lead = tab[LEAD, k]
+        acc[lead] = jnp.where(tab[FIRST, k] == 1, part, acc[lead] + part)
+
+
+def project_pieces(tab, start, x, pieces, w, acc):
     places = [(piece, i) for piece in pieces for i in range(piece.shape[0])]
 
     def w_of(k):
-        piece, i = places[k]
+        piece, i = places[k - start]
         gate, up = piece[i, 0], piece[i, 1]
         w[k, :, :B], w[k, :, B : 2 * B], w[k, :, 2 * B :] = gate, up, piece[i, 2]
         return jnp.concatenate([gate, up], axis=1)
 
-    project(n, tab, x, w_of, acc, flat)
+    project(tab, range(start, start + len(places)), lambda k: x[k], w_of, acc)
+
+
+def saved_first_kernel(tab, x, *refs):
+    *pieces, w, acc = refs
+    project_pieces(tab, 0, x, pieces, w, acc)
+
+
+def saved_more_kernel(start, tab, x, *refs):
+    *pieces, _, _, w, acc = refs
+    project_pieces(tab, start, x, pieces, w, acc)
+
+
+def saved_last_kernel(n, start, tab, x, *refs):
+    *pieces, _, _, w, acc, coef, h_turned = refs
+    project_pieces(tab, start, x, pieces, w, acc)
 
     def activate(ks):
         for k in ks:
@@ -172,13 +175,13 @@
     h_turned[n] = jnp.zeros((B, B), BF16)
 
 
-def forward_next_kernel(n, tab, x_next, w, h, acc, x, sems):
-    copies = pick(n, x_next, tab, ROWS, x, sems)
-    for copy in copies:
-        copy.start()
-    for copy in copies:
-        copy.wait()
-    project(n, tab, x, lambda k: w[k, :, : 2 * B], acc, loop)
+def forward_next_kernel(n, tab, x_next, w, h, acc, x, sem):
+    fetch_kernel(x_next, x, sem)
+
+    def some(ks):
+        project(tab, ks, lambda k: x[:, cols(tab[ROWS, k])], lambda k: w[k, :, : 2 * B], acc)
+
+    loop(n, UNROLL, some)
 
     def activate(ks):
         for k in ks:
@@ -273,8 +276,8 @@
 def tables(mine, g_rows, g_cols, g_live, d_rows, d_cols, d_live):
     n = g_rows.shape[0]
     ids = jnp.arange(n, dtype=jnp.int32)
-    kind = (ids // CHIPS + mine) % 2
-    j, i = (ids // SIDE) % SIDE, ids % SIDE
+    kind = (jnp.repeat(jnp.array(OTHER, jnp.int32), SIDE) + mine) % 2
+    j, i = jnp.repeat(jnp.array(STEPS, jnp.int32), SIDE), ids % SIDE
     x = (mine // (2 * SIDE) - jnp.where(kind == 0, i, j)) % SIDE
     y = ((mine // 2) % SIDE - jnp.where(kind == 0, j, i)) % SIDE
     owner = (x * SIDE + y) * 2 + kind
@@ -315,16 +318,28 @@
     up_pairs = [(s, (s + 1) % sections) for s in range(sections)]
     down_pairs = [(s, (s - 1) % sections) for s in range(sections)]
     asked = lax.ppermute(down_cols[0].reshape(1, n), "pipe", up_pairs)
+    one_copy = [pltpu.SemaphoreType.DMA]
+    [held_back] = call(fetch_kernel, [kept((tok, width), BF16)], one_copy, [], [], 2, far=[pending])
     [picked] = call(
-        part(pick_kernel, n),
-        [kept((n, tok, B), BF16)],
-        [pltpu.SemaphoreType.DMA((n,))],
-        [asked],
+        part(pick_kernel, n), [kept((n, tok, B), BF16)], [], [asked], [held_back], 2
+    )
+    cot = lax.ppermute(picked, "pipe", down_pairs)
+
+    [own] = call(
+        pack_kernel,
+        [kept((3, B, B), BF16)],
+        [pltpu.SemaphoreType.DMA((2,))],
+        [],
         [],
         2,
-        far=[pending],
-    )
-    cot = lax.ppermute(picked, "pipe", down_pairs)
+        far=[gate_up_tiles, down_tiles],
+    )
+    own = own[None]
+    one, three, two = send(own, 1, 0), send(own, -1, 0), send(own, 2, 0)
+    near = jnp.concatenate([own, one, two, three], axis=0)
+    near, gu_rows, gu_cols, down_rows = together(near, gu_rows, gu_cols, down_rows)
+    back, ahead = send(near, 0, 1), send(near, 0, -1)
+    near_core = core(near)
 
     tab = tables(
         mine,
@@ -338,34 +353,44 @@
     x_blocks, x_turned = call(
         part(saved_kernel, n),
         [kept((n, tok, B), BF16), kept((n, B, tok), BF16)],
-        [pltpu.SemaphoreType.DMA((n,))],
-        [tab],
-        [],
-        2,
+        [VMEM((tok, width), BF16), *one_copy],
+        [tab],
+        [],
+        4,
         far=[x_saved],
     )
-    [own] = call(
-        pack_kernel,
-        [kept((3, B, B), BF16)],
-        [pltpu.SemaphoreType.DMA((2,))],
-        [],
-        [],
-        2,
-        far=[gate_up_tiles, down_tiles],
-    )
-    pieces, (x_blocks, x_turned) = gather_tiles(own, [x_blocks, x_turned])
-    w, coef, h_turned = call(
-        part(forward_saved_kernel, n),
-        [kept((n, B, 3 * B), BF16), kept((n, tok, 2 * B), F32), kept((n + 1, B, tok), BF16)],
-        [VMEM((n, tok, 2 * B), F32)],
-        [tab],
-        [x_blocks, *pieces],
-        8,
-    )
-    ring = [[4 * j + i for i in range(SIDE)] for j in range(SIDE)]
-    late_slots = ring[1] + ring[3] + ring[0]
+    back, ahead, x_blocks, x_turned = together(back, ahead, x_blocks, x_turned)
+    low, high = send(back[:2], 0, 1), send(ahead[2:], 0, -1)
+    tiles, gates = kept((n, B, 3 * B), BF16), kept((n, tok, 2 * B), F32)
+    w, acc = call(
+        saved_first_kernel, [tiles, gates], [], [tab], [x_blocks, near, back, ahead, near_core], 6
+    )
+    low, high, w, acc = together(low, high, w, acc)
+    more = [low, high, core(back), core(ahead)]
+    w, acc = call(
+        part(saved_more_kernel, CHIPS),
+        [tiles, gates],
+        [],
+        [tab],
+        [x_blocks, *more, w, acc],
+        6,
+        aliases={6: 0, 7: 1},
+    )
+    last = [core(low), core(high)]
+    w, acc, coef, h_turned = call(
+        part(saved_last_kernel, n, n - SIDE),
+        [tiles, gates, gates, kept((n + 1, B, tok), BF16)],
+        [],
+        [tab],
+        [x_blocks, *last, w, acc],
+        6,
+        aliases={4: 0, 5: 1},
+    )
+    late_steps = (1, 3, 0)
+    own_late_slots = sum((group(0, j) for j in late_steps), [])
+    other_late_slots = sum((group(1, j) for j in late_steps), [])
     other_first, own_first, d_gu = call(
-        part(backward_kernel, n, [[CHIPS + k for k in ring[2]], ring[2]]),
+        part(backward_kernel, n, [group(1, 2), group(0, 2)]),
         [
             kept((SIDE, B, 3 * B), BF16),
             kept((SIDE, B, 3 * B), F32),
@@ -376,28 +401,28 @@
         [x_turned, w, coef, h_turned, cot],
         6,
     )
-    first = send(other_first, 0, 0, 1)
-    [other_late] = call(
-        part(grads_kernel, [[CHIPS + k for k in late_slots]]),
-        [kept((CHIPS - SIDE, B, 3 * B), BF16)],
+    first = core(other_first)
+    [own_late] = call(
+        part(grads_kernel, [own_late_slots]),
+        [kept((CHIPS - SIDE, B, 3 * B), F32)],
         [],
         [tab],
         [x_turned, h_turned, d_gu, cot],
         4,
     )
-    late = send(other_late, 0, 0, 1)
     held = plus(own_first, first)
+    held, own_late, d_gu = together(held, own_late, d_gu)
     low, high = send(held[:2], 0, -1), send(held[2:], 0, 1)
-    [own_late] = call(
-        part(grads_kernel, [late_slots]),
-        [kept((CHIPS - SIDE, B, 3 * B), F32)],
+    [other_late] = call(
+        part(grads_kernel, [other_late_slots]),
+        [kept((CHIPS - SIDE, B, 3 * B), BF16)],
         [],
         [tab],
         [x_turned, h_turned, d_gu, cot],
         4,
     )
+    late = core(other_late)
     both = (own_late + late.astype(F32)).reshape(SIDE - 1, SIDE, B, 3 * B)
-    both, d_gu = together(both, d_gu)
     [dx] = call(
         part(dx_kernel, n),
         [jax.ShapeDtypeStruct((1, tok, width), BF16)],
@@ -415,7 +440,7 @@
     [h_next] = call(
         part(forward_next_kernel, n),
         [kept((n + 1, tok, B), BF16)],
-        [VMEM((n, tok, 2 * B), F32), VMEM((n, tok, B), BF16), pltpu.SemaphoreType.DMA((n,))],
+        [VMEM((n, tok, 2 * B), F32), VMEM((tok, width), BF16), *one_copy],
         [tab],
         [w],
         9,

time: 76.7 us -> 74.9 us (0.977)
  the two profiles are of different devices: /device:TPU:8 before, /device:TPU:96 now
where the time goes in v4:
time: 74.9 us; the launch traced here: 74.6 us
  Pallas kernels  26.3 us (35%)
  starting transfers between devices  24.7 us (33%)
  waiting for transfers between devices  19.1 us (26%)
  other arithmetic  2.12 us (3%)
  local copies, waits for them, and re-layouts  1.34 us (2%)
  between operations  1.02 us (1%)
    pallas_call x14, Pallas kernels, call(): pl.pallas_call(body, out_shape=outs, in_specs=[pl.BlockSpec(memory_space=...  26.3 us
    ppermute x21, starting transfers between devices, send(): return lax.ppermute(value, 'tile', pairs(first, second, core))  21.5 us
    ppermute x21, waiting for transfers between devices, send(): return lax.ppermute(value, 'tile', pairs(first, second, core))  14.7 us
    ppermute x1, waiting for transfers between devices, per_device(): cot = lax.ppermute(picked, 'pipe', down_pairs)  4.36 us
    ppermute x1, starting transfers between devices, per_device(): asked = lax.ppermute(down_cols[0].reshape(1, n), 'pipe', up_pairs)  3.13 us
  transfers between devices with their start and end apart: 23, of which 13 were waited for; matrix products, arithmetic and copies ran while one was open for 3% of the time, Pallas kernels for 28%

profile of v4, /device:TPU:96, one launch (start us, length us, event | category | flops | bytes accessed | tf_op | source)
XLA Modules:
  0.0 74.6 jit_solution(597661332952981212)
XLA Ops:
  0.6 0.9 %shard_map.156 = bf16[3,128,128]{2,1,0:T(8,128)(2,1)S(1)} custom-call(bf16[1,1,1,2,128,128]{5,4,3,2,1,0:T(8,128)(2,1)} %gate_up.1, bf16[1,1,1,128,128]{4,3,2,1,0:T(8,128)(2,1)} %down.1), custom_call_target="tpu_custom_call" | custom-call | tf_op jit(solution)/shard_map/pallas_call | solution.py:88
  1.5 2.8 %collective-permute-start.2 = (bf16[1,3,128,128]{3,2,1,0:T(8,128)(2,1)S(1)}, bf16[1,3,128,128]{3,2,1,0:T(8,128)(2,1)S(1)}, u32[]{:S(2)}, u32[]{:S(2)}) collective-permute-start(bf16[1,3,128,128]{3,2,1,0:T(8,128)(2,1)S(1)} %bitcast.42), channel_id=1, source_target_pairs={{0,24},{1,7},{2,26},{3,1},{4,28},{5,3},{6,30},{7,5},{8,0},{9,15},{... | collective-permute-start | bytes 294920 | tf_op jit(solution)/shard_map/ppermute | solution.py:39
  4.3 0.8 %collective-permute-start.1 = (bf16[1,3,128,128]{3,2,1,0:T(8,128)(2,1)S(1)}, bf16[1,3,128,128]{3,2,1,0:T(8,128)(2,1)S(1)}, u32[]{:S(2)}, u32[]{:S(2)}) collective-permute-start(bf16[1,3,128,128]{3,2,1,0:T(8,128)(2,1)S(1)} %bitcast.43), channel_id=1, source_target_pairs={{0,16},{1,5},{2,18},{3,7},{4,20},{5,1},{6,22},{7,3},{8,24},{9,13},... | collective-permute-start | bytes 294920 | tf_op jit(solution)/shard_map/ppermute | solution.py:39
  5.1 0.9 %collective-permute-start = (bf16[1,3,128,128]{3,2,1,0:T(8,128)(2,1)S(1)}, bf16[1,3,128,128]{3,2,1,0:T(8,128)(2,1)S(1)}, u32[]{:S(2)}, u32[]{:S(2)}) collective-permute-start(bf16[1,3,128,128]{3,2,1,0:T(8,128)(2,1)S(1)} %bitcast.44), channel_id=1, source_target_pairs={{0,8},{1,3},{2,10},{3,5},{4,12},{5,7},{6,14},{7,1},{8,16},{9,11},{... | collective-permute-start | bytes 294920 | tf_op jit(solution)/shard_map/ppermute | solution.py:39
  6.0 3.1 %collective-permute-start.12 = (s32[1,32]{1,0:T(1,128)}, s32[1,32]{1,0:T(1,128)S(1)}, u32[]{:S(2)}, u32[]{:S(2)}) collective-permute-start(s32[1,32]{1,0:T(1,128)} %bitcast.54), channel_id=1, source_target_pairs={{0,32},{32,64},{64,96},{96,128},{128,160},{160,192},{192,224},{224... | collective-permute-start | bytes 392 | tf_op jit(solution)/shard_map/ppermute | solution.py:320
  9.2 0.7 broadcast_in_dim.82
  10.0 0.7 broadcast_add_fusion
  11.0 1.6 %shard_map.161.pending = bf16[128,8192]{1,0:T(8,128)(2,1)S(1)} custom-call(bf16[1,128,8192]{2,1,0:T(8,128)(2,1)} %source.1), custom_call_target="tpu_custom_call" | custom-call | tf_op jit(solution)/shard_map/pallas_call | solution.py:88
  12.7 0.8 %shard_map.162 = bf16[32,128,128]{2,1,0:T(8,128)(2,1)S(1)} custom-call(s32[1,32]{1,0:T(1,128)S(1)} %collective-permute-done.12.asked, bf16[128,8192]{1,0:T(8,128)(2,1)S(1)} %shard_map.161.pending), custom_call_target="tpu_custom_call" | custom-call | tf_op jit(solution)/shard_map/pallas_call | solution.py:88
  13.7 1.7 %collective-permute-start.3 = (bf16[4,3,128,128]{3,2,1,0:T(8,128)(2,1)S(1)}, bf16[4,3,128,128]{3,2,1,0:T(8,128)(2,1)S(1)}, u32[]{:S(2)}, u32[]{:S(2)}) collective-permute-start(bf16[4,3,128,128]{3,2,1,0:T(8,128)(2,1)S(1)} %pad_maximum_fusion.refs_0_), channel_id=1, source_target_pairs={{0,2},{1,9},{2,4},{3,11},{4,6},{5,13},{6,0},{7,15},{8,10},{9,17},{... | collective-permute-start | bytes 1179656 | tf_op jit(solution)/shard_map/ppermute | solution.py:39
  15.3 1.7 %collective-permute-start.4 = (bf16[4,3,128,128]{3,2,1,0:T(8,128)(2,1)S(1)}, bf16[4,3,128,128]{3,2,1,0:T(8,128)(2,1)S(1)}, u32[]{:S(2)}, u32[]{:S(2)}) collective-permute-start(bf16[4,3,128,128]{3,2,1,0:T(8,128)(2,1)S(1)} %pad_maximum_fusion.refs_0_), channel_id=1, source_target_pairs={{0,6},{1,25},{2,0},{3,27},{4,2},{5,29},{6,4},{7,31},{8,14},{9,1},{... | collective-permute-start | bytes 1179656 | tf_op jit(solution)/shard_map/ppermute | solution.py:39
  17.1 0.3 select_reduce_fusion
  17.3 0.2 select_reduce_fusion.3
  17.6 2.7 %shard_map.157 = (bf16[32,128,128]{2,1,0:T(8,128)(2,1)S(1)}, bf16[32,128,128]{2,1,0:T(8,128)(2,1)S(1)}) custom-call(s32[8,32]{1,0:T(8,128)S(1)} %stack.23.tab, bf16[1,128,8192]{2,1,0:T(8,128)(2,1)} %x_saved.1), custom_call_target="tpu_custom_call" | custom-call | tf_op jit(solution)/shard_map/pallas_call | solution.py:88
  20.2 2.5 %collective-permute-done.3.refs_1_ = bf16[4,3,128,128]{3,2,1,0:T(8,128)(2,1)S(1)} collective-permute-done((bf16[4,3,128,128]{3,2,1,0:T(8,128)(2,1)S(1)}, bf16[4,3,128,128]{3,2,1,0:T(8,128)(2,1)S(1)}, u32[]{:S(2)}, u32[]{:S(2)}) %collective-permute-start.3) | collective-permute-done | bytes 393248 | tf_op jit(solution)/shard_map/ppermute | solution.py:39
  22.8 0.4 collective-permute-done.4.refs_2_
  23.1 1.7 %collective-permute-start.5 = (bf16[2,3,128,128]{3,2,1,0:T(8,128)(2,1)S(1)}, bf16[2,3,128,128]{3,2,1,0:T(8,128)(2,1)S(1)}, u32[]{:S(2)}, u32[]{:S(2)}) collective-permute-start(bf16[2,3,128,128]{3,2,1,0:T(8,128)(2,1)S(1)} %slice.47), channel_id=1, source_target_pairs={{0,2},{1,9},{2,4},{3,11},{4,6},{5,13},{6,0},{7,15},{8,10},{9,17},{... | collective-permute-start | bytes 589832 | tf_op jit(solution)/shard_map/ppermute | solution.py:39
  24.8 1.7 %collective-permute-start.6 = (bf16[2,3,128,128]{3,2,1,0:T(8,128)(2,1)S(1)}, bf16[2,3,128,128]{3,2,1,0:T(8,128)(2,1)S(1)}, u32[]{:S(2)}, u32[]{:S(2)}) collective-permute-start(bf16[2,3,128,128]{3,2,1,0:T(8,128)(2,1)S(1)} %slice.48), channel_id=1, source_target_pairs={{0,6},{1,25},{2,0},{3,27},{4,2},{5,29},{6,4},{7,31},{8,14},{9,1},{... | collective-permute-start | bytes 589832 | tf_op jit(solution)/shard_map/ppermute | solution.py:39
  26.5 0.5 collective-permute-start.11
  27.1 1.7 %shard_map.158 = (bf16[32,128,384]{2,1,0:T(8,128)(2,1)S(1)}, f32[32,128,256]{2,1,0:T(8,128)S(1)}) custom-call(s32[8,32]{1,0:T(8,128)S(1)} %stack.23.tab, bf16[32,128,128]{2,1,0:T(8,128)(2,1)S(1)} %get-tuple-element.55.x, bf16[4,3,128,128]{3,2,1,0:T(8,128)(2,1)S(1)} %pad_maximum_fusion.refs_0_, bf16[4,3,128,128]{3,2,1,0:T(8,128)(2,1)S(1)} %collective-permute-done.3.refs_1_, ...), custom_call_target="tpu_custom_call" | custom-call | tf_op jit(solution)/shard_map/pallas_call | solution.py:88
  28.8 1.3 %collective-permute-done.5.refs_0_ = bf16[2,3,128,128]{3,2,1,0:T(8,128)(2,1)S(1)} collective-permute-done((bf16[2,3,128,128]{3,2,1,0:T(8,128)(2,1)S(1)}, bf16[2,3,128,128]{3,2,1,0:T(8,128)(2,1)S(1)}, u32[]{:S(2)}, u32[]{:S(2)}) %collective-permute-start.5) | collective-permute-done | bytes 196640 | tf_op jit(solution)/shard_map/ppermute | solution.py:39
  30.1 0.5 collective-permute-done.6.refs_1_
  30.6 0.5 collective-permute-start.9
  31.1 1.1 %shard_map.159 = (bf16[32,128,384]{2,1,0:T(8,128)(2,1)S(1)}, f32[32,128,256]{2,1,0:T(8,128)S(1)}) custom-call(s32[8,32]{1,0:T(8,128)S(1)} %stack.23.tab, bf16[32,128,128]{2,1,0:T(8,128)(2,1)S(1)} %get-tuple-element.55.x, bf16[2,3,128,128]{3,2,1,0:T(8,128)(2,1)S(1)} %collective-permute-done.5.refs_0_, ...), custom_call_target="tpu_custom_call", output_to_operand_aliasing={{0}: (6, {}), {1}: (7, {})} | custom-call | tf_op jit(solution)/shard_map/pallas_call | solution.py:88
  32.3 2.1 %shard_map.160 = (bf16[32,128,384]{2,1,0:T(8,128)(2,1)S(1)}, f32[32,128,256]{2,1,0:T(8,128)S(1)}, f32[32,128,256]{2,1,0:T(8,128)S(1)}, bf16[33,128,128]{2,1,0:T(8,128)(2,1)S(1)}) custom-call(s32[8,32]{1,0:T(8,128)S(1)} %stack.23.tab, bf16[32,128,128]{2,1,0:T(8,128)(2,1)S(1)} %get-tuple-element.55.x, ...), custom_call_target="tpu_custom_call", output_to_operand_aliasing={{0}: (4, {}), {1}: (5, {})} | custom-call | tf_op jit(solution)/shard_map/pallas_call | solution.py:88
  34.4 4.4 %collective-permute-done.13.cot = bf16[32,128,128]{2,1,0:T(8,128)(2,1)S(1)} collective-permute-done((bf16[32,128,128]{2,1,0:T(8,128)(2,1)S(1)}, bf16[32,128,128]{2,1,0:T(8,128)(2,1)S(1)}, u32[]{:S(2)}, u32[]{:S(2)}) %collective-permute-start.13) | collective-permute-done | bytes 1048608 | tf_op jit(solution)/shard_map/ppermute | solution.py:326
  38.7 2.6 %shard_map.163 = (bf16[4,128,384]{2,1,0:T(8,128)(2,1)S(1)}, f32[4,128,384]{2,1,0:T(8,128)S(1)}, bf16[32,128,256]{2,1,0:T(8,128)(2,1)S(1)}) custom-call(s32[8,32]{1,0:T(8,128)S(1)} %stack.23.tab, bf16[32,128,128]{2,1,0:T(8,128)(2,1)S(1)} %get-tuple-element.54.x_turned, bf16[32,128,384]{2,1,0:T(8,128)(2,1)S(1)} %get-tuple-element.66.w, ...), custom_call_target="tpu_custom_call" | custom-call | tf_op jit(solution)/shard_map/pallas_call | solution.py:88
  41.4 1.1 %shard_map.164 = f32[12,128,384]{2,1,0:T(8,128)S(1)} custom-call(s32[8,32]{1,0:T(8,128)S(1)} %stack.23.tab, bf16[32,128,128]{2,1,0:T(8,128)(2,1)S(1)} %get-tuple-element.54.x_turned, bf16[33,128,128]{2,1,0:T(8,128)(2,1)S(1)} %get-tuple-element.68.h_turned, bf16[32,128,256]{2,1,0:T(8,128)(2,1)S(1)} %get-tuple-element.73.d_gu, ...), custom_call_target="tpu_custom_call" | custom-call | tf_op jit(solution)/shard_map/pallas_call | solution.py:88
  42.5 0.6 collective-permute-done.14
  43.2 1.1 %shard_map.165 = bf16[12,128,384]{2,1,0:T(8,128)(2,1)S(1)} custom-call(s32[8,32]{1,0:T(8,128)S(1)} %stack.23.tab, bf16[32,128,128]{2,1,0:T(8,128)(2,1)S(1)} %get-tuple-element.54.x_turned, bf16[33,128,128]{2,1,0:T(8,128)(2,1)S(1)} %get-tuple-element.68.h_turned, bf16[32,128,256]{2,1,0:T(8,128)(2,1)S(1)} %get-tuple-element.73.d_gu, ...), custom_call_target="tpu_custom_call" | custom-call | tf_op jit(solution)/shard_map/pallas_call | solution.py:88
  44.3 0.2 collective-permute-start.15
  44.6 2.3 %collective-permute-start.16 = (bf16[2,128,384]{2,1,0:T(8,128)(2,1)S(1)}, bf16[2,128,384]{2,1,0:T(8,128)(2,1)S(1)}, u32[]{:S(2)}, u32[]{:S(2)}) collective-permute-start(bf16[2,128,384]{2,1,0:T(8,128)(2,1)S(1)} %get-tuple-element.108), channel_id=1, source_target_pairs={{0,6},{1,25},{2,0},{3,27},{4,2},{5,29},{6,4},{7,31},{8,14},{9,1},{... | collective-permute-start | bytes 589832 | tf_op jit(solution)/shard_map/ppermute | solution.py:39
  46.9 3.2 %shard_map.166 = bf16[1,128,8192]{2,1,0:T(8,128)(2,1)} custom-call(s32[8,32]{1,0:T(8,128)S(1)} %stack.23.tab, bf16[32,128,256]{2,1,0:T(8,128)(2,1)S(1)} %get-tuple-element.73.d_gu, bf16[32,128,384]{2,1,0:T(8,128)(2,1)S(1)} %get-tuple-element.66.w), custom_call_target="tpu_custom_call" | custom-call | flops 536870912 | bytes 2097152 | tf_op jit(solution)/shard_map/pallas_call | solution.py:88
  50.2 0.2 collective-permute-done.16
  50.3 3.5 %collective-permute-done.17 = bf16[2,128,384]{2,1,0:T(8,128)(2,1)S(1)} collective-permute-done((bf16[2,128,384]{2,1,0:T(8,128)(2,1)S(1)}, bf16[2,128,384]{2,1,0:T(8,128)(2,1)S(1)}, u32[]{:S(2)}, u32[]{:S(2)}) %collective-permute-start.17) | collective-permute-done | bytes 196640 | tf_op jit(solution)/shard_map/ppermute | solution.py:39
  53.8 0.3 convert_add_fusion
  54.1 0.2 convert.9
  54.6 2.0 %collective-permute-start.19 = (bf16[4,128,384]{2,1,0:T(8,128)(2,1)S(1)}, bf16[4,128,384]{2,1,0:T(8,128)(2,1)S(1)}, u32[]{:S(2)}, u32[]{:S(2)}) collective-permute-start(bf16[4,128,384]{2,1,0:T(8,128)(2,1)S(1)} %pad_maximum_fusion.2), channel_id=1, source_target_pairs={{0,2},{1,9},{2,4},{3,11},{4,6},{5,13},{6,0},{7,15},{8,10},{9,17},{... | collective-permute-start | bytes 1179656 | tf_op jit(solution)/shard_map/ppermute | solution.py:39
  56.6 3.8 %shard_map.167.h = bf16[33,128,128]{2,1,0:T(8,128)(2,1)S(1)} custom-call(s32[8,32]{1,0:T(8,128)S(1)} %stack.23.tab, bf16[1,128,8192]{2,1,0:T(8,128)(2,1)} %x_next, bf16[32,128,384]{2,1,0:T(8,128)(2,1)S(1)} %get-tuple-element.66.w), custom_call_target="tpu_custom_call" | custom-call | flops 536870912 | bytes 2097152 | tf_op jit(solution)/shard_map/pallas_call | solution.py:88
  60.5 1.9 %collective-permute-done.18 = bf16[4,128,384]{2,1,0:T(8,128)(2,1)S(1)} collective-permute-done((bf16[4,128,384]{2,1,0:T(8,128)(2,1)S(1)}, bf16[4,128,384]{2,1,0:T(8,128)(2,1)S(1)}, u32[]{:S(2)}, u32[]{:S(2)}) %collective-permute-start.18) | collective-permute-done | bytes 393248 | tf_op jit(solution)/shard_map/ppermute | solution.py:39
  62.4 1.3 %collective-permute-done.19 = bf16[4,128,384]{2,1,0:T(8,128)(2,1)S(1)} collective-permute-done((bf16[4,128,384]{2,1,0:T(8,128)(2,1)S(1)}, bf16[4,128,384]{2,1,0:T(8,128)(2,1)S(1)}, u32[]{:S(2)}, u32[]{:S(2)}) %collective-permute-start.19) | collective-permute-done | bytes 393248 | tf_op jit(solution)/shard_map/ppermute | solution.py:39
  63.9 2.8 %collective-permute-start.20 = (bf16[128,384]{1,0:T(8,128)(2,1)S(1)}, bf16[128,384]{1,0:T(8,128)(2,1)S(1)}, u32[]{:S(2)}, u32[]{:S(2)}) collective-permute-start(bf16[128,384]{1,0:T(8,128)(2,1)S(1)} %get-tuple-element.106), channel_id=1, source_target_pairs={{0,24},{1,7},{2,26},{3,1},{4,28},{5,3},{6,30},{7,5},{8,0},{9,15},{... | collective-permute-start | bytes 294920 | tf_op jit(solution)/shard_map/ppermute | solution.py:39
  66.7 0.8 %collective-permute-start.21 = (bf16[128,384]{1,0:T(8,128)(2,1)S(1)}, bf16[128,384]{1,0:T(8,128)(2,1)S(1)}, u32[]{:S(2)}, u32[]{:S(2)}) collective-permute-start(bf16[128,384]{1,0:T(8,128)(2,1)S(1)} %get-tuple-element.105), channel_id=1, source_target_pairs={{0,16},{1,5},{2,18},{3,7},{4,20},{5,1},{6,22},{7,3},{8,24},{9,13},... | collective-permute-start | bytes 294920 | tf_op jit(solution)/shard_map/ppermute | solution.py:39
  67.5 0.9 %collective-permute-start.22 = (bf16[128,384]{1,0:T(8,128)(2,1)S(1)}, bf16[128,384]{1,0:T(8,128)(2,1)S(1)}, u32[]{:S(2)}, u32[]{:S(2)}) collective-permute-start(bf16[128,384]{1,0:T(8,128)(2,1)S(1)} %get-tuple-element.104), channel_id=1, source_target_pairs={{0,8},{1,3},{2,10},{3,5},{4,12},{5,7},{6,14},{7,1},{8,16},{9,11},{... | collective-permute-start | bytes 294920 | tf_op jit(solution)/shard_map/ppermute | solution.py:39
  68.4 2.9 %shard_map.168 = bf16[1,128,8192]{2,1,0:T(8,128)(2,1)} custom-call(s32[8,32]{1,0:T(8,128)S(1)} %stack.23.tab, bf16[33,128,128]{2,1,0:T(8,128)(2,1)S(1)} %shard_map.167.h, bf16[32,128,384]{2,1,0:T(8,128)(2,1)S(1)} %get-tuple-element.66.w), custom_call_target="tpu_custom_call" | custom-call | flops 536870912 | bytes 2097152 | tf_op jit(solution)/shard_map/pallas_call | solution.py:88
  71.4 1.5 %collective-permute-done.21.two = bf16[128,384]{1,0:T(8,128)(2,1)S(1)} collective-permute-done((bf16[128,384]{1,0:T(8,128)(2,1)S(1)}, bf16[128,384]{1,0:T(8,128)(2,1)S(1)}, u32[]{:S(2)}, u32[]{:S(2)}) %collective-permute-start.21) | collective-permute-done | bytes 98336 | tf_op jit(solution)/shard_map/ppermute | solution.py:39
  72.9 1.0 %collective-permute-done.22.three = bf16[128,384]{1,0:T(8,128)(2,1)S(1)} collective-permute-done((bf16[128,384]{1,0:T(8,128)(2,1)S(1)}, bf16[128,384]{1,0:T(8,128)(2,1)S(1)}, u32[]{:S(2)}, u32[]{:S(2)}) %collective-permute-start.22) | collective-permute-done | bytes 98336 | tf_op jit(solution)/shard_map/ppermute | solution.py:39
  73.9 0.7 shard_map.169
  (53 shorter events, 1.5 us)
Async XLA Ops:
  1.5 12.1 %collective-permute-start.2 = (bf16[1,3,128,128]{3,2,1,0:T(8,128)(2,1)S(1)}, bf16[1,3,128,128]{3,2,1,0:T(8,128)(2,1)S(1)}, u32[]{:S(2)}, u32[]{:S(2)}) collective-permute-start(bf16[1,3,128,128]{3,2,1,0:T(8,128)(2,1)S(1)} %bitcast.42), channel_id=1, source_target_pairs={{0,24},{1,7},{2,26},{3,1},{4,28},{5,3},{6,30},{7,5},{8,0},{9,15},{... | collective-permute-start | bytes 294920 | tf_op jit(solution)/shard_map/ppermute | solution.py:39
  4.3 9.3 %collective-permute-start.1 = (bf16[1,3,128,128]{3,2,1,0:T(8,128)(2,1)S(1)}, bf16[1,3,128,128]{3,2,1,0:T(8,128)(2,1)S(1)}, u32[]{:S(2)}, u32[]{:S(2)}) collective-permute-start(bf16[1,3,128,128]{3,2,1,0:T(8,128)(2,1)S(1)} %bitcast.43), channel_id=1, source_target_pairs={{0,16},{1,5},{2,18},{3,7},{4,20},{5,1},{6,22},{7,3},{8,24},{9,13},... | collective-permute-start | bytes 294920 | tf_op jit(solution)/shard_map/ppermute | solution.py:39
  5.1 8.5 %collective-permute-start = (bf16[1,3,128,128]{3,2,1,0:T(8,128)(2,1)S(1)}, bf16[1,3,128,128]{3,2,1,0:T(8,128)(2,1)S(1)}, u32[]{:S(2)}, u32[]{:S(2)}) collective-permute-start(bf16[1,3,128,128]{3,2,1,0:T(8,128)(2,1)S(1)} %bitcast.44), channel_id=1, source_target_pairs={{0,8},{1,3},{2,10},{3,5},{4,12},{5,7},{6,14},{7,1},{8,16},{9,11},{... | collective-permute-start | bytes 294920 | tf_op jit(solution)/shard_map/ppermute | solution.py:39
  6.0 6.6 %collective-permute-start.12 = (s32[1,32]{1,0:T(1,128)}, s32[1,32]{1,0:T(1,128)S(1)}, u32[]{:S(2)}, u32[]{:S(2)}) collective-permute-start(s32[1,32]{1,0:T(1,128)} %bitcast.54), channel_id=1, source_target_pairs={{0,32},{32,64},{64,96},{96,128},{128,160},{160,192},{192,224},{224... | collective-permute-start | bytes 392 | tf_op jit(solution)/shard_map/ppermute | solution.py:320
  12.6 4.4 %copy-start = (s32[1,32]{1,0:T(1,128)S(1)}, s32[1,32]{1,0:T(1,128)}, u32[]{:S(2)}) copy-start(s32[1,32]{1,0:T(1,128)} %param.21) | copy-start | bytes 388
  12.6 4.4 %copy-start.1 = (s32[1,32]{1,0:T(1,128)S(1)}, s32[1,32]{1,0:T(1,128)}, u32[]{:S(2)}) copy-start(s32[1,32]{1,0:T(1,128)} %param.18) | copy-start | bytes 388
  12.6 4.4 %copy-start.2 = (s32[1,32,1]{1,2,0:T(1,128)S(1)}, s32[1,32,1]{1,2,0:T(1,128)}, u32[]{:S(2)}) copy-start(s32[1,32,1]{1,2,0:T(1,128)} %param.20) | copy-start | bytes 388
  12.6 4.4 %copy-start.3 = (s32[1,32,1]{1,2,0:T(1,128)S(1)}, s32[1,32,1]{1,2,0:T(1,128)}, u32[]{:S(2)}) copy-start(s32[1,32,1]{1,2,0:T(1,128)} %param.19) | copy-start | bytes 388
  12.6 4.4 %copy-start.4 = (s32[1,32,1]{1,2,0:T(1,128)S(1)}, s32[1,32,1]{1,2,0:T(1,128)}, u32[]{:S(2)}) copy-start(s32[1,32,1]{1,2,0:T(1,128)} %param.17) | copy-start | bytes 388
  12.7 4.4 %copy-start.5 = (s32[1,32,1]{1,2,0:T(1,128)S(1)}, s32[1,32,1]{1,2,0:T(1,128)}, u32[]{:S(2)}) copy-start(s32[1,32,1]{1,2,0:T(1,128)} %param.16) | copy-start | bytes 388
  13.5 25.2 %collective-permute-start.13 = (bf16[32,128,128]{2,1,0:T(8,128)(2,1)S(1)}, bf16[32,128,128]{2,1,0:T(8,128)(2,1)S(1)}, u32[]{:S(2)}, u32[]{:S(2)}) collective-permute-start(bf16[32,128,128]{2,1,0:T(8,128)(2,1)S(1)} %shard_map.162), channel_id=1, source_target_pairs={{0,224},{32,0},{64,32},{96,64},{128,96},{160,128},{192,160},{224,1... | collective-permute-start | bytes 3145736 | tf_op jit(solution)/shard_map/ppermute | solution.py:326
  13.7 9.1 %collective-permute-start.3 = (bf16[4,3,128,128]{3,2,1,0:T(8,128)(2,1)S(1)}, bf16[4,3,128,128]{3,2,1,0:T(8,128)(2,1)S(1)}, u32[]{:S(2)}, u32[]{:S(2)}) collective-permute-start(bf16[4,3,128,128]{3,2,1,0:T(8,128)(2,1)S(1)} %pad_maximum_fusion.refs_0_), channel_id=1, source_target_pairs={{0,2},{1,9},{2,4},{3,11},{4,6},{5,13},{6,0},{7,15},{8,10},{9,17},{... | collective-permute-start | bytes 1179656 | tf_op jit(solution)/shard_map/ppermute | solution.py:39
  15.3 7.8 %collective-permute-start.4 = (bf16[4,3,128,128]{3,2,1,0:T(8,128)(2,1)S(1)}, bf16[4,3,128,128]{3,2,1,0:T(8,128)(2,1)S(1)}, u32[]{:S(2)}, u32[]{:S(2)}) collective-permute-start(bf16[4,3,128,128]{3,2,1,0:T(8,128)(2,1)S(1)} %pad_maximum_fusion.refs_0_), channel_id=1, source_target_pairs={{0,6},{1,25},{2,0},{3,27},{4,2},{5,29},{6,4},{7,31},{8,14},{9,1},{... | collective-permute-start | bytes 1179656 | tf_op jit(solution)/shard_map/ppermute | solution.py:39
  17.0 9.5 %collective-permute-start.7 = (bf16[4,3,128,128]{3,2,1,0:T(8,128)(2,1)S(1)}, bf16[4,3,128,128]{3,2,1,0:T(8,128)(2,1)}, u32[]{:S(2)}, u32[]{:S(2)}) collective-permute-start(bf16[4,3,128,128]{3,2,1,0:T(8,128)(2,1)S(1)} %pad_maximum_fusion.refs_0_), channel_id=1, source_target_pairs={{0,1},{1,0},{2,3},{3,2},{4,5},{5,4},{6,7},{7,6},{8,9},{9,8},{10,11... | collective-permute-start | bytes 1179656 | tf_op jit(solution)/shard_map/ppermute | solution.py:39
  23.1 7.0 %collective-permute-start.5 = (bf16[2,3,128,128]{3,2,1,0:T(8,128)(2,1)S(1)}, bf16[2,3,128,128]{3,2,1,0:T(8,128)(2,1)S(1)}, u32[]{:S(2)}, u32[]{:S(2)}) collective-permute-start(bf16[2,3,128,128]{3,2,1,0:T(8,128)(2,1)S(1)} %slice.47), channel_id=1, source_target_pairs={{0,2},{1,9},{2,4},{3,11},{4,6},{5,13},{6,0},{7,15},{8,10},{9,17},{... | collective-permute-start | bytes 589832 | tf_op jit(solution)/shard_map/ppermute | solution.py:39
  24.8 5.7 %collective-permute-start.6 = (bf16[2,3,128,128]{3,2,1,0:T(8,128)(2,1)S(1)}, bf16[2,3,128,128]{3,2,1,0:T(8,128)(2,1)S(1)}, u32[]{:S(2)}, u32[]{:S(2)}) collective-permute-start(bf16[2,3,128,128]{3,2,1,0:T(8,128)(2,1)S(1)} %slice.48), channel_id=1, source_target_pairs={{0,6},{1,25},{2,0},{3,27},{4,2},{5,29},{6,4},{7,31},{8,14},{9,1},{... | collective-permute-start | bytes 589832 | tf_op jit(solution)/shard_map/ppermute | solution.py:39
  26.5 4.5 %collective-permute-start.10 = (bf16[4,3,128,128]{3,2,1,0:T(8,128)(2,1)S(1)}, bf16[4,3,128,128]{3,2,1,0:T(8,128)(2,1)S(1)}, u32[]{:S(2)}, u32[]{:S(2)}) collective-permute-start(bf16[4,3,128,128]{3,2,1,0:T(8,128)(2,1)S(1)} %collective-permute-done.3.refs_1_), channel_id=1, source_target_pairs={{0,1},{1,0},{2,3},{3,2},{4,5},{5,4},{6,7},{7,6},{8,9},{9,8},{10,11... | collective-permute-start | bytes 1179656 | tf_op jit(solution)/shard_map/ppermute | solution.py:39
  26.5 4.5 %collective-permute-start.11 = (bf16[4,3,128,128]{3,2,1,0:T(8,128)(2,1)S(1)}, bf16[4,3,128,128]{3,2,1,0:T(8,128)(2,1)S(1)}, u32[]{:S(2)}, u32[]{:S(2)}) collective-permute-start(bf16[4,3,128,128]{3,2,1,0:T(8,128)(2,1)S(1)} %collective-permute-done.4.refs_2_), channel_id=1, source_target_pairs={{0,1},{1,0},{2,3},{3,2},{4,5},{5,4},{6,7},{7,6},{8,9},{9,8},{10,11... | collective-permute-start | bytes 1179656 | tf_op jit(solution)/shard_map/ppermute | solution.py:39
  30.6 1.6 %collective-permute-start.8 = (bf16[2,3,128,128]{3,2,1,0:T(8,128)(2,1)S(1)}, bf16[2,3,128,128]{3,2,1,0:T(8,128)(2,1)S(1)}, u32[]{:S(2)}, u32[]{:S(2)}) collective-permute-start(bf16[2,3,128,128]{3,2,1,0:T(8,128)(2,1)S(1)} %collective-permute-done.5.refs_0_), channel_id=1, source_target_pairs={{0,1},{1,0},{2,3},{3,2},{4,5},{5,4},{6,7},{7,6},{8,9},{9,8},{10,11... | collective-permute-start | bytes 589832 | tf_op jit(solution)/shard_map/ppermute | solution.py:39
  30.6 1.7 %collective-permute-start.9 = (bf16[2,3,128,128]{3,2,1,0:T(8,128)(2,1)S(1)}, bf16[2,3,128,128]{3,2,1,0:T(8,128)(2,1)S(1)}, u32[]{:S(2)}, u32[]{:S(2)}) collective-permute-start(bf16[2,3,128,128]{3,2,1,0:T(8,128)(2,1)S(1)} %collective-permute-done.6.refs_1_), channel_id=1, source_target_pairs={{0,1},{1,0},{2,3},{3,2},{4,5},{5,4},{6,7},{7,6},{8,9},{9,8},{10,11... | collective-permute-start | bytes 589832 | tf_op jit(solution)/shard_map/ppermute | solution.py:39
  41.3 1.8 %collective-permute-start.14 = (bf16[4,128,384]{2,1,0:T(8,128)(2,1)S(1)}, bf16[4,128,384]{2,1,0:T(8,128)(2,1)S(1)}, u32[]{:S(2)}, u32[]{:S(2)}) collective-permute-start(bf16[4,128,384]{2,1,0:T(8,128)(2,1)S(1)} %get-tuple-element.70), channel_id=1, source_target_pairs={{0,1},{1,0},{2,3},{3,2},{4,5},{5,4},{6,7},{7,6},{8,9},{9,8},{10,11... | collective-permute-start | bytes 1179656 | tf_op jit(solution)/shard_map/ppermute | solution.py:39
  44.3 9.5 %collective-permute-start.15 = (bf16[12,128,384]{2,1,0:T(8,128)(2,1)S(1)}, bf16[12,128,384]{2,1,0:T(8,128)(2,1)S(1)}, u32[]{:S(2)}, u32[]{:S(2)}) collective-permute-start(bf16[12,128,384]{2,1,0:T(8,128)(2,1)S(1)} %shard_map.165), channel_id=1, source_target_pairs={{0,1},{1,0},{2,3},{3,2},{4,5},{5,4},{6,7},{7,6},{8,9},{9,8},{10,11... | collective-permute-start | bytes 3538952 | tf_op jit(solution)/shard_map/ppermute | solution.py:39
  44.6 5.7 %collective-permute-start.16 = (bf16[2,128,384]{2,1,0:T(8,128)(2,1)S(1)}, bf16[2,128,384]{2,1,0:T(8,128)(2,1)S(1)}, u32[]{:S(2)}, u32[]{:S(2)}) collective-permute-start(bf16[2,128,384]{2,1,0:T(8,128)(2,1)S(1)} %get-tuple-element.108), channel_id=1, source_target_pairs={{0,6},{1,25},{2,0},{3,27},{4,2},{5,29},{6,4},{7,31},{8,14},{9,1},{... | collective-permute-start | bytes 589832 | tf_op jit(solution)/shard_map/ppermute | solution.py:39
  46.9 6.9 %collective-permute-start.17 = (bf16[2,128,384]{2,1,0:T(8,128)(2,1)S(1)}, bf16[2,128,384]{2,1,0:T(8,128)(2,1)S(1)}, u32[]{:S(2)}, u32[]{:S(2)}) collective-permute-start(bf16[2,128,384]{2,1,0:T(8,128)(2,1)S(1)} %get-tuple-element.107), channel_id=1, source_target_pairs={{0,2},{1,9},{2,4},{3,11},{4,6},{5,13},{6,0},{7,15},{8,10},{9,17},{... | collective-permute-start | bytes 589832 | tf_op jit(solution)/shard_map/ppermute | solution.py:39
  54.5 7.9 %collective-permute-start.18 = (bf16[4,128,384]{2,1,0:T(8,128)(2,1)S(1)}, bf16[4,128,384]{2,1,0:T(8,128)(2,1)S(1)}, u32[]{:S(2)}, u32[]{:S(2)}) collective-permute-start(bf16[4,128,384]{2,1,0:T(8,128)(2,1)S(1)} %pad_maximum_fusion.1), channel_id=1, source_target_pairs={{0,6},{1,25},{2,0},{3,27},{4,2},{5,29},{6,4},{7,31},{8,14},{9,1},{... | collective-permute-start | bytes 1179656 | tf_op jit(solution)/shard_map/ppermute | solution.py:39
  54.6 9.1 %collective-permute-start.19 = (bf16[4,128,384]{2,1,0:T(8,128)(2,1)S(1)}, bf16[4,128,384]{2,1,0:T(8,128)(2,1)S(1)}, u32[]{:S(2)}, u32[]{:S(2)}) collective-permute-start(bf16[4,128,384]{2,1,0:T(8,128)(2,1)S(1)} %pad_maximum_fusion.2), channel_id=1, source_target_pairs={{0,2},{1,9},{2,4},{3,11},{4,6},{5,13},{6,0},{7,15},{8,10},{9,17},{... | collective-permute-start | bytes 1179656 | tf_op jit(solution)/shard_map/ppermute | solution.py:39
  63.9 7.5 %collective-permute-start.20 = (bf16[128,384]{1,0:T(8,128)(2,1)S(1)}, bf16[128,384]{1,0:T(8,128)(2,1)S(1)}, u32[]{:S(2)}, u32[]{:S(2)}) collective-permute-start(bf16[128,384]{1,0:T(8,128)(2,1)S(1)} %get-tuple-element.106), channel_id=1, source_target_pairs={{0,24},{1,7},{2,26},{3,1},{4,28},{5,3},{6,30},{7,5},{8,0},{9,15},{... | collective-permute-start | bytes 294920 | tf_op jit(solution)/shard_map/ppermute | solution.py:39
  66.7 6.2 %collective-permute-start.21 = (bf16[128,384]{1,0:T(8,128)(2,1)S(1)}, bf16[128,384]{1,0:T(8,128)(2,1)S(1)}, u32[]{:S(2)}, u32[]{:S(2)}) collective-permute-start(bf16[128,384]{1,0:T(8,128)(2,1)S(1)} %get-tuple-element.105), channel_id=1, source_target_pairs={{0,16},{1,5},{2,18},{3,7},{4,20},{5,1},{6,22},{7,3},{8,24},{9,13},... | collective-permute-start | bytes 294920 | tf_op jit(solution)/shard_map/ppermute | solution.py:39
  67.5 6.4 %collective-permute-start.22 = (bf16[128,384]{1,0:T(8,128)(2,1)S(1)}, bf16[128,384]{1,0:T(8,128)(2,1)S(1)}, u32[]{:S(2)}, u32[]{:S(2)}) collective-permute-start(bf16[128,384]{1,0:T(8,128)(2,1)S(1)} %get-tuple-element.104), channel_id=1, source_target_pairs={{0,8},{1,3},{2,10},{3,5},{4,12},{5,7},{6,14},{7,1},{8,16},{9,11},{... | collective-permute-start | bytes 294920 | tf_op jit(solution)/shard_map/ppermute | solution.py:39

commit v5 on v4

--- a/solution.py
+++ b/solution.py
@@ -2,6 +2,7 @@
 
 import jax
 import jax.numpy as jnp
+import numpy as np
 from jax import lax
 from jax.experimental import pallas as pl
 from jax.experimental.pallas import tpu as pltpu
@@ -99,10 +100,18 @@
     )(*scalars, *[pltpu.with_memory_space_constraint(a, pltpu.HBM) for a in far], *[pltpu.with_memory_space_constraint(a, VMEM) for a in arrays])
 
 
-def pack_kernel(gate_up, down, out, sems):
+def row_copies(source, out, sems):
+    count = sems.shape[0]
+    each = out.shape[0] // count
+    rows = [pl.ds(q * each, each) for q in range(count)]
+    return [pltpu.make_async_copy(source.at[0, r], out.at[r], sems.at[q]) for q, r in enumerate(rows)]
+
+
+def pack_kernel(gate_up, down, pending, out, held, sems, row_sems):
     copies = [
         pltpu.make_async_copy(gate_up.at[0, 0, 0], out.at[pl.ds(0, 2)], sems.at[0]),
         pltpu.make_async_copy(down.at[0, 0, 0], out.at[2], sems.at[1]),
+        *row_copies(pending, held, row_sems),
     ]
     for copy in copies:
         copy.start()
@@ -110,23 +119,23 @@
         copy.wait()
 
 
-def fetch_kernel(source, out, sem):
-    copy = pltpu.make_async_copy(source.at[0], out, sem)
-    copy.start()
-    copy.wait()
-
-
 def pick_kernel(n, asked, pending, out):
     for k in range(n):
         out[k] = pending[:, cols(asked[0, k])]
 
 
-def saved_kernel(n, tab, x_saved, out, turned, x, sem):
-    fetch_kernel(x_saved, x, sem)
+def saved_kernel(n, tab, x_saved, x_next, out, turned, later, x, sems, later_sems):
+    now, then = row_copies(x_saved, x, sems), row_copies(x_next, later, later_sems)
+    for copy in now + then:
+        copy.start()
+    for copy in now:
+        copy.wait()
     for k in range(n):
         block = x[:, cols(tab[ROWS, k])]
         out[k] = block
         turned[k] = block.T
+    for copy in then:
+        copy.wait()
 
 
 def project(tab, slots, x_of, w_of, acc):
@@ -173,23 +182,6 @@
 
     loop(n, 4, activate)
     h_turned[n] = jnp.zeros((B, B), BF16)
-
-
-def forward_next_kernel(n, tab, x_next, w, h, acc, x, sem):
-    fetch_kernel(x_next, x, sem)
-
-    def some(ks):
-        project(tab, ks, lambda k: x[:, cols(tab[ROWS, k])], lambda k: w[k, :, : 2 * B], acc)
-
-    loop(n, UNROLL, some)
-
-    def activate(ks):
-        for k in ks:
-            gate, up = acc[k, :, :B], acc[k, :, B:]
-            h[k] = (gate * jax.nn.sigmoid(gate) * up).astype(BF16)
-
-    loop(n, 4, activate)
-    h[n] = jnp.zeros((B, B), BF16)
 
 
 def put(acc, out, staged, sems):
@@ -207,16 +199,28 @@
         copy.wait()
 
 
-def down_next_kernel(n, tab, h, w, y, acc, staged, sems):
-    acc[...] = jnp.zeros_like(acc)
+def next_kernel(n, tab, x, w, y, acc, h, y_acc, staged, sems):
+    def some(ks):
+        project(tab, ks, lambda k: x[:, cols(tab[ROWS, k])], lambda k: w[k, :, : 2 * B], acc)
+
+    loop(n, UNROLL, some)
+
+    def activate(ks):
+        for k in ks:
+            gate, up = acc[k, :, :B], acc[k, :, B:]
+            h[k] = (gate * jax.nn.sigmoid(gate) * up).astype(BF16)
+
+    loop(n, 4, activate)
+    h[n] = jnp.zeros((B, B), BF16)
+    y_acc[...] = jnp.zeros_like(y_acc)
 
     def down(js):
         parts = [rounded(dot(h[tab[HSLOT, j]], w[j, :, 2 * B :]) * live(tab, DLIVE, j)) for j in js]
         for j, part in zip(js, parts):
-            acc[tab[DCOLS, j]] += part
+            y_acc[tab[DCOLS, j]] += part
 
     loop(n, UNROLL, down)
-    put(acc, y, staged, sems)
+    put(y_acc, y, staged, sems)
 
 
 def grads(tab, slots, x_turned, h_turned, d_gu, cot, out):
@@ -227,7 +231,7 @@
         out[k, :, 2 * B :] = down.astype(out.dtype)
 
 
-def backward_kernel(n, slots, tab, x_turned, w, coef, h_turned, cot, others, own, d_gu, dh):
+def backward_kernel(n, slots, tab, x_turned, w, coef, h_turned, cot, others, d_gu, dh):
     dh[...] = jnp.zeros_like(dh)
 
     def down(js):
@@ -243,8 +247,7 @@
             d_gu[k, :, B:] = (dh[k] * coef[k, :, B:]).astype(BF16)
 
     loop(n, 4, scale)
-    for some, out in zip(slots, (others, own)):
-        grads(tab, some, x_turned, h_turned, d_gu, cot, out)
+    grads(tab, slots, x_turned, h_turned, d_gu, cot, others)
 
 
 def grads_kernel(slots, tab, x_turned, h_turned, d_gu, cot, *outs):
@@ -276,8 +279,8 @@
 def tables(mine, g_rows, g_cols, g_live, d_rows, d_cols, d_live):
     n = g_rows.shape[0]
     ids = jnp.arange(n, dtype=jnp.int32)
-    kind = (jnp.repeat(jnp.array(OTHER, jnp.int32), SIDE) + mine) % 2
-    j, i = jnp.repeat(jnp.array(STEPS, jnp.int32), SIDE), ids % SIDE
+    kind = (np.repeat(np.array(OTHER, np.int32), SIDE) + mine) % 2
+    j, i = np.repeat(np.array(STEPS, np.int32), SIDE), ids % SIDE
     x = (mine // (2 * SIDE) - jnp.where(kind == 0, i, j)) % SIDE
     y = ((mine // 2) % SIDE - jnp.where(kind == 0, j, i)) % SIDE
     owner = (x * SIDE + y) * 2 + kind
@@ -318,22 +321,21 @@
     up_pairs = [(s, (s + 1) % sections) for s in range(sections)]
     down_pairs = [(s, (s - 1) % sections) for s in range(sections)]
     asked = lax.ppermute(down_cols[0].reshape(1, n), "pipe", up_pairs)
-    one_copy = [pltpu.SemaphoreType.DMA]
-    [held_back] = call(fetch_kernel, [kept((tok, width), BF16)], one_copy, [], [], 2, far=[pending])
+    rows, sems = kept((tok, width), BF16), pltpu.SemaphoreType.DMA
+    own, held_back = call(
+        pack_kernel,
+        [kept((3, B, B), BF16), rows],
+        [sems((2,)), sems((8,))],
+        [],
+        [],
+        2,
+        far=[gate_up_tiles, down_tiles, pending],
+    )
     [picked] = call(
         part(pick_kernel, n), [kept((n, tok, B), BF16)], [], [asked], [held_back], 2
     )
     cot = lax.ppermute(picked, "pipe", down_pairs)
 
-    [own] = call(
-        pack_kernel,
-        [kept((3, B, B), BF16)],
-        [pltpu.SemaphoreType.DMA((2,))],
-        [],
-        [],
-        2,
-        far=[gate_up_tiles, down_tiles],
-    )
     own = own[None]
     one, three, two = send(own, 1, 0), send(own, -1, 0), send(own, 2, 0)
     near = jnp.concatenate([own, one, two, three], axis=0)
@@ -350,14 +352,14 @@
         down_cols[0].reshape(-1),
         down_live[0],
     )
-    x_blocks, x_turned = call(
+    x_blocks, x_turned, x_late = call(
         part(saved_kernel, n),
-        [kept((n, tok, B), BF16), kept((n, B, tok), BF16)],
-        [VMEM((tok, width), BF16), *one_copy],
+        [kept((n, tok, B), BF16), kept((n, B, tok), BF16), rows],
+        [VMEM((tok, width), BF16), sems((8,)), sems((8,))],
         [tab],
         [],
         4,
-        far=[x_saved],
+        far=[x_saved, x_next],
     )
     back, ahead, x_blocks, x_turned = together(back, ahead, x_blocks, x_turned)
     low, high = send(back[:2], 0, 1), send(ahead[2:], 0, -1)
@@ -386,84 +388,70 @@
         6,
         aliases={4: 0, 5: 1},
     )
-    late_steps = (1, 3, 0)
-    own_late_slots = sum((group(0, j) for j in late_steps), [])
-    other_late_slots = sum((group(1, j) for j in late_steps), [])
-    other_first, own_first, d_gu = call(
-        part(backward_kernel, n, [group(1, 2), group(0, 2)]),
-        [
-            kept((SIDE, B, 3 * B), BF16),
-            kept((SIDE, B, 3 * B), F32),
-            kept((n, tok, 2 * B), BF16),
-        ],
+    other_first, d_gu = call(
+        part(backward_kernel, n, group(1, 2)),
+        [kept((SIDE, B, 3 * B), BF16), kept((n, tok, 2 * B), BF16)],
         [VMEM((n + 1, tok, B), F32)],
         [tab],
         [x_turned, w, coef, h_turned, cot],
         6,
     )
+
+    def products(d_gu, *outs):
+        return call(
+            part(grads_kernel, [slots for slots, _ in outs]),
+            [kept((len(slots), B, 3 * B), dtype) for slots, dtype in outs],
+            [],
+            [tab],
+            [x_turned, h_turned, d_gu, cot],
+            4,
+        )
+
     first = core(other_first)
-    [own_late] = call(
-        part(grads_kernel, [own_late_slots]),
-        [kept((CHIPS - SIDE, B, 3 * B), F32)],
-        [],
-        [tab],
-        [x_turned, h_turned, d_gu, cot],
-        4,
-    )
+    own_first, own_next = products(d_gu, (group(0, 2), F32), (group(0, 1) + group(0, 3), F32))
     held = plus(own_first, first)
-    held, own_late, d_gu = together(held, own_late, d_gu)
+    held, own_next, d_gu = together(held, own_next, d_gu)
     low, high = send(held[:2], 0, -1), send(held[2:], 0, 1)
-    [other_late] = call(
-        part(grads_kernel, [other_late_slots]),
-        [kept((CHIPS - SIDE, B, 3 * B), BF16)],
-        [],
-        [tab],
-        [x_turned, h_turned, d_gu, cot],
-        4,
-    )
-    late = core(other_late)
-    both = (own_late + late.astype(F32)).reshape(SIDE - 1, SIDE, B, 3 * B)
+    [other_next] = products(d_gu, (group(1, 1) + group(1, 3), BF16))
+    arrived = core(other_next)
     [dx] = call(
         part(dx_kernel, n),
         [jax.ShapeDtypeStruct((1, tok, width), BF16)],
-        [VMEM((blocks, tok, B), F32), VMEM((tok, width), BF16), pltpu.SemaphoreType.DMA((4,))],
+        [VMEM((blocks, tok, B), F32), VMEM((tok, width), BF16), sems((4,))],
         [tab],
         [d_gu, w],
         8,
         4 * n * product,
         out_space=pltpu.HBM,
     )
-    low, high, dx = together(low, high, dx)
+    low, high, dx, d_gu = together(low, high, dx, d_gu)
+    both = (own_next + arrived.astype(F32)).reshape(2, SIDE, B, 3 * B)
     to_back = jnp.concatenate([plus(both[0, :2], low), both[0, 2:].astype(BF16)], axis=0)
     to_ahead = jnp.concatenate([both[1, :2].astype(BF16), plus(both[1, 2:], high)], axis=0)
-    to_back, to_ahead, x_next = together(to_back, to_ahead, x_next)
-    [h_next] = call(
-        part(forward_next_kernel, n),
-        [kept((n + 1, tok, B), BF16)],
-        [VMEM((n, tok, 2 * B), F32), VMEM((tok, width), BF16), *one_copy],
-        [tab],
-        [w],
-        9,
-        4 * n * product,
-        [x_next],
-    )
+    to_back, to_ahead, x_late, d_gu = together(to_back, to_ahead, x_late, d_gu)
     from_ahead, from_back = send(to_back, 0, -1), send(to_ahead, 0, 1)
-    from_ahead, from_back, h_next = together(from_ahead, from_back, h_next)
-    row = both[2] + from_ahead.astype(F32) + from_back.astype(F32)
-    row, h_next = together(row, h_next)
+    other_last, own_last = products(d_gu, (group(1, 0), BF16), (group(0, 0), F32))
+    last = core(other_last)
     [y] = call(
-        part(down_next_kernel, n),
+        part(next_kernel, n),
         [jax.ShapeDtypeStruct((1, tok, width), BF16)],
-        [VMEM((blocks, tok, B), F32), VMEM((tok, width), BF16), pltpu.SemaphoreType.DMA((4,))],
-        [tab],
-        [h_next, w],
-        8,
-        4 * n * product,
+        [
+            VMEM((n, tok, 2 * B), F32),
+            VMEM((n + 1, tok, B), BF16),
+            VMEM((blocks, tok, B), F32),
+            VMEM((tok, width), BF16),
+            sems((4,)),
+        ],
+        [tab],
+        [x_late, w],
+        14,
+        8 * n * product,
         out_space=pltpu.HBM,
     )
+    from_ahead, from_back, y = together(from_ahead, from_back, y)
+    row = own_last + last.astype(F32) + from_ahead.astype(F32) + from_back.astype(F32)
     out = row[1:].astype(BF16)
     one, two, three = send(out[0], -1, 0), send(out[1], 2, 0), send(out[2], 1, 0)
-    one, two, three, y = together(one, two, three, y)
     grad_gu, grad_down = call(
         total_kernel,
         [

time: 74.9 us -> 74.7 us (level)
  the two profiles are of different devices: /device:TPU:96 before, /device:TPU:6 now
where the time goes in v5:
time: 74.7 us; the launch traced here: 74.5 us
  starting transfers between devices  25.4 us (34%)
  Pallas kernels  24.7 us (33%)
  waiting for transfers between devices  21.3 us (29%)
  other arithmetic  1.98 us (3%)
  between operations  0.94 us (1%)
    pallas_call x13, Pallas kernels, call(): pl.pallas_call(body, out_shape=outs, in_specs=[pl.BlockSpec(memory_space=...  24.7 us
    ppermute x22, starting transfers between devices, send(): return lax.ppermute(value, 'tile', pairs(first, second, core))  21.4 us
    ppermute x22, waiting for transfers between devices, send(): return lax.ppermute(value, 'tile', pairs(first, second, core))  15.8 us
    ppermute x1, waiting for transfers between devices, per_device(): asked = lax.ppermute(down_cols[0].reshape(1, n), 'pipe', up_pairs)  5.43 us
    ppermute x1, starting transfers between devices, per_device(): cot = lax.ppermute(picked, 'pipe', down_pairs)  2.1 us
    ppermute x1, starting transfers between devices, per_device(): asked = lax.ppermute(down_cols[0].reshape(1, n), 'pipe', up_pairs)  1.92 us
  transfers between devices with their start and end apart: 24, of which 12 were waited for; matrix products, arithmetic and copies ran while one was open for 2% of the time, Pallas kernels for 25%

profile of v5, /device:TPU:6, one launch (start us, length us, event | category | flops | bytes accessed | tf_op | source)
XLA Modules:
  0.0 74.5 jit_solution(1000379359663022400)
XLA Ops:
  0.7 1.6 %shard_map.156 = (bf16[3,128,128]{2,1,0:T(8,128)(2,1)S(1)}, bf16[128,8192]{1,0:T(8,128)(2,1)S(1)}) custom-call(bf16[1,1,1,2,128,128]{5,4,3,2,1,0:T(8,128)(2,1)} %gate_up.1, bf16[1,1,1,128,128]{4,3,2,1,0:T(8,128)(2,1)} %down.1, bf16[1,128,8192]{2,1,0:T(8,128)(2,1)} %pending.1), custom_call_target="tpu_custom_call" | custom-call | tf_op jit(solution)/shard_map/pallas_call | solution.py:89
  2.3 0.9 %collective-permute-start.2 = (bf16[1,3,128,128]{3,2,1,0:T(8,128)(2,1)S(1)}, bf16[1,3,128,128]{3,2,1,0:T(8,128)(2,1)S(1)}, u32[]{:S(2)}, u32[]{:S(2)}) collective-permute-start(bf16[1,3,128,128]{3,2,1,0:T(8,128)(2,1)S(1)} %bitcast.43), channel_id=1, source_target_pairs={{0,24},{1,7},{2,26},{3,1},{4,28},{5,3},{6,30},{7,5},{8,0},{9,15},{... | collective-permute-start | bytes 294920 | tf_op jit(solution)/shard_map/ppermute | solution.py:40
  3.2 2.8 %collective-permute-start.1 = (bf16[1,3,128,128]{3,2,1,0:T(8,128)(2,1)S(1)}, bf16[1,3,128,128]{3,2,1,0:T(8,128)(2,1)S(1)}, u32[]{:S(2)}, u32[]{:S(2)}) collective-permute-start(bf16[1,3,128,128]{3,2,1,0:T(8,128)(2,1)S(1)} %bitcast.44), channel_id=1, source_target_pairs={{0,16},{1,5},{2,18},{3,7},{4,20},{5,1},{6,22},{7,3},{8,24},{9,13},... | collective-permute-start | bytes 294920 | tf_op jit(solution)/shard_map/ppermute | solution.py:40
  6.1 0.4 collective-permute-start
  6.4 1.9 %collective-permute-start.12 = (s32[1,32]{1,0:T(1,128)S(1)}, s32[1,32]{1,0:T(1,128)S(1)}, u32[]{:S(2)}, u32[]{:S(2)}) collective-permute-start(s32[1,32]{1,0:T(1,128)S(1)} %bitcast.57), channel_id=1, source_target_pairs={{0,32},{32,64},{64,96},{96,128},{128,160},{160,192},{192,224},{224... | collective-permute-start | bytes 392 | tf_op jit(solution)/shard_map/ppermute | solution.py:323
  8.4 5.4 %collective-permute-done.12.asked = s32[1,32]{1,0:T(1,128)S(1)} collective-permute-done((s32[1,32]{1,0:T(1,128)S(1)}, s32[1,32]{1,0:T(1,128)S(1)}, u32[]{:S(2)}, u32[]{:S(2)}) %collective-permute-start.12) | collective-permute-done | bytes 160 | tf_op jit(solution)/shard_map/ppermute | solution.py:323
  13.8 0.8 %shard_map.161 = bf16[32,128,128]{2,1,0:T(8,128)(2,1)S(1)} custom-call(s32[1,32]{1,0:T(1,128)S(1)} %collective-permute-done.12.asked, bf16[128,8192]{1,0:T(8,128)(2,1)S(1)} %get-tuple-element.72.pending), custom_call_target="tpu_custom_call" | custom-call | tf_op jit(solution)/shard_map/pallas_call | solution.py:89
  14.6 2.1 %collective-permute-start.13 = (bf16[32,128,128]{2,1,0:T(8,128)(2,1)S(1)}, bf16[32,128,128]{2,1,0:T(8,128)(2,1)S(1)}, u32[]{:S(2)}, u32[]{:S(2)}) collective-permute-start(bf16[32,128,128]{2,1,0:T(8,128)(2,1)S(1)} %shard_map.161), channel_id=1, source_target_pairs={{0,224},{32,0},{64,32},{96,64},{128,96},{160,128},{192,160},{224,1... | collective-permute-start | bytes 3145736 | tf_op jit(solution)/shard_map/ppermute | solution.py:337
  16.8 0.1 collective-permute-start.7
  16.9 3.1 %collective-permute-start.4 = (bf16[4,3,128,128]{3,2,1,0:T(8,128)(2,1)S(1)}, bf16[4,3,128,128]{3,2,1,0:T(8,128)(2,1)S(1)}, u32[]{:S(2)}, u32[]{:S(2)}) collective-permute-start(bf16[4,3,128,128]{3,2,1,0:T(8,128)(2,1)S(1)} %pad_maximum_fusion.refs_0_), channel_id=1, source_target_pairs={{0,6},{1,25},{2,0},{3,27},{4,2},{5,29},{6,4},{7,31},{8,14},{9,1},{... | collective-permute-start | bytes 1179656 | tf_op jit(solution)/shard_map/ppermute | solution.py:40
  20.0 1.0 %select_reduce_fusion = (s32[32]{0:T(128)S(1)}, s32[32]{0:T(128)S(1)}, s32[32]{0:T(128)S(1)}, s32[32]{0:T(128)S(1)}, s32[32]{0:T(128)S(1)}, /*index=5*/s32[32]{0:T(128)S(1)}) fusion(s32[32]{0:T(128)S(1)} %bitcast.54, s32[32]{0:T(128)S(1)} %multiply_add_fusion, s32[32]{0:T(128)S(1)} %bitcast.55, s32[32]{0:T(128)} %bitcast.56, s32[32]{0:T(128)} %bitcast.58, ...), kind=kLoop, calls=%fused_computation.18 | loop fusion | flops 13120 | bytes 1664 | tf_op jit(solution)/shard_map/reduce_sum | solution.py:290
  21.0 0.2 select_reduce_fusion.3
  21.2 3.3 %shard_map.157 = (bf16[32,128,128]{2,1,0:T(8,128)(2,1)S(1)}, bf16[32,128,128]{2,1,0:T(8,128)(2,1)S(1)}, bf16[128,8192]{1,0:T(8,128)(2,1)S(1)}) custom-call(s32[8,32]{1,0:T(8,128)S(1)} %stack.26.tab, bf16[1,128,8192]{2,1,0:T(8,128)(2,1)} %x_saved.1, bf16[1,128,8192]{2,1,0:T(8,128)(2,1)} %x_next.1), custom_call_target="tpu_custom_call" | custom-call | tf_op jit(solution)/shard_map/pallas_call | solution.py:89
  24.5 0.8 %collective-permute-done.4.refs_2_ = bf16[4,3,128,128]{3,2,1,0:T(8,128)(2,1)S(1)} collective-permute-done((bf16[4,3,128,128]{3,2,1,0:T(8,128)(2,1)S(1)}, bf16[4,3,128,128]{3,2,1,0:T(8,128)(2,1)S(1)}, u32[]{:S(2)}, u32[]{:S(2)}) %collective-permute-start.4) | collective-permute-done | bytes 393248 | tf_op jit(solution)/shard_map/ppermute | solution.py:40
  25.3 3.7 %collective-permute-done.3.refs_1_ = bf16[4,3,128,128]{3,2,1,0:T(8,128)(2,1)S(1)} collective-permute-done((bf16[4,3,128,128]{3,2,1,0:T(8,128)(2,1)S(1)}, bf16[4,3,128,128]{3,2,1,0:T(8,128)(2,1)S(1)}, u32[]{:S(2)}, u32[]{:S(2)}) %collective-permute-start.3) | collective-permute-done | bytes 393248 | tf_op jit(solution)/shard_map/ppermute | solution.py:40
  29.1 2.0 %collective-permute-start.5 = (bf16[2,3,128,128]{3,2,1,0:T(8,128)(2,1)S(1)}, bf16[2,3,128,128]{3,2,1,0:T(8,128)(2,1)S(1)}, u32[]{:S(2)}, u32[]{:S(2)}) collective-permute-start(bf16[2,3,128,128]{3,2,1,0:T(8,128)(2,1)S(1)} %slice.43), channel_id=1, source_target_pairs={{0,2},{1,9},{2,4},{3,11},{4,6},{5,13},{6,0},{7,15},{8,10},{9,17},{... | collective-permute-start | bytes 589832 | tf_op jit(solution)/shard_map/ppermute | solution.py:40
  31.2 0.5 collective-permute-start.11
  31.7 1.7 %shard_map.158 = (bf16[32,128,384]{2,1,0:T(8,128)(2,1)S(1)}, f32[32,128,256]{2,1,0:T(8,128)S(1)}) custom-call(s32[8,32]{1,0:T(8,128)S(1)} %stack.26.tab, bf16[32,128,128]{2,1,0:T(8,128)(2,1)S(1)} %get-tuple-element.58.x, bf16[4,3,128,128]{3,2,1,0:T(8,128)(2,1)S(1)} %pad_maximum_fusion.refs_0_, bf16[4,3,128,128]{3,2,1,0:T(8,128)(2,1)S(1)} %collective-permute-done.3.refs_1_, ...), custom_call_target="tpu_custom_call" | custom-call | tf_op jit(solution)/shard_map/pallas_call | solution.py:89
  33.4 1.4 %collective-permute-done.6.refs_1_ = bf16[2,3,128,128]{3,2,1,0:T(8,128)(2,1)S(1)} collective-permute-done((bf16[2,3,128,128]{3,2,1,0:T(8,128)(2,1)S(1)}, bf16[2,3,128,128]{3,2,1,0:T(8,128)(2,1)S(1)}, u32[]{:S(2)}, u32[]{:S(2)}) %collective-permute-start.6) | collective-permute-done | bytes 196640 | tf_op jit(solution)/shard_map/ppermute | solution.py:40
  34.8 1.3 %collective-permute-done.5.refs_0_ = bf16[2,3,128,128]{3,2,1,0:T(8,128)(2,1)S(1)} collective-permute-done((bf16[2,3,128,128]{3,2,1,0:T(8,128)(2,1)S(1)}, bf16[2,3,128,128]{3,2,1,0:T(8,128)(2,1)S(1)}, u32[]{:S(2)}, u32[]{:S(2)}) %collective-permute-start.5) | collective-permute-done | bytes 196640 | tf_op jit(solution)/shard_map/ppermute | solution.py:40
  36.1 0.5 collective-permute-start.9
  36.6 1.1 %shard_map.159 = (bf16[32,128,384]{2,1,0:T(8,128)(2,1)S(1)}, f32[32,128,256]{2,1,0:T(8,128)S(1)}) custom-call(s32[8,32]{1,0:T(8,128)S(1)} %stack.26.tab, bf16[32,128,128]{2,1,0:T(8,128)(2,1)S(1)} %get-tuple-element.58.x, bf16[2,3,128,128]{3,2,1,0:T(8,128)(2,1)S(1)} %collective-permute-done.5.refs_0_, ...), custom_call_target="tpu_custom_call", output_to_operand_aliasing={{0}: (6, {}), {1}: (7, {})} | custom-call | tf_op jit(solution)/shard_map/pallas_call | solution.py:89
  37.8 2.1 %shard_map.160 = (bf16[32,128,384]{2,1,0:T(8,128)(2,1)S(1)}, f32[32,128,256]{2,1,0:T(8,128)S(1)}, f32[32,128,256]{2,1,0:T(8,128)S(1)}, bf16[33,128,128]{2,1,0:T(8,128)(2,1)S(1)}) custom-call(s32[8,32]{1,0:T(8,128)S(1)} %stack.26.tab, bf16[32,128,128]{2,1,0:T(8,128)(2,1)S(1)} %get-tuple-element.58.x, ...), custom_call_target="tpu_custom_call", output_to_operand_aliasing={{0}: (4, {}), {1}: (5, {})} | custom-call | tf_op jit(solution)/shard_map/pallas_call | solution.py:89
  39.9 2.5 %shard_map.162 = (bf16[4,128,384]{2,1,0:T(8,128)(2,1)S(1)}, bf16[32,128,256]{2,1,0:T(8,128)(2,1)S(1)}) custom-call(s32[8,32]{1,0:T(8,128)S(1)} %stack.26.tab, bf16[32,128,128]{2,1,0:T(8,128)(2,1)S(1)} %get-tuple-element.57.x_turned, bf16[32,128,384]{2,1,0:T(8,128)(2,1)S(1)} %get-tuple-element.70.w, f32[32,128,256]{2,1,0:T(8,128)S(1)} %get-tuple-element.71.coef, ...), custom_call_target="tpu_custom_call" | custom-call | tf_op jit(solution)/shard_map/pallas_call | solution.py:89
  42.4 0.3 collective-permute-start.14
  42.7 1.1 %shard_map.163 = (f32[4,128,384]{2,1,0:T(8,128)S(1)}, f32[8,128,384]{2,1,0:T(8,128)S(1)}) custom-call(s32[8,32]{1,0:T(8,128)S(1)} %stack.26.tab, bf16[32,128,128]{2,1,0:T(8,128)(2,1)S(1)} %get-tuple-element.57.x_turned, bf16[33,128,128]{2,1,0:T(8,128)(2,1)S(1)} %get-tuple-element.69.h_turned, bf16[32,128,256]{2,1,0:T(8,128)(2,1)S(1)} %get-tuple-element.89.d_gu, ...), custom_call_target="tpu_custom_call" | custom-call | tf_op jit(solution)/shard_map/pallas_call | solution.py:89
  43.8 0.4 collective-permute-done.14
  44.2 0.1 add_convert_fusion
  44.3 1.0 %shard_map.164 = bf16[8,128,384]{2,1,0:T(8,128)(2,1)S(1)} custom-call(s32[8,32]{1,0:T(8,128)S(1)} %stack.26.tab, bf16[32,128,128]{2,1,0:T(8,128)(2,1)S(1)} %get-tuple-element.57.x_turned, bf16[33,128,128]{2,1,0:T(8,128)(2,1)S(1)} %get-tuple-element.69.h_turned, bf16[32,128,256]{2,1,0:T(8,128)(2,1)S(1)} %get-tuple-element.89.d_gu, ...), custom_call_target="tpu_custom_call" | custom-call | tf_op jit(solution)/shard_map/pallas_call | solution.py:89
  45.3 0.3 collective-permute-start.15
  45.7 0.8 %collective-permute-start.17 = (bf16[2,128,384]{2,1,0:T(8,128)(2,1)S(1)}, bf16[2,128,384]{2,1,0:T(8,128)(2,1)S(1)}, u32[]{:S(2)}, u32[]{:S(2)}) collective-permute-start(bf16[2,128,384]{2,1,0:T(8,128)(2,1)S(1)} %get-tuple-element.113), channel_id=1, source_target_pairs={{0,2},{1,9},{2,4},{3,11},{4,6},{5,13},{6,0},{7,15},{8,10},{9,17},{... | collective-permute-start | bytes 589832 | tf_op jit(solution)/shard_map/ppermute | solution.py:40
  46.5 2.5 %collective-permute-start.16 = (bf16[2,128,384]{2,1,0:T(8,128)(2,1)S(1)}, bf16[2,128,384]{2,1,0:T(8,128)(2,1)S(1)}, u32[]{:S(2)}, u32[]{:S(2)}) collective-permute-start(bf16[2,128,384]{2,1,0:T(8,128)(2,1)S(1)} %get-tuple-element.114), channel_id=1, source_target_pairs={{0,6},{1,25},{2,0},{3,27},{4,2},{5,29},{6,4},{7,31},{8,14},{9,1},{... | collective-permute-start | bytes 589832 | tf_op jit(solution)/shard_map/ppermute | solution.py:40
  49.0 3.3 %shard_map.165 = bf16[1,128,8192]{2,1,0:T(8,128)(2,1)} custom-call(s32[8,32]{1,0:T(8,128)S(1)} %stack.26.tab, bf16[32,128,256]{2,1,0:T(8,128)(2,1)S(1)} %get-tuple-element.89.d_gu, bf16[32,128,384]{2,1,0:T(8,128)(2,1)S(1)} %get-tuple-element.70.w), custom_call_target="tpu_custom_call" | custom-call | flops 536870912 | bytes 2097152 | tf_op jit(solution)/shard_map/pallas_call | solution.py:89
  52.3 0.4 collective-permute-done.17
  52.6 0.1 convert_add_fusion
  52.8 0.1 convert.9
  53.1 3.3 %collective-permute-start.18 = (bf16[4,128,384]{2,1,0:T(8,128)(2,1)S(1)}, bf16[4,128,384]{2,1,0:T(8,128)(2,1)S(1)}, u32[]{:S(2)}, u32[]{:S(2)}) collective-permute-start(bf16[4,128,384]{2,1,0:T(8,128)(2,1)S(1)} %pad_maximum_fusion.1), channel_id=1, source_target_pairs={{0,6},{1,25},{2,0},{3,27},{4,2},{5,29},{6,4},{7,31},{8,14},{9,1},{... | collective-permute-start | bytes 1179656 | tf_op jit(solution)/shard_map/ppermute | solution.py:40
  56.4 1.0 %shard_map.167 = (bf16[4,128,384]{2,1,0:T(8,128)(2,1)S(1)}, f32[4,128,384]{2,1,0:T(8,128)S(1)}) custom-call(s32[8,32]{1,0:T(8,128)S(1)} %stack.26.tab, bf16[32,128,128]{2,1,0:T(8,128)(2,1)S(1)} %get-tuple-element.57.x_turned, bf16[33,128,128]{2,1,0:T(8,128)(2,1)S(1)} %get-tuple-element.69.h_turned, bf16[32,128,256]{2,1,0:T(8,128)(2,1)S(1)} %get-tuple-element.89.d_gu, ...), custom_call_target="tpu_custom_call" | custom-call | tf_op jit(solution)/shard_map/pallas_call | solution.py:89
  57.5 4.6 %shard_map.166 = bf16[1,128,8192]{2,1,0:T(8,128)(2,1)} custom-call(s32[8,32]{1,0:T(8,128)S(1)} %stack.26.tab, bf16[128,8192]{1,0:T(8,128)(2,1)S(1)} %get-tuple-element.86.x, bf16[32,128,384]{2,1,0:T(8,128)(2,1)S(1)} %get-tuple-element.70.w), custom_call_target="tpu_custom_call" | custom-call | flops 1073741824 | bytes 4194304 | tf_op jit(solution)/shard_map/pallas_call | solution.py:89
  62.2 3.3 %collective-permute-done.19 = bf16[4,128,384]{2,1,0:T(8,128)(2,1)S(1)} collective-permute-done((bf16[4,128,384]{2,1,0:T(8,128)(2,1)S(1)}, bf16[4,128,384]{2,1,0:T(8,128)(2,1)S(1)}, u32[]{:S(2)}, u32[]{:S(2)}) %collective-permute-start.19) | collective-permute-done | bytes 393248 | tf_op jit(solution)/shard_map/ppermute | solution.py:40
  65.4 0.2 fusion.13
  65.7 1.0 %collective-permute-start.23 = (bf16[128,384]{1,0:T(8,128)(2,1)S(1)}, bf16[128,384]{1,0:T(8,128)(2,1)S(1)}, u32[]{:S(2)}, u32[]{:S(2)}) collective-permute-start(bf16[128,384]{1,0:T(8,128)(2,1)S(1)} %get-tuple-element.110), channel_id=1, source_target_pairs={{0,8},{1,3},{2,10},{3,5},{4,12},{5,7},{6,14},{7,1},{8,16},{9,11},{... | collective-permute-start | bytes 294920 | tf_op jit(solution)/shard_map/ppermute | solution.py:40
  66.7 1.4 %collective-permute-start.22 = (bf16[128,384]{1,0:T(8,128)(2,1)S(1)}, bf16[128,384]{1,0:T(8,128)(2,1)S(1)}, u32[]{:S(2)}, u32[]{:S(2)}) collective-permute-start(bf16[128,384]{1,0:T(8,128)(2,1)S(1)} %get-tuple-element.111), channel_id=1, source_target_pairs={{0,16},{1,5},{2,18},{3,7},{4,20},{5,1},{6,22},{7,3},{8,24},{9,13},... | collective-permute-start | bytes 294920 | tf_op jit(solution)/shard_map/ppermute | solution.py:40
  68.0 1.3 %collective-permute-start.21 = (bf16[128,384]{1,0:T(8,128)(2,1)S(1)}, bf16[128,384]{1,0:T(8,128)(2,1)S(1)}, u32[]{:S(2)}, u32[]{:S(2)}) collective-permute-start(bf16[128,384]{1,0:T(8,128)(2,1)S(1)} %get-tuple-element.112), channel_id=1, source_target_pairs={{0,24},{1,7},{2,26},{3,1},{4,28},{5,3},{6,30},{7,5},{8,0},{9,15},{... | collective-permute-start | bytes 294920 | tf_op jit(solution)/shard_map/ppermute | solution.py:40
  69.3 1.0 %collective-permute-done.23.three = bf16[128,384]{1,0:T(8,128)(2,1)S(1)} collective-permute-done((bf16[128,384]{1,0:T(8,128)(2,1)S(1)}, bf16[128,384]{1,0:T(8,128)(2,1)S(1)}, u32[]{:S(2)}, u32[]{:S(2)}) %collective-permute-start.23) | collective-permute-done | bytes 98336 | tf_op jit(solution)/shard_map/ppermute | solution.py:40
  70.4 2.4 %collective-permute-done.22.two = bf16[128,384]{1,0:T(8,128)(2,1)S(1)} collective-permute-done((bf16[128,384]{1,0:T(8,128)(2,1)S(1)}, bf16[128,384]{1,0:T(8,128)(2,1)S(1)}, u32[]{:S(2)}, u32[]{:S(2)}) %collective-permute-start.22) | collective-permute-done | bytes 98336 | tf_op jit(solution)/shard_map/ppermute | solution.py:40
  72.8 1.1 %collective-permute-done.21.one = bf16[128,384]{1,0:T(8,128)(2,1)S(1)} collective-permute-done((bf16[128,384]{1,0:T(8,128)(2,1)S(1)}, bf16[128,384]{1,0:T(8,128)(2,1)S(1)}, u32[]{:S(2)}, u32[]{:S(2)}) %collective-permute-start.21) | collective-permute-done | bytes 98336 | tf_op jit(solution)/shard_map/ppermute | solution.py:40
  73.8 0.7 shard_map.168
  (43 shorter events, 0.8 us)
Async XLA Ops:
  0.6 7.7 %copy-start = (s32[32]{0:T(128)S(1)}, s32[32]{0:T(128)}, u32[]{:S(2)}) copy-start(s32[32]{0:T(128)} %constant.81.clone) | copy-start | bytes 388
  0.6 7.7 %copy-start.1 = (s32[32]{0:T(128)S(1)}, s32[32]{0:T(128)}, u32[]{:S(2)}) copy-start(s32[32]{0:T(128)} %constant.80.clone) | copy-start | bytes 388
  0.7 5.8 %copy-start.4 = (s32[1,32,1]{1,2,0:T(1,128)S(1)}, s32[1,32,1]{1,2,0:T(1,128)}, u32[]{:S(2)}) copy-start(s32[1,32,1]{1,2,0:T(1,128)} %param.20) | copy-start | bytes 388
  2.3 17.7 %copy-start.2 = (s32[1,32]{1,0:T(1,128)S(1)}, s32[1,32]{1,0:T(1,128)}, u32[]{:S(2)}) copy-start(s32[1,32]{1,0:T(1,128)} %param.21) | copy-start | bytes 388
  2.3 17.7 %copy-start.3 = (s32[1,32]{1,0:T(1,128)S(1)}, s32[1,32]{1,0:T(1,128)}, u32[]{:S(2)}) copy-start(s32[1,32]{1,0:T(1,128)} %param.18) | copy-start | bytes 388
  2.3 14.4 %collective-permute-start.2 = (bf16[1,3,128,128]{3,2,1,0:T(8,128)(2,1)S(1)}, bf16[1,3,128,128]{3,2,1,0:T(8,128)(2,1)S(1)}, u32[]{:S(2)}, u32[]{:S(2)}) collective-permute-start(bf16[1,3,128,128]{3,2,1,0:T(8,128)(2,1)S(1)} %bitcast.43), channel_id=1, source_target_pairs={{0,24},{1,7},{2,26},{3,1},{4,28},{5,3},{6,30},{7,5},{8,0},{9,15},{... | collective-permute-start | bytes 294920 | tf_op jit(solution)/shard_map/ppermute | solution.py:40
  3.2 13.5 %collective-permute-start.1 = (bf16[1,3,128,128]{3,2,1,0:T(8,128)(2,1)S(1)}, bf16[1,3,128,128]{3,2,1,0:T(8,128)(2,1)S(1)}, u32[]{:S(2)}, u32[]{:S(2)}) collective-permute-start(bf16[1,3,128,128]{3,2,1,0:T(8,128)(2,1)S(1)} %bitcast.44), channel_id=1, source_target_pairs={{0,16},{1,5},{2,18},{3,7},{4,20},{5,1},{6,22},{7,3},{8,24},{9,13},... | collective-permute-start | bytes 294920 | tf_op jit(solution)/shard_map/ppermute | solution.py:40
  6.1 10.7 %collective-permute-start = (bf16[1,3,128,128]{3,2,1,0:T(8,128)(2,1)S(1)}, bf16[1,3,128,128]{3,2,1,0:T(8,128)(2,1)S(1)}, u32[]{:S(2)}, u32[]{:S(2)}) collective-permute-start(bf16[1,3,128,128]{3,2,1,0:T(8,128)(2,1)S(1)} %bitcast.45), channel_id=1, source_target_pairs={{0,8},{1,3},{2,10},{3,5},{4,12},{5,7},{6,14},{7,1},{8,16},{9,11},{... | collective-permute-start | bytes 294920 | tf_op jit(solution)/shard_map/ppermute | solution.py:40
  6.4 7.4 %collective-permute-start.12 = (s32[1,32]{1,0:T(1,128)S(1)}, s32[1,32]{1,0:T(1,128)S(1)}, u32[]{:S(2)}, u32[]{:S(2)}) collective-permute-start(s32[1,32]{1,0:T(1,128)S(1)} %bitcast.57), channel_id=1, source_target_pairs={{0,32},{32,64},{64,96},{96,128},{128,160},{160,192},{192,224},{224... | collective-permute-start | bytes 392 | tf_op jit(solution)/shard_map/ppermute | solution.py:323
  14.6 25.3 %collective-permute-start.13 = (bf16[32,128,128]{2,1,0:T(8,128)(2,1)S(1)}, bf16[32,128,128]{2,1,0:T(8,128)(2,1)S(1)}, u32[]{:S(2)}, u32[]{:S(2)}) collective-permute-start(bf16[32,128,128]{2,1,0:T(8,128)(2,1)S(1)} %shard_map.161), channel_id=1, source_target_pairs={{0,224},{32,0},{64,32},{96,64},{128,96},{160,128},{192,160},{224,1... | collective-permute-start | bytes 3145736 | tf_op jit(solution)/shard_map/ppermute | solution.py:337
  16.8 14.3 %collective-permute-start.7 = (bf16[4,3,128,128]{3,2,1,0:T(8,128)(2,1)S(1)}, bf16[4,3,128,128]{3,2,1,0:T(8,128)(2,1)}, u32[]{:S(2)}, u32[]{:S(2)}) collective-permute-start(bf16[4,3,128,128]{3,2,1,0:T(8,128)(2,1)S(1)} %pad_maximum_fusion.refs_0_), channel_id=1, source_target_pairs={{0,1},{1,0},{2,3},{3,2},{4,5},{5,4},{6,7},{7,6},{8,9},{9,8},{10,11... | collective-permute-start | bytes 1179656 | tf_op jit(solution)/shard_map/ppermute | solution.py:40
  16.9 8.4 %collective-permute-start.4 = (bf16[4,3,128,128]{3,2,1,0:T(8,128)(2,1)S(1)}, bf16[4,3,128,128]{3,2,1,0:T(8,128)(2,1)S(1)}, u32[]{:S(2)}, u32[]{:S(2)}) collective-permute-start(bf16[4,3,128,128]{3,2,1,0:T(8,128)(2,1)S(1)} %pad_maximum_fusion.refs_0_), channel_id=1, source_target_pairs={{0,6},{1,25},{2,0},{3,27},{4,2},{5,29},{6,4},{7,31},{8,14},{9,1},{... | collective-permute-start | bytes 1179656 | tf_op jit(solution)/shard_map/ppermute | solution.py:40
  20.0 9.0 %collective-permute-start.3 = (bf16[4,3,128,128]{3,2,1,0:T(8,128)(2,1)S(1)}, bf16[4,3,128,128]{3,2,1,0:T(8,128)(2,1)S(1)}, u32[]{:S(2)}, u32[]{:S(2)}) collective-permute-start(bf16[4,3,128,128]{3,2,1,0:T(8,128)(2,1)S(1)} %pad_maximum_fusion.refs_0_), channel_id=1, source_target_pairs={{0,2},{1,9},{2,4},{3,11},{4,6},{5,13},{6,0},{7,15},{8,10},{9,17},{... | collective-permute-start | bytes 1179656 | tf_op jit(solution)/shard_map/ppermute | solution.py:40
  29.0 5.7 %collective-permute-start.6 = (bf16[2,3,128,128]{3,2,1,0:T(8,128)(2,1)S(1)}, bf16[2,3,128,128]{3,2,1,0:T(8,128)(2,1)S(1)}, u32[]{:S(2)}, u32[]{:S(2)}) collective-permute-start(bf16[2,3,128,128]{3,2,1,0:T(8,128)(2,1)S(1)} %slice.44), channel_id=1, source_target_pairs={{0,6},{1,25},{2,0},{3,27},{4,2},{5,29},{6,4},{7,31},{8,14},{9,1},{... | collective-permute-start | bytes 589832 | tf_op jit(solution)/shard_map/ppermute | solution.py:40
  29.1 7.0 %collective-permute-start.5 = (bf16[2,3,128,128]{3,2,1,0:T(8,128)(2,1)S(1)}, bf16[2,3,128,128]{3,2,1,0:T(8,128)(2,1)S(1)}, u32[]{:S(2)}, u32[]{:S(2)}) collective-permute-start(bf16[2,3,128,128]{3,2,1,0:T(8,128)(2,1)S(1)} %slice.43), channel_id=1, source_target_pairs={{0,2},{1,9},{2,4},{3,11},{4,6},{5,13},{6,0},{7,15},{8,10},{9,17},{... | collective-permute-start | bytes 589832 | tf_op jit(solution)/shard_map/ppermute | solution.py:40
  31.1 5.5 %collective-permute-start.10 = (bf16[4,3,128,128]{3,2,1,0:T(8,128)(2,1)S(1)}, bf16[4,3,128,128]{3,2,1,0:T(8,128)(2,1)S(1)}, u32[]{:S(2)}, u32[]{:S(2)}) collective-permute-start(bf16[4,3,128,128]{3,2,1,0:T(8,128)(2,1)S(1)} %collective-permute-done.3.refs_1_), channel_id=1, source_target_pairs={{0,1},{1,0},{2,3},{3,2},{4,5},{5,4},{6,7},{7,6},{8,9},{9,8},{10,11... | collective-permute-start | bytes 1179656 | tf_op jit(solution)/shard_map/ppermute | solution.py:40
  31.2 5.5 %collective-permute-start.11 = (bf16[4,3,128,128]{3,2,1,0:T(8,128)(2,1)S(1)}, bf16[4,3,128,128]{3,2,1,0:T(8,128)(2,1)S(1)}, u32[]{:S(2)}, u32[]{:S(2)}) collective-permute-start(bf16[4,3,128,128]{3,2,1,0:T(8,128)(2,1)S(1)} %collective-permute-done.4.refs_2_), channel_id=1, source_target_pairs={{0,1},{1,0},{2,3},{3,2},{4,5},{5,4},{6,7},{7,6},{8,9},{9,8},{10,11... | collective-permute-start | bytes 1179656 | tf_op jit(solution)/shard_map/ppermute | solution.py:40
  36.1 1.6 %collective-permute-start.8 = (bf16[2,3,128,128]{3,2,1,0:T(8,128)(2,1)S(1)}, bf16[2,3,128,128]{3,2,1,0:T(8,128)(2,1)S(1)}, u32[]{:S(2)}, u32[]{:S(2)}) collective-permute-start(bf16[2,3,128,128]{3,2,1,0:T(8,128)(2,1)S(1)} %collective-permute-done.5.refs_0_), channel_id=1, source_target_pairs={{0,1},{1,0},{2,3},{3,2},{4,5},{5,4},{6,7},{7,6},{8,9},{9,8},{10,11... | collective-permute-start | bytes 589832 | tf_op jit(solution)/shard_map/ppermute | solution.py:40
  36.1 1.7 %collective-permute-start.9 = (bf16[2,3,128,128]{3,2,1,0:T(8,128)(2,1)S(1)}, bf16[2,3,128,128]{3,2,1,0:T(8,128)(2,1)S(1)}, u32[]{:S(2)}, u32[]{:S(2)}) collective-permute-start(bf16[2,3,128,128]{3,2,1,0:T(8,128)(2,1)S(1)} %collective-permute-done.6.refs_1_), channel_id=1, source_target_pairs={{0,1},{1,0},{2,3},{3,2},{4,5},{5,4},{6,7},{7,6},{8,9},{9,8},{10,11... | collective-permute-start | bytes 589832 | tf_op jit(solution)/shard_map/ppermute | solution.py:40
  42.4 1.8 %collective-permute-start.14 = (bf16[4,128,384]{2,1,0:T(8,128)(2,1)S(1)}, bf16[4,128,384]{2,1,0:T(8,128)(2,1)S(1)}, u32[]{:S(2)}, u32[]{:S(2)}) collective-permute-start(bf16[4,128,384]{2,1,0:T(8,128)(2,1)S(1)} %get-tuple-element.75), channel_id=1, source_target_pairs={{0,1},{1,0},{2,3},{3,2},{4,5},{5,4},{6,7},{7,6},{8,9},{9,8},{10,11... | collective-permute-start | bytes 1179656 | tf_op jit(solution)/shard_map/ppermute | solution.py:40
  45.3 7.3 %collective-permute-start.15 = (bf16[8,128,384]{2,1,0:T(8,128)(2,1)S(1)}, bf16[8,128,384]{2,1,0:T(8,128)(2,1)S(1)}, u32[]{:S(2)}, u32[]{:S(2)}) collective-permute-start(bf16[8,128,384]{2,1,0:T(8,128)(2,1)S(1)} %shard_map.164), channel_id=1, source_target_pairs={{0,1},{1,0},{2,3},{3,2},{4,5},{5,4},{6,7},{7,6},{8,9},{9,8},{10,11... | collective-permute-start | bytes 2359304 | tf_op jit(solution)/shard_map/ppermute | solution.py:40
  45.7 7.0 %collective-permute-start.17 = (bf16[2,128,384]{2,1,0:T(8,128)(2,1)S(1)}, bf16[2,128,384]{2,1,0:T(8,128)(2,1)S(1)}, u32[]{:S(2)}, u32[]{:S(2)}) collective-permute-start(bf16[2,128,384]{2,1,0:T(8,128)(2,1)S(1)} %get-tuple-element.113), channel_id=1, source_target_pairs={{0,2},{1,9},{2,4},{3,11},{4,6},{5,13},{6,0},{7,15},{8,10},{9,17},{... | collective-permute-start | bytes 589832 | tf_op jit(solution)/shard_map/ppermute | solution.py:40
  46.5 6.1 %collective-permute-start.16 = (bf16[2,128,384]{2,1,0:T(8,128)(2,1)S(1)}, bf16[2,128,384]{2,1,0:T(8,128)(2,1)S(1)}, u32[]{:S(2)}, u32[]{:S(2)}) collective-permute-start(bf16[2,128,384]{2,1,0:T(8,128)(2,1)S(1)} %get-tuple-element.114), channel_id=1, source_target_pairs={{0,6},{1,25},{2,0},{3,27},{4,2},{5,29},{6,4},{7,31},{8,14},{9,1},{... | collective-permute-start | bytes 589832 | tf_op jit(solution)/shard_map/ppermute | solution.py:40
  53.1 9.0 %collective-permute-start.18 = (bf16[4,128,384]{2,1,0:T(8,128)(2,1)S(1)}, bf16[4,128,384]{2,1,0:T(8,128)(2,1)S(1)}, u32[]{:S(2)}, u32[]{:S(2)}) collective-permute-start(bf16[4,128,384]{2,1,0:T(8,128)(2,1)S(1)} %pad_maximum_fusion.1), channel_id=1, source_target_pairs={{0,6},{1,25},{2,0},{3,27},{4,2},{5,29},{6,4},{7,31},{8,14},{9,1},{... | collective-permute-start | bytes 1179656 | tf_op jit(solution)/shard_map/ppermute | solution.py:40
  56.4 9.0 %collective-permute-start.19 = (bf16[4,128,384]{2,1,0:T(8,128)(2,1)S(1)}, bf16[4,128,384]{2,1,0:T(8,128)(2,1)S(1)}, u32[]{:S(2)}, u32[]{:S(2)}) collective-permute-start(bf16[4,128,384]{2,1,0:T(8,128)(2,1)S(1)} %pad_maximum_fusion.2), channel_id=1, source_target_pairs={{0,2},{1,9},{2,4},{3,11},{4,6},{5,13},{6,0},{7,15},{8,10},{9,17},{... | collective-permute-start | bytes 1179656 | tf_op jit(solution)/shard_map/ppermute | solution.py:40
  57.4 8.0 %collective-permute-start.20 = (bf16[4,128,384]{2,1,0:T(8,128)(2,1)S(1)}, bf16[4,128,384]{2,1,0:T(8,128)(2,1)S(1)}, u32[]{:S(2)}, u32[]{:S(2)}) collective-permute-start(bf16[4,128,384]{2,1,0:T(8,128)(2,1)S(1)} %get-tuple-element.91), channel_id=1, source_target_pairs={{0,1},{1,0},{2,3},{3,2},{4,5},{5,4},{6,7},{7,6},{8,9},{9,8},{10,11... | collective-permute-start | bytes 1179656 | tf_op jit(solution)/shard_map/ppermute | solution.py:40
  65.7 4.7 %collective-permute-start.23 = (bf16[128,384]{1,0:T(8,128)(2,1)S(1)}, bf16[128,384]{1,0:T(8,128)(2,1)S(1)}, u32[]{:S(2)}, u32[]{:S(2)}) collective-permute-start(bf16[128,384]{1,0:T(8,128)(2,1)S(1)} %get-tuple-element.110), channel_id=1, source_target_pairs={{0,8},{1,3},{2,10},{3,5},{4,12},{5,7},{6,14},{7,1},{8,16},{9,11},{... | collective-permute-start | bytes 294920 | tf_op jit(solution)/shard_map/ppermute | solution.py:40
  66.7 6.1 %collective-permute-start.22 = (bf16[128,384]{1,0:T(8,128)(2,1)S(1)}, bf16[128,384]{1,0:T(8,128)(2,1)S(1)}, u32[]{:S(2)}, u32[]{:S(2)}) collective-permute-start(bf16[128,384]{1,0:T(8,128)(2,1)S(1)} %get-tuple-element.111), channel_id=1, source_target_pairs={{0,16},{1,5},{2,18},{3,7},{4,20},{5,1},{6,22},{7,3},{8,24},{9,13},... | collective-permute-start | bytes 294920 | tf_op jit(solution)/shard_map/ppermute | solution.py:40
  68.0 5.8 %collective-permute-start.21 = (bf16[128,384]{1,0:T(8,128)(2,1)S(1)}, bf16[128,384]{1,0:T(8,128)(2,1)S(1)}, u32[]{:S(2)}, u32[]{:S(2)}) collective-permute-start(bf16[128,384]{1,0:T(8,128)(2,1)S(1)} %get-tuple-element.112), channel_id=1, source_target_pairs={{0,24},{1,7},{2,26},{3,1},{4,28},{5,3},{6,30},{7,5},{8,0},{9,15},{... | collective-permute-start | bytes 294920 | tf_op jit(solution)/shard_map/ppermute | solution.py:40

commit v6 on v5

--- a/solution.py
+++ b/solution.py
@@ -16,8 +16,8 @@
 UNROLL = 16
 ROWS, LEAD, FIRST, HSLOT, DCOLS, OWNER, GLIVE, DLIVE = range(8)
 
-OTHER = (0, 0, 0, 1, 0, 1, 1, 1)
-STEPS = (0, 1, 3, 0, 2, 1, 3, 2)
+OTHER = (0, 0, 0, 0, 1, 1, 1, 1)
+STEPS = (0, 1, 3, 2, 0, 1, 3, 2)
 
 
 def group(other, j):
@@ -199,7 +199,7 @@
         copy.wait()
 
 
-def next_kernel(n, tab, x, w, y, acc, h, y_acc, staged, sems):
+def forward_next_kernel(n, tab, x, w, h, acc):
     def some(ks):
         project(tab, ks, lambda k: x[:, cols(tab[ROWS, k])], lambda k: w[k, :, : 2 * B], acc)
 
@@ -212,15 +212,18 @@
 
     loop(n, 4, activate)
     h[n] = jnp.zeros((B, B), BF16)
-    y_acc[...] = jnp.zeros_like(y_acc)
+
+
+def down_next_kernel(n, tab, h, w, y, acc, staged, sems):
+    acc[...] = jnp.zeros_like(acc)
 
     def down(js):
         parts = [rounded(dot(h[tab[HSLOT, j]], w[j, :, 2 * B :]) * live(tab, DLIVE, j)) for j in js]
         for j, part in zip(js, parts):
-            y_acc[tab[DCOLS, j]] += part
+            acc[tab[DCOLS, j]] += part
 
     loop(n, UNROLL, down)
-    put(y_acc, y, staged, sems)
+    put(acc, y, staged, sems)
 
 
 def grads(tab, slots, x_turned, h_turned, d_gu, cot, out):
@@ -331,17 +334,15 @@
         2,
         far=[gate_up_tiles, down_tiles, pending],
     )
+    own, asked = together(own[None], asked)
+    one, three, two = send(own, 1, 0), send(own, -1, 0), send(own, 2, 0)
     [picked] = call(
         part(pick_kernel, n), [kept((n, tok, B), BF16)], [], [asked], [held_back], 2
     )
     cot = lax.ppermute(picked, "pipe", down_pairs)
-
-    own = own[None]
-    one, three, two = send(own, 1, 0), send(own, -1, 0), send(own, 2, 0)
     near = jnp.concatenate([own, one, two, three], axis=0)
     near, gu_rows, gu_cols, down_rows = together(near, gu_rows, gu_cols, down_rows)
     back, ahead = send(near, 0, 1), send(near, 0, -1)
-    near_core = core(near)
 
     tab = tables(
         mine,
@@ -361,22 +362,22 @@
         4,
         far=[x_saved, x_next],
     )
-    back, ahead, x_blocks, x_turned = together(back, ahead, x_blocks, x_turned)
+    back, ahead, near, x_blocks, x_turned = together(back, ahead, near, x_blocks, x_turned)
     low, high = send(back[:2], 0, 1), send(ahead[2:], 0, -1)
     tiles, gates = kept((n, B, 3 * B), BF16), kept((n, tok, 2 * B), F32)
     w, acc = call(
-        saved_first_kernel, [tiles, gates], [], [tab], [x_blocks, near, back, ahead, near_core], 6
+        saved_first_kernel, [tiles, gates], [], [tab], [x_blocks, near, back, ahead], 6
     )
     low, high, w, acc = together(low, high, w, acc)
-    more = [low, high, core(back), core(ahead)]
+    more = [low, high, core(near), core(back), core(ahead)]
     w, acc = call(
-        part(saved_more_kernel, CHIPS),
+        part(saved_more_kernel, CHIPS - SIDE),
         [tiles, gates],
         [],
         [tab],
         [x_blocks, *more, w, acc],
         6,
-        aliases={6: 0, 7: 1},
+        aliases={7: 0, 8: 1},
     )
     last = [core(low), core(high)]
     w, acc, coef, h_turned = call(
@@ -432,26 +433,31 @@
     from_ahead, from_back = send(to_back, 0, -1), send(to_ahead, 0, 1)
     other_last, own_last = products(d_gu, (group(1, 0), BF16), (group(0, 0), F32))
     last = core(other_last)
+    [h_next] = call(
+        part(forward_next_kernel, n),
+        [kept((n + 1, tok, B), BF16)],
+        [VMEM((n, tok, 2 * B), F32)],
+        [tab],
+        [x_late, w],
+        6,
+        4 * n * product,
+    )
+    from_ahead, from_back, h_next = together(from_ahead, from_back, h_next)
+    row = own_last + last.astype(F32) + from_ahead.astype(F32) + from_back.astype(F32)
+    row, h_next = together(row, h_next)
     [y] = call(
-        part(next_kernel, n),
+        part(down_next_kernel, n),
         [jax.ShapeDtypeStruct((1, tok, width), BF16)],
-        [
-            VMEM((n, tok, 2 * B), F32),
-            VMEM((n + 1, tok, B), BF16),
-            VMEM((blocks, tok, B), F32),
-            VMEM((tok, width), BF16),
-            sems((4,)),
-        ],
-        [tab],
-        [x_late, w],
-        14,
-        8 * n * product,
+        [VMEM((blocks, tok, B), F32), VMEM((tok, width), BF16), sems((4,))],
+        [tab],
+        [h_next, w],
+        8,
+        4 * n * product,
         out_space=pltpu.HBM,
     )
-    from_ahead, from_back, y = together(from_ahead, from_back, y)
-    row = own_last + last.astype(F32) + from_ahead.astype(F32) + from_back.astype(F32)
     out = row[1:].astype(BF16)
     one, two, three = send(out[0], -1, 0), send(out[1], 2, 0), send(out[2], 1, 0)
+    one, two, three, y = together(one, two, three, y)
     grad_gu, grad_down = call(
         total_kernel,
         [

time: 74.7 us -> 76 us (1.017)
  starting transfers between devices: 25.4 us -> 26.9 us
    ppermute x22, waiting for transfers between devices: 15.8 us -> 17.6 us  [send(): return lax.ppermute(value, 'tile', pairs(first, second, core))]
    ppermute x1, waiting for transfers between devices: 5.43 us -> 3.9 us  [per_device(): asked = lax.ppermute(down_cols[0].reshape(1, n), 'pipe', up_pairs)]
    ppermute x22, starting transfers between devices: 21.4 us -> 22.8 us  [send(): return lax.ppermute(value, 'tile', pairs(first, second, core))]
    pallas_call x13 -> x14, Pallas kernels: 24.7 us -> 24.9 us  [call(): pl.pallas_call(body, out_shape=outs, in_specs=[pl.BlockSpec(memory_space=...]
  transfers between devices with their start and end apart: 24 -> 24, of which waited for: 12 -> 12; matrix products, arithmetic and copies ran while one was open for 2% -> 1% of each run, Pallas kernels for 25% -> 27%
where the time goes in v6:
time: 76 us; the launch traced here: 75.8 us
  starting transfers between devices  26.9 us (35%)
  Pallas kernels  24.9 us (33%)
  waiting for transfers between devices  21.5 us (28%)
  other arithmetic  1.33 us (2%)
  between operations  1.01 us (1%)
    pallas_call x14, Pallas kernels, call(): pl.pallas_call(body, out_shape=outs, in_specs=[pl.BlockSpec(memory_space=...  24.9 us
    ppermute x22, starting transfers between devices, send(): return lax.ppermute(value, 'tile', pairs(first, second, core))  22.8 us
    ppermute x22, waiting for transfers between devices, send(): return lax.ppermute(value, 'tile', pairs(first, second, core))  17.6 us
    ppermute x1, waiting for transfers between devices, per_device(): asked = lax.ppermute(down_cols[0].reshape(1, n), 'pipe', up_pairs)  3.9 us
    ppermute x1, starting transfers between devices, per_device(): cot = lax.ppermute(picked, 'pipe', down_pairs)  2.09 us
    ppermute x1, starting transfers between devices, per_device(): asked = lax.ppermute(down_cols[0].reshape(1, n), 'pipe', up_pairs)  1.99 us
  transfers between devices with their start and end apart: 24, of which 12 were waited for; matrix products, arithmetic and copies ran while one was open for 1% of the time, Pallas kernels for 27%

profile of v6, /device:TPU:6, one launch (start us, length us, event | category | flops | bytes accessed | tf_op | source)
XLA Modules:
  0.0 75.8 jit_solution(1692279447731946940)
XLA Ops:
  0.7 2.0 %collective-permute-start = (s32[1,32]{1,0:T(1,128)}, s32[1,32]{1,0:T(1,128)S(1)}, u32[]{:S(2)}, u32[]{:S(2)}) collective-permute-start(s32[1,32]{1,0:T(1,128)} %bitcast.56), channel_id=1, source_target_pairs={{0,32},{32,64},{64,96},{96,128},{128,160},{160,192},{192,224},{224... | collective-permute-start | bytes 392 | tf_op jit(solution)/shard_map/ppermute | solution.py:326
  2.7 1.6 %shard_map.156 = (bf16[3,128,128]{2,1,0:T(8,128)(2,1)S(1)}, bf16[128,8192]{1,0:T(8,128)(2,1)S(1)}) custom-call(bf16[1,1,1,2,128,128]{5,4,3,2,1,0:T(8,128)(2,1)} %gate_up.1, bf16[1,1,1,128,128]{4,3,2,1,0:T(8,128)(2,1)} %down.1, bf16[1,128,8192]{2,1,0:T(8,128)(2,1)} %pending.1), custom_call_target="tpu_custom_call" | custom-call | tf_op jit(solution)/shard_map/pallas_call | solution.py:89
  4.3 3.9 %collective-permute-done.asked = s32[1,32]{1,0:T(1,128)S(1)} collective-permute-done((s32[1,32]{1,0:T(1,128)}, s32[1,32]{1,0:T(1,128)S(1)}, u32[]{:S(2)}, u32[]{:S(2)}) %collective-permute-start) | collective-permute-done | bytes 160 | tf_op jit(solution)/shard_map/ppermute | solution.py:326
  8.2 0.8 %collective-permute-start.3 = (bf16[1,3,128,128]{3,2,1,0:T(8,128)(2,1)S(1)}, bf16[1,3,128,128]{3,2,1,0:T(8,128)(2,1)S(1)}, u32[]{:S(2)}, u32[]{:S(2)}) collective-permute-start(bf16[1,3,128,128]{3,2,1,0:T(8,128)(2,1)S(1)} %bitcast.43), channel_id=1, source_target_pairs={{0,24},{1,7},{2,26},{3,1},{4,28},{5,3},{6,30},{7,5},{8,0},{9,15},{... | collective-permute-start | bytes 294920 | tf_op jit(solution)/shard_map/ppermute | solution.py:40
  9.1 1.1 %collective-permute-start.2 = (bf16[1,3,128,128]{3,2,1,0:T(8,128)(2,1)S(1)}, bf16[1,3,128,128]{3,2,1,0:T(8,128)(2,1)S(1)}, u32[]{:S(2)}, u32[]{:S(2)}) collective-permute-start(bf16[1,3,128,128]{3,2,1,0:T(8,128)(2,1)S(1)} %bitcast.44), channel_id=1, source_target_pairs={{0,16},{1,5},{2,18},{3,7},{4,20},{5,1},{6,22},{7,3},{8,24},{9,13},... | collective-permute-start | bytes 294920 | tf_op jit(solution)/shard_map/ppermute | solution.py:40
  10.2 2.1 %collective-permute-start.1 = (bf16[1,3,128,128]{3,2,1,0:T(8,128)(2,1)S(1)}, bf16[1,3,128,128]{3,2,1,0:T(8,128)(2,1)S(1)}, u32[]{:S(2)}, u32[]{:S(2)}) collective-permute-start(bf16[1,3,128,128]{3,2,1,0:T(8,128)(2,1)S(1)} %bitcast.45), channel_id=1, source_target_pairs={{0,8},{1,3},{2,10},{3,5},{4,12},{5,7},{6,14},{7,1},{8,16},{9,11},{... | collective-permute-start | bytes 294920 | tf_op jit(solution)/shard_map/ppermute | solution.py:40
  12.3 0.8 %shard_map.161 = bf16[32,128,128]{2,1,0:T(8,128)(2,1)S(1)} custom-call(s32[1,32]{1,0:T(1,128)S(1)} %collective-permute-done.asked, bf16[128,8192]{1,0:T(8,128)(2,1)S(1)} %get-tuple-element.84.pending), custom_call_target="tpu_custom_call" | custom-call | tf_op jit(solution)/shard_map/pallas_call | solution.py:89
  13.1 2.1 %collective-permute-start.13 = (bf16[32,128,128]{2,1,0:T(8,128)(2,1)S(1)}, bf16[32,128,128]{2,1,0:T(8,128)(2,1)S(1)}, u32[]{:S(2)}, u32[]{:S(2)}) collective-permute-start(bf16[32,128,128]{2,1,0:T(8,128)(2,1)S(1)} %shard_map.161), channel_id=1, source_target_pairs={{0,224},{32,0},{64,32},{96,64},{128,96},{160,128},{192,160},{224,1... | collective-permute-start | bytes 3145736 | tf_op jit(solution)/shard_map/ppermute | solution.py:342
  15.2 0.7 collective-permute-done.1
  16.0 3.1 %collective-permute-start.5 = (bf16[4,3,128,128]{3,2,1,0:T(8,128)(2,1)S(1)}, bf16[4,3,128,128]{3,2,1,0:T(8,128)(2,1)S(1)}, u32[]{:S(2)}, u32[]{:S(2)}) collective-permute-start(bf16[4,3,128,128]{3,2,1,0:T(8,128)(2,1)S(1)} %pad_maximum_fusion.refs_0_), channel_id=1, source_target_pairs={{0,6},{1,25},{2,0},{3,27},{4,2},{5,29},{6,4},{7,31},{8,14},{9,1},{... | collective-permute-start | bytes 1179656 | tf_op jit(solution)/shard_map/ppermute | solution.py:40
  19.2 0.3 select_reduce_fusion
  19.4 0.2 select_reduce_fusion.3
  19.7 3.3 %shard_map.157 = (bf16[32,128,128]{2,1,0:T(8,128)(2,1)S(1)}, bf16[32,128,128]{2,1,0:T(8,128)(2,1)S(1)}, bf16[128,8192]{1,0:T(8,128)(2,1)S(1)}) custom-call(s32[8,32]{1,0:T(8,128)S(1)} %stack.26.tab, bf16[1,128,8192]{2,1,0:T(8,128)(2,1)} %x_saved.1, bf16[1,128,8192]{2,1,0:T(8,128)(2,1)} %x_next.1), custom_call_target="tpu_custom_call" | custom-call | tf_op jit(solution)/shard_map/pallas_call | solution.py:89
  22.9 1.5 %collective-permute-done.5.refs_2_ = bf16[4,3,128,128]{3,2,1,0:T(8,128)(2,1)S(1)} collective-permute-done((bf16[4,3,128,128]{3,2,1,0:T(8,128)(2,1)S(1)}, bf16[4,3,128,128]{3,2,1,0:T(8,128)(2,1)S(1)}, u32[]{:S(2)}, u32[]{:S(2)}) %collective-permute-start.5) | collective-permute-done | bytes 393248 | tf_op jit(solution)/shard_map/ppermute | solution.py:40
  24.4 3.7 %collective-permute-done.4.refs_1_ = bf16[4,3,128,128]{3,2,1,0:T(8,128)(2,1)S(1)} collective-permute-done((bf16[4,3,128,128]{3,2,1,0:T(8,128)(2,1)S(1)}, bf16[4,3,128,128]{3,2,1,0:T(8,128)(2,1)S(1)}, u32[]{:S(2)}, u32[]{:S(2)}) %collective-permute-start.4) | collective-permute-done | bytes 393248 | tf_op jit(solution)/shard_map/ppermute | solution.py:40
  28.4 2.0 %collective-permute-start.6 = (bf16[2,3,128,128]{3,2,1,0:T(8,128)(2,1)S(1)}, bf16[2,3,128,128]{3,2,1,0:T(8,128)(2,1)S(1)}, u32[]{:S(2)}, u32[]{:S(2)}) collective-permute-start(bf16[2,3,128,128]{3,2,1,0:T(8,128)(2,1)S(1)} %slice.43), channel_id=1, source_target_pairs={{0,2},{1,9},{2,4},{3,11},{4,6},{5,13},{6,0},{7,15},{8,10},{9,17},{... | collective-permute-start | bytes 589832 | tf_op jit(solution)/shard_map/ppermute | solution.py:40
  30.3 1.0 %collective-permute-start.11 = (bf16[4,3,128,128]{3,2,1,0:T(8,128)(2,1)S(1)}, bf16[4,3,128,128]{3,2,1,0:T(8,128)(2,1)S(1)}, u32[]{:S(2)}, u32[]{:S(2)}) collective-permute-start(bf16[4,3,128,128]{3,2,1,0:T(8,128)(2,1)S(1)} %collective-permute-done.4.refs_1_), channel_id=1, source_target_pairs={{0,1},{1,0},{2,3},{3,2},{4,5},{5,4},{6,7},{7,6},{8,9},{9,8},{10,11... | collective-permute-start | bytes 1179656 | tf_op jit(solution)/shard_map/ppermute | solution.py:40
  31.3 2.6 %collective-permute-done.7.refs_1_ = bf16[2,3,128,128]{3,2,1,0:T(8,128)(2,1)S(1)} collective-permute-done((bf16[2,3,128,128]{3,2,1,0:T(8,128)(2,1)S(1)}, bf16[2,3,128,128]{3,2,1,0:T(8,128)(2,1)S(1)}, u32[]{:S(2)}, u32[]{:S(2)}) %collective-permute-start.7) | collective-permute-done | bytes 196640 | tf_op jit(solution)/shard_map/ppermute | solution.py:40
  33.9 1.1 %shard_map.158 = (bf16[32,128,384]{2,1,0:T(8,128)(2,1)S(1)}, f32[32,128,256]{2,1,0:T(8,128)S(1)}) custom-call(s32[8,32]{1,0:T(8,128)S(1)} %stack.26.tab, bf16[32,128,128]{2,1,0:T(8,128)(2,1)S(1)} %get-tuple-element.68.x, bf16[4,3,128,128]{3,2,1,0:T(8,128)(2,1)S(1)} %pad_maximum_fusion.refs_0_, bf16[4,3,128,128]{3,2,1,0:T(8,128)(2,1)S(1)} %collective-permute-done.4.refs_1_, ...), custom_call_target="tpu_custom_call" | custom-call | tf_op jit(solution)/shard_map/pallas_call | solution.py:89
  35.0 0.3 collective-permute-done.6.refs_0_
  35.3 0.3 collective-permute-start.8
  35.6 0.3 collective-permute-start.9
  35.9 1.3 %shard_map.159 = (bf16[32,128,384]{2,1,0:T(8,128)(2,1)S(1)}, f32[32,128,256]{2,1,0:T(8,128)S(1)}) custom-call(s32[8,32]{1,0:T(8,128)S(1)} %stack.26.tab, bf16[32,128,128]{2,1,0:T(8,128)(2,1)S(1)} %get-tuple-element.68.x, bf16[2,3,128,128]{3,2,1,0:T(8,128)(2,1)S(1)} %collective-permute-done.6.refs_0_, ...), custom_call_target="tpu_custom_call", output_to_operand_aliasing={{0}: (7, {}), {1}: (8, {})} | custom-call | tf_op jit(solution)/shard_map/pallas_call | solution.py:89
  37.3 2.1 %shard_map.160 = (bf16[32,128,384]{2,1,0:T(8,128)(2,1)S(1)}, f32[32,128,256]{2,1,0:T(8,128)S(1)}, f32[32,128,256]{2,1,0:T(8,128)S(1)}, bf16[33,128,128]{2,1,0:T(8,128)(2,1)S(1)}) custom-call(s32[8,32]{1,0:T(8,128)S(1)} %stack.26.tab, bf16[32,128,128]{2,1,0:T(8,128)(2,1)S(1)} %get-tuple-element.68.x, ...), custom_call_target="tpu_custom_call", output_to_operand_aliasing={{0}: (4, {}), {1}: (5, {})} | custom-call | tf_op jit(solution)/shard_map/pallas_call | solution.py:89
  39.4 2.5 %shard_map.162 = (bf16[4,128,384]{2,1,0:T(8,128)(2,1)S(1)}, bf16[32,128,256]{2,1,0:T(8,128)(2,1)S(1)}) custom-call(s32[8,32]{1,0:T(8,128)S(1)} %stack.26.tab, bf16[32,128,128]{2,1,0:T(8,128)(2,1)S(1)} %get-tuple-element.67.x_turned, bf16[32,128,384]{2,1,0:T(8,128)(2,1)S(1)} %get-tuple-element.81.w, f32[32,128,256]{2,1,0:T(8,128)S(1)} %get-tuple-element.82.coef, ...), custom_call_target="tpu_custom_call" | custom-call | tf_op jit(solution)/shard_map/pallas_call | solution.py:89
  41.9 0.3 collective-permute-start.14
  42.2 1.1 %shard_map.163 = (f32[4,128,384]{2,1,0:T(8,128)S(1)}, f32[8,128,384]{2,1,0:T(8,128)S(1)}) custom-call(s32[8,32]{1,0:T(8,128)S(1)} %stack.26.tab, bf16[32,128,128]{2,1,0:T(8,128)(2,1)S(1)} %get-tuple-element.67.x_turned, bf16[33,128,128]{2,1,0:T(8,128)(2,1)S(1)} %get-tuple-element.80.h_turned, bf16[32,128,256]{2,1,0:T(8,128)(2,1)S(1)} %get-tuple-element.96.d_gu, ...), custom_call_target="tpu_custom_call" | custom-call | tf_op jit(solution)/shard_map/pallas_call | solution.py:89
  43.3 0.4 collective-permute-done.14
  43.8 1.0 %shard_map.164 = bf16[8,128,384]{2,1,0:T(8,128)(2,1)S(1)} custom-call(s32[8,32]{1,0:T(8,128)S(1)} %stack.26.tab, bf16[32,128,128]{2,1,0:T(8,128)(2,1)S(1)} %get-tuple-element.67.x_turned, bf16[33,128,128]{2,1,0:T(8,128)(2,1)S(1)} %get-tuple-element.80.h_turned, bf16[32,128,256]{2,1,0:T(8,128)(2,1)S(1)} %get-tuple-element.96.d_gu, ...), custom_call_target="tpu_custom_call" | custom-call | tf_op jit(solution)/shard_map/pallas_call | solution.py:89
  44.8 0.3 collective-permute-start.15
  45.1 0.6 collective-permute-start.17
  45.7 2.7 %collective-permute-start.16 = (bf16[2,128,384]{2,1,0:T(8,128)(2,1)S(1)}, bf16[2,128,384]{2,1,0:T(8,128)(2,1)S(1)}, u32[]{:S(2)}, u32[]{:S(2)}) collective-permute-start(bf16[2,128,384]{2,1,0:T(8,128)(2,1)S(1)} %get-tuple-element.130), channel_id=1, source_target_pairs={{0,6},{1,25},{2,0},{3,27},{4,2},{5,29},{6,4},{7,31},{8,14},{9,1},{... | collective-permute-start | bytes 589832 | tf_op jit(solution)/shard_map/ppermute | solution.py:40
  48.4 3.3 %shard_map.165 = bf16[1,128,8192]{2,1,0:T(8,128)(2,1)} custom-call(s32[8,32]{1,0:T(8,128)S(1)} %stack.26.tab, bf16[32,128,256]{2,1,0:T(8,128)(2,1)S(1)} %get-tuple-element.96.d_gu, bf16[32,128,384]{2,1,0:T(8,128)(2,1)S(1)} %get-tuple-element.81.w), custom_call_target="tpu_custom_call" | custom-call | flops 536870912 | bytes 2097152 | tf_op jit(solution)/shard_map/pallas_call | solution.py:89
  51.7 0.4 collective-permute-done.17
  52.6 3.3 %collective-permute-start.19 = (bf16[4,128,384]{2,1,0:T(8,128)(2,1)S(1)}, bf16[4,128,384]{2,1,0:T(8,128)(2,1)S(1)}, u32[]{:S(2)}, u32[]{:S(2)}) collective-permute-start(bf16[4,128,384]{2,1,0:T(8,128)(2,1)S(1)} %pad_maximum_fusion.1), channel_id=1, source_target_pairs={{0,6},{1,25},{2,0},{3,27},{4,2},{5,29},{6,4},{7,31},{8,14},{9,1},{... | collective-permute-start | bytes 1179656 | tf_op jit(solution)/shard_map/ppermute | solution.py:40
  55.9 1.0 %shard_map.166 = (bf16[4,128,384]{2,1,0:T(8,128)(2,1)S(1)}, f32[4,128,384]{2,1,0:T(8,128)S(1)}) custom-call(s32[8,32]{1,0:T(8,128)S(1)} %stack.26.tab, bf16[32,128,128]{2,1,0:T(8,128)(2,1)S(1)} %get-tuple-element.67.x_turned, bf16[33,128,128]{2,1,0:T(8,128)(2,1)S(1)} %get-tuple-element.80.h_turned, bf16[32,128,256]{2,1,0:T(8,128)(2,1)S(1)} %get-tuple-element.96.d_gu, ...), custom_call_target="tpu_custom_call" | custom-call | tf_op jit(solution)/shard_map/pallas_call | solution.py:89
  56.9 1.0 %collective-permute-start.18 = (bf16[4,128,384]{2,1,0:T(8,128)(2,1)S(1)}, bf16[4,128,384]{2,1,0:T(8,128)(2,1)S(1)}, u32[]{:S(2)}, u32[]{:S(2)}) collective-permute-start(bf16[4,128,384]{2,1,0:T(8,128)(2,1)S(1)} %get-tuple-element.98), channel_id=1, source_target_pairs={{0,1},{1,0},{2,3},{3,2},{4,5},{5,4},{6,7},{7,6},{8,9},{9,8},{10,11... | collective-permute-start | bytes 1179656 | tf_op jit(solution)/shard_map/ppermute | solution.py:40
  57.9 2.2 %shard_map.167.h = bf16[33,128,128]{2,1,0:T(8,128)(2,1)S(1)} custom-call(s32[8,32]{1,0:T(8,128)S(1)} %stack.26.tab, bf16[128,8192]{1,0:T(8,128)(2,1)S(1)} %get-tuple-element.101.x, bf16[32,128,384]{2,1,0:T(8,128)(2,1)S(1)} %get-tuple-element.81.w), custom_call_target="tpu_custom_call" | custom-call | flops 536870912 | bytes 2097152 | tf_op jit(solution)/shard_map/pallas_call | solution.py:89
  60.2 1.1 %collective-permute-done.19 = bf16[4,128,384]{2,1,0:T(8,128)(2,1)S(1)} collective-permute-done((bf16[4,128,384]{2,1,0:T(8,128)(2,1)S(1)}, bf16[4,128,384]{2,1,0:T(8,128)(2,1)S(1)}, u32[]{:S(2)}, u32[]{:S(2)}) %collective-permute-start.19) | collective-permute-done | bytes 393248 | tf_op jit(solution)/shard_map/ppermute | solution.py:40
  61.2 3.7 %collective-permute-done.20 = bf16[4,128,384]{2,1,0:T(8,128)(2,1)S(1)} collective-permute-done((bf16[4,128,384]{2,1,0:T(8,128)(2,1)S(1)}, bf16[4,128,384]{2,1,0:T(8,128)(2,1)S(1)}, u32[]{:S(2)}, u32[]{:S(2)}) %collective-permute-start.20) | collective-permute-done | bytes 393248 | tf_op jit(solution)/shard_map/ppermute | solution.py:40
  64.9 0.2 convert_add_fusion.1
  65.2 2.7 %collective-permute-start.23 = (bf16[128,384]{1,0:T(8,128)(2,1)S(1)}, bf16[128,384]{1,0:T(8,128)(2,1)S(1)}, u32[]{:S(2)}, u32[]{:S(2)}) collective-permute-start(bf16[128,384]{1,0:T(8,128)(2,1)S(1)} %get-tuple-element.126), channel_id=1, source_target_pairs={{0,8},{1,3},{2,10},{3,5},{4,12},{5,7},{6,14},{7,1},{8,16},{9,11},{... | collective-permute-start | bytes 294920 | tf_op jit(solution)/shard_map/ppermute | solution.py:40
  68.0 0.6 collective-permute-start.22
  68.6 0.4 collective-permute-start.21
  68.9 3.0 %shard_map.168 = bf16[1,128,8192]{2,1,0:T(8,128)(2,1)} custom-call(s32[8,32]{1,0:T(8,128)S(1)} %stack.26.tab, bf16[33,128,128]{2,1,0:T(8,128)(2,1)S(1)} %shard_map.167.h, bf16[32,128,384]{2,1,0:T(8,128)(2,1)S(1)} %get-tuple-element.81.w), custom_call_target="tpu_custom_call" | custom-call | flops 536870912 | bytes 2097152 | tf_op jit(solution)/shard_map/pallas_call | solution.py:89
  71.9 2.3 %collective-permute-done.22.two = bf16[128,384]{1,0:T(8,128)(2,1)S(1)} collective-permute-done((bf16[128,384]{1,0:T(8,128)(2,1)S(1)}, bf16[128,384]{1,0:T(8,128)(2,1)S(1)}, u32[]{:S(2)}, u32[]{:S(2)}) %collective-permute-start.22) | collective-permute-done | bytes 98336 | tf_op jit(solution)/shard_map/ppermute | solution.py:40
  74.2 1.0 %collective-permute-done.21.one = bf16[128,384]{1,0:T(8,128)(2,1)S(1)} collective-permute-done((bf16[128,384]{1,0:T(8,128)(2,1)S(1)}, bf16[128,384]{1,0:T(8,128)(2,1)S(1)}, u32[]{:S(2)}, u32[]{:S(2)}) %collective-permute-start.21) | collective-permute-done | bytes 98336 | tf_op jit(solution)/shard_map/ppermute | solution.py:40
  75.1 0.7 shard_map.169
  (51 shorter events, 1.1 us)
Async XLA Ops:
  0.6 11.7 %copy-start = (s32[32]{0:T(128)S(1)}, s32[32]{0:T(128)}, u32[]{:S(2)}) copy-start(s32[32]{0:T(128)} %constant.81.clone) | copy-start | bytes 388
  0.6 11.6 %copy-start.1 = (s32[32]{0:T(128)S(1)}, s32[32]{0:T(128)}, u32[]{:S(2)}) copy-start(s32[32]{0:T(128)} %constant.80.clone) | copy-start | bytes 388
  0.7 7.6 %collective-permute-start = (s32[1,32]{1,0:T(1,128)}, s32[1,32]{1,0:T(1,128)S(1)}, u32[]{:S(2)}, u32[]{:S(2)}) collective-permute-start(s32[1,32]{1,0:T(1,128)} %bitcast.56), channel_id=1, source_target_pairs={{0,32},{32,64},{64,96},{96,128},{128,160},{160,192},{192,224},{224... | collective-permute-start | bytes 392 | tf_op jit(solution)/shard_map/ppermute | solution.py:326
  4.3 14.9 %copy-start.2 = (s32[1,32]{1,0:T(1,128)S(1)}, s32[1,32]{1,0:T(1,128)}, u32[]{:S(2)}) copy-start(s32[1,32]{1,0:T(1,128)} %param.21) | copy-start | bytes 388
  4.3 14.9 %copy-start.3 = (s32[1,32]{1,0:T(1,128)S(1)}, s32[1,32]{1,0:T(1,128)}, u32[]{:S(2)}) copy-start(s32[1,32]{1,0:T(1,128)} %param.18) | copy-start | bytes 388
  4.3 14.8 %copy-start.4 = (s32[1,32,1]{1,2,0:T(1,128)S(1)}, s32[1,32,1]{1,2,0:T(1,128)}, u32[]{:S(2)}) copy-start(s32[1,32,1]{1,2,0:T(1,128)} %param.20) | copy-start | bytes 388
  4.3 14.8 %copy-start.5 = (s32[1,32,1]{1,2,0:T(1,128)S(1)}, s32[1,32,1]{1,2,0:T(1,128)}, u32[]{:S(2)}) copy-start(s32[1,32,1]{1,2,0:T(1,128)} %param.19) | copy-start | bytes 388
  4.3 14.8 %copy-start.6 = (s32[1,32,1]{1,2,0:T(1,128)S(1)}, s32[1,32,1]{1,2,0:T(1,128)}, u32[]{:S(2)}) copy-start(s32[1,32,1]{1,2,0:T(1,128)} %param.17) | copy-start | bytes 388
  4.3 14.8 %copy-start.7 = (s32[1,32,1]{1,2,0:T(1,128)S(1)}, s32[1,32,1]{1,2,0:T(1,128)}, u32[]{:S(2)}) copy-start(s32[1,32,1]{1,2,0:T(1,128)} %param.16) | copy-start | bytes 388
  8.2 7.0 %collective-permute-start.3 = (bf16[1,3,128,128]{3,2,1,0:T(8,128)(2,1)S(1)}, bf16[1,3,128,128]{3,2,1,0:T(8,128)(2,1)S(1)}, u32[]{:S(2)}, u32[]{:S(2)}) collective-permute-start(bf16[1,3,128,128]{3,2,1,0:T(8,128)(2,1)S(1)} %bitcast.43), channel_id=1, source_target_pairs={{0,24},{1,7},{2,26},{3,1},{4,28},{5,3},{6,30},{7,5},{8,0},{9,15},{... | collective-permute-start | bytes 294920 | tf_op jit(solution)/shard_map/ppermute | solution.py:40
  9.1 6.2 %collective-permute-start.2 = (bf16[1,3,128,128]{3,2,1,0:T(8,128)(2,1)S(1)}, bf16[1,3,128,128]{3,2,1,0:T(8,128)(2,1)S(1)}, u32[]{:S(2)}, u32[]{:S(2)}) collective-permute-start(bf16[1,3,128,128]{3,2,1,0:T(8,128)(2,1)S(1)} %bitcast.44), channel_id=1, source_target_pairs={{0,16},{1,5},{2,18},{3,7},{4,20},{5,1},{6,22},{7,3},{8,24},{9,13},... | collective-permute-start | bytes 294920 | tf_op jit(solution)/shard_map/ppermute | solution.py:40
  10.2 5.8 %collective-permute-start.1 = (bf16[1,3,128,128]{3,2,1,0:T(8,128)(2,1)S(1)}, bf16[1,3,128,128]{3,2,1,0:T(8,128)(2,1)S(1)}, u32[]{:S(2)}, u32[]{:S(2)}) collective-permute-start(bf16[1,3,128,128]{3,2,1,0:T(8,128)(2,1)S(1)} %bitcast.45), channel_id=1, source_target_pairs={{0,8},{1,3},{2,10},{3,5},{4,12},{5,7},{6,14},{7,1},{8,16},{9,11},{... | collective-permute-start | bytes 294920 | tf_op jit(solution)/shard_map/ppermute | solution.py:40
  13.1 26.2 %collective-permute-start.13 = (bf16[32,128,128]{2,1,0:T(8,128)(2,1)S(1)}, bf16[32,128,128]{2,1,0:T(8,128)(2,1)S(1)}, u32[]{:S(2)}, u32[]{:S(2)}) collective-permute-start(bf16[32,128,128]{2,1,0:T(8,128)(2,1)S(1)} %shard_map.161), channel_id=1, source_target_pairs={{0,224},{32,0},{64,32},{96,64},{128,96},{160,128},{192,160},{224,1... | collective-permute-start | bytes 3145736 | tf_op jit(solution)/shard_map/ppermute | solution.py:342
  16.0 8.4 %collective-permute-start.5 = (bf16[4,3,128,128]{3,2,1,0:T(8,128)(2,1)S(1)}, bf16[4,3,128,128]{3,2,1,0:T(8,128)(2,1)S(1)}, u32[]{:S(2)}, u32[]{:S(2)}) collective-permute-start(bf16[4,3,128,128]{3,2,1,0:T(8,128)(2,1)S(1)} %pad_maximum_fusion.refs_0_), channel_id=1, source_target_pairs={{0,6},{1,25},{2,0},{3,27},{4,2},{5,29},{6,4},{7,31},{8,14},{9,1},{... | collective-permute-start | bytes 1179656 | tf_op jit(solution)/shard_map/ppermute | solution.py:40
  19.1 9.0 %collective-permute-start.4 = (bf16[4,3,128,128]{3,2,1,0:T(8,128)(2,1)S(1)}, bf16[4,3,128,128]{3,2,1,0:T(8,128)(2,1)S(1)}, u32[]{:S(2)}, u32[]{:S(2)}) collective-permute-start(bf16[4,3,128,128]{3,2,1,0:T(8,128)(2,1)S(1)} %pad_maximum_fusion.refs_0_), channel_id=1, source_target_pairs={{0,2},{1,9},{2,4},{3,11},{4,6},{5,13},{6,0},{7,15},{8,10},{9,17},{... | collective-permute-start | bytes 1179656 | tf_op jit(solution)/shard_map/ppermute | solution.py:40
  28.1 5.7 %collective-permute-start.7 = (bf16[2,3,128,128]{3,2,1,0:T(8,128)(2,1)S(1)}, bf16[2,3,128,128]{3,2,1,0:T(8,128)(2,1)S(1)}, u32[]{:S(2)}, u32[]{:S(2)}) collective-permute-start(bf16[2,3,128,128]{3,2,1,0:T(8,128)(2,1)S(1)} %slice.44), channel_id=1, source_target_pairs={{0,6},{1,25},{2,0},{3,27},{4,2},{5,29},{6,4},{7,31},{8,14},{9,1},{... | collective-permute-start | bytes 589832 | tf_op jit(solution)/shard_map/ppermute | solution.py:40
  28.2 7.4 %collective-permute-start.10 = (bf16[4,3,128,128]{3,2,1,0:T(8,128)(2,1)S(1)}, bf16[4,3,128,128]{3,2,1,0:T(8,128)(2,1)S(1)}, u32[]{:S(2)}, u32[]{:S(2)}) collective-permute-start(bf16[4,3,128,128]{3,2,1,0:T(8,128)(2,1)S(1)} %pad_maximum_fusion.refs_0_), channel_id=1, source_target_pairs={{0,1},{1,0},{2,3},{3,2},{4,5},{5,4},{6,7},{7,6},{8,9},{9,8},{10,11... | collective-permute-start | bytes 1179656 | tf_op jit(solution)/shard_map/ppermute | solution.py:40
  28.4 7.0 %collective-permute-start.6 = (bf16[2,3,128,128]{3,2,1,0:T(8,128)(2,1)S(1)}, bf16[2,3,128,128]{3,2,1,0:T(8,128)(2,1)S(1)}, u32[]{:S(2)}, u32[]{:S(2)}) collective-permute-start(bf16[2,3,128,128]{3,2,1,0:T(8,128)(2,1)S(1)} %slice.43), channel_id=1, source_target_pairs={{0,2},{1,9},{2,4},{3,11},{4,6},{5,13},{6,0},{7,15},{8,10},{9,17},{... | collective-permute-start | bytes 589832 | tf_op jit(solution)/shard_map/ppermute | solution.py:40
  30.3 5.6 %collective-permute-start.11 = (bf16[4,3,128,128]{3,2,1,0:T(8,128)(2,1)S(1)}, bf16[4,3,128,128]{3,2,1,0:T(8,128)(2,1)S(1)}, u32[]{:S(2)}, u32[]{:S(2)}) collective-permute-start(bf16[4,3,128,128]{3,2,1,0:T(8,128)(2,1)S(1)} %collective-permute-done.4.refs_1_), channel_id=1, source_target_pairs={{0,1},{1,0},{2,3},{3,2},{4,5},{5,4},{6,7},{7,6},{8,9},{9,8},{10,11... | collective-permute-start | bytes 1179656 | tf_op jit(solution)/shard_map/ppermute | solution.py:40
  33.9 2.0 %collective-permute-start.12 = (bf16[4,3,128,128]{3,2,1,0:T(8,128)(2,1)S(1)}, bf16[4,3,128,128]{3,2,1,0:T(8,128)(2,1)S(1)}, u32[]{:S(2)}, u32[]{:S(2)}) collective-permute-start(bf16[4,3,128,128]{3,2,1,0:T(8,128)(2,1)S(1)} %collective-permute-done.5.refs_2_), channel_id=1, source_target_pairs={{0,1},{1,0},{2,3},{3,2},{4,5},{5,4},{6,7},{7,6},{8,9},{9,8},{10,11... | collective-permute-start | bytes 1179656 | tf_op jit(solution)/shard_map/ppermute | solution.py:40
  35.3 1.9 %collective-permute-start.8 = (bf16[2,3,128,128]{3,2,1,0:T(8,128)(2,1)S(1)}, bf16[2,3,128,128]{3,2,1,0:T(8,128)(2,1)S(1)}, u32[]{:S(2)}, u32[]{:S(2)}) collective-permute-start(bf16[2,3,128,128]{3,2,1,0:T(8,128)(2,1)S(1)} %collective-permute-done.6.refs_0_), channel_id=1, source_target_pairs={{0,1},{1,0},{2,3},{3,2},{4,5},{5,4},{6,7},{7,6},{8,9},{9,8},{10,11... | collective-permute-start | bytes 589832 | tf_op jit(solution)/shard_map/ppermute | solution.py:40
  35.6 1.6 %collective-permute-start.9 = (bf16[2,3,128,128]{3,2,1,0:T(8,128)(2,1)S(1)}, bf16[2,3,128,128]{3,2,1,0:T(8,128)(2,1)S(1)}, u32[]{:S(2)}, u32[]{:S(2)}) collective-permute-start(bf16[2,3,128,128]{3,2,1,0:T(8,128)(2,1)S(1)} %collective-permute-done.7.refs_1_), channel_id=1, source_target_pairs={{0,1},{1,0},{2,3},{3,2},{4,5},{5,4},{6,7},{7,6},{8,9},{9,8},{10,11... | collective-permute-start | bytes 589832 | tf_op jit(solution)/shard_map/ppermute | solution.py:40
  41.9 1.8 %collective-permute-start.14 = (bf16[4,128,384]{2,1,0:T(8,128)(2,1)S(1)}, bf16[4,128,384]{2,1,0:T(8,128)(2,1)S(1)}, u32[]{:S(2)}, u32[]{:S(2)}) collective-permute-start(bf16[4,128,384]{2,1,0:T(8,128)(2,1)S(1)} %get-tuple-element.87), channel_id=1, source_target_pairs={{0,1},{1,0},{2,3},{3,2},{4,5},{5,4},{6,7},{7,6},{8,9},{9,8},{10,11... | collective-permute-start | bytes 1179656 | tf_op jit(solution)/shard_map/ppermute | solution.py:40
  44.8 7.3 %collective-permute-start.15 = (bf16[8,128,384]{2,1,0:T(8,128)(2,1)S(1)}, bf16[8,128,384]{2,1,0:T(8,128)(2,1)S(1)}, u32[]{:S(2)}, u32[]{:S(2)}) collective-permute-start(bf16[8,128,384]{2,1,0:T(8,128)(2,1)S(1)} %shard_map.164), channel_id=1, source_target_pairs={{0,1},{1,0},{2,3},{3,2},{4,5},{5,4},{6,7},{7,6},{8,9},{9,8},{10,11... | collective-permute-start | bytes 2359304 | tf_op jit(solution)/shard_map/ppermute | solution.py:40
  45.1 7.0 %collective-permute-start.17 = (bf16[2,128,384]{2,1,0:T(8,128)(2,1)S(1)}, bf16[2,128,384]{2,1,0:T(8,128)(2,1)S(1)}, u32[]{:S(2)}, u32[]{:S(2)}) collective-permute-start(bf16[2,128,384]{2,1,0:T(8,128)(2,1)S(1)} %get-tuple-element.129), channel_id=1, source_target_pairs={{0,2},{1,9},{2,4},{3,11},{4,6},{5,13},{6,0},{7,15},{8,10},{9,17},{... | collective-permute-start | bytes 589832 | tf_op jit(solution)/shard_map/ppermute | solution.py:40
  45.7 6.4 %collective-permute-start.16 = (bf16[2,128,384]{2,1,0:T(8,128)(2,1)S(1)}, bf16[2,128,384]{2,1,0:T(8,128)(2,1)S(1)}, u32[]{:S(2)}, u32[]{:S(2)}) collective-permute-start(bf16[2,128,384]{2,1,0:T(8,128)(2,1)S(1)} %get-tuple-element.130), channel_id=1, source_target_pairs={{0,6},{1,25},{2,0},{3,27},{4,2},{5,29},{6,4},{7,31},{8,14},{9,1},{... | collective-permute-start | bytes 589832 | tf_op jit(solution)/shard_map/ppermute | solution.py:40
  52.6 8.6 %collective-permute-start.19 = (bf16[4,128,384]{2,1,0:T(8,128)(2,1)S(1)}, bf16[4,128,384]{2,1,0:T(8,128)(2,1)S(1)}, u32[]{:S(2)}, u32[]{:S(2)}) collective-permute-start(bf16[4,128,384]{2,1,0:T(8,128)(2,1)S(1)} %pad_maximum_fusion.1), channel_id=1, source_target_pairs={{0,6},{1,25},{2,0},{3,27},{4,2},{5,29},{6,4},{7,31},{8,14},{9,1},{... | collective-permute-start | bytes 1179656 | tf_op jit(solution)/shard_map/ppermute | solution.py:40
  55.9 9.0 %collective-permute-start.20 = (bf16[4,128,384]{2,1,0:T(8,128)(2,1)S(1)}, bf16[4,128,384]{2,1,0:T(8,128)(2,1)S(1)}, u32[]{:S(2)}, u32[]{:S(2)}) collective-permute-start(bf16[4,128,384]{2,1,0:T(8,128)(2,1)S(1)} %pad_maximum_fusion.2), channel_id=1, source_target_pairs={{0,2},{1,9},{2,4},{3,11},{4,6},{5,13},{6,0},{7,15},{8,10},{9,17},{... | collective-permute-start | bytes 1179656 | tf_op jit(solution)/shard_map/ppermute | solution.py:40
  56.9 8.0 %collective-permute-start.18 = (bf16[4,128,384]{2,1,0:T(8,128)(2,1)S(1)}, bf16[4,128,384]{2,1,0:T(8,128)(2,1)S(1)}, u32[]{:S(2)}, u32[]{:S(2)}) collective-permute-start(bf16[4,128,384]{2,1,0:T(8,128)(2,1)S(1)} %get-tuple-element.98), channel_id=1, source_target_pairs={{0,1},{1,0},{2,3},{3,2},{4,5},{5,4},{6,7},{7,6},{8,9},{9,8},{10,11... | collective-permute-start | bytes 1179656 | tf_op jit(solution)/shard_map/ppermute | solution.py:40
  65.2 6.7 %collective-permute-start.23 = (bf16[128,384]{1,0:T(8,128)(2,1)S(1)}, bf16[128,384]{1,0:T(8,128)(2,1)S(1)}, u32[]{:S(2)}, u32[]{:S(2)}) collective-permute-start(bf16[128,384]{1,0:T(8,128)(2,1)S(1)} %get-tuple-element.126), channel_id=1, source_target_pairs={{0,8},{1,3},{2,10},{3,5},{4,12},{5,7},{6,14},{7,1},{8,16},{9,11},{... | collective-permute-start | bytes 294920 | tf_op jit(solution)/shard_map/ppermute | solution.py:40
  68.0 6.2 %collective-permute-start.22 = (bf16[128,384]{1,0:T(8,128)(2,1)S(1)}, bf16[128,384]{1,0:T(8,128)(2,1)S(1)}, u32[]{:S(2)}, u32[]{:S(2)}) collective-permute-start(bf16[128,384]{1,0:T(8,128)(2,1)S(1)} %get-tuple-element.127), channel_id=1, source_target_pairs={{0,16},{1,5},{2,18},{3,7},{4,20},{5,1},{6,22},{7,3},{8,24},{9,13},... | collective-permute-start | bytes 294920 | tf_op jit(solution)/shard_map/ppermute | solution.py:40
  68.6 6.6 %collective-permute-start.21 = (bf16[128,384]{1,0:T(8,128)(2,1)S(1)}, bf16[128,384]{1,0:T(8,128)(2,1)S(1)}, u32[]{:S(2)}, u32[]{:S(2)}) collective-permute-start(bf16[128,384]{1,0:T(8,128)(2,1)S(1)} %get-tuple-element.128), channel_id=1, source_target_pairs={{0,24},{1,7},{2,26},{3,1},{4,28},{5,3},{6,30},{7,5},{8,0},{9,15},{... | collective-permute-start | bytes 294920 | tf_op jit(solution)/shard_map/ppermute | solution.py:40

commit v7 on v6

--- a/solution.py
+++ b/solution.py
@@ -16,8 +16,8 @@
 UNROLL = 16
 ROWS, LEAD, FIRST, HSLOT, DCOLS, OWNER, GLIVE, DLIVE = range(8)
 
-OTHER = (0, 0, 0, 0, 1, 1, 1, 1)
-STEPS = (0, 1, 3, 2, 0, 1, 3, 2)
+OTHER = (0, 0, 0, 1, 0, 1, 1, 1)
+STEPS = (0, 1, 3, 0, 2, 1, 3, 2)
 
 
 def group(other, j):
@@ -270,6 +270,19 @@
 
     loop(n, UNROLL, back)
     put(acc, dx, staged, sems)
+
+
+def second_kernel(own, other, low, high, back, ahead):
+    half = low.shape[0]
+    for i in range(SIDE):
+        to_back = own[i] + other[i].astype(F32)
+        to_ahead = own[SIDE + i] + other[SIDE + i].astype(F32)
+        if i < half:
+            to_back += low[i].astype(F32)
+        else:
+            to_ahead += high[i - half].astype(F32)
+        back[i] = to_back.astype(BF16)
+        ahead[i] = to_ahead.astype(BF16)
 
 
 def total_kernel(row, one, two, three, grad_gu, grad_down):
@@ -362,22 +375,24 @@
         4,
         far=[x_saved, x_next],
     )
-    back, ahead, near, x_blocks, x_turned = together(back, ahead, near, x_blocks, x_turned)
+    near, x_blocks, x_turned = together(near, x_blocks, x_turned)
+    near_core = core(near)
+    back, ahead, near_core, x_blocks, x_turned = together(back, ahead, near_core, x_blocks, x_turned)
     low, high = send(back[:2], 0, 1), send(ahead[2:], 0, -1)
     tiles, gates = kept((n, B, 3 * B), BF16), kept((n, tok, 2 * B), F32)
     w, acc = call(
-        saved_first_kernel, [tiles, gates], [], [tab], [x_blocks, near, back, ahead], 6
+        saved_first_kernel, [tiles, gates], [], [tab], [x_blocks, near, back, ahead, near_core], 6
     )
     low, high, w, acc = together(low, high, w, acc)
-    more = [low, high, core(near), core(back), core(ahead)]
+    more = [low, high, core(back), core(ahead)]
     w, acc = call(
-        part(saved_more_kernel, CHIPS - SIDE),
+        part(saved_more_kernel, CHIPS),
         [tiles, gates],
         [],
         [tab],
         [x_blocks, *more, w, acc],
         6,
-        aliases={7: 0, 8: 1},
+        aliases={6: 0, 7: 1},
     )
     last = [core(low), core(high)]
     w, acc, coef, h_turned = call(
@@ -426,9 +441,14 @@
         out_space=pltpu.HBM,
     )
     low, high, dx, d_gu = together(low, high, dx, d_gu)
-    both = (own_next + arrived.astype(F32)).reshape(2, SIDE, B, 3 * B)
-    to_back = jnp.concatenate([plus(both[0, :2], low), both[0, 2:].astype(BF16)], axis=0)
-    to_ahead = jnp.concatenate([both[1, :2].astype(BF16), plus(both[1, 2:], high)], axis=0)
+    to_back, to_ahead = call(
+        second_kernel,
+        [kept((SIDE, B, 3 * B), BF16), kept((SIDE, B, 3 * B), BF16)],
+        [],
+        [],
+        [own_next, arrived, low, high],
+        2,
+    )
     to_back, to_ahead, x_late, d_gu = together(to_back, to_ahead, x_late, d_gu)
     from_ahead, from_back = send(to_back, 0, -1), send(to_ahead, 0, 1)
     other_last, own_last = products(d_gu, (group(1, 0), BF16), (group(0, 0), F32))

time: 76 us -> 75.3 us (level)
    pallas_call x14 -> x15, Pallas kernels: 24.9 us -> 25 us  [call(): pl.pallas_call(body, out_shape=outs, in_specs=[pl.BlockSpec(memory_space=...]
  transfers between devices with their start and end apart: 24 -> 24, of which waited for: 12 -> 13; matrix products, arithmetic and copies ran while one was open for 1% -> 1% of each run, Pallas kernels for 27% -> 28%
where the time goes in v7:
time: 75.3 us; the launch traced here: 75.2 us
  starting transfers between devices  26.5 us (35%)
  Pallas kernels  25 us (33%)
  waiting for transfers between devices  21.7 us (29%)
  between operations  0.96 us (1%)
  other arithmetic  0.85 us (1%)
    pallas_call x15, Pallas kernels, call(): pl.pallas_call(body, out_shape=outs, in_specs=[pl.BlockSpec(memory_space=...  25 us
    ppermute x22, starting transfers between devices, send(): return lax.ppermute(value, 'tile', pairs(first, second, core))  22.4 us
    ppermute x22, waiting for transfers between devices, send(): return lax.ppermute(value, 'tile', pairs(first, second, core))  17.8 us
    ppermute x1, waiting for transfers between devices, per_device(): asked = lax.ppermute(down_cols[0].reshape(1, n), 'pipe', up_pairs)  3.9 us
    ppermute x1, starting transfers between devices, per_device(): cot = lax.ppermute(picked, 'pipe', down_pairs)  2.09 us
    ppermute x1, starting transfers between devices, per_device(): asked = lax.ppermute(down_cols[0].reshape(1, n), 'pipe', up_pairs)  1.99 us
  transfers between devices with their start and end apart: 24, of which 13 were waited for; matrix products, arithmetic and copies ran while one was open for 1% of the time, Pallas kernels for 28%

profile of v7, /device:TPU:6, one launch (start us, length us, event | category | flops | bytes accessed | tf_op | source)
XLA Modules:
  0.0 75.2 jit_solution(3073671587524019582)
XLA Ops:
  0.7 2.0 %collective-permute-start = (s32[1,32]{1,0:T(1,128)}, s32[1,32]{1,0:T(1,128)S(1)}, u32[]{:S(2)}, u32[]{:S(2)}) collective-permute-start(s32[1,32]{1,0:T(1,128)} %bitcast.37), channel_id=1, source_target_pairs={{0,32},{32,64},{64,96},{96,128},{128,160},{160,192},{192,224},{224... | collective-permute-start | bytes 392 | tf_op jit(solution)/shard_map/ppermute | solution.py:339
  2.7 1.6 %shard_map.156 = (bf16[3,128,128]{2,1,0:T(8,128)(2,1)S(1)}, bf16[128,8192]{1,0:T(8,128)(2,1)S(1)}) custom-call(bf16[1,1,1,2,128,128]{5,4,3,2,1,0:T(8,128)(2,1)} %gate_up.1, bf16[1,1,1,128,128]{4,3,2,1,0:T(8,128)(2,1)} %down.1, bf16[1,128,8192]{2,1,0:T(8,128)(2,1)} %pending.1), custom_call_target="tpu_custom_call" | custom-call | tf_op jit(solution)/shard_map/pallas_call | solution.py:89
  4.3 3.9 %collective-permute-done.asked = s32[1,32]{1,0:T(1,128)S(1)} collective-permute-done((s32[1,32]{1,0:T(1,128)}, s32[1,32]{1,0:T(1,128)S(1)}, u32[]{:S(2)}, u32[]{:S(2)}) %collective-permute-start) | collective-permute-done | bytes 160 | tf_op jit(solution)/shard_map/ppermute | solution.py:339
  8.2 0.8 %collective-permute-start.3 = (bf16[1,3,128,128]{3,2,1,0:T(8,128)(2,1)S(1)}, bf16[1,3,128,128]{3,2,1,0:T(8,128)(2,1)S(1)}, u32[]{:S(2)}, u32[]{:S(2)}) collective-permute-start(bf16[1,3,128,128]{3,2,1,0:T(8,128)(2,1)S(1)} %bitcast.26), channel_id=1, source_target_pairs={{0,24},{1,7},{2,26},{3,1},{4,28},{5,3},{6,30},{7,5},{8,0},{9,15},{... | collective-permute-start | bytes 294920 | tf_op jit(solution)/shard_map/ppermute | solution.py:40
  9.1 1.1 %collective-permute-start.2 = (bf16[1,3,128,128]{3,2,1,0:T(8,128)(2,1)S(1)}, bf16[1,3,128,128]{3,2,1,0:T(8,128)(2,1)S(1)}, u32[]{:S(2)}, u32[]{:S(2)}) collective-permute-start(bf16[1,3,128,128]{3,2,1,0:T(8,128)(2,1)S(1)} %bitcast.27), channel_id=1, source_target_pairs={{0,16},{1,5},{2,18},{3,7},{4,20},{5,1},{6,22},{7,3},{8,24},{9,13},... | collective-permute-start | bytes 294920 | tf_op jit(solution)/shard_map/ppermute | solution.py:40
  10.2 2.1 %collective-permute-start.1 = (bf16[1,3,128,128]{3,2,1,0:T(8,128)(2,1)S(1)}, bf16[1,3,128,128]{3,2,1,0:T(8,128)(2,1)S(1)}, u32[]{:S(2)}, u32[]{:S(2)}) collective-permute-start(bf16[1,3,128,128]{3,2,1,0:T(8,128)(2,1)S(1)} %bitcast.28), channel_id=1, source_target_pairs={{0,8},{1,3},{2,10},{3,5},{4,12},{5,7},{6,14},{7,1},{8,16},{9,11},{... | collective-permute-start | bytes 294920 | tf_op jit(solution)/shard_map/ppermute | solution.py:40
  12.3 0.8 %shard_map.161 = bf16[32,128,128]{2,1,0:T(8,128)(2,1)S(1)} custom-call(s32[1,32]{1,0:T(1,128)S(1)} %collective-permute-done.asked, bf16[128,8192]{1,0:T(8,128)(2,1)S(1)} %get-tuple-element.92.pending), custom_call_target="tpu_custom_call" | custom-call | tf_op jit(solution)/shard_map/pallas_call | solution.py:89
  13.1 2.1 %collective-permute-start.13 = (bf16[32,128,128]{2,1,0:T(8,128)(2,1)S(1)}, bf16[32,128,128]{2,1,0:T(8,128)(2,1)S(1)}, u32[]{:S(2)}, u32[]{:S(2)}) collective-permute-start(bf16[32,128,128]{2,1,0:T(8,128)(2,1)S(1)} %shard_map.161), channel_id=1, source_target_pairs={{0,224},{32,0},{64,32},{96,64},{128,96},{160,128},{192,160},{224,1... | collective-permute-start | bytes 3145736 | tf_op jit(solution)/shard_map/ppermute | solution.py:355
  15.2 0.7 collective-permute-done.1
  16.0 3.1 %collective-permute-start.5 = (bf16[4,3,128,128]{3,2,1,0:T(8,128)(2,1)S(1)}, bf16[4,3,128,128]{3,2,1,0:T(8,128)(2,1)S(1)}, u32[]{:S(2)}, u32[]{:S(2)}) collective-permute-start(bf16[4,3,128,128]{3,2,1,0:T(8,128)(2,1)S(1)} %pad_maximum_fusion.refs_0_), channel_id=1, source_target_pairs={{0,6},{1,25},{2,0},{3,27},{4,2},{5,29},{6,4},{7,31},{8,14},{9,1},{... | collective-permute-start | bytes 1179656 | tf_op jit(solution)/shard_map/ppermute | solution.py:40
  19.2 0.3 select_reduce_fusion
  19.4 0.2 select_reduce_fusion.3
  19.7 3.3 %shard_map.157 = (bf16[32,128,128]{2,1,0:T(8,128)(2,1)S(1)}, bf16[32,128,128]{2,1,0:T(8,128)(2,1)S(1)}, bf16[128,8192]{1,0:T(8,128)(2,1)S(1)}) custom-call(s32[8,32]{1,0:T(8,128)S(1)} %stack.26.tab, bf16[1,128,8192]{2,1,0:T(8,128)(2,1)} %x_saved.1, bf16[1,128,8192]{2,1,0:T(8,128)(2,1)} %x_next.1), custom_call_target="tpu_custom_call" | custom-call | tf_op jit(solution)/shard_map/pallas_call | solution.py:89
  23.1 1.4 %collective-permute-done.5.refs_2_ = bf16[4,3,128,128]{3,2,1,0:T(8,128)(2,1)S(1)} collective-permute-done((bf16[4,3,128,128]{3,2,1,0:T(8,128)(2,1)S(1)}, bf16[4,3,128,128]{3,2,1,0:T(8,128)(2,1)S(1)}, u32[]{:S(2)}, u32[]{:S(2)}) %collective-permute-start.5) | collective-permute-done | bytes 393248 | tf_op jit(solution)/shard_map/ppermute | solution.py:40
  24.4 3.7 %collective-permute-done.4.refs_1_ = bf16[4,3,128,128]{3,2,1,0:T(8,128)(2,1)S(1)} collective-permute-done((bf16[4,3,128,128]{3,2,1,0:T(8,128)(2,1)S(1)}, bf16[4,3,128,128]{3,2,1,0:T(8,128)(2,1)S(1)}, u32[]{:S(2)}, u32[]{:S(2)}) %collective-permute-start.4) | collective-permute-done | bytes 393248 | tf_op jit(solution)/shard_map/ppermute | solution.py:40
  28.3 2.0 %collective-permute-start.7 = (bf16[2,3,128,128]{3,2,1,0:T(8,128)(2,1)S(1)}, bf16[2,3,128,128]{3,2,1,0:T(8,128)(2,1)S(1)}, u32[]{:S(2)}, u32[]{:S(2)}) collective-permute-start(bf16[2,3,128,128]{3,2,1,0:T(8,128)(2,1)S(1)} %slice.29), channel_id=1, source_target_pairs={{0,2},{1,9},{2,4},{3,11},{4,6},{5,13},{6,0},{7,15},{8,10},{9,17},{... | collective-permute-start | bytes 589832 | tf_op jit(solution)/shard_map/ppermute | solution.py:40
  30.3 0.5 collective-permute-start.12
  30.8 1.3 %shard_map.158 = (bf16[32,128,384]{2,1,0:T(8,128)(2,1)S(1)}, f32[32,128,256]{2,1,0:T(8,128)S(1)}) custom-call(s32[8,32]{1,0:T(8,128)S(1)} %stack.26.tab, bf16[32,128,128]{2,1,0:T(8,128)(2,1)S(1)} %get-tuple-element.76.x, bf16[4,3,128,128]{3,2,1,0:T(8,128)(2,1)S(1)} %pad_maximum_fusion.refs_0_, bf16[4,3,128,128]{3,2,1,0:T(8,128)(2,1)S(1)} %collective-permute-done.4.refs_1_, ...), custom_call_target="tpu_custom_call" | custom-call | tf_op jit(solution)/shard_map/pallas_call | solution.py:89
  32.1 1.8 %collective-permute-done.8.refs_1_ = bf16[2,3,128,128]{3,2,1,0:T(8,128)(2,1)S(1)} collective-permute-done((bf16[2,3,128,128]{3,2,1,0:T(8,128)(2,1)S(1)}, bf16[2,3,128,128]{3,2,1,0:T(8,128)(2,1)S(1)}, u32[]{:S(2)}, u32[]{:S(2)}) %collective-permute-start.8) | collective-permute-done | bytes 196640 | tf_op jit(solution)/shard_map/ppermute | solution.py:40
  33.9 1.3 %collective-permute-done.7.refs_0_ = bf16[2,3,128,128]{3,2,1,0:T(8,128)(2,1)S(1)} collective-permute-done((bf16[2,3,128,128]{3,2,1,0:T(8,128)(2,1)S(1)}, bf16[2,3,128,128]{3,2,1,0:T(8,128)(2,1)S(1)}, u32[]{:S(2)}, u32[]{:S(2)}) %collective-permute-start.7) | collective-permute-done | bytes 196640 | tf_op jit(solution)/shard_map/ppermute | solution.py:40
  35.2 0.5 collective-permute-start.10
  35.7 1.1 %shard_map.159 = (bf16[32,128,384]{2,1,0:T(8,128)(2,1)S(1)}, f32[32,128,256]{2,1,0:T(8,128)S(1)}) custom-call(s32[8,32]{1,0:T(8,128)S(1)} %stack.26.tab, bf16[32,128,128]{2,1,0:T(8,128)(2,1)S(1)} %get-tuple-element.76.x, bf16[2,3,128,128]{3,2,1,0:T(8,128)(2,1)S(1)} %collective-permute-done.7.refs_0_, ...), custom_call_target="tpu_custom_call", output_to_operand_aliasing={{0}: (6, {}), {1}: (7, {})} | custom-call | tf_op jit(solution)/shard_map/pallas_call | solution.py:89
  36.9 2.1 %shard_map.160 = (bf16[32,128,384]{2,1,0:T(8,128)(2,1)S(1)}, f32[32,128,256]{2,1,0:T(8,128)S(1)}, f32[32,128,256]{2,1,0:T(8,128)S(1)}, bf16[33,128,128]{2,1,0:T(8,128)(2,1)S(1)}) custom-call(s32[8,32]{1,0:T(8,128)S(1)} %stack.26.tab, bf16[32,128,128]{2,1,0:T(8,128)(2,1)S(1)} %get-tuple-element.76.x, ...), custom_call_target="tpu_custom_call", output_to_operand_aliasing={{0}: (4, {}), {1}: (5, {})} | custom-call | tf_op jit(solution)/shard_map/pallas_call | solution.py:89
  39.1 2.5 %shard_map.162 = (bf16[4,128,384]{2,1,0:T(8,128)(2,1)S(1)}, bf16[32,128,256]{2,1,0:T(8,128)(2,1)S(1)}) custom-call(s32[8,32]{1,0:T(8,128)S(1)} %stack.26.tab, bf16[32,128,128]{2,1,0:T(8,128)(2,1)S(1)} %get-tuple-element.75.x_turned, bf16[32,128,384]{2,1,0:T(8,128)(2,1)S(1)} %get-tuple-element.89.w, f32[32,128,256]{2,1,0:T(8,128)S(1)} %get-tuple-element.90.coef, ...), custom_call_target="tpu_custom_call" | custom-call | tf_op jit(solution)/shard_map/pallas_call | solution.py:89
  41.5 0.3 collective-permute-start.14
  41.9 1.1 %shard_map.163 = (f32[4,128,384]{2,1,0:T(8,128)S(1)}, f32[8,128,384]{2,1,0:T(8,128)S(1)}) custom-call(s32[8,32]{1,0:T(8,128)S(1)} %stack.26.tab, bf16[32,128,128]{2,1,0:T(8,128)(2,1)S(1)} %get-tuple-element.75.x_turned, bf16[33,128,128]{2,1,0:T(8,128)(2,1)S(1)} %get-tuple-element.88.h_turned, bf16[32,128,256]{2,1,0:T(8,128)(2,1)S(1)} %get-tuple-element.106.d_gu, ...), custom_call_target="tpu_custom_call" | custom-call | tf_op jit(solution)/shard_map/pallas_call | solution.py:89
  42.9 0.4 collective-permute-done.14
  43.4 1.0 %shard_map.164 = bf16[8,128,384]{2,1,0:T(8,128)(2,1)S(1)} custom-call(s32[8,32]{1,0:T(8,128)S(1)} %stack.26.tab, bf16[32,128,128]{2,1,0:T(8,128)(2,1)S(1)} %get-tuple-element.75.x_turned, bf16[33,128,128]{2,1,0:T(8,128)(2,1)S(1)} %get-tuple-element.88.h_turned, bf16[32,128,256]{2,1,0:T(8,128)(2,1)S(1)} %get-tuple-element.106.d_gu, ...), custom_call_target="tpu_custom_call" | custom-call | tf_op jit(solution)/shard_map/pallas_call | solution.py:89
  44.4 0.3 collective-permute-start.15
  44.8 0.8 %collective-permute-start.17 = (bf16[2,128,384]{2,1,0:T(8,128)(2,1)S(1)}, bf16[2,128,384]{2,1,0:T(8,128)(2,1)S(1)}, u32[]{:S(2)}, u32[]{:S(2)}) collective-permute-start(bf16[2,128,384]{2,1,0:T(8,128)(2,1)S(1)} %get-tuple-element.135), channel_id=1, source_target_pairs={{0,2},{1,9},{2,4},{3,11},{4,6},{5,13},{6,0},{7,15},{8,10},{9,17},{... | collective-permute-start | bytes 589832 | tf_op jit(solution)/shard_map/ppermute | solution.py:40
  45.6 2.5 %collective-permute-start.16 = (bf16[2,128,384]{2,1,0:T(8,128)(2,1)S(1)}, bf16[2,128,384]{2,1,0:T(8,128)(2,1)S(1)}, u32[]{:S(2)}, u32[]{:S(2)}) collective-permute-start(bf16[2,128,384]{2,1,0:T(8,128)(2,1)S(1)} %get-tuple-element.136), channel_id=1, source_target_pairs={{0,6},{1,25},{2,0},{3,27},{4,2},{5,29},{6,4},{7,31},{8,14},{9,1},{... | collective-permute-start | bytes 589832 | tf_op jit(solution)/shard_map/ppermute | solution.py:40
  48.1 3.2 %shard_map.165 = bf16[1,128,8192]{2,1,0:T(8,128)(2,1)} custom-call(s32[8,32]{1,0:T(8,128)S(1)} %stack.26.tab, bf16[32,128,256]{2,1,0:T(8,128)(2,1)S(1)} %get-tuple-element.106.d_gu, bf16[32,128,384]{2,1,0:T(8,128)(2,1)S(1)} %get-tuple-element.89.w), custom_call_target="tpu_custom_call" | custom-call | flops 536870912 | bytes 2097152 | tf_op jit(solution)/shard_map/pallas_call | solution.py:89
  51.3 0.4 collective-permute-done.17.high
  51.7 0.2 shard_map.166
  51.9 3.3 %collective-permute-start.19 = (bf16[4,128,384]{2,1,0:T(8,128)(2,1)S(1)}, bf16[4,128,384]{2,1,0:T(8,128)(2,1)S(1)}, u32[]{:S(2)}, u32[]{:S(2)}) collective-permute-start(bf16[4,128,384]{2,1,0:T(8,128)(2,1)S(1)} %get-tuple-element.109), channel_id=1, source_target_pairs={{0,6},{1,25},{2,0},{3,27},{4,2},{5,29},{6,4},{7,31},{8,14},{9,1},{... | collective-permute-start | bytes 1179656 | tf_op jit(solution)/shard_map/ppermute | solution.py:40
  55.2 1.0 %shard_map.167 = (bf16[4,128,384]{2,1,0:T(8,128)(2,1)S(1)}, f32[4,128,384]{2,1,0:T(8,128)S(1)}) custom-call(s32[8,32]{1,0:T(8,128)S(1)} %stack.26.tab, bf16[32,128,128]{2,1,0:T(8,128)(2,1)S(1)} %get-tuple-element.75.x_turned, bf16[33,128,128]{2,1,0:T(8,128)(2,1)S(1)} %get-tuple-element.88.h_turned, bf16[32,128,256]{2,1,0:T(8,128)(2,1)S(1)} %get-tuple-element.106.d_gu, ...), custom_call_target="tpu_custom_call" | custom-call | tf_op jit(solution)/shard_map/pallas_call | solution.py:89
  56.2 1.0 %collective-permute-start.18 = (bf16[4,128,384]{2,1,0:T(8,128)(2,1)S(1)}, bf16[4,128,384]{2,1,0:T(8,128)(2,1)S(1)}, u32[]{:S(2)}, u32[]{:S(2)}) collective-permute-start(bf16[4,128,384]{2,1,0:T(8,128)(2,1)S(1)} %get-tuple-element.108), channel_id=1, source_target_pairs={{0,1},{1,0},{2,3},{3,2},{4,5},{5,4},{6,7},{7,6},{8,9},{9,8},{10,11... | collective-permute-start | bytes 1179656 | tf_op jit(solution)/shard_map/ppermute | solution.py:40
  57.3 2.2 %shard_map.168.h = bf16[33,128,128]{2,1,0:T(8,128)(2,1)S(1)} custom-call(s32[8,32]{1,0:T(8,128)S(1)} %stack.26.tab, bf16[128,8192]{1,0:T(8,128)(2,1)S(1)} %get-tuple-element.111.x, bf16[32,128,384]{2,1,0:T(8,128)(2,1)S(1)} %get-tuple-element.89.w), custom_call_target="tpu_custom_call" | custom-call | flops 536870912 | bytes 2097152 | tf_op jit(solution)/shard_map/pallas_call | solution.py:89
  59.5 1.0 %collective-permute-done.19 = bf16[4,128,384]{2,1,0:T(8,128)(2,1)S(1)} collective-permute-done((bf16[4,128,384]{2,1,0:T(8,128)(2,1)S(1)}, bf16[4,128,384]{2,1,0:T(8,128)(2,1)S(1)}, u32[]{:S(2)}, u32[]{:S(2)}) %collective-permute-start.19) | collective-permute-done | bytes 393248 | tf_op jit(solution)/shard_map/ppermute | solution.py:40
  60.5 3.7 %collective-permute-done.20 = bf16[4,128,384]{2,1,0:T(8,128)(2,1)S(1)} collective-permute-done((bf16[4,128,384]{2,1,0:T(8,128)(2,1)S(1)}, bf16[4,128,384]{2,1,0:T(8,128)(2,1)S(1)}, u32[]{:S(2)}, u32[]{:S(2)}) %collective-permute-start.20) | collective-permute-done | bytes 393248 | tf_op jit(solution)/shard_map/ppermute | solution.py:40
  64.2 0.2 convert_add_fusion
  64.5 2.8 %collective-permute-start.23 = (bf16[128,384]{1,0:T(8,128)(2,1)S(1)}, bf16[128,384]{1,0:T(8,128)(2,1)S(1)}, u32[]{:S(2)}, u32[]{:S(2)}) collective-permute-start(bf16[128,384]{1,0:T(8,128)(2,1)S(1)} %get-tuple-element.132), channel_id=1, source_target_pairs={{0,8},{1,3},{2,10},{3,5},{4,12},{5,7},{6,14},{7,1},{8,16},{9,11},{... | collective-permute-start | bytes 294920 | tf_op jit(solution)/shard_map/ppermute | solution.py:40
  67.3 0.6 collective-permute-start.22
  67.9 0.4 collective-permute-start.21
  68.2 3.0 %shard_map.169 = bf16[1,128,8192]{2,1,0:T(8,128)(2,1)} custom-call(s32[8,32]{1,0:T(8,128)S(1)} %stack.26.tab, bf16[33,128,128]{2,1,0:T(8,128)(2,1)S(1)} %shard_map.168.h, bf16[32,128,384]{2,1,0:T(8,128)(2,1)S(1)} %get-tuple-element.89.w), custom_call_target="tpu_custom_call" | custom-call | flops 536870912 | bytes 2097152 | tf_op jit(solution)/shard_map/pallas_call | solution.py:89
  71.2 2.3 %collective-permute-done.22.two = bf16[128,384]{1,0:T(8,128)(2,1)S(1)} collective-permute-done((bf16[128,384]{1,0:T(8,128)(2,1)S(1)}, bf16[128,384]{1,0:T(8,128)(2,1)S(1)}, u32[]{:S(2)}, u32[]{:S(2)}) %collective-permute-start.22) | collective-permute-done | bytes 98336 | tf_op jit(solution)/shard_map/ppermute | solution.py:40
  73.5 1.0 %collective-permute-done.21.one = bf16[128,384]{1,0:T(8,128)(2,1)S(1)} collective-permute-done((bf16[128,384]{1,0:T(8,128)(2,1)S(1)}, bf16[128,384]{1,0:T(8,128)(2,1)S(1)}, u32[]{:S(2)}, u32[]{:S(2)}) %collective-permute-start.21) | collective-permute-done | bytes 98336 | tf_op jit(solution)/shard_map/ppermute | solution.py:40
  74.4 0.7 shard_map.170
  (46 shorter events, 0.7 us)
Async XLA Ops:
  0.6 11.7 %copy-start = (s32[32]{0:T(128)S(1)}, s32[32]{0:T(128)}, u32[]{:S(2)}) copy-start(s32[32]{0:T(128)} %constant.81.clone) | copy-start | bytes 388
  0.6 11.6 %copy-start.1 = (s32[32]{0:T(128)S(1)}, s32[32]{0:T(128)}, u32[]{:S(2)}) copy-start(s32[32]{0:T(128)} %constant.80.clone) | copy-start | bytes 388
  0.7 7.6 %collective-permute-start = (s32[1,32]{1,0:T(1,128)}, s32[1,32]{1,0:T(1,128)S(1)}, u32[]{:S(2)}, u32[]{:S(2)}) collective-permute-start(s32[1,32]{1,0:T(1,128)} %bitcast.37), channel_id=1, source_target_pairs={{0,32},{32,64},{64,96},{96,128},{128,160},{160,192},{192,224},{224... | collective-permute-start | bytes 392 | tf_op jit(solution)/shard_map/ppermute | solution.py:339
  4.3 14.9 %copy-start.2 = (s32[1,32]{1,0:T(1,128)S(1)}, s32[1,32]{1,0:T(1,128)}, u32[]{:S(2)}) copy-start(s32[1,32]{1,0:T(1,128)} %param.21) | copy-start | bytes 388
  4.3 14.9 %copy-start.3 = (s32[1,32]{1,0:T(1,128)S(1)}, s32[1,32]{1,0:T(1,128)}, u32[]{:S(2)}) copy-start(s32[1,32]{1,0:T(1,128)} %param.18) | copy-start | bytes 388
  4.3 14.8 %copy-start.4 = (s32[1,32,1]{1,2,0:T(1,128)S(1)}, s32[1,32,1]{1,2,0:T(1,128)}, u32[]{:S(2)}) copy-start(s32[1,32,1]{1,2,0:T(1,128)} %param.20) | copy-start | bytes 388
  4.3 14.8 %copy-start.5 = (s32[1,32,1]{1,2,0:T(1,128)S(1)}, s32[1,32,1]{1,2,0:T(1,128)}, u32[]{:S(2)}) copy-start(s32[1,32,1]{1,2,0:T(1,128)} %param.19) | copy-start | bytes 388
  4.3 14.8 %copy-start.6 = (s32[1,32,1]{1,2,0:T(1,128)S(1)}, s32[1,32,1]{1,2,0:T(1,128)}, u32[]{:S(2)}) copy-start(s32[1,32,1]{1,2,0:T(1,128)} %param.17) | copy-start | bytes 388
  4.3 14.8 %copy-start.7 = (s32[1,32,1]{1,2,0:T(1,128)S(1)}, s32[1,32,1]{1,2,0:T(1,128)}, u32[]{:S(2)}) copy-start(s32[1,32,1]{1,2,0:T(1,128)} %param.16) | copy-start | bytes 388
  8.2 7.0 %collective-permute-start.3 = (bf16[1,3,128,128]{3,2,1,0:T(8,128)(2,1)S(1)}, bf16[1,3,128,128]{3,2,1,0:T(8,128)(2,1)S(1)}, u32[]{:S(2)}, u32[]{:S(2)}) collective-permute-start(bf16[1,3,128,128]{3,2,1,0:T(8,128)(2,1)S(1)} %bitcast.26), channel_id=1, source_target_pairs={{0,24},{1,7},{2,26},{3,1},{4,28},{5,3},{6,30},{7,5},{8,0},{9,15},{... | collective-permute-start | bytes 294920 | tf_op jit(solution)/shard_map/ppermute | solution.py:40
  9.1 6.2 %collective-permute-start.2 = (bf16[1,3,128,128]{3,2,1,0:T(8,128)(2,1)S(1)}, bf16[1,3,128,128]{3,2,1,0:T(8,128)(2,1)S(1)}, u32[]{:S(2)}, u32[]{:S(2)}) collective-permute-start(bf16[1,3,128,128]{3,2,1,0:T(8,128)(2,1)S(1)} %bitcast.27), channel_id=1, source_target_pairs={{0,16},{1,5},{2,18},{3,7},{4,20},{5,1},{6,22},{7,3},{8,24},{9,13},... | collective-permute-start | bytes 294920 | tf_op jit(solution)/shard_map/ppermute | solution.py:40
  10.2 5.8 %collective-permute-start.1 = (bf16[1,3,128,128]{3,2,1,0:T(8,128)(2,1)S(1)}, bf16[1,3,128,128]{3,2,1,0:T(8,128)(2,1)S(1)}, u32[]{:S(2)}, u32[]{:S(2)}) collective-permute-start(bf16[1,3,128,128]{3,2,1,0:T(8,128)(2,1)S(1)} %bitcast.28), channel_id=1, source_target_pairs={{0,8},{1,3},{2,10},{3,5},{4,12},{5,7},{6,14},{7,1},{8,16},{9,11},{... | collective-permute-start | bytes 294920 | tf_op jit(solution)/shard_map/ppermute | solution.py:40
  13.1 25.9 %collective-permute-start.13 = (bf16[32,128,128]{2,1,0:T(8,128)(2,1)S(1)}, bf16[32,128,128]{2,1,0:T(8,128)(2,1)S(1)}, u32[]{:S(2)}, u32[]{:S(2)}) collective-permute-start(bf16[32,128,128]{2,1,0:T(8,128)(2,1)S(1)} %shard_map.161), channel_id=1, source_target_pairs={{0,224},{32,0},{64,32},{96,64},{128,96},{160,128},{192,160},{224,1... | collective-permute-start | bytes 3145736 | tf_op jit(solution)/shard_map/ppermute | solution.py:355
  16.0 8.4 %collective-permute-start.5 = (bf16[4,3,128,128]{3,2,1,0:T(8,128)(2,1)S(1)}, bf16[4,3,128,128]{3,2,1,0:T(8,128)(2,1)S(1)}, u32[]{:S(2)}, u32[]{:S(2)}) collective-permute-start(bf16[4,3,128,128]{3,2,1,0:T(8,128)(2,1)S(1)} %pad_maximum_fusion.refs_0_), channel_id=1, source_target_pairs={{0,6},{1,25},{2,0},{3,27},{4,2},{5,29},{6,4},{7,31},{8,14},{9,1},{... | collective-permute-start | bytes 1179656 | tf_op jit(solution)/shard_map/ppermute | solution.py:40
  19.1 9.0 %collective-permute-start.4 = (bf16[4,3,128,128]{3,2,1,0:T(8,128)(2,1)S(1)}, bf16[4,3,128,128]{3,2,1,0:T(8,128)(2,1)S(1)}, u32[]{:S(2)}, u32[]{:S(2)}) collective-permute-start(bf16[4,3,128,128]{3,2,1,0:T(8,128)(2,1)S(1)} %pad_maximum_fusion.refs_0_), channel_id=1, source_target_pairs={{0,2},{1,9},{2,4},{3,11},{4,6},{5,13},{6,0},{7,15},{8,10},{9,17},{... | collective-permute-start | bytes 1179656 | tf_op jit(solution)/shard_map/ppermute | solution.py:40
  23.0 5.2 %collective-permute-start.6 = (bf16[4,3,128,128]{3,2,1,0:T(8,128)(2,1)S(1)}, bf16[4,3,128,128]{3,2,1,0:T(8,128)(2,1)S(1)}, u32[]{:S(2)}, u32[]{:S(2)}) collective-permute-start(bf16[4,3,128,128]{3,2,1,0:T(8,128)(2,1)S(1)} %pad_maximum_fusion.refs_0_), channel_id=1, source_target_pairs={{0,1},{1,0},{2,3},{3,2},{4,5},{5,4},{6,7},{7,6},{8,9},{9,8},{10,11... | collective-permute-start | bytes 1179656 | tf_op jit(solution)/shard_map/ppermute | solution.py:40
  28.2 5.7 %collective-permute-start.8 = (bf16[2,3,128,128]{3,2,1,0:T(8,128)(2,1)S(1)}, bf16[2,3,128,128]{3,2,1,0:T(8,128)(2,1)S(1)}, u32[]{:S(2)}, u32[]{:S(2)}) collective-permute-start(bf16[2,3,128,128]{3,2,1,0:T(8,128)(2,1)S(1)} %slice.30), channel_id=1, source_target_pairs={{0,6},{1,25},{2,0},{3,27},{4,2},{5,29},{6,4},{7,31},{8,14},{9,1},{... | collective-permute-start | bytes 589832 | tf_op jit(solution)/shard_map/ppermute | solution.py:40
  28.3 7.0 %collective-permute-start.7 = (bf16[2,3,128,128]{3,2,1,0:T(8,128)(2,1)S(1)}, bf16[2,3,128,128]{3,2,1,0:T(8,128)(2,1)S(1)}, u32[]{:S(2)}, u32[]{:S(2)}) collective-permute-start(bf16[2,3,128,128]{3,2,1,0:T(8,128)(2,1)S(1)} %slice.29), channel_id=1, source_target_pairs={{0,2},{1,9},{2,4},{3,11},{4,6},{5,13},{6,0},{7,15},{8,10},{9,17},{... | collective-permute-start | bytes 589832 | tf_op jit(solution)/shard_map/ppermute | solution.py:40
  30.3 5.5 %collective-permute-start.11 = (bf16[4,3,128,128]{3,2,1,0:T(8,128)(2,1)S(1)}, bf16[4,3,128,128]{3,2,1,0:T(8,128)(2,1)S(1)}, u32[]{:S(2)}, u32[]{:S(2)}) collective-permute-start(bf16[4,3,128,128]{3,2,1,0:T(8,128)(2,1)S(1)} %collective-permute-done.4.refs_1_), channel_id=1, source_target_pairs={{0,1},{1,0},{2,3},{3,2},{4,5},{5,4},{6,7},{7,6},{8,9},{9,8},{10,11... | collective-permute-start | bytes 1179656 | tf_op jit(solution)/shard_map/ppermute | solution.py:40
  30.3 5.5 %collective-permute-start.12 = (bf16[4,3,128,128]{3,2,1,0:T(8,128)(2,1)S(1)}, bf16[4,3,128,128]{3,2,1,0:T(8,128)(2,1)S(1)}, u32[]{:S(2)}, u32[]{:S(2)}) collective-permute-start(bf16[4,3,128,128]{3,2,1,0:T(8,128)(2,1)S(1)} %collective-permute-done.5.refs_2_), channel_id=1, source_target_pairs={{0,1},{1,0},{2,3},{3,2},{4,5},{5,4},{6,7},{7,6},{8,9},{9,8},{10,11... | collective-permute-start | bytes 1179656 | tf_op jit(solution)/shard_map/ppermute | solution.py:40
  35.2 1.6 %collective-permute-start.9 = (bf16[2,3,128,128]{3,2,1,0:T(8,128)(2,1)S(1)}, bf16[2,3,128,128]{3,2,1,0:T(8,128)(2,1)S(1)}, u32[]{:S(2)}, u32[]{:S(2)}) collective-permute-start(bf16[2,3,128,128]{3,2,1,0:T(8,128)(2,1)S(1)} %collective-permute-done.7.refs_0_), channel_id=1, source_target_pairs={{0,1},{1,0},{2,3},{3,2},{4,5},{5,4},{6,7},{7,6},{8,9},{9,8},{10,11... | collective-permute-start | bytes 589832 | tf_op jit(solution)/shard_map/ppermute | solution.py:40
  35.2 1.7 %collective-permute-start.10 = (bf16[2,3,128,128]{3,2,1,0:T(8,128)(2,1)S(1)}, bf16[2,3,128,128]{3,2,1,0:T(8,128)(2,1)S(1)}, u32[]{:S(2)}, u32[]{:S(2)}) collective-permute-start(bf16[2,3,128,128]{3,2,1,0:T(8,128)(2,1)S(1)} %collective-permute-done.8.refs_1_), channel_id=1, source_target_pairs={{0,1},{1,0},{2,3},{3,2},{4,5},{5,4},{6,7},{7,6},{8,9},{9,8},{10,11... | collective-permute-start | bytes 589832 | tf_op jit(solution)/shard_map/ppermute | solution.py:40
  41.5 1.8 %collective-permute-start.14 = (bf16[4,128,384]{2,1,0:T(8,128)(2,1)S(1)}, bf16[4,128,384]{2,1,0:T(8,128)(2,1)S(1)}, u32[]{:S(2)}, u32[]{:S(2)}) collective-permute-start(bf16[4,128,384]{2,1,0:T(8,128)(2,1)S(1)} %get-tuple-element.95), channel_id=1, source_target_pairs={{0,1},{1,0},{2,3},{3,2},{4,5},{5,4},{6,7},{7,6},{8,9},{9,8},{10,11... | collective-permute-start | bytes 1179656 | tf_op jit(solution)/shard_map/ppermute | solution.py:40
  44.4 7.3 %collective-permute-start.15 = (bf16[8,128,384]{2,1,0:T(8,128)(2,1)S(1)}, bf16[8,128,384]{2,1,0:T(8,128)(2,1)S(1)}, u32[]{:S(2)}, u32[]{:S(2)}) collective-permute-start(bf16[8,128,384]{2,1,0:T(8,128)(2,1)S(1)} %shard_map.164), channel_id=1, source_target_pairs={{0,1},{1,0},{2,3},{3,2},{4,5},{5,4},{6,7},{7,6},{8,9},{9,8},{10,11... | collective-permute-start | bytes 2359304 | tf_op jit(solution)/shard_map/ppermute | solution.py:40
  44.8 7.0 %collective-permute-start.17 = (bf16[2,128,384]{2,1,0:T(8,128)(2,1)S(1)}, bf16[2,128,384]{2,1,0:T(8,128)(2,1)S(1)}, u32[]{:S(2)}, u32[]{:S(2)}) collective-permute-start(bf16[2,128,384]{2,1,0:T(8,128)(2,1)S(1)} %get-tuple-element.135), channel_id=1, source_target_pairs={{0,2},{1,9},{2,4},{3,11},{4,6},{5,13},{6,0},{7,15},{8,10},{9,17},{... | collective-permute-start | bytes 589832 | tf_op jit(solution)/shard_map/ppermute | solution.py:40
  45.6 6.2 %collective-permute-start.16 = (bf16[2,128,384]{2,1,0:T(8,128)(2,1)S(1)}, bf16[2,128,384]{2,1,0:T(8,128)(2,1)S(1)}, u32[]{:S(2)}, u32[]{:S(2)}) collective-permute-start(bf16[2,128,384]{2,1,0:T(8,128)(2,1)S(1)} %get-tuple-element.136), channel_id=1, source_target_pairs={{0,6},{1,25},{2,0},{3,27},{4,2},{5,29},{6,4},{7,31},{8,14},{9,1},{... | collective-permute-start | bytes 589832 | tf_op jit(solution)/shard_map/ppermute | solution.py:40
  51.9 8.6 %collective-permute-start.19 = (bf16[4,128,384]{2,1,0:T(8,128)(2,1)S(1)}, bf16[4,128,384]{2,1,0:T(8,128)(2,1)S(1)}, u32[]{:S(2)}, u32[]{:S(2)}) collective-permute-start(bf16[4,128,384]{2,1,0:T(8,128)(2,1)S(1)} %get-tuple-element.109), channel_id=1, source_target_pairs={{0,6},{1,25},{2,0},{3,27},{4,2},{5,29},{6,4},{7,31},{8,14},{9,1},{... | collective-permute-start | bytes 1179656 | tf_op jit(solution)/shard_map/ppermute | solution.py:40
  55.2 9.0 %collective-permute-start.20 = (bf16[4,128,384]{2,1,0:T(8,128)(2,1)S(1)}, bf16[4,128,384]{2,1,0:T(8,128)(2,1)S(1)}, u32[]{:S(2)}, u32[]{:S(2)}) collective-permute-start(bf16[4,128,384]{2,1,0:T(8,128)(2,1)S(1)} %get-tuple-element.110), channel_id=1, source_target_pairs={{0,2},{1,9},{2,4},{3,11},{4,6},{5,13},{6,0},{7,15},{8,10},{9,17},{... | collective-permute-start | bytes 1179656 | tf_op jit(solution)/shard_map/ppermute | solution.py:40
  56.2 8.0 %collective-permute-start.18 = (bf16[4,128,384]{2,1,0:T(8,128)(2,1)S(1)}, bf16[4,128,384]{2,1,0:T(8,128)(2,1)S(1)}, u32[]{:S(2)}, u32[]{:S(2)}) collective-permute-start(bf16[4,128,384]{2,1,0:T(8,128)(2,1)S(1)} %get-tuple-element.108), channel_id=1, source_target_pairs={{0,1},{1,0},{2,3},{3,2},{4,5},{5,4},{6,7},{7,6},{8,9},{9,8},{10,11... | collective-permute-start | bytes 1179656 | tf_op jit(solution)/shard_map/ppermute | solution.py:40
  64.5 6.7 %collective-permute-start.23 = (bf16[128,384]{1,0:T(8,128)(2,1)S(1)}, bf16[128,384]{1,0:T(8,128)(2,1)S(1)}, u32[]{:S(2)}, u32[]{:S(2)}) collective-permute-start(bf16[128,384]{1,0:T(8,128)(2,1)S(1)} %get-tuple-element.132), channel_id=1, source_target_pairs={{0,8},{1,3},{2,10},{3,5},{4,12},{5,7},{6,14},{7,1},{8,16},{9,11},{... | collective-permute-start | bytes 294920 | tf_op jit(solution)/shard_map/ppermute | solution.py:40
  67.3 6.2 %collective-permute-start.22 = (bf16[128,384]{1,0:T(8,128)(2,1)S(1)}, bf16[128,384]{1,0:T(8,128)(2,1)S(1)}, u32[]{:S(2)}, u32[]{:S(2)}) collective-permute-start(bf16[128,384]{1,0:T(8,128)(2,1)S(1)} %get-tuple-element.133), channel_id=1, source_target_pairs={{0,16},{1,5},{2,18},{3,7},{4,20},{5,1},{6,22},{7,3},{8,24},{9,13},... | collective-permute-start | bytes 294920 | tf_op jit(solution)/shard_map/ppermute | solution.py:40
  67.9 6.6 %collective-permute-start.21 = (bf16[128,384]{1,0:T(8,128)(2,1)S(1)}, bf16[128,384]{1,0:T(8,128)(2,1)S(1)}, u32[]{:S(2)}, u32[]{:S(2)}) collective-permute-start(bf16[128,384]{1,0:T(8,128)(2,1)S(1)} %get-tuple-element.134), channel_id=1, source_target_pairs={{0,24},{1,7},{2,26},{3,1},{4,28},{5,3},{6,30},{7,5},{8,0},{9,15},{... | collective-permute-start | bytes 294920 | tf_op jit(solution)/shard_map/ppermute | solution.py:40

commit v8 on v7

--- a/solution.py
+++ b/solution.py
@@ -107,12 +107,19 @@
     return [pltpu.make_async_copy(source.at[0, r], out.at[r], sems.at[q]) for q, r in enumerate(rows)]
 
 
-def pack_kernel(gate_up, down, pending, out, held, sems, row_sems):
+def pack_kernel(gate_up, down, out, sems):
     copies = [
         pltpu.make_async_copy(gate_up.at[0, 0, 0], out.at[pl.ds(0, 2)], sems.at[0]),
         pltpu.make_async_copy(down.at[0, 0, 0], out.at[2], sems.at[1]),
-        *row_copies(pending, held, row_sems),
     ]
+    for copy in copies:
+        copy.start()
+    for copy in copies:
+        copy.wait()
+
+
+def fetch_kernel(source, out, sems):
+    copies = row_copies(source, out, sems)
     for copy in copies:
         copy.start()
     for copy in copies:
@@ -338,17 +345,18 @@
     down_pairs = [(s, (s - 1) % sections) for s in range(sections)]
     asked = lax.ppermute(down_cols[0].reshape(1, n), "pipe", up_pairs)
     rows, sems = kept((tok, width), BF16), pltpu.SemaphoreType.DMA
-    own, held_back = call(
+    [own] = call(
         pack_kernel,
-        [kept((3, B, B), BF16), rows],
-        [sems((2,)), sems((8,))],
+        [kept((3, B, B), BF16)],
+        [sems((2,))],
         [],
         [],
         2,
-        far=[gate_up_tiles, down_tiles, pending],
-    )
-    own, asked = together(own[None], asked)
+        far=[gate_up_tiles, down_tiles],
+    )
+    own = own[None]
     one, three, two = send(own, 1, 0), send(own, -1, 0), send(own, 2, 0)
+    [held_back] = call(fetch_kernel, [rows], [sems((8,))], [], [], 2, far=[pending])
     [picked] = call(
         part(pick_kernel, n), [kept((n, tok, B), BF16)], [], [asked], [held_back], 2
     )

time: 75.3 us -> 72.9 us (0.968)
  the two profiles are of different devices: /device:TPU:6 before, /device:TPU:96 now
where the time goes in v8:
time: 72.9 us; the launch traced here: 72.8 us
  Pallas kernels  25.8 us (35%)
  starting transfers between devices  24.9 us (34%)
  waiting for transfers between devices  19.4 us (27%)
  other arithmetic  1.52 us (2%)
  between operations  0.98 us (1%)
    pallas_call x16, Pallas kernels, call(): pl.pallas_call(body, out_shape=outs, in_specs=[pl.BlockSpec(memory_space=...  25.8 us
    ppermute x22, starting transfers between devices, send(): return lax.ppermute(value, 'tile', pairs(first, second, core))  21.7 us
    ppermute x22, waiting for transfers between devices, send(): return lax.ppermute(value, 'tile', pairs(first, second, core))  15 us
    ppermute x1, waiting for transfers between devices, per_device(): cot = lax.ppermute(picked, 'pipe', down_pairs)  4.35 us
    ppermute x1, starting transfers between devices, per_device(): asked = lax.ppermute(down_cols[0].reshape(1, n), 'pipe', up_pairs)  3.13 us
  transfers between devices with their start and end apart: 24, of which 13 were waited for; matrix products, arithmetic and copies ran while one was open for 2% of the time, Pallas kernels for 28%

profile of v8, /device:TPU:96, one launch (start us, length us, event | category | flops | bytes accessed | tf_op | source)
XLA Modules:
  0.0 72.8 jit_solution(17348627948920280119)
XLA Ops:
  0.6 0.9 %shard_map.156 = bf16[3,128,128]{2,1,0:T(8,128)(2,1)S(1)} custom-call(bf16[1,1,1,2,128,128]{5,4,3,2,1,0:T(8,128)(2,1)} %gate_up.1, bf16[1,1,1,128,128]{4,3,2,1,0:T(8,128)(2,1)} %down.1), custom_call_target="tpu_custom_call" | custom-call | tf_op jit(solution)/shard_map/pallas_call | solution.py:89
  1.5 2.8 %collective-permute-start.2 = (bf16[1,3,128,128]{3,2,1,0:T(8,128)(2,1)S(1)}, bf16[1,3,128,128]{3,2,1,0:T(8,128)(2,1)S(1)}, u32[]{:S(2)}, u32[]{:S(2)}) collective-permute-start(bf16[1,3,128,128]{3,2,1,0:T(8,128)(2,1)S(1)} %bitcast.26), channel_id=1, source_target_pairs={{0,24},{1,7},{2,26},{3,1},{4,28},{5,3},{6,30},{7,5},{8,0},{9,15},{... | collective-permute-start | bytes 294920 | tf_op jit(solution)/shard_map/ppermute | solution.py:40
  4.3 0.8 %collective-permute-start.1 = (bf16[1,3,128,128]{3,2,1,0:T(8,128)(2,1)S(1)}, bf16[1,3,128,128]{3,2,1,0:T(8,128)(2,1)S(1)}, u32[]{:S(2)}, u32[]{:S(2)}) collective-permute-start(bf16[1,3,128,128]{3,2,1,0:T(8,128)(2,1)S(1)} %bitcast.27), channel_id=1, source_target_pairs={{0,16},{1,5},{2,18},{3,7},{4,20},{5,1},{6,22},{7,3},{8,24},{9,13},... | collective-permute-start | bytes 294920 | tf_op jit(solution)/shard_map/ppermute | solution.py:40
  5.1 0.9 %collective-permute-start = (bf16[1,3,128,128]{3,2,1,0:T(8,128)(2,1)S(1)}, bf16[1,3,128,128]{3,2,1,0:T(8,128)(2,1)S(1)}, u32[]{:S(2)}, u32[]{:S(2)}) collective-permute-start(bf16[1,3,128,128]{3,2,1,0:T(8,128)(2,1)S(1)} %bitcast.28), channel_id=1, source_target_pairs={{0,8},{1,3},{2,10},{3,5},{4,12},{5,7},{6,14},{7,1},{8,16},{9,11},{... | collective-permute-start | bytes 294920 | tf_op jit(solution)/shard_map/ppermute | solution.py:40
  6.0 3.1 %collective-permute-start.12 = (s32[1,32]{1,0:T(1,128)}, s32[1,32]{1,0:T(1,128)S(1)}, u32[]{:S(2)}, u32[]{:S(2)}) collective-permute-start(s32[1,32]{1,0:T(1,128)} %bitcast.37), channel_id=1, source_target_pairs={{0,32},{32,64},{64,96},{96,128},{128,160},{160,192},{192,224},{224... | collective-permute-start | bytes 392 | tf_op jit(solution)/shard_map/ppermute | solution.py:346
  9.2 0.7 multiply_add_fusion
  9.8 1.6 %shard_map.161.pending = bf16[128,8192]{1,0:T(8,128)(2,1)S(1)} custom-call(bf16[1,128,8192]{2,1,0:T(8,128)(2,1)} %source.1), custom_call_target="tpu_custom_call" | custom-call | tf_op jit(solution)/shard_map/pallas_call | solution.py:89
  11.5 0.8 %shard_map.162 = bf16[32,128,128]{2,1,0:T(8,128)(2,1)S(1)} custom-call(s32[1,32]{1,0:T(1,128)S(1)} %collective-permute-done.12.asked, bf16[128,8192]{1,0:T(8,128)(2,1)S(1)} %shard_map.161.pending), custom_call_target="tpu_custom_call" | custom-call | tf_op jit(solution)/shard_map/pallas_call | solution.py:89
  12.5 1.7 %collective-permute-start.3 = (bf16[4,3,128,128]{3,2,1,0:T(8,128)(2,1)S(1)}, bf16[4,3,128,128]{3,2,1,0:T(8,128)(2,1)S(1)}, u32[]{:S(2)}, u32[]{:S(2)}) collective-permute-start(bf16[4,3,128,128]{3,2,1,0:T(8,128)(2,1)S(1)} %pad_maximum_fusion.refs_0_), channel_id=1, source_target_pairs={{0,2},{1,9},{2,4},{3,11},{4,6},{5,13},{6,0},{7,15},{8,10},{9,17},{... | collective-permute-start | bytes 1179656 | tf_op jit(solution)/shard_map/ppermute | solution.py:40
  14.2 1.7 %collective-permute-start.4 = (bf16[4,3,128,128]{3,2,1,0:T(8,128)(2,1)S(1)}, bf16[4,3,128,128]{3,2,1,0:T(8,128)(2,1)S(1)}, u32[]{:S(2)}, u32[]{:S(2)}) collective-permute-start(bf16[4,3,128,128]{3,2,1,0:T(8,128)(2,1)S(1)} %pad_maximum_fusion.refs_0_), channel_id=1, source_target_pairs={{0,6},{1,25},{2,0},{3,27},{4,2},{5,29},{6,4},{7,31},{8,14},{9,1},{... | collective-permute-start | bytes 1179656 | tf_op jit(solution)/shard_map/ppermute | solution.py:40
  15.9 0.3 select_reduce_fusion
  16.1 0.2 select_reduce_fusion.3
  16.4 3.3 %shard_map.157 = (bf16[32,128,128]{2,1,0:T(8,128)(2,1)S(1)}, bf16[32,128,128]{2,1,0:T(8,128)(2,1)S(1)}, bf16[128,8192]{1,0:T(8,128)(2,1)S(1)}) custom-call(s32[8,32]{1,0:T(8,128)S(1)} %stack.26.tab, bf16[1,128,8192]{2,1,0:T(8,128)(2,1)} %x_saved.1, bf16[1,128,8192]{2,1,0:T(8,128)(2,1)} %x_next.1), custom_call_target="tpu_custom_call" | custom-call | tf_op jit(solution)/shard_map/pallas_call | solution.py:89
  19.7 1.8 %collective-permute-done.3.refs_1_ = bf16[4,3,128,128]{3,2,1,0:T(8,128)(2,1)S(1)} collective-permute-done((bf16[4,3,128,128]{3,2,1,0:T(8,128)(2,1)S(1)}, bf16[4,3,128,128]{3,2,1,0:T(8,128)(2,1)S(1)}, u32[]{:S(2)}, u32[]{:S(2)}) %collective-permute-start.3) | collective-permute-done | bytes 393248 | tf_op jit(solution)/shard_map/ppermute | solution.py:40
  21.6 0.4 collective-permute-done.4.refs_2_
  22.0 1.7 %collective-permute-start.6 = (bf16[2,3,128,128]{3,2,1,0:T(8,128)(2,1)S(1)}, bf16[2,3,128,128]{3,2,1,0:T(8,128)(2,1)S(1)}, u32[]{:S(2)}, u32[]{:S(2)}) collective-permute-start(bf16[2,3,128,128]{3,2,1,0:T(8,128)(2,1)S(1)} %slice.29), channel_id=1, source_target_pairs={{0,2},{1,9},{2,4},{3,11},{4,6},{5,13},{6,0},{7,15},{8,10},{9,17},{... | collective-permute-start | bytes 589832 | tf_op jit(solution)/shard_map/ppermute | solution.py:40
  23.6 1.7 %collective-permute-start.7 = (bf16[2,3,128,128]{3,2,1,0:T(8,128)(2,1)S(1)}, bf16[2,3,128,128]{3,2,1,0:T(8,128)(2,1)S(1)}, u32[]{:S(2)}, u32[]{:S(2)}) collective-permute-start(bf16[2,3,128,128]{3,2,1,0:T(8,128)(2,1)S(1)} %slice.30), channel_id=1, source_target_pairs={{0,6},{1,25},{2,0},{3,27},{4,2},{5,29},{6,4},{7,31},{8,14},{9,1},{... | collective-permute-start | bytes 589832 | tf_op jit(solution)/shard_map/ppermute | solution.py:40
  25.4 0.5 collective-permute-start.11
  25.9 1.3 %shard_map.158 = (bf16[32,128,384]{2,1,0:T(8,128)(2,1)S(1)}, f32[32,128,256]{2,1,0:T(8,128)S(1)}) custom-call(s32[8,32]{1,0:T(8,128)S(1)} %stack.26.tab, bf16[32,128,128]{2,1,0:T(8,128)(2,1)S(1)} %get-tuple-element.70.x, bf16[4,3,128,128]{3,2,1,0:T(8,128)(2,1)S(1)} %pad_maximum_fusion.refs_0_, bf16[4,3,128,128]{3,2,1,0:T(8,128)(2,1)S(1)} %collective-permute-done.3.refs_1_, ...), custom_call_target="tpu_custom_call" | custom-call | tf_op jit(solution)/shard_map/pallas_call | solution.py:89
  27.2 1.7 %collective-permute-done.6.refs_0_ = bf16[2,3,128,128]{3,2,1,0:T(8,128)(2,1)S(1)} collective-permute-done((bf16[2,3,128,128]{3,2,1,0:T(8,128)(2,1)S(1)}, bf16[2,3,128,128]{3,2,1,0:T(8,128)(2,1)S(1)}, u32[]{:S(2)}, u32[]{:S(2)}) %collective-permute-start.6) | collective-permute-done | bytes 196640 | tf_op jit(solution)/shard_map/ppermute | solution.py:40
  28.9 0.5 collective-permute-done.7.refs_1_
  29.4 0.5 collective-permute-start.9
  29.9 1.1 %shard_map.159 = (bf16[32,128,384]{2,1,0:T(8,128)(2,1)S(1)}, f32[32,128,256]{2,1,0:T(8,128)S(1)}) custom-call(s32[8,32]{1,0:T(8,128)S(1)} %stack.26.tab, bf16[32,128,128]{2,1,0:T(8,128)(2,1)S(1)} %get-tuple-element.70.x, bf16[2,3,128,128]{3,2,1,0:T(8,128)(2,1)S(1)} %collective-permute-done.6.refs_0_, ...), custom_call_target="tpu_custom_call", output_to_operand_aliasing={{0}: (6, {}), {1}: (7, {})} | custom-call | tf_op jit(solution)/shard_map/pallas_call | solution.py:89
  31.1 2.1 %shard_map.160 = (bf16[32,128,384]{2,1,0:T(8,128)(2,1)S(1)}, f32[32,128,256]{2,1,0:T(8,128)S(1)}, f32[32,128,256]{2,1,0:T(8,128)S(1)}, bf16[33,128,128]{2,1,0:T(8,128)(2,1)S(1)}) custom-call(s32[8,32]{1,0:T(8,128)S(1)} %stack.26.tab, bf16[32,128,128]{2,1,0:T(8,128)(2,1)S(1)} %get-tuple-element.70.x, ...), custom_call_target="tpu_custom_call", output_to_operand_aliasing={{0}: (4, {}), {1}: (5, {})} | custom-call | tf_op jit(solution)/shard_map/pallas_call | solution.py:89
  33.2 4.4 %collective-permute-done.13.cot = bf16[32,128,128]{2,1,0:T(8,128)(2,1)S(1)} collective-permute-done((bf16[32,128,128]{2,1,0:T(8,128)(2,1)S(1)}, bf16[32,128,128]{2,1,0:T(8,128)(2,1)S(1)}, u32[]{:S(2)}, u32[]{:S(2)}) %collective-permute-start.13) | collective-permute-done | bytes 1048608 | tf_op jit(solution)/shard_map/ppermute | solution.py:363
  37.6 2.5 %shard_map.163 = (bf16[4,128,384]{2,1,0:T(8,128)(2,1)S(1)}, bf16[32,128,256]{2,1,0:T(8,128)(2,1)S(1)}) custom-call(s32[8,32]{1,0:T(8,128)S(1)} %stack.26.tab, bf16[32,128,128]{2,1,0:T(8,128)(2,1)S(1)} %get-tuple-element.69.x_turned, bf16[32,128,384]{2,1,0:T(8,128)(2,1)S(1)} %get-tuple-element.83.w, f32[32,128,256]{2,1,0:T(8,128)S(1)} %get-tuple-element.84.coef, ...), custom_call_target="tpu_custom_call" | custom-call | tf_op jit(solution)/shard_map/pallas_call | solution.py:89
  40.1 1.1 %shard_map.164 = (f32[4,128,384]{2,1,0:T(8,128)S(1)}, f32[8,128,384]{2,1,0:T(8,128)S(1)}) custom-call(s32[8,32]{1,0:T(8,128)S(1)} %stack.26.tab, bf16[32,128,128]{2,1,0:T(8,128)(2,1)S(1)} %get-tuple-element.69.x_turned, bf16[33,128,128]{2,1,0:T(8,128)(2,1)S(1)} %get-tuple-element.82.h_turned, bf16[32,128,256]{2,1,0:T(8,128)(2,1)S(1)} %get-tuple-element.98.d_gu, ...), custom_call_target="tpu_custom_call" | custom-call | tf_op jit(solution)/shard_map/pallas_call | solution.py:89
  41.2 0.6 collective-permute-done.14
  41.9 1.0 %shard_map.165 = bf16[8,128,384]{2,1,0:T(8,128)(2,1)S(1)} custom-call(s32[8,32]{1,0:T(8,128)S(1)} %stack.26.tab, bf16[32,128,128]{2,1,0:T(8,128)(2,1)S(1)} %get-tuple-element.69.x_turned, bf16[33,128,128]{2,1,0:T(8,128)(2,1)S(1)} %get-tuple-element.82.h_turned, bf16[32,128,256]{2,1,0:T(8,128)(2,1)S(1)} %get-tuple-element.98.d_gu, ...), custom_call_target="tpu_custom_call" | custom-call | tf_op jit(solution)/shard_map/pallas_call | solution.py:89
  42.9 0.2 collective-permute-start.15
  43.2 2.4 %collective-permute-start.16 = (bf16[2,128,384]{2,1,0:T(8,128)(2,1)S(1)}, bf16[2,128,384]{2,1,0:T(8,128)(2,1)S(1)}, u32[]{:S(2)}, u32[]{:S(2)}) collective-permute-start(bf16[2,128,384]{2,1,0:T(8,128)(2,1)S(1)} %get-tuple-element.128), channel_id=1, source_target_pairs={{0,6},{1,25},{2,0},{3,27},{4,2},{5,29},{6,4},{7,31},{8,14},{9,1},{... | collective-permute-start | bytes 589832 | tf_op jit(solution)/shard_map/ppermute | solution.py:40
  45.5 3.2 %shard_map.166 = bf16[1,128,8192]{2,1,0:T(8,128)(2,1)} custom-call(s32[8,32]{1,0:T(8,128)S(1)} %stack.26.tab, bf16[32,128,256]{2,1,0:T(8,128)(2,1)S(1)} %get-tuple-element.98.d_gu, bf16[32,128,384]{2,1,0:T(8,128)(2,1)S(1)} %get-tuple-element.83.w), custom_call_target="tpu_custom_call" | custom-call | flops 536870912 | bytes 2097152 | tf_op jit(solution)/shard_map/pallas_call | solution.py:89
  48.8 0.2 collective-permute-done.16.low
  48.9 3.5 %collective-permute-done.17.high = bf16[2,128,384]{2,1,0:T(8,128)(2,1)S(1)} collective-permute-done((bf16[2,128,384]{2,1,0:T(8,128)(2,1)S(1)}, bf16[2,128,384]{2,1,0:T(8,128)(2,1)S(1)}, u32[]{:S(2)}, u32[]{:S(2)}) %collective-permute-start.17) | collective-permute-done | bytes 196640 | tf_op jit(solution)/shard_map/ppermute | solution.py:40
  52.4 0.2 shard_map.167
  52.7 2.0 %collective-permute-start.20 = (bf16[4,128,384]{2,1,0:T(8,128)(2,1)S(1)}, bf16[4,128,384]{2,1,0:T(8,128)(2,1)S(1)}, u32[]{:S(2)}, u32[]{:S(2)}) collective-permute-start(bf16[4,128,384]{2,1,0:T(8,128)(2,1)S(1)} %get-tuple-element.102), channel_id=1, source_target_pairs={{0,2},{1,9},{2,4},{3,11},{4,6},{5,13},{6,0},{7,15},{8,10},{9,17},{... | collective-permute-start | bytes 1179656 | tf_op jit(solution)/shard_map/ppermute | solution.py:40
  54.7 1.0 %shard_map.168 = (bf16[4,128,384]{2,1,0:T(8,128)(2,1)S(1)}, f32[4,128,384]{2,1,0:T(8,128)S(1)}) custom-call(s32[8,32]{1,0:T(8,128)S(1)} %stack.26.tab, bf16[32,128,128]{2,1,0:T(8,128)(2,1)S(1)} %get-tuple-element.69.x_turned, bf16[33,128,128]{2,1,0:T(8,128)(2,1)S(1)} %get-tuple-element.82.h_turned, bf16[32,128,256]{2,1,0:T(8,128)(2,1)S(1)} %get-tuple-element.98.d_gu, ...), custom_call_target="tpu_custom_call" | custom-call | tf_op jit(solution)/shard_map/pallas_call | solution.py:89
  55.8 2.2 %shard_map.169.h = bf16[33,128,128]{2,1,0:T(8,128)(2,1)S(1)} custom-call(s32[8,32]{1,0:T(8,128)S(1)} %stack.26.tab, bf16[128,8192]{1,0:T(8,128)(2,1)S(1)} %get-tuple-element.103.x, bf16[32,128,384]{2,1,0:T(8,128)(2,1)S(1)} %get-tuple-element.83.w), custom_call_target="tpu_custom_call" | custom-call | flops 536870912 | bytes 2097152 | tf_op jit(solution)/shard_map/pallas_call | solution.py:89
  58.0 2.4 %collective-permute-done.19 = bf16[4,128,384]{2,1,0:T(8,128)(2,1)S(1)} collective-permute-done((bf16[4,128,384]{2,1,0:T(8,128)(2,1)S(1)}, bf16[4,128,384]{2,1,0:T(8,128)(2,1)S(1)}, u32[]{:S(2)}, u32[]{:S(2)}) %collective-permute-start.19) | collective-permute-done | bytes 393248 | tf_op jit(solution)/shard_map/ppermute | solution.py:40
  60.5 1.3 %collective-permute-done.20 = bf16[4,128,384]{2,1,0:T(8,128)(2,1)S(1)} collective-permute-done((bf16[4,128,384]{2,1,0:T(8,128)(2,1)S(1)}, bf16[4,128,384]{2,1,0:T(8,128)(2,1)S(1)}, u32[]{:S(2)}, u32[]{:S(2)}) %collective-permute-start.20) | collective-permute-done | bytes 393248 | tf_op jit(solution)/shard_map/ppermute | solution.py:40
  61.8 0.2 convert_add_fusion
  62.1 2.8 %collective-permute-start.21 = (bf16[128,384]{1,0:T(8,128)(2,1)S(1)}, bf16[128,384]{1,0:T(8,128)(2,1)S(1)}, u32[]{:S(2)}, u32[]{:S(2)}) collective-permute-start(bf16[128,384]{1,0:T(8,128)(2,1)S(1)} %get-tuple-element.126), channel_id=1, source_target_pairs={{0,24},{1,7},{2,26},{3,1},{4,28},{5,3},{6,30},{7,5},{8,0},{9,15},{... | collective-permute-start | bytes 294920 | tf_op jit(solution)/shard_map/ppermute | solution.py:40
  64.9 0.8 %collective-permute-start.22 = (bf16[128,384]{1,0:T(8,128)(2,1)S(1)}, bf16[128,384]{1,0:T(8,128)(2,1)S(1)}, u32[]{:S(2)}, u32[]{:S(2)}) collective-permute-start(bf16[128,384]{1,0:T(8,128)(2,1)S(1)} %get-tuple-element.125), channel_id=1, source_target_pairs={{0,16},{1,5},{2,18},{3,7},{4,20},{5,1},{6,22},{7,3},{8,24},{9,13},... | collective-permute-start | bytes 294920 | tf_op jit(solution)/shard_map/ppermute | solution.py:40
  65.7 0.9 %collective-permute-start.23 = (bf16[128,384]{1,0:T(8,128)(2,1)S(1)}, bf16[128,384]{1,0:T(8,128)(2,1)S(1)}, u32[]{:S(2)}, u32[]{:S(2)}) collective-permute-start(bf16[128,384]{1,0:T(8,128)(2,1)S(1)} %get-tuple-element.124), channel_id=1, source_target_pairs={{0,8},{1,3},{2,10},{3,5},{4,12},{5,7},{6,14},{7,1},{8,16},{9,11},{... | collective-permute-start | bytes 294920 | tf_op jit(solution)/shard_map/ppermute | solution.py:40
  66.6 3.0 %shard_map.170 = bf16[1,128,8192]{2,1,0:T(8,128)(2,1)} custom-call(s32[8,32]{1,0:T(8,128)S(1)} %stack.26.tab, bf16[33,128,128]{2,1,0:T(8,128)(2,1)S(1)} %shard_map.169.h, bf16[32,128,384]{2,1,0:T(8,128)(2,1)S(1)} %get-tuple-element.83.w), custom_call_target="tpu_custom_call" | custom-call | flops 536870912 | bytes 2097152 | tf_op jit(solution)/shard_map/pallas_call | solution.py:89
  69.6 1.5 %collective-permute-done.22.two = bf16[128,384]{1,0:T(8,128)(2,1)S(1)} collective-permute-done((bf16[128,384]{1,0:T(8,128)(2,1)S(1)}, bf16[128,384]{1,0:T(8,128)(2,1)S(1)}, u32[]{:S(2)}, u32[]{:S(2)}) %collective-permute-start.22) | collective-permute-done | bytes 98336 | tf_op jit(solution)/shard_map/ppermute | solution.py:40
  71.1 1.0 %collective-permute-done.23.three = bf16[128,384]{1,0:T(8,128)(2,1)S(1)} collective-permute-done((bf16[128,384]{1,0:T(8,128)(2,1)S(1)}, bf16[128,384]{1,0:T(8,128)(2,1)S(1)}, u32[]{:S(2)}, u32[]{:S(2)}) %collective-permute-start.23) | collective-permute-done | bytes 98336 | tf_op jit(solution)/shard_map/ppermute | solution.py:40
  72.1 0.7 shard_map.171
  (43 shorter events, 0.9 us)
Async XLA Ops:
  1.5 10.9 %collective-permute-start.2 = (bf16[1,3,128,128]{3,2,1,0:T(8,128)(2,1)S(1)}, bf16[1,3,128,128]{3,2,1,0:T(8,128)(2,1)S(1)}, u32[]{:S(2)}, u32[]{:S(2)}) collective-permute-start(bf16[1,3,128,128]{3,2,1,0:T(8,128)(2,1)S(1)} %bitcast.26), channel_id=1, source_target_pairs={{0,24},{1,7},{2,26},{3,1},{4,28},{5,3},{6,30},{7,5},{8,0},{9,15},{... | collective-permute-start | bytes 294920 | tf_op jit(solution)/shard_map/ppermute | solution.py:40
  4.3 8.1 %collective-permute-start.1 = (bf16[1,3,128,128]{3,2,1,0:T(8,128)(2,1)S(1)}, bf16[1,3,128,128]{3,2,1,0:T(8,128)(2,1)S(1)}, u32[]{:S(2)}, u32[]{:S(2)}) collective-permute-start(bf16[1,3,128,128]{3,2,1,0:T(8,128)(2,1)S(1)} %bitcast.27), channel_id=1, source_target_pairs={{0,16},{1,5},{2,18},{3,7},{4,20},{5,1},{6,22},{7,3},{8,24},{9,13},... | collective-permute-start | bytes 294920 | tf_op jit(solution)/shard_map/ppermute | solution.py:40
  5.1 7.3 %collective-permute-start = (bf16[1,3,128,128]{3,2,1,0:T(8,128)(2,1)S(1)}, bf16[1,3,128,128]{3,2,1,0:T(8,128)(2,1)S(1)}, u32[]{:S(2)}, u32[]{:S(2)}) collective-permute-start(bf16[1,3,128,128]{3,2,1,0:T(8,128)(2,1)S(1)} %bitcast.28), channel_id=1, source_target_pairs={{0,8},{1,3},{2,10},{3,5},{4,12},{5,7},{6,14},{7,1},{8,16},{9,11},{... | collective-permute-start | bytes 294920 | tf_op jit(solution)/shard_map/ppermute | solution.py:40
  6.0 5.5 %collective-permute-start.12 = (s32[1,32]{1,0:T(1,128)}, s32[1,32]{1,0:T(1,128)S(1)}, u32[]{:S(2)}, u32[]{:S(2)}) collective-permute-start(s32[1,32]{1,0:T(1,128)} %bitcast.37), channel_id=1, source_target_pairs={{0,32},{32,64},{64,96},{96,128},{128,160},{160,192},{192,224},{224... | collective-permute-start | bytes 392 | tf_op jit(solution)/shard_map/ppermute | solution.py:346
  11.4 4.4 %copy-start = (s32[1,32]{1,0:T(1,128)S(1)}, s32[1,32]{1,0:T(1,128)}, u32[]{:S(2)}) copy-start(s32[1,32]{1,0:T(1,128)} %param.21) | copy-start | bytes 388
  11.4 4.4 %copy-start.1 = (s32[1,32]{1,0:T(1,128)S(1)}, s32[1,32]{1,0:T(1,128)}, u32[]{:S(2)}) copy-start(s32[1,32]{1,0:T(1,128)} %param.18) | copy-start | bytes 388
  11.5 4.4 %copy-start.2 = (s32[1,32,1]{1,2,0:T(1,128)S(1)}, s32[1,32,1]{1,2,0:T(1,128)}, u32[]{:S(2)}) copy-start(s32[1,32,1]{1,2,0:T(1,128)} %param.20) | copy-start | bytes 388
  11.5 4.4 %copy-start.3 = (s32[1,32,1]{1,2,0:T(1,128)S(1)}, s32[1,32,1]{1,2,0:T(1,128)}, u32[]{:S(2)}) copy-start(s32[1,32,1]{1,2,0:T(1,128)} %param.19) | copy-start | bytes 388
  11.5 4.4 %copy-start.4 = (s32[1,32,1]{1,2,0:T(1,128)S(1)}, s32[1,32,1]{1,2,0:T(1,128)}, u32[]{:S(2)}) copy-start(s32[1,32,1]{1,2,0:T(1,128)} %param.17) | copy-start | bytes 388
  11.5 4.4 %copy-start.5 = (s32[1,32,1]{1,2,0:T(1,128)S(1)}, s32[1,32,1]{1,2,0:T(1,128)}, u32[]{:S(2)}) copy-start(s32[1,32,1]{1,2,0:T(1,128)} %param.16) | copy-start | bytes 388
  12.3 25.2 %collective-permute-start.13 = (bf16[32,128,128]{2,1,0:T(8,128)(2,1)S(1)}, bf16[32,128,128]{2,1,0:T(8,128)(2,1)S(1)}, u32[]{:S(2)}, u32[]{:S(2)}) collective-permute-start(bf16[32,128,128]{2,1,0:T(8,128)(2,1)S(1)} %shard_map.162), channel_id=1, source_target_pairs={{0,224},{32,0},{64,32},{96,64},{128,96},{160,128},{192,160},{224,1... | collective-permute-start | bytes 3145736 | tf_op jit(solution)/shard_map/ppermute | solution.py:363
  12.5 9.1 %collective-permute-start.3 = (bf16[4,3,128,128]{3,2,1,0:T(8,128)(2,1)S(1)}, bf16[4,3,128,128]{3,2,1,0:T(8,128)(2,1)S(1)}, u32[]{:S(2)}, u32[]{:S(2)}) collective-permute-start(bf16[4,3,128,128]{3,2,1,0:T(8,128)(2,1)S(1)} %pad_maximum_fusion.refs_0_), channel_id=1, source_target_pairs={{0,2},{1,9},{2,4},{3,11},{4,6},{5,13},{6,0},{7,15},{8,10},{9,17},{... | collective-permute-start | bytes 1179656 | tf_op jit(solution)/shard_map/ppermute | solution.py:40
  14.2 7.8 %collective-permute-start.4 = (bf16[4,3,128,128]{3,2,1,0:T(8,128)(2,1)S(1)}, bf16[4,3,128,128]{3,2,1,0:T(8,128)(2,1)S(1)}, u32[]{:S(2)}, u32[]{:S(2)}) collective-permute-start(bf16[4,3,128,128]{3,2,1,0:T(8,128)(2,1)S(1)} %pad_maximum_fusion.refs_0_), channel_id=1, source_target_pairs={{0,6},{1,25},{2,0},{3,27},{4,2},{5,29},{6,4},{7,31},{8,14},{9,1},{... | collective-permute-start | bytes 1179656 | tf_op jit(solution)/shard_map/ppermute | solution.py:40
  19.6 2.3 %collective-permute-start.5 = (bf16[4,3,128,128]{3,2,1,0:T(8,128)(2,1)S(1)}, bf16[4,3,128,128]{3,2,1,0:T(8,128)(2,1)S(1)}, u32[]{:S(2)}, u32[]{:S(2)}) collective-permute-start(bf16[4,3,128,128]{3,2,1,0:T(8,128)(2,1)S(1)} %pad_maximum_fusion.refs_0_), channel_id=1, source_target_pairs={{0,1},{1,0},{2,3},{3,2},{4,5},{5,4},{6,7},{7,6},{8,9},{9,8},{10,11... | collective-permute-start | bytes 1179656 | tf_op jit(solution)/shard_map/ppermute | solution.py:40
  22.0 7.0 %collective-permute-start.6 = (bf16[2,3,128,128]{3,2,1,0:T(8,128)(2,1)S(1)}, bf16[2,3,128,128]{3,2,1,0:T(8,128)(2,1)S(1)}, u32[]{:S(2)}, u32[]{:S(2)}) collective-permute-start(bf16[2,3,128,128]{3,2,1,0:T(8,128)(2,1)S(1)} %slice.29), channel_id=1, source_target_pairs={{0,2},{1,9},{2,4},{3,11},{4,6},{5,13},{6,0},{7,15},{8,10},{9,17},{... | collective-permute-start | bytes 589832 | tf_op jit(solution)/shard_map/ppermute | solution.py:40
  23.6 5.7 %collective-permute-start.7 = (bf16[2,3,128,128]{3,2,1,0:T(8,128)(2,1)S(1)}, bf16[2,3,128,128]{3,2,1,0:T(8,128)(2,1)S(1)}, u32[]{:S(2)}, u32[]{:S(2)}) collective-permute-start(bf16[2,3,128,128]{3,2,1,0:T(8,128)(2,1)S(1)} %slice.30), channel_id=1, source_target_pairs={{0,6},{1,25},{2,0},{3,27},{4,2},{5,29},{6,4},{7,31},{8,14},{9,1},{... | collective-permute-start | bytes 589832 | tf_op jit(solution)/shard_map/ppermute | solution.py:40
  25.4 4.5 %collective-permute-start.10 = (bf16[4,3,128,128]{3,2,1,0:T(8,128)(2,1)S(1)}, bf16[4,3,128,128]{3,2,1,0:T(8,128)(2,1)S(1)}, u32[]{:S(2)}, u32[]{:S(2)}) collective-permute-start(bf16[4,3,128,128]{3,2,1,0:T(8,128)(2,1)S(1)} %collective-permute-done.3.refs_1_), channel_id=1, source_target_pairs={{0,1},{1,0},{2,3},{3,2},{4,5},{5,4},{6,7},{7,6},{8,9},{9,8},{10,11... | collective-permute-start | bytes 1179656 | tf_op jit(solution)/shard_map/ppermute | solution.py:40
  25.4 4.5 %collective-permute-start.11 = (bf16[4,3,128,128]{3,2,1,0:T(8,128)(2,1)S(1)}, bf16[4,3,128,128]{3,2,1,0:T(8,128)(2,1)S(1)}, u32[]{:S(2)}, u32[]{:S(2)}) collective-permute-start(bf16[4,3,128,128]{3,2,1,0:T(8,128)(2,1)S(1)} %collective-permute-done.4.refs_2_), channel_id=1, source_target_pairs={{0,1},{1,0},{2,3},{3,2},{4,5},{5,4},{6,7},{7,6},{8,9},{9,8},{10,11... | collective-permute-start | bytes 1179656 | tf_op jit(solution)/shard_map/ppermute | solution.py:40
  29.4 1.6 %collective-permute-start.8 = (bf16[2,3,128,128]{3,2,1,0:T(8,128)(2,1)S(1)}, bf16[2,3,128,128]{3,2,1,0:T(8,128)(2,1)S(1)}, u32[]{:S(2)}, u32[]{:S(2)}) collective-permute-start(bf16[2,3,128,128]{3,2,1,0:T(8,128)(2,1)S(1)} %collective-permute-done.6.refs_0_), channel_id=1, source_target_pairs={{0,1},{1,0},{2,3},{3,2},{4,5},{5,4},{6,7},{7,6},{8,9},{9,8},{10,11... | collective-permute-start | bytes 589832 | tf_op jit(solution)/shard_map/ppermute | solution.py:40
  29.4 1.7 %collective-permute-start.9 = (bf16[2,3,128,128]{3,2,1,0:T(8,128)(2,1)S(1)}, bf16[2,3,128,128]{3,2,1,0:T(8,128)(2,1)S(1)}, u32[]{:S(2)}, u32[]{:S(2)}) collective-permute-start(bf16[2,3,128,128]{3,2,1,0:T(8,128)(2,1)S(1)} %collective-permute-done.7.refs_1_), channel_id=1, source_target_pairs={{0,1},{1,0},{2,3},{3,2},{4,5},{5,4},{6,7},{7,6},{8,9},{9,8},{10,11... | collective-permute-start | bytes 589832 | tf_op jit(solution)/shard_map/ppermute | solution.py:40
  40.0 1.8 %collective-permute-start.14 = (bf16[4,128,384]{2,1,0:T(8,128)(2,1)S(1)}, bf16[4,128,384]{2,1,0:T(8,128)(2,1)S(1)}, u32[]{:S(2)}, u32[]{:S(2)}) collective-permute-start(bf16[4,128,384]{2,1,0:T(8,128)(2,1)S(1)} %get-tuple-element.87), channel_id=1, source_target_pairs={{0,1},{1,0},{2,3},{3,2},{4,5},{5,4},{6,7},{7,6},{8,9},{9,8},{10,11... | collective-permute-start | bytes 1179656 | tf_op jit(solution)/shard_map/ppermute | solution.py:40
  42.9 9.5 %collective-permute-start.15 = (bf16[8,128,384]{2,1,0:T(8,128)(2,1)S(1)}, bf16[8,128,384]{2,1,0:T(8,128)(2,1)S(1)}, u32[]{:S(2)}, u32[]{:S(2)}) collective-permute-start(bf16[8,128,384]{2,1,0:T(8,128)(2,1)S(1)} %shard_map.165), channel_id=1, source_target_pairs={{0,1},{1,0},{2,3},{3,2},{4,5},{5,4},{6,7},{7,6},{8,9},{9,8},{10,11... | collective-permute-start | bytes 2359304 | tf_op jit(solution)/shard_map/ppermute | solution.py:40
  43.2 5.7 %collective-permute-start.16 = (bf16[2,128,384]{2,1,0:T(8,128)(2,1)S(1)}, bf16[2,128,384]{2,1,0:T(8,128)(2,1)S(1)}, u32[]{:S(2)}, u32[]{:S(2)}) collective-permute-start(bf16[2,128,384]{2,1,0:T(8,128)(2,1)S(1)} %get-tuple-element.128), channel_id=1, source_target_pairs={{0,6},{1,25},{2,0},{3,27},{4,2},{5,29},{6,4},{7,31},{8,14},{9,1},{... | collective-permute-start | bytes 589832 | tf_op jit(solution)/shard_map/ppermute | solution.py:40
  45.5 6.9 %collective-permute-start.17 = (bf16[2,128,384]{2,1,0:T(8,128)(2,1)S(1)}, bf16[2,128,384]{2,1,0:T(8,128)(2,1)S(1)}, u32[]{:S(2)}, u32[]{:S(2)}) collective-permute-start(bf16[2,128,384]{2,1,0:T(8,128)(2,1)S(1)} %get-tuple-element.127), channel_id=1, source_target_pairs={{0,2},{1,9},{2,4},{3,11},{4,6},{5,13},{6,0},{7,15},{8,10},{9,17},{... | collective-permute-start | bytes 589832 | tf_op jit(solution)/shard_map/ppermute | solution.py:40
  52.6 7.9 %collective-permute-start.19 = (bf16[4,128,384]{2,1,0:T(8,128)(2,1)S(1)}, bf16[4,128,384]{2,1,0:T(8,128)(2,1)S(1)}, u32[]{:S(2)}, u32[]{:S(2)}) collective-permute-start(bf16[4,128,384]{2,1,0:T(8,128)(2,1)S(1)} %get-tuple-element.101), channel_id=1, source_target_pairs={{0,6},{1,25},{2,0},{3,27},{4,2},{5,29},{6,4},{7,31},{8,14},{9,1},{... | collective-permute-start | bytes 1179656 | tf_op jit(solution)/shard_map/ppermute | solution.py:40
  52.7 9.1 %collective-permute-start.20 = (bf16[4,128,384]{2,1,0:T(8,128)(2,1)S(1)}, bf16[4,128,384]{2,1,0:T(8,128)(2,1)S(1)}, u32[]{:S(2)}, u32[]{:S(2)}) collective-permute-start(bf16[4,128,384]{2,1,0:T(8,128)(2,1)S(1)} %get-tuple-element.102), channel_id=1, source_target_pairs={{0,2},{1,9},{2,4},{3,11},{4,6},{5,13},{6,0},{7,15},{8,10},{9,17},{... | collective-permute-start | bytes 1179656 | tf_op jit(solution)/shard_map/ppermute | solution.py:40
  55.7 6.1 %collective-permute-start.18 = (bf16[4,128,384]{2,1,0:T(8,128)(2,1)S(1)}, bf16[4,128,384]{2,1,0:T(8,128)(2,1)S(1)}, u32[]{:S(2)}, u32[]{:S(2)}) collective-permute-start(bf16[4,128,384]{2,1,0:T(8,128)(2,1)S(1)} %get-tuple-element.100), channel_id=1, source_target_pairs={{0,1},{1,0},{2,3},{3,2},{4,5},{5,4},{6,7},{7,6},{8,9},{9,8},{10,11... | collective-permute-start | bytes 1179656 | tf_op jit(solution)/shard_map/ppermute | solution.py:40
  62.1 7.5 %collective-permute-start.21 = (bf16[128,384]{1,0:T(8,128)(2,1)S(1)}, bf16[128,384]{1,0:T(8,128)(2,1)S(1)}, u32[]{:S(2)}, u32[]{:S(2)}) collective-permute-start(bf16[128,384]{1,0:T(8,128)(2,1)S(1)} %get-tuple-element.126), channel_id=1, source_target_pairs={{0,24},{1,7},{2,26},{3,1},{4,28},{5,3},{6,30},{7,5},{8,0},{9,15},{... | collective-permute-start | bytes 294920 | tf_op jit(solution)/shard_map/ppermute | solution.py:40
  64.9 6.2 %collective-permute-start.22 = (bf16[128,384]{1,0:T(8,128)(2,1)S(1)}, bf16[128,384]{1,0:T(8,128)(2,1)S(1)}, u32[]{:S(2)}, u32[]{:S(2)}) collective-permute-start(bf16[128,384]{1,0:T(8,128)(2,1)S(1)} %get-tuple-element.125), channel_id=1, source_target_pairs={{0,16},{1,5},{2,18},{3,7},{4,20},{5,1},{6,22},{7,3},{8,24},{9,13},... | collective-permute-start | bytes 294920 | tf_op jit(solution)/shard_map/ppermute | solution.py:40
  65.7 6.4 %collective-permute-start.23 = (bf16[128,384]{1,0:T(8,128)(2,1)S(1)}, bf16[128,384]{1,0:T(8,128)(2,1)S(1)}, u32[]{:S(2)}, u32[]{:S(2)}) collective-permute-start(bf16[128,384]{1,0:T(8,128)(2,1)S(1)} %get-tuple-element.124), channel_id=1, source_target_pairs={{0,8},{1,3},{2,10},{3,5},{4,12},{5,7},{6,14},{7,1},{8,16},{9,11},{... | collective-permute-start | bytes 294920 | tf_op jit(solution)/shard_map/ppermute | solution.py:40
